TPU v7x, 128 devices: a whole 4x4x4 slice. The times are simulated.
128 devices in a mesh: dp: 16 (over y, z), tensor: 8 (over x, core).
Axes of the slice: x: 4, y: 4, z: 4, core: 2. Of those that a mesh axis runs over, the one named last changes fastest.
Arguments:
- activations: bfloat16 [16384, 6144], P(('dp', 'tensor')), may hold values from -6 to 6
- cotangent: bfloat16 [16384, 3072], P('dp', 'tensor'), may hold values from -6 to 6
- weight: bfloat16 [6144, 3072], P(None, 'tensor'), may hold values from -0.109375 to 0.109375
- residual: bfloat16 [16, 6144, 3072], P('dp', None, 'tensor'), may hold values from -4 to 4
- warm_factor: float32 [3072, 32], P('tensor'), may hold values from -6 to 6
Outputs:
- new_factor: float32 [3072, 32], P('tensor')
- new_residual: bfloat16 [16, 6144, 3072], P('dp', None, 'tensor')
- input_grads: bfloat16 [16384, 6144], P(('dp', 'tensor'))
All inputs are finite; a program needn't handle non-finite values.
Results may differ from a plain program's by a relative error of at most 0.001.
Values may be sent and summed in bfloat16 or wider, within the bound.
No kernel may reach another device: no remote copies, remote signals or barrier semaphores. Data moves between devices by JAX's collectives and lax.ppermute only.
A program may use at most 128 MiB of HBM per device.

v0:
```python
import jax
import jax.numpy as jnp
from jax import lax
from jax.sharding import PartitionSpec as P


def gram_schmidt(matrix):
    result = jnp.zeros_like(matrix)
    for column in range(matrix.shape[1]):
        vector = matrix[:, column]
        projection = jnp.dot(result.T, vector, precision=lax.Precision.HIGHEST)
        vector = vector - jnp.dot(result, projection, precision=lax.Precision.HIGHEST)
        vector = vector / jnp.sqrt(jnp.sum(vector * vector))
        result = result.at[:, column].set(vector)
    return result


def per_device(activations, cotangent, weight, residual, warm_factor):
    token_scale = cotangent.shape[0] ** (-0.5)
    cot_rows = cotangent
    gradient = lax.dot_general(
        lax.all_gather(activations, "tensor", axis=0, tiled=True),
        cot_rows,
        (((0,), (0,)), ((), ())),
        preferred_element_type=jnp.float32,
    )
    merged = gradient * token_scale + residual[0].astype(jnp.float32)
    partial_left = jnp.dot(merged, warm_factor, precision=lax.Precision.HIGHEST)
    left = lax.psum(partial_left, ("dp", "tensor"))
    basis_full = gram_schmidt(left)
    right_part = jnp.dot(merged.T, basis_full, precision=lax.Precision.HIGHEST)
    new_factor = lax.psum(right_part, "dp") / lax.axis_size("dp")
    approx = jnp.dot(basis_full, new_factor.T, precision=lax.Precision.HIGHEST)
    new_residual = (merged - approx).astype(jnp.bfloat16)[None]
    cot_rows = cotangent
    input_grads = lax.psum_scatter(
        lax.dot_general(
            cot_rows, weight, (((1,), (1,)), ((), ())), preferred_element_type=jnp.float32
        ),
        "tensor",
        scatter_dimension=0,
        tiled=True,
    ).astype(jnp.bfloat16)
    return (new_factor, new_residual, input_grads)


def solution(mesh):
    in_specs = (
        P(("dp", "tensor"), None),
        P("dp", "tensor"),
        P(None, "tensor"),
        P("dp", None, "tensor"),
        P("tensor", None),
    )
    out_specs = (P("tensor", None), P("dp", None, "tensor"), P(("dp", "tensor"), None))
    return jax.shard_map(
        per_device, mesh=mesh, in_specs=in_specs, out_specs=out_specs, check_vma=False
    )
```

profile of v0, /device:TPU:0, one launch (start us, length us, event | category | flops | bytes accessed | tf_op | source)
XLA Modules:
  0.0 484.2 jit_solution(15779368432241691753)
XLA Ops:
  8.0 71.5 %all-gather.2.cloned.1.call-done = bf16[1024,6144]{1,0:T(8,128)(2,1)} async-done(((bf16[128,6144]{1,0:T(8,128)(2,1)}), bf16[1024,6144]{1,0:T(8,128)(2,1)}) %all-gather.2.cloned.1.call-update) | async-done | bytes 12582928 | tf_op jit(solution)/shard_map/all_gather | solution.py:22
  79.5 10.5 %convert_add_fusion = f32[6144,384]{1,0:T(8,128)S(1)} fusion(bf16[1024,6144]{1,0:T(8,128)(2,1)} %all-gather.2.cloned.1.call-done, bf16[1024,384]{1,0:T(8,128)(2,1)S(1)} %copy-done, bf16[1,6144,384]{2,1,0:T(8,128)(2,1)} %param.72), kind=kOutput, calls=%fused_computation | convolution fusion | flops 4838916096 | bytes 27525120 | tf_op jit(solution)/shard_map/dot_general | solution.py:21
  90.0 3.6 copy-done.2
  93.6 9.9 %fusion.74 = f32[6144,32]{0,1:T(8,128)} fusion(f32[6144,384]{1,0:T(8,128)S(1)} %convert_add_fusion, f32[384,32]{0,1:T(8,128)S(1)} %copy-done.5), kind=kOutput, calls=%fused_computation.234 | convolution fusion | flops 905969664 | bytes 10272768 | tf_op jit(solution)/shard_map/dot_general | solution.py:28
  103.7 14.1 %fusion.106 = f32[1024,6144]{1,0:T(8,128)} fusion(bf16[1024,384]{1,0:T(8,128)(2,1)S(1)} %copy-done, bf16[6144,384]{1,0:T(8,128)(2,1)} %param.71), kind=kOutput, calls=%fused_computation.266 | convolution fusion | flops 4831838208 | bytes 30670848 | tf_op jit(solution)/shard_map/dot_general | solution.py:37
  118.5 0.7 compare_reduce_fusion.29
  121.2 0.7 compare_reduce_fusion.25
  122.5 0.7 compare_reduce_fusion.23
  126.5 0.7 compare_reduce_fusion.17
  129.2 0.7 compare_reduce_fusion.13
  132.0 0.7 compare_reduce_fusion.9
  132.7 0.7 compare_reduce_fusion.8
  134.1 0.7 compare_reduce_fusion.6
  136.3 0.7 compare_reduce_fusion.3
  137.7 0.7 compare_reduce_fusion.1
  139.1 111.7 %all-reduce.3.cloned.1.call-done = f32[6144,32]{0,1:T(8,128)} async-done(((f32[6144,32]{0,1:T(8,128)}), f32[6144,32]{0,1:T(8,128)}) %all-reduce.3.cloned.1.call-update) | async-done | bytes 786448 | tf_op jit(solution)/shard_map/psum | solution.py:29
  250.8 2.6 fusion.73
  253.4 1.2 fusion.36
  257.2 1.5 convolution_bitcast_fusion.30
  261.7 1.6 convolution_bitcast_fusion.29
  266.4 1.7 convolution_bitcast_fusion.28
  271.2 1.6 convolution_bitcast_fusion.27
  275.9 1.6 convolution_bitcast_fusion.26
  279.4 0.7 broadcast_select_fusion.25
  280.8 0.7 convolution_bitcast_fusion.25
  284.0 1.0 scatter.116
  285.0 0.7 convolution_bitcast_fusion.24
  287.6 0.7 broadcast_select_fusion.23
  288.9 0.7 convolution_bitcast_fusion.23
  292.7 0.7 convolution_bitcast_fusion.22
  296.5 0.7 convolution_bitcast_fusion.21
  300.3 0.7 convolution_bitcast_fusion.20
  304.1 0.7 convolution_bitcast_fusion.19
  307.9 0.7 convolution_bitcast_fusion.18
  310.8 0.7 broadcast_select_fusion.17
  312.2 0.7 convolution_bitcast_fusion.17
  315.9 0.7 convolution_bitcast_fusion.16
  319.2 0.8 scatter.131
  320.0 0.7 convolution_bitcast_fusion.15
  323.8 0.7 convolution_bitcast_fusion.14
  326.4 0.7 broadcast_select_fusion.13
  327.7 0.7 convolution_bitcast_fusion.13
  331.6 0.7 convolution_bitcast_fusion.12
  335.4 0.7 convolution_bitcast_fusion.11
  339.2 0.7 convolution_bitcast_fusion.10
  341.8 0.7 broadcast_select_fusion.9
  343.1 0.7 convolution_bitcast_fusion.9
  345.7 0.7 broadcast_select_fusion.8
  347.1 0.7 convolution_bitcast_fusion.8
  350.9 0.7 convolution_bitcast_fusion.7
  354.2 0.8 scatter.146
  355.0 0.7 convolution_bitcast_fusion.6
  358.8 0.7 convolution_bitcast_fusion.5
  362.7 0.7 convolution_bitcast_fusion.4
  365.3 0.7 broadcast_select_fusion.3
  366.6 0.7 convolution_bitcast_fusion.3
  370.4 0.7 convolution_bitcast_fusion.2
  373.0 0.7 broadcast_select_fusion.1
  374.3 0.7 convolution_bitcast_fusion.1
  378.1 0.7 convolution_bitcast_fusion
  381.3 7.8 %fusion.105 = f32[384,32]{0,1:T(8,128)S(1)} fusion(f32[6144,384]{1,0:T(8,128)} %copy-done.2, f32[6144,32]{0,1:T(8,128)S(1)} %scatter.159), kind=kOutput, calls=%fused_computation.265 | convolution fusion | flops 905969664 | bytes 10272768 | tf_op jit(solution)/shard_map/dot_general | solution.py:31
  389.2 73.4 %psum.15 = f32[384,32]{0,1:T(8,128)S(1)} all-reduce(f32[384,32]{0,1:T(8,128)S(1)} %fusion.105), channel_id=1, replica_groups=mesh['dp'=16,'tensor'=8] {'dp'}, use_global_device_ids=true, to_apply=%region_64.0 | all-reduce | flops 12288 | bytes 98304 | tf_op jit(solution)/shard_map/psum | solution.py:32
  462.6 11.4 %fusion = bf16[1,6144,384]{2,1,0:T(8,128)(2,1)} fusion(f32[6144,384]{1,0:T(8,128)} %copy-done.2, f32[6144,32]{0,1:T(8,128)S(1)} %scatter.159, f32[384,32]{0,1:T(8,128)S(1)} %broadcast_multiply_fusion), kind=kOutput, calls=%fused_computation.2 | convolution fusion | flops 910688256 | bytes 14991360 | tf_op jit(solution)/shard_map/dot_general | solution.py:33
  474.0 3.2 convert_element_type.15
  (187 shorter events, 83.8 us)
Async XLA Ops:
  7.2 72.3 %copy-start = (bf16[1024,384]{1,0:T(8,128)(2,1)S(1)}, bf16[1024,384]{1,0:T(8,128)(2,1)}, u32[]{:S(2)}) copy-start(bf16[1024,384]{1,0:T(8,128)(2,1)} %param.70) | copy-start | bytes 2359300
  7.2 72.3 %all-gather.2.cloned.1.call-start = ((), (), s32[]{:S(2)}) async-start(), calls=%async_computation.1 | async-start | bytes 14155776 | tf_op jit(solution)/shard_map/all_gather | solution.py:22
  7.9 85.7 %copy-start.5 = (f32[384,32]{0,1:T(8,128)S(1)}, f32[384,32]{0,1:T(8,128)}, u32[]{:S(2)}) copy-start(f32[384,32]{0,1:T(8,128)} %param.73) | copy-start | bytes 147460
  7.9 242.8 %all-reduce.3.cloned.1.call-start = ((), (), s32[]{:S(2)}) async-start(), calls=%async_computation.2 | async-start | bytes 1572864 | tf_op jit(solution)/shard_map/psum | solution.py:29
  90.0 3.6 copy-start.2
  103.5 370.6 %reduce-scatter.2.cloned.1.call-start = ((), (), s32[]{:S(2)}) async-start(), calls=%async_computation.3 | async-start | bytes 28311552 | tf_op jit(solution)/shard_map/reduce_scatter | solution.py:36
  250.8 30.0 %copy-start.3 = (f32[6144,32]{0,1:T(8,128)S(1)}, f32[6144,32]{0,1:T(8,128)}, u32[]{:S(2)}) copy-start(f32[6144,32]{0,1:T(8,128)} %all-reduce.3.cloned.1.call-done) | copy-start | bytes 2359300
  462.6 14.7 %copy-start.1 = (bf16[1024,384]{1,0:T(8,128)(2,1)S(1)}, bf16[1024,384]{1,0:T(8,128)(2,1)}, u32[]{:S(2)}) copy-start(bf16[1024,384]{1,0:T(8,128)(2,1)} %param.70) | copy-start | bytes 2359300
  462.6 14.7 %copy-start.4 = (f32[384,32]{0,1:T(8,128)}, f32[384,32]{0,1:T(8,128)S(1)}, u32[]{:S(2)}) copy-start(f32[384,32]{0,1:T(8,128)S(1)} %broadcast_multiply_fusion) | copy-start | bytes 147460
Sparse Core Ops, SparseCore 0:
  9.7 69.7 all-gather.1
  103.6 147.1 all-reduce.2
  253.2 129.3 reduce-scatter.1
where the time goes:
time: 493 us; the launch traced here: 484 us
  waiting for transfers between devices  184 us (37%)
  matrix products  98.2 us (20%)
  blocking collectives  73.4 us (15%)
  other arithmetic  65 us (13%)
  between operations  37.3 us (8%)
  local copies, waits for them, and re-layouts  26.1 us (5%)
    psum x1, waiting for transfers between devices, per_device(): left = lax.psum(partial_left, ('dp', 'tensor'))  112 us
    psum x1, blocking collectives, per_device(): new_factor = lax.psum(right_part, 'dp') / lax.axis_size('dp')  73.4 us
    all_gather x1, waiting for transfers between devices, per_device(): lax.all_gather(activations, 'tensor', axis=0, tiled=True)  71.5 us
    another operation x62, other arithmetic  42.1 us
    dot_general x32, matrix products, gram_schmidt(): projection = jnp.dot(result.T, vector, precision=lax.Precision.HIGHEST)  27.8 us
    reduce_sum x32, other arithmetic, gram_schmidt(): vector = vector / jnp.sqrt(jnp.sum(vector * vector))  19.4 us
    scatter x32, local copies, waits for them, and re-layouts, gram_schmidt(): result = result.at[:, column].set(vector)  18.9 us
    dot_general x31, matrix products, gram_schmidt(): jnp.dot(result, projection, precision=lax.Precision.HIGHEST)  16.6 us
  transfers between devices with their start and end apart: 3, of which 2 were waited for; matrix products, arithmetic and copies ran while one was open for 33% of the time, Pallas kernels for 0%

commit v1 on v0

v1 whole, which is shorter than its diff:
```python
import functools

import jax
import jax.numpy as jnp
from jax import lax
from jax.experimental import pallas as pl
from jax.experimental.pallas import tpu as pltpu
from jax.sharding import Mesh, PartitionSpec as P

BF16, F32 = jnp.bfloat16, jnp.float32
SIZE = {"y": 4, "z": 4, "x": 4, "core": 2}
VMEM_LIMIT = 56 * 1024 * 1024


def shift(value, axis, step):
    n = SIZE[axis]
    return lax.ppermute(value, axis, [(i, (i + step) % n) for i in range(n)])


def split3(value):
    high = lax.reduce_precision(value, 8, 7)
    rest = value - high
    mid = lax.reduce_precision(rest, 8, 7)
    return high.astype(BF16), mid.astype(BF16), (rest - mid).astype(BF16)


def fold3(value):
    rows = value.shape[0] // 3
    return value[:rows] + value[rows : 2 * rows] + value[2 * rows :]


def mm(a, b, ca, cb):
    return lax.dot_general(a, b, (((ca,), (cb,)), ((), ())), preferred_element_type=F32)


def block(value, index):
    return lax.dynamic_index_in_dim(value, index, 0, False)


def reduce_scatter(value, axis):
    n, me = SIZE[axis], lax.axis_index(axis)
    parts = [shift(block(value, (me + s) % n), axis, s) for s in range(1, n)]
    total = block(value, me)
    for part in parts:
        total = total + part
    return total


def all_sum(value, axis):
    parts = [shift(value, axis, s) for s in range(1, SIZE[axis])]
    for part in parts:
        value = value + part
    return value


def all_blocks(value, axis):
    n, me = SIZE[axis], lax.axis_index(axis)
    parts = [value] + [shift(value, axis, s) for s in range(1, n)]
    result = jnp.zeros((n,) + value.shape, value.dtype)
    for s, part in enumerate(parts):
        result = lax.dynamic_update_index_in_dim(result, part, (me - s) % n, 0)
    return result


def ring(value, axis, halves):
    low = shift(value, axis, 1)
    high = shift(value, axis, -1)
    first, second = halves
    far_a = shift(first(low), axis, 1)
    far_b = shift(second(high), axis, -1)
    return low, high, far_a, far_b


def inverse_kernel(gram_ref, out_ref):
    n = gram_ref.shape[0]
    row = lax.broadcasted_iota(jnp.int32, (n, 2 * n), 0)
    col = lax.broadcasted_iota(jnp.int32, (n, 2 * n), 1)
    eye = jnp.where(row + n == col, 1.0, 0.0).astype(F32)
    work = jnp.concatenate([gram_ref[...], jnp.zeros((n, n), F32)], axis=1) + eye
    for k in range(n):
        pivot_row = work[k : k + 1, :]
        pivot = jnp.sum(jnp.where(col[:1] == k, pivot_row, 0.0), axis=1, keepdims=True)
        column = jnp.sum(jnp.where(col == k, work, 0.0), axis=1, keepdims=True)
        factor = jnp.where(row[:, :1] > k, column / pivot, 0.0)
        root = lax.rsqrt(pivot)
        root = root * (1.5 - 0.5 * pivot * root * root)
        scale = jnp.where(row[:, :1] == k, root, 1.0)
        work = (work - factor * pivot_row) * scale
    out_ref[...] = work[:, n:]


def inverse_of_factor(gram):
    return pl.pallas_call(
        inverse_kernel,
        out_shape=jax.ShapeDtypeStruct(gram.shape, F32),
        name="inverse_of_factor",
    )(gram)


def grad_kernel(groups, final, starts_ref, *refs):
    n = sum(groups)
    pieces, (cot_ref, base_ref) = refs[:n], refs[n : n + 2]
    total = base_ref[...].astype(F32)
    at = 0
    for size in groups:
        left, right = [], []
        for i in range(at, at + size):
            left.append(pieces[i][...])
            rows = pieces[i].shape[0]
            right.append(cot_ref[pl.ds(pl.multiple_of(starts_ref[i], rows), rows), :])
        at += size
        total = total + mm(jnp.concatenate(left, 0), jnp.concatenate(right, 0), 0, 0)
    if final:
        basis_ref, factor_ref, out_ref = refs[n + 2 :]
        total = total - mm(basis_ref[...], factor_ref[...], 0, 0)
    else:
        (out_ref,) = refs[n + 2 :]
    out_ref[...] = total.astype(out_ref.dtype)


def grad_call(pieces, groups, starts, cot, base, low_rank, tile):
    d, cols = base.shape
    final = low_rank is not None
    in_specs = [pl.BlockSpec((p.shape[0], tile), lambda i, s: (0, i)) for p in pieces]
    in_specs += [pl.BlockSpec(cot.shape, lambda i, s: (0, 0)), pl.BlockSpec((tile, cols), lambda i, s: (i, 0))]
    args = list(pieces) + [cot, base]
    k = sum(p.shape[0] for p in pieces)
    if final:
        basis, factor = low_rank
        in_specs += [pl.BlockSpec((basis.shape[0], tile), lambda i, s: (0, i)), pl.BlockSpec(factor.shape, lambda i, s: (0, 0))]
        args += [basis, factor]
        k += basis.shape[0]
    out = jax.ShapeDtypeStruct((d, cols), BF16 if final else F32)
    return pl.pallas_call(
        functools.partial(grad_kernel, tuple(groups), final),
        out_shape=out,
        grid_spec=pltpu.PrefetchScalarGridSpec(
            num_scalar_prefetch=1,
            grid=(d // tile,),
            in_specs=in_specs,
            out_specs=pl.BlockSpec((tile, cols), lambda i, s: (i, 0)),
        ),
        compiler_params=pltpu.CompilerParams(vmem_limit_bytes=VMEM_LIMIT),
        cost_estimate=pl.CostEstimate(flops=2 * d * cols * k, bytes_accessed=2 * d * k + 6 * d * cols, transcendentals=0),
        name="gradient_final" if final else "gradient_part",
    )(starts, *args)


def input_kernel(n_cot, n_w, quarter_ref, *refs):
    cots, refs = refs[:n_cot], refs[n_cot:]
    own_ref, sib_ref, refs = refs[0], refs[1], refs[2:]
    w_own, w_sib, out_ref = refs[:n_w], refs[n_w : 2 * n_w], refs[2 * n_w]
    tokens = jnp.concatenate([c[...] for c in cots], 0)
    wide = 2 * own_ref.shape[1]
    total = mm(tokens[:, :wide], jnp.concatenate([own_ref[...], sib_ref[...]], 1), 1, 1)
    for s in range(w_own[0].shape[0]):
        rows = [jnp.concatenate([o[s], b[s]], 1) for o, b in zip(w_own, w_sib)]
        total = total + mm(tokens[:, (s + 1) * wide : (s + 2) * wide], jnp.concatenate(rows, 0), 1, 1)
    out_ref[...] = total.astype(BF16)


def input_call(cots, own, sib, where, w_own, w_sib):
    rows = sum(w.shape[1] for w in w_own)
    cols = own.shape[1]
    tokens = sum(c.shape[0] for c in cots)
    whole = lambda a: pl.BlockSpec(a.shape, lambda i, q, n=a.ndim: (0,) * n)
    spec = pl.BlockSpec((rows, cols), lambda i, q: (q[0], 0))
    return pl.pallas_call(
        functools.partial(input_kernel, len(cots), len(w_own)),
        out_shape=jax.ShapeDtypeStruct((tokens, rows), BF16),
        grid_spec=pltpu.PrefetchScalarGridSpec(
            num_scalar_prefetch=1,
            grid=(1,),
            in_specs=[whole(c) for c in cots] + [spec, spec] + [whole(w) for w in w_own + w_sib],
            out_specs=pl.BlockSpec((tokens, rows), lambda i, q: (0, 0)),
        ),
        compiler_params=pltpu.CompilerParams(vmem_limit_bytes=VMEM_LIMIT),
        cost_estimate=pl.CostEstimate(
            flops=2 * tokens * rows * cols * 8, bytes_accessed=16 * cols * (tokens + rows) + 2 * tokens * rows, transcendentals=0
        ),
        name="input_grads_part",
    )(jnp.reshape(where, (1,)).astype(jnp.int32), *cots, own, sib, *w_own, *w_sib)


def place_kernel(at_ref, *refs):
    ins, out_ref = refs[:-1], refs[-1]
    k = 0
    for ref in ins:
        for j in range(ref.shape[0]):
            width = ref.shape[2]
            out_ref[:, pl.ds(pl.multiple_of(at_ref[k] * width, 128), width)] = ref[j]
            k += 1


def place_call(pieces, at):
    tokens, width = pieces[0].shape[1:]
    total = width * sum(p.shape[0] for p in pieces)
    return pl.pallas_call(
        place_kernel,
        out_shape=jax.ShapeDtypeStruct((tokens, total), BF16),
        grid_spec=pltpu.PrefetchScalarGridSpec(
            num_scalar_prefetch=1,
            grid=(1,),
            in_specs=[pl.BlockSpec(p.shape, lambda i, a: (0, 0, 0)) for p in pieces],
            out_specs=pl.BlockSpec((tokens, total), lambda i, a: (0, 0)),
        ),
        compiler_params=pltpu.CompilerParams(vmem_limit_bytes=VMEM_LIMIT),
        cost_estimate=pl.CostEstimate(flops=0, bytes_accessed=4 * tokens * total, transcendentals=0),
        name="place_blocks",
    )(at.astype(jnp.int32), *pieces)


def per_device(activations, cotangent, weight, residual, warm_factor):
    iy, iz, ix, ic = (lax.axis_index(a) for a in ("y", "z", "x", "core"))
    tok, d = activations.shape
    tok_dev, cols = cotangent.shape
    rank = warm_factor.shape[1]
    residual = residual[0]
    scale = tok_dev ** (-0.5)
    quarter = d // 4
    sub = quarter // 4

    warm3 = jnp.concatenate(split3(warm_factor.T), 0)
    cw = fold3(mm(warm3, cotangent, 1, 1)) * scale
    cw = reduce_scatter(cw.reshape(rank, 4, 2 * tok).transpose(1, 0, 2), "x")
    cw = reduce_scatter(cw.reshape(rank, 2, tok).transpose(1, 0, 2), "core")

    cot_blocks = cotangent.reshape(4, 2, tok, cols)
    cot_mine = lax.dynamic_index_in_dim(cot_blocks, ic, 1, False)
    cot_sib = shift(lax.dynamic_index_in_dim(cot_blocks, 1 - ic, 1, False), "core", 1)
    w_quarter = lax.dynamic_slice_in_dim(weight, iz * quarter, quarter, 0)
    w_quarter_sib = shift(w_quarter, "core", 1)
    w_send = lax.dynamic_slice_in_dim(weight, iz * quarter + iy * sub, sub, 0)
    got = []
    for s in (1, 3, 2):
        to = (ix + s) % 4
        got.append((s, shift(jnp.concatenate([block(cot_mine, to), block(cot_sib, to), w_send], 0), "x", s)))
    got = [g for _, g in sorted(got, key=lambda p: p[0])]
    cot_own = jnp.concatenate(
        [block(cot_mine, ix), block(cot_sib, ix)] + [g[i * tok : (i + 1) * tok] for g in got for i in (0, 1)], 1
    )
    w_own = jnp.stack([g[2 * tok :] for g in got])

    half = tok // 2
    c_low, c_high, c_far_a, c_far_b = ring(cot_own, "z", (lambda v: v[:half], lambda v: v[half:]))
    hs = sub // 2
    w_low, w_high, w_far_a, w_far_b = ring(w_own, "y", (lambda v: v[:, :hs], lambda v: v[:, hs:]))

    act, _ = lax.optimization_barrier((activations, got[0]))
    a_low, a_high, a_far_a, a_far_b = ring(act, "x", (lambda v: v[:half], lambda v: v[half:]))
    a_sib = shift(activations, "core", 1)
    a_low_sib, a_high_sib, a_far_a_sib, a_far_b_sib = (shift(v, "core", 1) for v in (a_low, a_high, a_far_a, a_far_b))

    cw3 = jnp.concatenate(split3(cw), 0)
    left = fold3(mm(cw3, activations, 1, 0)) + fold3(mm(warm3, residual, 1, 1))
    tiles = left.reshape(rank // 8, 8, d // 128, 128).transpose(0, 2, 1, 3).reshape(-1, 8, 128)
    n_tiles = tiles.shape[0]
    part = reduce_scatter(tiles.reshape(2, n_tiles // 2, 8, 128), "core")
    part = reduce_scatter(part.reshape(4, n_tiles // 8, 8, 128), "y")
    part = reduce_scatter(part.reshape(4, n_tiles // 32, 8, 128), "z")
    part = all_sum(part, "x")
    part = all_blocks(part, "z").reshape(-1, 8, 128)
    part = all_blocks(part, "y").reshape(-1, 8, 128)
    part = all_blocks(part, "core")
    left = part.reshape(rank // 8, d // 128, 8, 128).transpose(0, 2, 1, 3).reshape(rank, d)

    left3 = jnp.concatenate(split3(left), 0)
    right = fold3(mm(left3, activations, 1, 1)) * scale
    right = all_blocks(right, "core").transpose(1, 0, 2).reshape(rank, 2 * tok)
    right = all_blocks(right, "x").transpose(1, 0, 2).reshape(rank, 8 * tok)
    right3 = jnp.concatenate(split3(right), 0)
    sums = fold3(mm(right3, cotangent, 1, 0)) + fold3(mm(left3, residual, 1, 0))
    sums = all_sum(all_sum(sums, "y"), "z")
    gram = mm(left3, left3, 1, 1).reshape(3, rank, 3, rank).sum((0, 2))
    inverse = inverse_of_factor(gram)
    basis = jnp.dot(inverse, left, precision=lax.Precision.HIGHEST)
    factor = jnp.dot(inverse, sums, precision=lax.Precision.HIGHEST) * (1.0 / 16)
    b_h, b_m, b_l = split3(basis)
    f_h, f_m, f_l = split3(factor)
    basis6 = jnp.concatenate([b_h, b_m, b_l, b_h, b_m, b_h], 0)
    factor6 = jnp.concatenate([f_h, f_h, f_h, f_m, f_m, f_l], 0)

    cots = [cot_own, c_low, c_high, c_far_a, c_far_b]
    w_sets = [[w_own], [w_low], [w_high], [w_far_a, w_far_b]]
    parts = []
    for step, w_set in zip((0, -1, 1, 2), w_sets):
        sib_set = [shift(w, "core", 1) for w in w_set]
        parts.append(input_call(cots, w_quarter, w_quarter_sib, (iy + step) % 4, w_set, sib_set))
    grads = jnp.stack([p.reshape(4, tok, sub) for p in parts], 1)
    back = [grads[0], shift(grads[1], "z", -1), shift(grads[2], "z", 1), shift(grads[3], "z", 2)]
    ys = jnp.stack([(iy + s) % 4 for s in (0, -1, 1, 2)])
    at = jnp.concatenate([((iz + s) % 4) * 4 + ys for s in (0, 1, -1, 2)])
    input_grads = place_call(back, at)

    cot_scaled = (cotangent.astype(F32) * scale).astype(BF16)

    def start(step, sib):
        return ((ix + step) % 4) * 2 * tok + (1 - ic if sib else ic) * tok

    near = [activations, a_sib, a_low, a_low_sib, a_high, a_high_sib]
    starts = jnp.stack([start(s, b) for s in (0, -1, 1) for b in (False, True)]).astype(jnp.int32)
    merged = grad_call(near, (2, 2, 2), starts, cot_scaled, residual, None, 512)
    far = [a_far_a, a_far_b, a_far_a_sib, a_far_b_sib]
    starts = jnp.stack([start(2, b) + h for b in (False, True) for h in (0, half)]).astype(jnp.int32)
    new_residual = grad_call(far, (4,), starts, cot_scaled, merged, (basis6, factor6), 512)
    return factor.T, new_residual[None], input_grads


def solution(mesh):
    fine = Mesh(mesh.devices.reshape(4, 4, 4, 2), ("y", "z", "x", "core"))
    dp, tensor = ("y", "z"), ("x", "core")
    in_specs = (
        P(dp + tensor, None),
        P(dp, tensor),
        P(None, tensor),
        P(dp, None, tensor),
        P(tensor, None),
    )
    out_specs = (P(tensor, None), P(dp, None, tensor), P(dp + tensor, None))
    return jax.shard_map(per_device, mesh=fine, in_specs=in_specs, out_specs=out_specs, check_vma=False)
```

time: 493 us -> 288 us (0.58); the launches traced: 484 us -> 286 us
  waiting for transfers between devices: 184 us -> 88 us
  matrix products: 98.2 us -> 17.9 us
  blocking collectives: 73.4 us -> 0 us
  starting transfers between devices: 0.33 us -> 71.9 us
  Pallas kernels: 0 us -> 58.9 us
  other arithmetic: 65 us -> 13.5 us
  between operations: 37.3 us -> 1.54 us
  local copies, waits for them, and re-layouts: 26.1 us -> 33.7 us
    psum x1 -> x0, waiting for transfers between devices: 112 us -> none  [per_device(): left = lax.psum(partial_left, ('dp', 'tensor'))]
    ppermute x0 -> x61, waiting for transfers between devices: none -> 88 us  [shift(): return lax.ppermute(value, axis, [(i, (i + step) % n) for i in range(n)])]
    dot_general x68 -> x9, matrix products: 98.2 us -> 17.9 us  [the longest x7 14.2 us: mm(): lax.dot_general(a, b, (((ca,), (cb,)), ((), ())), preferred_element_type=...]
    psum x1 -> x0, blocking collectives: 73.4 us -> none  [per_device(): new_factor = lax.psum(right_part, 'dp') / lax.axis_size('dp')]
    ppermute x0 -> x61, starting transfers between devices: none -> 71.9 us  [shift(): return lax.ppermute(value, axis, [(i, (i + step) % n) for i in range(n)])]
    all_gather x1 -> x0, waiting for transfers between devices: 71.5 us -> none  [per_device(): lax.all_gather(activations, 'tensor', axis=0, tiled=True)]
    pallas_call x0 -> x8, Pallas kernels: none -> 58.9 us  [the longest x2 30.8 us: grad_call(): pl.pallas_call(functools.partial(grad_kernel, tuple(groups), final), out_...]
    another operation x62 -> x3, other arithmetic: 42.1 us -> 2.9 us  [the longest x1 1.24 us: per_device(): grads = jnp.stack([p.reshape(4, tok, sub) for p in parts], 1)]
  transfers between devices with their start and end apart: 3 -> 61, of which waited for: 2 -> 18; matrix products, arithmetic and copies ran while one was open for 33% -> 21% of each run, Pallas kernels for 0% -> 16%
where the time goes in v1:
time: 288 us; the launch traced here: 286 us
  waiting for transfers between devices  88 us (31%)
  starting transfers between devices  71.9 us (25%)
  Pallas kernels  58.9 us (20%)
  local copies, waits for them, and re-layouts  33.7 us (12%)
  matrix products  17.9 us (6%)
  other arithmetic  13.5 us (5%)
    ppermute x61, waiting for transfers between devices, shift(): return lax.ppermute(value, axis, [(i, (i + step) % n) for i in range(n)])  88 us
    ppermute x61, starting transfers between devices, shift(): return lax.ppermute(value, axis, [(i, (i + step) % n) for i in range(n)])  71.9 us
    pallas_call x2, Pallas kernels, grad_call(): pl.pallas_call(functools.partial(grad_kernel, tuple(groups), final), out_...  30.8 us
    pallas_call x4, Pallas kernels, input_call(): pl.pallas_call(functools.partial(input_kernel, len(cots), len(w_own)), ou...  20.5 us
    dot_general x7, matrix products, mm(): lax.dot_general(a, b, (((ca,), (cb,)), ((), ())), preferred_element_type=...  14.2 us
    unnamed x86, local copies, waits for them, and re-layouts  11.7 us
  transfers between devices with their start and end apart: 61, of which 18 were waited for; matrix products, arithmetic and copies ran while one was open for 21% of the time, Pallas kernels for 16%

profile of v1, /device:TPU:0, one launch (start us, length us, event | category | flops | bytes accessed | tf_op | source)
XLA Modules:
  0.0 285.6 jit_solution(11251334193469482757)
XLA Ops:
  0.7 1.9 dynamic-slice_bitcast_fusion
  2.5 1.4 constant_dynamic-slice_fusion.refs_5_
  5.8 1.6 collective-permute-start
  8.0 2.7 collective-permute-start.1
  11.3 1.4 collective-permute-start.2
  12.8 5.3 %fusion.24 = f32[96,6144]{1,0:T(8,128)} fusion(bf16[32,384]{1,0:T(8,128)(2,1)S(1)} %get-tuple-element.39, bf16[32,384]{1,0:T(8,128)(2,1)S(1)} %get-tuple-element.40, bf16[32,384]{1,0:T(8,128)(2,1)S(1)} %get-tuple-element.38, bf16[1,6144,384]{2,1,0:T(8,128)(2,1)} %param.8), kind=kOutput, calls=%fused_computation.112 | convolution fusion | flops 453206016 | bytes 7151616 | tf_op jit(solution)/shard_map/dot_general | solution.py:33
  22.0 1.9 fusion.26
  28.3 1.1 bitcast_add_fusion
  30.1 1.6 collective-permute-start.5
  31.7 2.9 %collective-permute-start.6 = (f32[24,8,128]{2,1,0:T(8,128)}, f32[24,8,128]{2,1,0:T(8,128)S(1)}, u32[]{:S(2)}, u32[]{:S(2)}) collective-permute-start(f32[24,8,128]{2,1,0:T(8,128)} %get-tuple-element.24), channel_id=1, source_target_pairs={{0,64},{32,96},{64,0},{96,32},{1,65},{33,97},{65,1},{97,33},{2,66}... | collective-permute-start | bytes 294920 | tf_op jit(solution)/shard_map/ppermute | solution.py:17
  34.6 1.3 collective-permute-start.7
  37.1 2.8 collective-permute-done.6
  40.8 4.1 %collective-permute-start.10 = (f32[6,8,128]{2,1,0:T(8,128)S(1)}, f32[6,8,128]{2,1,0:T(8,128)S(1)}, u32[]{:S(2)}, u32[]{:S(2)}) collective-permute-start(f32[6,8,128]{2,1,0:T(8,128)S(1)} %get-tuple-element.36), channel_id=1, source_target_pairs={{0,24},{8,0},{16,8},{24,16},{1,25},{9,1},{17,9},{25,17},{2,26},{10... | collective-permute-start | bytes 73736 | tf_op jit(solution)/shard_map/ppermute | solution.py:17
  45.0 1.9 collective-permute-start.9
  47.8 2.1 collective-permute-done.8
  51.8 1.9 collective-permute-start.13
  55.4 1.4 collective-permute-start.42
  56.8 2.5 collective-permute-start.43
  60.0 1.6 bitcast_dynamic-update-slice_fusion.2
  61.6 2.9 %collective-permute-done.14 = f32[6,8,128]{2,1,0:T(8,128)S(1)} collective-permute-done((f32[6,8,128]{2,1,0:T(8,128)S(1)}, f32[6,8,128]{2,1,0:T(8,128)S(1)}, u32[]{:S(2)}, u32[]{:S(2)}) %collective-permute-start.14) | collective-permute-done | bytes 24608 | tf_op jit(solution)/shard_map/ppermute | solution.py:17
  64.5 1.2 collective-permute-start.15
  65.8 4.1 %collective-permute-done.15 = f32[6,8,128]{2,1,0:T(8,128)S(1)} collective-permute-done((f32[6,8,128]{2,1,0:T(8,128)S(1)}, f32[6,8,128]{2,1,0:T(8,128)S(1)}, u32[]{:S(2)}, u32[]{:S(2)}) %collective-permute-start.15) | collective-permute-done | bytes 24608 | tf_op jit(solution)/shard_map/ppermute | solution.py:17
  69.9 2.0 collective-permute-start.16
  71.9 1.8 collective-permute-done.16
  73.7 1.2 collective-permute-start.17
  75.0 4.5 %collective-permute-done.17 = f32[24,8,128]{2,1,0:T(8,128)S(1)} collective-permute-done((f32[24,8,128]{2,1,0:T(8,128)S(1)}, f32[24,8,128]{2,1,0:T(8,128)S(1)}, u32[]{:S(2)}, u32[]{:S(2)}) %collective-permute-start.17) | collective-permute-done | bytes 98336 | tf_op jit(solution)/shard_map/ppermute | solution.py:17
  79.5 1.5 collective-permute-start.18
  81.0 4.7 %collective-permute-done.18 = f32[24,8,128]{2,1,0:T(8,128)S(1)} collective-permute-done((f32[24,8,128]{2,1,0:T(8,128)S(1)}, f32[24,8,128]{2,1,0:T(8,128)S(1)}, u32[]{:S(2)}, u32[]{:S(2)}) %collective-permute-start.18) | collective-permute-done | bytes 98336 | tf_op jit(solution)/shard_map/ppermute | solution.py:17
  86.6 3.7 %collective-permute-done.19 = f32[24,8,128]{2,1,0:T(8,128)S(1)} collective-permute-done((f32[24,8,128]{2,1,0:T(8,128)S(1)}, f32[24,8,128]{2,1,0:T(8,128)S(1)}, u32[]{:S(2)}, u32[]{:S(2)}) %collective-permute-start.19) | collective-permute-done | bytes 98336 | tf_op jit(solution)/shard_map/ppermute | solution.py:17
  99.3 4.3 %inverse_of_factor.1 = f32[32,32]{1,0:T(8,128)} custom-call(f32[32,32]{1,0:T(8,128)} %reduce_sum.9.gram_ref), custom_call_target="tpu_custom_call" | custom-call | tf_op jit(solution)/shard_map/inverse_of_factor/pallas_call | solution.py:93
  103.6 2.7 constant_dynamic-update-slice_fusion.2
  106.9 1.4 dynamic_update_slice.63
  108.4 1.4 dynamic_update_slice.64
  110.6 6.4 %collective-permute-start.22 = (f32[32,256]{1,0:T(8,128)S(1)}, f32[32,256]{1,0:T(8,128)}, u32[]{:S(2)}, u32[]{:S(2)}) collective-permute-start(f32[32,256]{1,0:T(8,128)S(1)} %bitcast.202), channel_id=1, source_target_pairs={{0,2},{2,4},{4,6},{6,0},{1,3},{3,5},{5,7},{7,1},{8,10},{10,12},{12... | collective-permute-start | bytes 98312 | tf_op jit(solution)/shard_map/ppermute | solution.py:17
  117.0 2.7 collective-permute-start.24
  120.5 3.0 %collective-permute-start.45 = (bf16[128,3072]{1,0:T(8,128)(2,1)}, bf16[128,3072]{1,0:T(8,128)(2,1)}, u32[]{:S(2)}, u32[]{:S(2)}) collective-permute-start(bf16[128,3072]{1,0:T(8,128)(2,1)} %slice_dynamic-update-slice_fusion.refs_0_), channel_id=1, source_target_pairs={{0,24},{8,0},{16,8},{24,16},{1,25},{9,1},{17,9},{25,17},{2,26},{10... | collective-permute-start | bytes 2359304 | tf_op jit(solution)/shard_map/ppermute | solution.py:17
  123.4 3.2 %collective-permute-start.52 = (bf16[3,384,384]{2,1,0:T(8,128)(2,1)}, bf16[3,384,384]{2,1,0:T(8,128)(2,1)}, u32[]{:S(2)}, u32[]{:S(2)}) collective-permute-start(bf16[3,384,384]{2,1,0:T(8,128)(2,1)} %pad_maximum_fusion.2.refs_7_), channel_id=1, source_target_pairs={{0,96},{32,0},{64,32},{96,64},{1,97},{33,1},{65,33},{97,65},{2,98}... | collective-permute-start | bytes 2654216 | tf_op jit(solution)/shard_map/ppermute | solution.py:17
  126.7 4.1 %fusion.40 = f32[96,384]{1,0:T(8,128)} fusion(bf16[1,6144,384]{2,1,0:T(8,128)(2,1)} %param.8, bf16[32,6144]{1,0:T(8,128)(2,1)} %copy-done.25, bf16[32,6144]{1,0:T(8,128)(2,1)} %copy-done.26, bf16[32,6144]{1,0:T(8,128)(2,1)S(1)} %get-tuple-element.16), kind=kOutput, calls=%fused_computation.158 | convolution fusion | flops 456523776 | bytes 6045696 | tf_op jit(solution)/shard_map/dot_general | solution.py:33
  134.8 1.4 fusion.4
  137.5 2.9 %collective-permute-done.45.refs_2_ = bf16[128,3072]{1,0:T(8,128)(2,1)} collective-permute-done((bf16[128,3072]{1,0:T(8,128)(2,1)}, bf16[128,3072]{1,0:T(8,128)(2,1)}, u32[]{:S(2)}, u32[]{:S(2)}) %collective-permute-start.45) | collective-permute-done | bytes 786464 | tf_op jit(solution)/shard_map/ppermute | solution.py:17
  141.4 5.7 %collective-permute-done.50.refs_7_ = bf16[3,384,384]{2,1,0:T(8,128)(2,1)} collective-permute-done((bf16[3,384,384]{2,1,0:T(8,128)(2,1)}, bf16[3,384,384]{2,1,0:T(8,128)(2,1)}, u32[]{:S(2)}, u32[]{:S(2)}) %collective-permute-start.50) | collective-permute-done | bytes 884768 | tf_op jit(solution)/shard_map/ppermute | solution.py:17
  150.0 1.1 slice.180
  151.1 3.3 %collective-permute-start.47 = (bf16[64,3072]{1,0:T(8,128)(2,1)S(1)}, bf16[64,3072]{1,0:T(8,128)(2,1)S(1)}, u32[]{:S(2)}, u32[]{:S(2)}) collective-permute-start(bf16[64,3072]{1,0:T(8,128)(2,1)S(1)} %slice.175), channel_id=1, source_target_pairs={{0,24},{8,0},{16,8},{24,16},{1,25},{9,1},{17,9},{25,17},{2,26},{10... | collective-permute-start | bytes 1179656 | tf_op jit(solution)/shard_map/ppermute | solution.py:17
  154.4 2.0 collective-permute-start.54
  156.4 1.5 collective-permute-start.55
  159.2 5.7 %collective-permute-done.54.refs_7_ = bf16[3,192,384]{2,1,0:T(8,128)(2,1)} collective-permute-done((bf16[3,192,384]{2,1,0:T(8,128)(2,1)S(1)}, bf16[3,192,384]{2,1,0:T(8,128)(2,1)}, u32[]{:S(2)}, u32[]{:S(2)}) %collective-permute-start.54) | collective-permute-done | bytes 442400 | tf_op jit(solution)/shard_map/ppermute | solution.py:17
  166.2 5.1 %input_grads_part.4 = bf16[512,384]{1,0:T(8,128)(2,1)} custom-call(s32[1]{0:T(128)} %bitcast.64.quarter_ref, bf16[128,3072]{1,0:T(8,128)(2,1)} %slice_dynamic-update-slice_fusion.refs_0_, bf16[128,3072]{1,0:T(8,128)(2,1)} %collective-permute-done.44.refs_1_, bf16[128,3072]{1,0:T(8,128)(2,1)} %collective-permute-done.45.refs_2_, bf16[64,3072]{1,0:T(8,128)(2,1)} %copy-done.7, ...), custom_call_target="tpu_custom_call" | custom-call | flops 1207959552 | bytes 5898240 | tf_op jit(solution)/shard_map/input_grads_part/pallas_call | solution.py:168
  171.3 2.6 collective-permute-start.35
  173.9 5.1 %input_grads_part.5 = bf16[512,384]{1,0:T(8,128)(2,1)} custom-call(s32[1]{0:T(128)} %bitcast.65.quarter_ref, bf16[128,3072]{1,0:T(8,128)(2,1)} %slice_dynamic-update-slice_fusion.refs_0_, bf16[128,3072]{1,0:T(8,128)(2,1)} %collective-permute-done.44.refs_1_, bf16[128,3072]{1,0:T(8,128)(2,1)} %collective-permute-done.45.refs_2_, bf16[64,3072]{1,0:T(8,128)(2,1)} %copy-done.7, ...), custom_call_target="tpu_custom_call" | custom-call | flops 1207959552 | bytes 5898240 | tf_op jit(solution)/shard_map/input_grads_part/pallas_call | solution.py:168
  179.1 5.1 %input_grads_part.6 = bf16[512,384]{1,0:T(8,128)(2,1)} custom-call(s32[1]{0:T(128)} %bitcast.66.quarter_ref, bf16[128,3072]{1,0:T(8,128)(2,1)} %slice_dynamic-update-slice_fusion.refs_0_, bf16[128,3072]{1,0:T(8,128)(2,1)} %collective-permute-done.44.refs_1_, bf16[128,3072]{1,0:T(8,128)(2,1)} %collective-permute-done.45.refs_2_, bf16[64,3072]{1,0:T(8,128)(2,1)} %copy-done.7, ...), custom_call_target="tpu_custom_call" | custom-call | flops 1207959552 | bytes 5898240 | tf_op jit(solution)/shard_map/input_grads_part/pallas_call | solution.py:168
  184.2 1.9 collective-permute-start.29
  186.1 1.5 collective-permute-start.30
  187.6 5.1 %input_grads_part.7 = bf16[512,384]{1,0:T(8,128)(2,1)} custom-call(s32[1]{0:T(128)} %bitcast.67.quarter_ref, bf16[128,3072]{1,0:T(8,128)(2,1)} %slice_dynamic-update-slice_fusion.refs_0_, bf16[128,3072]{1,0:T(8,128)(2,1)} %collective-permute-done.44.refs_1_, bf16[128,3072]{1,0:T(8,128)(2,1)} %collective-permute-done.45.refs_2_, bf16[64,3072]{1,0:T(8,128)(2,1)} %copy-done.7, ...), custom_call_target="tpu_custom_call" | custom-call | flops 1207959552 | bytes 5898240 | tf_op jit(solution)/shard_map/input_grads_part/pallas_call | solution.py:168
  192.7 1.2 pad_maximum_fusion
  196.6 6.5 %collective-permute-done.33.refs_2_ = bf16[128,6144]{1,0:T(8,128)(2,1)S(1)} collective-permute-done((bf16[128,6144]{1,0:T(8,128)(2,1)S(1)}, bf16[128,6144]{1,0:T(8,128)(2,1)S(1)}, u32[]{:S(2)}, u32[]{:S(2)}) %collective-permute-start.33) | collective-permute-done | bytes 1572896 | tf_op jit(solution)/shard_map/ppermute | solution.py:17
  203.1 4.6 %collective-permute-done.35.refs_4_ = bf16[128,6144]{1,0:T(8,128)(2,1)S(1)} collective-permute-done((bf16[128,6144]{1,0:T(8,128)(2,1)S(1)}, bf16[128,6144]{1,0:T(8,128)(2,1)S(1)}, u32[]{:S(2)}, u32[]{:S(2)}) %collective-permute-start.35) | collective-permute-done | bytes 1572896 | tf_op jit(solution)/shard_map/ppermute | solution.py:17
  207.8 1.8 collective-permute-start.60
  210.5 18.3 %collective-permute-done.59.refs_2_ = bf16[4,128,384]{2,1,0:T(8,128)(2,1)S(1)} collective-permute-done((bf16[4,128,384]{2,1,0:T(8,128)(2,1)S(1)}, bf16[4,128,384]{2,1,0:T(8,128)(2,1)S(1)}, u32[]{:S(2)}, u32[]{:S(2)}) %collective-permute-start.59) | collective-permute-done | bytes 393248 | tf_op jit(solution)/shard_map/ppermute | solution.py:17
  229.0 3.5 %collective-permute-start.36 = (bf16[64,6144]{1,0:T(8,128)(2,1)S(1)}, bf16[64,6144]{1,0:T(8,128)(2,1)}, u32[]{:S(2)}, u32[]{:S(2)}) collective-permute-start(bf16[64,6144]{1,0:T(8,128)(2,1)S(1)} %slice.167), channel_id=1, source_target_pairs={{0,6},{2,0},{4,2},{6,4},{1,7},{3,1},{5,3},{7,5},{8,14},{10,8},{12,... | collective-permute-start | bytes 2359304 | tf_op jit(solution)/shard_map/ppermute | solution.py:17
  233.6 16.1 %collective-permute-done.34.refs_0_ = bf16[64,6144]{1,0:T(8,128)(2,1)S(1)} collective-permute-done((bf16[64,6144]{1,0:T(8,128)(2,1)S(1)}, bf16[64,6144]{1,0:T(8,128)(2,1)S(1)}, u32[]{:S(2)}, u32[]{:S(2)}) %collective-permute-start.34) | collective-permute-done | bytes 786464 | tf_op jit(solution)/shard_map/ppermute | solution.py:17
  250.3 3.3 %place_blocks.1 = bf16[128,6144]{1,0:T(8,128)(2,1)} custom-call(s32[16]{0:T(128)} %pad_add_fusion.2.at_ref, bf16[4,128,384]{2,1,0:T(8,128)(2,1)} %get-tuple-element.12.refs_0_, bf16[4,128,384]{2,1,0:T(8,128)(2,1)} %copy-done.24, bf16[4,128,384]{2,1,0:T(8,128)(2,1)} %copy-done.27, bf16[4,128,384]{2,1,0:T(8,128)(2,1)} %copy-done.28), custom_call_target="tpu_custom_call" | custom-call | bytes 3145728 | tf_op jit(solution)/shard_map/place_blocks/pallas_call | solution.py:198
  253.6 1.1 copy-done.17
  254.7 16.8 %gradient_part.1.refs_5_ = f32[6144,384]{1,0:T(8,128)} custom-call(s32[6]{0:T(128)} %stack.77.starts_ref, bf16[128,6144]{1,0:T(8,128)(2,1)} %refs_0_.1, bf16[128,6144]{1,0:T(8,128)(2,1)} %copy-done.17, bf16[128,6144]{1,0:T(8,128)(2,1)} %copy-done.9, bf16[128,6144]{1,0:T(8,128)(2,1)} %collective-permute-done.40.refs_3_, bf16[128,6144]{1,0:T(8,128)(2,1)} %copy-done.10, ...), custom_call_target="tpu_custom_call" | custom-call | flops 3623878656 | bytes 23592960 | tf_op jit(solution)/shard_map/gradient_part/pallas_call | solution.py:134
  271.6 14.0 %gradient_final.1 = bf16[6144,384]{1,0:T(8,128)(2,1)} custom-call(s32[4]{0:T(128)} %pad_add_fusion.starts_ref, bf16[64,6144]{1,0:T(8,128)(2,1)} %copy-done.19, bf16[64,6144]{1,0:T(8,128)(2,1)} %collective-permute-done.36.refs_1_, bf16[64,6144]{1,0:T(8,128)(2,1)} %collective-permute-done.37.refs_2_, bf16[64,6144]{1,0:T(8,128)(2,1)} %collective-permute-done.38.refs_3_, ...), custom_call_target="tpu_custom_call" | custom-call | flops 2113929216 | bytes 19660800 | tf_op jit(solution)/shard_map/gradient_final/pallas_call | solution.py:134
  (242 shorter events, 48.4 us)
Async XLA Ops:
  2.5 44.3 %collective-permute-start.31 = (bf16[4,128,384]{2,1,0:T(8,128)(2,1)}, bf16[4,128,384]{2,1,0:T(8,128)(2,1)}, u32[]{:S(2)}, u32[]{:S(2)}) collective-permute-start(bf16[4,128,384]{2,1,0:T(8,128)(2,1)} %dynamic-slice_bitcast_fusion), channel_id=1, source_target_pairs={{0,1},{1,0},{2,3},{3,2},{4,5},{5,4},{6,7},{7,6},{8,9},{9,8},{10,11... | collective-permute-start | bytes 1179656 | tf_op jit(solution)/shard_map/ppermute | solution.py:17
  3.9 133.5 %collective-permute-start.48 = (bf16[1536,384]{1,0:T(8,128)(2,1)S(1)}, bf16[1536,384]{1,0:T(8,128)(2,1)S(1)}, u32[]{:S(2)}, u32[]{:S(2)}) collective-permute-start(bf16[1536,384]{1,0:T(8,128)(2,1)S(1)} %constant_dynamic-slice_fusion.refs_5_), channel_id=1, source_target_pairs={{0,1},{1,0},{2,3},{3,2},{4,5},{5,4},{6,7},{7,6},{8,9},{9,8},{10,11... | collective-permute-start | bytes 3538952 | tf_op jit(solution)/shard_map/ppermute | solution.py:17
  5.8 14.0 %collective-permute-start = (f32[32,256]{1,0:T(8,128)}, f32[32,256]{1,0:T(8,128)S(1)}, u32[]{:S(2)}, u32[]{:S(2)}) collective-permute-start(f32[32,256]{1,0:T(8,128)} %bitcast.169), channel_id=1, source_target_pairs={{0,2},{2,4},{4,6},{6,0},{1,3},{3,5},{5,7},{7,1},{8,10},{10,12},{12... | collective-permute-start | bytes 98312 | tf_op jit(solution)/shard_map/ppermute | solution.py:17
  8.0 11.8 %collective-permute-start.1 = (f32[32,256]{1,0:T(8,128)}, f32[32,256]{1,0:T(8,128)}, u32[]{:S(2)}, u32[]{:S(2)}) collective-permute-start(f32[32,256]{1,0:T(8,128)} %bitcast.168), channel_id=1, source_target_pairs={{0,4},{2,6},{4,0},{6,2},{1,5},{3,7},{5,1},{7,3},{8,12},{10,14},{12... | collective-permute-start | bytes 98312 | tf_op jit(solution)/shard_map/ppermute | solution.py:17
  11.3 8.5 %collective-permute-start.2 = (f32[32,256]{1,0:T(8,128)}, f32[32,256]{1,0:T(8,128)}, u32[]{:S(2)}, u32[]{:S(2)}) collective-permute-start(f32[32,256]{1,0:T(8,128)} %bitcast.167), channel_id=1, source_target_pairs={{0,6},{2,0},{4,2},{6,4},{1,7},{3,1},{5,3},{7,5},{8,14},{10,8},{12,... | collective-permute-start | bytes 98312 | tf_op jit(solution)/shard_map/ppermute | solution.py:17
  20.7 1.3 collective-permute-start.3
  25.7 2.5 collective-permute-start.4
  30.1 7.0 %collective-permute-start.5 = (f32[24,8,128]{2,1,0:T(8,128)}, f32[24,8,128]{2,1,0:T(8,128)S(1)}, u32[]{:S(2)}, u32[]{:S(2)}) collective-permute-start(f32[24,8,128]{2,1,0:T(8,128)} %get-tuple-element.22), channel_id=1, source_target_pairs={{0,32},{32,64},{64,96},{96,0},{1,33},{33,65},{65,97},{97,1},{2,34}... | collective-permute-start | bytes 294920 | tf_op jit(solution)/shard_map/ppermute | solution.py:17
  31.7 8.2 %collective-permute-start.6 = (f32[24,8,128]{2,1,0:T(8,128)}, f32[24,8,128]{2,1,0:T(8,128)S(1)}, u32[]{:S(2)}, u32[]{:S(2)}) collective-permute-start(f32[24,8,128]{2,1,0:T(8,128)} %get-tuple-element.24), channel_id=1, source_target_pairs={{0,64},{32,96},{64,0},{96,32},{1,65},{33,97},{65,1},{97,33},{2,66}... | collective-permute-start | bytes 294920 | tf_op jit(solution)/shard_map/ppermute | solution.py:17
  34.6 5.3 %collective-permute-start.7 = (f32[24,8,128]{2,1,0:T(8,128)}, f32[24,8,128]{2,1,0:T(8,128)}, u32[]{:S(2)}, u32[]{:S(2)}) collective-permute-start(f32[24,8,128]{2,1,0:T(8,128)} %get-tuple-element.23), channel_id=1, source_target_pairs={{0,96},{32,0},{64,32},{96,64},{1,97},{33,1},{65,33},{97,65},{2,98}... | collective-permute-start | bytes 294920 | tf_op jit(solution)/shard_map/ppermute | solution.py:17
  40.8 7.0 %collective-permute-start.10 = (f32[6,8,128]{2,1,0:T(8,128)S(1)}, f32[6,8,128]{2,1,0:T(8,128)S(1)}, u32[]{:S(2)}, u32[]{:S(2)}) collective-permute-start(f32[6,8,128]{2,1,0:T(8,128)S(1)} %get-tuple-element.36), channel_id=1, source_target_pairs={{0,24},{8,0},{16,8},{24,16},{1,25},{9,1},{17,9},{25,17},{2,26},{10... | collective-permute-start | bytes 73736 | tf_op jit(solution)/shard_map/ppermute | solution.py:17
  44.9 5.0 %collective-permute-start.8 = (f32[6,8,128]{2,1,0:T(8,128)S(1)}, f32[6,8,128]{2,1,0:T(8,128)S(1)}, u32[]{:S(2)}, u32[]{:S(2)}) collective-permute-start(f32[6,8,128]{2,1,0:T(8,128)S(1)} %get-tuple-element.35), channel_id=1, source_target_pairs={{0,8},{8,16},{16,24},{24,0},{1,9},{9,17},{17,25},{25,1},{2,10},{10... | collective-permute-start | bytes 73736 | tf_op jit(solution)/shard_map/ppermute | solution.py:17
  45.0 5.3 %collective-permute-start.9 = (f32[6,8,128]{2,1,0:T(8,128)S(1)}, f32[6,8,128]{2,1,0:T(8,128)S(1)}, u32[]{:S(2)}, u32[]{:S(2)}) collective-permute-start(f32[6,8,128]{2,1,0:T(8,128)S(1)} %get-tuple-element.37), channel_id=1, source_target_pairs={{0,16},{8,24},{16,0},{24,8},{1,17},{9,25},{17,1},{25,9},{2,18},{10... | collective-permute-start | bytes 73736 | tf_op jit(solution)/shard_map/ppermute | solution.py:17
  50.3 5.1 %collective-permute-start.11 = (f32[6,8,128]{2,1,0:T(8,128)S(1)}, f32[6,8,128]{2,1,0:T(8,128)S(1)}, u32[]{:S(2)}, u32[]{:S(2)}) collective-permute-start(f32[6,8,128]{2,1,0:T(8,128)S(1)} %fusion.33), channel_id=1, source_target_pairs={{0,2},{2,4},{4,6},{6,0},{1,3},{3,5},{5,7},{7,1},{8,10},{10,12},{12... | collective-permute-start | bytes 73736 | tf_op jit(solution)/shard_map/ppermute | solution.py:17
  51.0 5.9 %collective-permute-start.12 = (f32[6,8,128]{2,1,0:T(8,128)S(1)}, f32[6,8,128]{2,1,0:T(8,128)S(1)}, u32[]{:S(2)}, u32[]{:S(2)}) collective-permute-start(f32[6,8,128]{2,1,0:T(8,128)S(1)} %fusion.33), channel_id=1, source_target_pairs={{0,4},{2,6},{4,0},{6,2},{1,5},{3,7},{5,1},{7,3},{8,12},{10,14},{12... | collective-permute-start | bytes 73736 | tf_op jit(solution)/shard_map/ppermute | solution.py:17
  51.8 7.5 %collective-permute-start.13 = (f32[6,8,128]{2,1,0:T(8,128)S(1)}, f32[6,8,128]{2,1,0:T(8,128)S(1)}, u32[]{:S(2)}, u32[]{:S(2)}) collective-permute-start(f32[6,8,128]{2,1,0:T(8,128)S(1)} %fusion.33), channel_id=1, source_target_pairs={{0,6},{2,0},{4,2},{6,4},{1,7},{3,1},{5,3},{7,5},{8,14},{10,8},{12,... | collective-permute-start | bytes 73736 | tf_op jit(solution)/shard_map/ppermute | solution.py:17
  53.9 36.6 %collective-permute-start.32 = (bf16[640,384]{1,0:T(8,128)(2,1)S(1)}, bf16[640,384]{1,0:T(8,128)(2,1)S(1)}, u32[]{:S(2)}, u32[]{:S(2)}) collective-permute-start(bf16[640,384]{1,0:T(8,128)(2,1)S(1)} %get-tuple-element.27), channel_id=1, source_target_pairs={{0,2},{2,4},{4,6},{6,0},{1,3},{3,5},{5,7},{7,1},{8,10},{10,12},{12... | collective-permute-start | bytes 1474568 | tf_op jit(solution)/shard_map/ppermute | solution.py:17
  55.4 36.4 %collective-permute-start.42 = (bf16[640,384]{1,0:T(8,128)(2,1)S(1)}, bf16[640,384]{1,0:T(8,128)(2,1)S(1)}, u32[]{:S(2)}, u32[]{:S(2)}) collective-permute-start(bf16[640,384]{1,0:T(8,128)(2,1)S(1)} %get-tuple-element.26), channel_id=1, source_target_pairs={{0,4},{2,6},{4,0},{6,2},{1,5},{3,7},{5,1},{7,3},{8,12},{10,14},{12... | collective-permute-start | bytes 1474568 | tf_op jit(solution)/shard_map/ppermute | solution.py:17
  56.8 36.3 %collective-permute-start.43 = (bf16[640,384]{1,0:T(8,128)(2,1)S(1)}, bf16[640,384]{1,0:T(8,128)(2,1)S(1)}, u32[]{:S(2)}, u32[]{:S(2)}) collective-permute-start(bf16[640,384]{1,0:T(8,128)(2,1)S(1)} %get-tuple-element.25), channel_id=1, source_target_pairs={{0,6},{2,0},{4,2},{6,4},{1,7},{3,1},{5,3},{7,5},{8,14},{10,8},{12,... | collective-permute-start | bytes 1474568 | tf_op jit(solution)/shard_map/ppermute | solution.py:17
  59.4 5.1 %collective-permute-start.14 = (f32[6,8,128]{2,1,0:T(8,128)S(1)}, f32[6,8,128]{2,1,0:T(8,128)S(1)}, u32[]{:S(2)}, u32[]{:S(2)}) collective-permute-start(f32[6,8,128]{2,1,0:T(8,128)S(1)} %get-tuple-element.8), channel_id=1, source_target_pairs={{0,8},{8,16},{16,24},{24,0},{1,9},{9,17},{17,25},{25,1},{2,10},{10... | collective-permute-start | bytes 73736 | tf_op jit(solution)/shard_map/ppermute | solution.py:17
  64.5 5.3 %collective-permute-start.15 = (f32[6,8,128]{2,1,0:T(8,128)S(1)}, f32[6,8,128]{2,1,0:T(8,128)S(1)}, u32[]{:S(2)}, u32[]{:S(2)}) collective-permute-start(f32[6,8,128]{2,1,0:T(8,128)S(1)} %get-tuple-element.8), channel_id=1, source_target_pairs={{0,16},{8,24},{16,0},{24,8},{1,17},{9,25},{17,1},{25,9},{2,18},{10... | collective-permute-start | bytes 73736 | tf_op jit(solution)/shard_map/ppermute | solution.py:17
  69.9 3.8 %collective-permute-start.16 = (f32[6,8,128]{2,1,0:T(8,128)S(1)}, f32[6,8,128]{2,1,0:T(8,128)S(1)}, u32[]{:S(2)}, u32[]{:S(2)}) collective-permute-start(f32[6,8,128]{2,1,0:T(8,128)S(1)} %get-tuple-element.8), channel_id=1, source_target_pairs={{0,24},{8,0},{16,8},{24,16},{1,25},{9,1},{17,9},{25,17},{2,26},{10... | collective-permute-start | bytes 73736 | tf_op jit(solution)/shard_map/ppermute | solution.py:17
  73.7 5.8 %collective-permute-start.17 = (f32[24,8,128]{2,1,0:T(8,128)S(1)}, f32[24,8,128]{2,1,0:T(8,128)S(1)}, u32[]{:S(2)}, u32[]{:S(2)}) collective-permute-start(f32[24,8,128]{2,1,0:T(8,128)S(1)} %bitcast.192), channel_id=1, source_target_pairs={{0,32},{32,64},{64,96},{96,0},{1,33},{33,65},{65,97},{97,1},{2,34}... | collective-permute-start | bytes 294920 | tf_op jit(solution)/shard_map/ppermute | solution.py:17
  79.5 6.1 %collective-permute-start.18 = (f32[24,8,128]{2,1,0:T(8,128)S(1)}, f32[24,8,128]{2,1,0:T(8,128)S(1)}, u32[]{:S(2)}, u32[]{:S(2)}) collective-permute-start(f32[24,8,128]{2,1,0:T(8,128)S(1)} %bitcast.194), channel_id=1, source_target_pairs={{0,64},{32,96},{64,0},{96,32},{1,65},{33,97},{65,1},{97,33},{2,66}... | collective-permute-start | bytes 294920 | tf_op jit(solution)/shard_map/ppermute | solution.py:17
  85.6 4.6 %collective-permute-start.19 = (f32[24,8,128]{2,1,0:T(8,128)S(1)}, f32[24,8,128]{2,1,0:T(8,128)S(1)}, u32[]{:S(2)}, u32[]{:S(2)}) collective-permute-start(f32[24,8,128]{2,1,0:T(8,128)S(1)} %bitcast.195), channel_id=1, source_target_pairs={{0,96},{32,0},{64,32},{96,64},{1,97},{33,1},{65,33},{97,65},{2,98}... | collective-permute-start | bytes 294920 | tf_op jit(solution)/shard_map/ppermute | solution.py:17
  90.3 5.4 %collective-permute-start.20 = (f32[96,8,128]{2,1,0:T(8,128)S(1)}, f32[96,8,128]{2,1,0:T(8,128)S(1)}, u32[]{:S(2)}, u32[]{:S(2)}) collective-permute-start(f32[96,8,128]{2,1,0:T(8,128)S(1)} %bitcast.182), channel_id=1, source_target_pairs={{0,1},{1,0},{2,3},{3,2},{4,5},{5,4},{6,7},{7,6},{8,9},{9,8},{10,11... | collective-permute-start | bytes 1179656 | tf_op jit(solution)/shard_map/ppermute | solution.py:17
  94.5 41.8 %collective-permute-start.44 = (bf16[128,3072]{1,0:T(8,128)(2,1)}, bf16[128,3072]{1,0:T(8,128)(2,1)}, u32[]{:S(2)}, u32[]{:S(2)}) collective-permute-start(bf16[128,3072]{1,0:T(8,128)(2,1)} %slice_dynamic-update-slice_fusion.refs_0_), channel_id=1, source_target_pairs={{0,8},{8,16},{16,24},{24,0},{1,9},{9,17},{17,25},{25,1},{2,10},{10... | collective-permute-start | bytes 2359304 | tf_op jit(solution)/shard_map/ppermute | solution.py:17
  97.9 10.5 %collective-permute-start.21 = (f32[32,128]{1,0:T(8,128)S(1)}, f32[32,128]{1,0:T(8,128)}, u32[]{:S(2)}, u32[]{:S(2)}) collective-permute-start(f32[32,128]{1,0:T(8,128)S(1)} %fusion.35), channel_id=1, source_target_pairs={{0,1},{1,0},{2,3},{3,2},{4,5},{5,4},{6,7},{7,6},{8,9},{9,8},{10,11... | collective-permute-start | bytes 49160 | tf_op jit(solution)/shard_map/ppermute | solution.py:17
  110.6 9.9 %collective-permute-start.22 = (f32[32,256]{1,0:T(8,128)S(1)}, f32[32,256]{1,0:T(8,128)}, u32[]{:S(2)}, u32[]{:S(2)}) collective-permute-start(f32[32,256]{1,0:T(8,128)S(1)} %bitcast.202), channel_id=1, source_target_pairs={{0,2},{2,4},{4,6},{6,0},{1,3},{3,5},{5,7},{7,1},{8,10},{10,12},{12... | collective-permute-start | bytes 98312 | tf_op jit(solution)/shard_map/ppermute | solution.py:17
  117.0 6.5 %collective-permute-start.23 = (f32[32,256]{1,0:T(8,128)S(1)}, f32[32,256]{1,0:T(8,128)}, u32[]{:S(2)}, u32[]{:S(2)}) collective-permute-start(f32[32,256]{1,0:T(8,128)S(1)} %bitcast.203), channel_id=1, source_target_pairs={{0,4},{2,6},{4,0},{6,2},{1,5},{3,7},{5,1},{7,3},{8,12},{10,14},{12... | collective-permute-start | bytes 98312 | tf_op jit(solution)/shard_map/ppermute | solution.py:17
  117.0 6.5 %collective-permute-start.24 = (f32[32,256]{1,0:T(8,128)S(1)}, f32[32,256]{1,0:T(8,128)}, u32[]{:S(2)}, u32[]{:S(2)}) collective-permute-start(f32[32,256]{1,0:T(8,128)S(1)} %bitcast.204), channel_id=1, source_target_pairs={{0,6},{2,0},{4,2},{6,4},{1,7},{3,1},{5,3},{7,5},{8,14},{10,8},{12,... | collective-permute-start | bytes 98312 | tf_op jit(solution)/shard_map/ppermute | solution.py:17
  120.5 20.0 %collective-permute-start.45 = (bf16[128,3072]{1,0:T(8,128)(2,1)}, bf16[128,3072]{1,0:T(8,128)(2,1)}, u32[]{:S(2)}, u32[]{:S(2)}) collective-permute-start(bf16[128,3072]{1,0:T(8,128)(2,1)} %slice_dynamic-update-slice_fusion.refs_0_), channel_id=1, source_target_pairs={{0,24},{8,0},{16,8},{24,16},{1,25},{9,1},{17,9},{25,17},{2,26},{10... | collective-permute-start | bytes 2359304 | tf_op jit(solution)/shard_map/ppermute | solution.py:17
  123.4 23.6 %collective-permute-start.50 = (bf16[3,384,384]{2,1,0:T(8,128)(2,1)}, bf16[3,384,384]{2,1,0:T(8,128)(2,1)}, u32[]{:S(2)}, u32[]{:S(2)}) collective-permute-start(bf16[3,384,384]{2,1,0:T(8,128)(2,1)} %pad_maximum_fusion.2.refs_7_), channel_id=1, source_target_pairs={{0,32},{32,64},{64,96},{96,0},{1,33},{33,65},{65,97},{97,1},{2,34}... | collective-permute-start | bytes 2654216 | tf_op jit(solution)/shard_map/ppermute | solution.py:17
  123.4 23.6 %collective-permute-start.52 = (bf16[3,384,384]{2,1,0:T(8,128)(2,1)}, bf16[3,384,384]{2,1,0:T(8,128)(2,1)}, u32[]{:S(2)}, u32[]{:S(2)}) collective-permute-start(bf16[3,384,384]{2,1,0:T(8,128)(2,1)} %pad_maximum_fusion.2.refs_7_), channel_id=1, source_target_pairs={{0,96},{32,0},{64,32},{96,64},{1,97},{33,1},{65,33},{97,65},{2,98}... | collective-permute-start | bytes 2654216 | tf_op jit(solution)/shard_map/ppermute | solution.py:17
  136.3 21.7 %collective-permute-start.49 = (bf16[3,384,384]{2,1,0:T(8,128)(2,1)}, bf16[3,384,384]{2,1,0:T(8,128)(2,1)S(1)}, u32[]{:S(2)}, u32[]{:S(2)}) collective-permute-start(bf16[3,384,384]{2,1,0:T(8,128)(2,1)} %pad_maximum_fusion.2.refs_7_), channel_id=1, source_target_pairs={{0,1},{1,0},{2,3},{3,2},{4,5},{5,4},{6,7},{7,6},{8,9},{9,8},{10,11... | collective-permute-start | bytes 2654216 | tf_op jit(solution)/shard_map/ppermute | solution.py:17
  137.4 13.7 %collective-permute-start.25 = (f32[32,384]{1,0:T(8,128)S(1)}, f32[32,384]{1,0:T(8,128)S(1)}, u32[]{:S(2)}, u32[]{:S(2)}) collective-permute-start(f32[32,384]{1,0:T(8,128)S(1)} %fusion.18), channel_id=1, source_target_pairs={{0,32},{32,64},{64,96},{96,0},{1,33},{33,65},{65,97},{97,1},{2,34}... | collective-permute-start | bytes 147464 | tf_op jit(solution)/shard_map/ppermute | solution.py:17
  140.4 13.9 %collective-permute-start.26 = (f32[32,384]{1,0:T(8,128)S(1)}, f32[32,384]{1,0:T(8,128)S(1)}, u32[]{:S(2)}, u32[]{:S(2)}) collective-permute-start(f32[32,384]{1,0:T(8,128)S(1)} %fusion.18), channel_id=1, source_target_pairs={{0,64},{32,96},{64,0},{96,32},{1,65},{33,97},{65,1},{97,33},{2,66}... | collective-permute-start | bytes 147464 | tf_op jit(solution)/shard_map/ppermute | solution.py:17
  147.0 9.4 %collective-permute-start.27 = (f32[32,384]{1,0:T(8,128)S(1)}, f32[32,384]{1,0:T(8,128)S(1)}, u32[]{:S(2)}, u32[]{:S(2)}) collective-permute-start(f32[32,384]{1,0:T(8,128)S(1)} %fusion.18), channel_id=1, source_target_pairs={{0,96},{32,0},{64,32},{96,64},{1,97},{33,1},{65,33},{97,65},{2,98}... | collective-permute-start | bytes 147464 | tf_op jit(solution)/shard_map/ppermute | solution.py:17
  147.0 10.9 %collective-permute-start.46 = (bf16[64,3072]{1,0:T(8,128)(2,1)S(1)}, bf16[64,3072]{1,0:T(8,128)(2,1)S(1)}, u32[]{:S(2)}, u32[]{:S(2)}) collective-permute-start(bf16[64,3072]{1,0:T(8,128)(2,1)S(1)} %slice.174), channel_id=1, source_target_pairs={{0,8},{8,16},{16,24},{24,0},{1,9},{9,17},{17,25},{25,1},{2,10},{10... | collective-permute-start | bytes 1179656 | tf_op jit(solution)/shard_map/ppermute | solution.py:17
  151.1 14.4 %collective-permute-start.47 = (bf16[64,3072]{1,0:T(8,128)(2,1)S(1)}, bf16[64,3072]{1,0:T(8,128)(2,1)S(1)}, u32[]{:S(2)}, u32[]{:S(2)}) collective-permute-start(bf16[64,3072]{1,0:T(8,128)(2,1)S(1)} %slice.175), channel_id=1, source_target_pairs={{0,24},{8,0},{16,8},{24,16},{1,25},{9,1},{17,9},{25,17},{2,26},{10... | collective-permute-start | bytes 1179656 | tf_op jit(solution)/shard_map/ppermute | solution.py:17
  154.4 10.5 %collective-permute-start.54 = (bf16[3,192,384]{2,1,0:T(8,128)(2,1)S(1)}, bf16[3,192,384]{2,1,0:T(8,128)(2,1)}, u32[]{:S(2)}, u32[]{:S(2)}) collective-permute-start(bf16[3,192,384]{2,1,0:T(8,128)(2,1)S(1)} %slice.179), channel_id=1, source_target_pairs={{0,32},{32,64},{64,96},{96,0},{1,33},{33,65},{65,97},{97,1},{2,34}... | collective-permute-start | bytes 1327112 | tf_op jit(solution)/shard_map/ppermute | solution.py:17
  156.4 8.5 %collective-permute-start.55 = (bf16[3,192,384]{2,1,0:T(8,128)(2,1)S(1)}, bf16[3,192,384]{2,1,0:T(8,128)(2,1)}, u32[]{:S(2)}, u32[]{:S(2)}) collective-permute-start(bf16[3,192,384]{2,1,0:T(8,128)(2,1)S(1)} %slice.180), channel_id=1, source_target_pairs={{0,96},{32,0},{64,32},{96,64},{1,97},{33,1},{65,33},{97,65},{2,98}... | collective-permute-start | bytes 1327112 | tf_op jit(solution)/shard_map/ppermute | solution.py:17
  157.9 13.4 %collective-permute-start.51 = (bf16[3,384,384]{2,1,0:T(8,128)(2,1)}, bf16[3,384,384]{2,1,0:T(8,128)(2,1)}, u32[]{:S(2)}, u32[]{:S(2)}) collective-permute-start(bf16[3,384,384]{2,1,0:T(8,128)(2,1)} %collective-permute-done.50.refs_7_), channel_id=1, source_target_pairs={{0,1},{1,0},{2,3},{3,2},{4,5},{5,4},{6,7},{7,6},{8,9},{9,8},{10,11... | collective-permute-start | bytes 2654216 | tf_op jit(solution)/shard_map/ppermute | solution.py:17
  158.0 21.1 %collective-permute-start.53 = (bf16[3,384,384]{2,1,0:T(8,128)(2,1)}, bf16[3,384,384]{2,1,0:T(8,128)(2,1)}, u32[]{:S(2)}, u32[]{:S(2)}) collective-permute-start(bf16[3,384,384]{2,1,0:T(8,128)(2,1)} %collective-permute-done.52.refs_7_), channel_id=1, source_target_pairs={{0,1},{1,0},{2,3},{3,2},{4,5},{5,4},{6,7},{7,6},{8,9},{9,8},{10,11... | collective-permute-start | bytes 2654216 | tf_op jit(solution)/shard_map/ppermute | solution.py:17
  164.9 19.3 %collective-permute-start.56 = (bf16[3,192,384]{2,1,0:T(8,128)(2,1)}, bf16[3,192,384]{2,1,0:T(8,128)(2,1)S(1)}, u32[]{:S(2)}, u32[]{:S(2)}) collective-permute-start(bf16[3,192,384]{2,1,0:T(8,128)(2,1)} %collective-permute-done.54.refs_7_), channel_id=1, source_target_pairs={{0,1},{1,0},{2,3},{3,2},{4,5},{5,4},{6,7},{7,6},{8,9},{9,8},{10,11... | collective-permute-start | bytes 1327112 | tf_op jit(solution)/shard_map/ppermute | solution.py:17
  164.9 21.2 %collective-permute-start.57 = (bf16[3,192,384]{2,1,0:T(8,128)(2,1)}, bf16[3,192,384]{2,1,0:T(8,128)(2,1)S(1)}, u32[]{:S(2)}, u32[]{:S(2)}) collective-permute-start(bf16[3,192,384]{2,1,0:T(8,128)(2,1)} %collective-permute-done.55.refs_8_), channel_id=1, source_target_pairs={{0,1},{1,0},{2,3},{3,2},{4,5},{5,4},{6,7},{7,6},{8,9},{9,8},{10,11... | collective-permute-start | bytes 1327112 | tf_op jit(solution)/shard_map/ppermute | solution.py:17
  165.5 37.6 %collective-permute-start.33 = (bf16[128,6144]{1,0:T(8,128)(2,1)S(1)}, bf16[128,6144]{1,0:T(8,128)(2,1)S(1)}, u32[]{:S(2)}, u32[]{:S(2)}) collective-permute-start(bf16[128,6144]{1,0:T(8,128)(2,1)S(1)} %copy-done.6), channel_id=1, source_target_pairs={{0,2},{2,4},{4,6},{6,0},{1,3},{3,5},{5,7},{7,1},{8,10},{10,12},{12... | collective-permute-start | bytes 4718600 | tf_op jit(solution)/shard_map/ppermute | solution.py:17
  171.3 36.3 %collective-permute-start.35 = (bf16[128,6144]{1,0:T(8,128)(2,1)S(1)}, bf16[128,6144]{1,0:T(8,128)(2,1)S(1)}, u32[]{:S(2)}, u32[]{:S(2)}) collective-permute-start(bf16[128,6144]{1,0:T(8,128)(2,1)S(1)} %copy-done.6), channel_id=1, source_target_pairs={{0,6},{2,0},{4,2},{6,4},{1,7},{3,1},{5,3},{7,5},{8,14},{10,8},{12,... | collective-permute-start | bytes 4718600 | tf_op jit(solution)/shard_map/ppermute | solution.py:17
  179.1 15.9 %collective-permute-start.28 = (f32[32,384]{1,0:T(8,128)S(1)}, f32[32,384]{1,0:T(8,128)}, u32[]{:S(2)}, u32[]{:S(2)}) collective-permute-start(f32[32,384]{1,0:T(8,128)S(1)} %add_add_fusion), channel_id=1, source_target_pairs={{0,8},{8,16},{16,24},{24,0},{1,9},{9,17},{17,25},{25,1},{2,10},{10... | collective-permute-start | bytes 147464 | tf_op jit(solution)/shard_map/ppermute | solution.py:17
  184.2 12.4 %collective-permute-start.29 = (f32[32,384]{1,0:T(8,128)S(1)}, f32[32,384]{1,0:T(8,128)}, u32[]{:S(2)}, u32[]{:S(2)}) collective-permute-start(f32[32,384]{1,0:T(8,128)S(1)} %add_add_fusion), channel_id=1, source_target_pairs={{0,16},{8,24},{16,0},{24,8},{1,17},{9,25},{17,1},{25,9},{2,18},{10... | collective-permute-start | bytes 147464 | tf_op jit(solution)/shard_map/ppermute | solution.py:17
  186.1 21.5 %collective-permute-start.30 = (f32[32,384]{1,0:T(8,128)S(1)}, f32[32,384]{1,0:T(8,128)}, u32[]{:S(2)}, u32[]{:S(2)}) collective-permute-start(f32[32,384]{1,0:T(8,128)S(1)} %add_add_fusion), channel_id=1, source_target_pairs={{0,24},{8,0},{16,8},{24,16},{1,25},{9,1},{17,9},{25,17},{2,26},{10... | collective-permute-start | bytes 147464 | tf_op jit(solution)/shard_map/ppermute | solution.py:17
  194.9 12.8 %collective-permute-start.58 = (bf16[4,128,384]{2,1,0:T(8,128)(2,1)S(1)}, bf16[4,128,384]{2,1,0:T(8,128)(2,1)S(1)}, u32[]{:S(2)}, u32[]{:S(2)}) collective-permute-start(bf16[4,128,384]{2,1,0:T(8,128)(2,1)S(1)} %get-tuple-element.11), channel_id=1, source_target_pairs={{0,24},{8,0},{16,8},{24,16},{1,25},{9,1},{17,9},{25,17},{2,26},{10... | collective-permute-start | bytes 1179656 | tf_op jit(solution)/shard_map/ppermute | solution.py:17
  196.6 35.8 %copy-start.31 = (f32[32,384]{1,0:T(8,128)S(1)}, f32[32,384]{1,0:T(8,128)}, u32[]{:S(2)}) copy-start(f32[32,384]{1,0:T(8,128)} %copy-done.30) | copy-start | bytes 147460
  196.6 35.8 %copy-start.32 = (f32[32,32]{1,0:T(8,128)S(1)}, f32[32,32]{1,0:T(8,128)}, u32[]{:S(2)}) copy-start(f32[32,32]{1,0:T(8,128)} %inverse_of_factor.1) | copy-start | bytes 12292
  196.6 57.0 %collective-permute-start.39 = (bf16[128,6144]{1,0:T(8,128)(2,1)S(1)}, bf16[128,6144]{1,0:T(8,128)(2,1)S(1)}, u32[]{:S(2)}, u32[]{:S(2)}) collective-permute-start(bf16[128,6144]{1,0:T(8,128)(2,1)S(1)} %copy-done.6), channel_id=1, source_target_pairs={{0,1},{1,0},{2,3},{3,2},{4,5},{5,4},{6,7},{7,6},{8,9},{9,8},{10,11... | collective-permute-start | bytes 4718600 | tf_op jit(solution)/shard_map/ppermute | solution.py:17
  203.1 50.5 %collective-permute-start.40 = (bf16[128,6144]{1,0:T(8,128)(2,1)S(1)}, bf16[128,6144]{1,0:T(8,128)(2,1)}, u32[]{:S(2)}, u32[]{:S(2)}) collective-permute-start(bf16[128,6144]{1,0:T(8,128)(2,1)S(1)} %collective-permute-done.33.refs_2_), channel_id=1, source_target_pairs={{0,1},{1,0},{2,3},{3,2},{4,5},{5,4},{6,7},{7,6},{8,9},{9,8},{10,11... | collective-permute-start | bytes 4718600 | tf_op jit(solution)/shard_map/ppermute | solution.py:17
  207.6 45.9 %collective-permute-start.41 = (bf16[128,6144]{1,0:T(8,128)(2,1)S(1)}, bf16[128,6144]{1,0:T(8,128)(2,1)}, u32[]{:S(2)}, u32[]{:S(2)}) collective-permute-start(bf16[128,6144]{1,0:T(8,128)(2,1)S(1)} %collective-permute-done.35.refs_4_), channel_id=1, source_target_pairs={{0,1},{1,0},{2,3},{3,2},{4,5},{5,4},{6,7},{7,6},{8,9},{9,8},{10,11... | collective-permute-start | bytes 4718600 | tf_op jit(solution)/shard_map/ppermute | solution.py:17
  207.7 21.2 %collective-permute-start.59 = (bf16[4,128,384]{2,1,0:T(8,128)(2,1)S(1)}, bf16[4,128,384]{2,1,0:T(8,128)(2,1)S(1)}, u32[]{:S(2)}, u32[]{:S(2)}) collective-permute-start(bf16[4,128,384]{2,1,0:T(8,128)(2,1)S(1)} %get-tuple-element.10), channel_id=1, source_target_pairs={{0,8},{8,16},{16,24},{24,0},{1,9},{9,17},{17,25},{25,1},{2,10},{10... | collective-permute-start | bytes 1179656 | tf_op jit(solution)/shard_map/ppermute | solution.py:17
  207.8 21.2 %collective-permute-start.60 = (bf16[4,128,384]{2,1,0:T(8,128)(2,1)S(1)}, bf16[4,128,384]{2,1,0:T(8,128)(2,1)S(1)}, u32[]{:S(2)}, u32[]{:S(2)}) collective-permute-start(bf16[4,128,384]{2,1,0:T(8,128)(2,1)S(1)} %get-tuple-element.9), channel_id=1, source_target_pairs={{0,16},{8,24},{16,0},{24,8},{1,17},{9,25},{17,1},{25,9},{2,18},{10... | collective-permute-start | bytes 1179656 | tf_op jit(solution)/shard_map/ppermute | solution.py:17
  228.8 20.9 %collective-permute-start.34 = (bf16[64,6144]{1,0:T(8,128)(2,1)S(1)}, bf16[64,6144]{1,0:T(8,128)(2,1)S(1)}, u32[]{:S(2)}, u32[]{:S(2)}) collective-permute-start(bf16[64,6144]{1,0:T(8,128)(2,1)S(1)} %slice.166), channel_id=1, source_target_pairs={{0,2},{2,4},{4,6},{6,0},{1,3},{3,5},{5,7},{7,1},{8,10},{10,12},{12... | collective-permute-start | bytes 2359304 | tf_op jit(solution)/shard_map/ppermute | solution.py:17
  229.0 20.7 %collective-permute-start.36 = (bf16[64,6144]{1,0:T(8,128)(2,1)S(1)}, bf16[64,6144]{1,0:T(8,128)(2,1)}, u32[]{:S(2)}, u32[]{:S(2)}) collective-permute-start(bf16[64,6144]{1,0:T(8,128)(2,1)S(1)} %slice.167), channel_id=1, source_target_pairs={{0,6},{2,0},{4,2},{6,4},{1,7},{3,1},{5,3},{7,5},{8,14},{10,8},{12,... | collective-permute-start | bytes 2359304 | tf_op jit(solution)/shard_map/ppermute | solution.py:17
  233.5 38.1 %copy-start.13 = (f32[32,384]{1,0:T(8,128)}, f32[32,384]{1,0:T(8,128)S(1)}, u32[]{:S(2)}) copy-start(f32[32,384]{1,0:T(8,128)S(1)} %get-tuple-element.52) | copy-start | bytes 147460
  249.7 21.9 %collective-permute-start.37 = (bf16[64,6144]{1,0:T(8,128)(2,1)S(1)}, bf16[64,6144]{1,0:T(8,128)(2,1)}, u32[]{:S(2)}, u32[]{:S(2)}) collective-permute-start(bf16[64,6144]{1,0:T(8,128)(2,1)S(1)} %collective-permute-done.34.refs_0_), channel_id=1, source_target_pairs={{0,1},{1,0},{2,3},{3,2},{4,5},{5,4},{6,7},{7,6},{8,9},{9,8},{10,11... | collective-permute-start | bytes 2359304 | tf_op jit(solution)/shard_map/ppermute | solution.py:17
  249.7 21.9 %collective-permute-start.38 = (bf16[64,6144]{1,0:T(8,128)(2,1)}, bf16[64,6144]{1,0:T(8,128)(2,1)}, u32[]{:S(2)}, u32[]{:S(2)}) collective-permute-start(bf16[64,6144]{1,0:T(8,128)(2,1)} %collective-permute-done.36.refs_1_), channel_id=1, source_target_pairs={{0,1},{1,0},{2,3},{3,2},{4,5},{5,4},{6,7},{7,6},{8,9},{9,8},{10,11... | collective-permute-start | bytes 2359304 | tf_op jit(solution)/shard_map/ppermute | solution.py:17
  (34 other events, 379.6 us)

commit v2 on v0

v2 whole, which is shorter than its diff:
```python
import functools
import math

import jax
import jax.numpy as jnp
from jax import lax
from jax.experimental import pallas as pl
from jax.experimental.pallas import tpu as pltpu
from jax.sharding import Mesh, PartitionSpec as P

BF16, F32 = jnp.bfloat16, jnp.float32
SIZE = {"y": 4, "z": 4, "x": 4, "core": 2}
VMEM_LIMIT = 56 * 1024 * 1024


def shift(value, axis, step):
    n = SIZE[axis]
    return lax.ppermute(value, axis, [(i, (i + step) % n) for i in range(n)])


def split3(value):
    high = lax.reduce_precision(value, 8, 7)
    rest = value - high
    mid = lax.reduce_precision(rest, 8, 7)
    return high.astype(BF16), mid.astype(BF16), (rest - mid).astype(BF16)


def fold3(value):
    rows = value.shape[0] // 3
    return value[:rows] + value[rows : 2 * rows] + value[2 * rows :]


def mm(a, b, ca, cb):
    return lax.dot_general(a, b, (((ca,), (cb,)), ((), ())), preferred_element_type=F32)


def block(value, index):
    return lax.dynamic_index_in_dim(value, index, 0, False)


def reduce_scatter(value, axis):
    n, me = SIZE[axis], lax.axis_index(axis)
    parts = [shift(block(value, (me + s) % n), axis, s) for s in range(1, n)]
    total = block(value, me)
    for part in parts:
        total = total + part
    return total


def all_sum(value, axis):
    parts = [shift(value, axis, s) for s in range(1, SIZE[axis])]
    for part in parts:
        value = value + part
    return value


def all_blocks(value, axis):
    n = math.prod(SIZE[a] for a in axis)
    return lax.all_to_all(jnp.broadcast_to(value[None], (n,) + value.shape), axis, 0, 0)


def both_cores(value):
    other = shift(value, "core", 1)
    first = lax.axis_index("core") == 0
    return jnp.stack([jnp.where(first, value, other), jnp.where(first, other, value)])


def inverse_kernel(left_ref, out_ref):
    n = out_ref.shape[0]
    grams = mm(left_ref[...], left_ref[...], 1, 1)
    gram = fold3(grams[:, :n] + grams[:, n : 2 * n] + grams[:, 2 * n :])
    row = lax.broadcasted_iota(jnp.int32, (n, 2 * n), 0)
    col = lax.broadcasted_iota(jnp.int32, (n, 2 * n), 1)
    eye = jnp.where(row + n == col, 1.0, 0.0).astype(F32)
    work = jnp.concatenate([gram, jnp.zeros((n, n), F32)], axis=1) + eye
    for k in range(n):
        pivot_row = work[k : k + 1, :]
        pivot = jnp.sum(jnp.where(col[:1] == k, pivot_row, 0.0), axis=1, keepdims=True)
        column = jnp.sum(jnp.where(col == k, work, 0.0), axis=1, keepdims=True)
        factor = jnp.where(row[:, :1] > k, column / pivot, 0.0)
        root = lax.rsqrt(pivot)
        root = root * (1.5 - 0.5 * pivot * root * root)
        scale = jnp.where(row[:, :1] == k, root, 1.0)
        work = (work - factor * pivot_row) * scale
    out_ref[...] = work[:, n:]


def inverse_of_factor(left3):
    rank = left3.shape[0] // 3
    return pl.pallas_call(
        inverse_kernel,
        out_shape=jax.ShapeDtypeStruct((rank, rank), F32),
        name="inverse_of_factor",
    )(left3)


def parts3(value):
    high = value.astype(BF16)
    rest = value - high.astype(F32)
    mid = rest.astype(BF16)
    return high, mid, (rest - mid.astype(F32)).astype(BF16)


def residual_kernel(act_ref, cot_ref, residual_ref, left_ref, inverse_ref, factor_ref, out_ref):
    basis = lax.dot_general(
        inverse_ref[...], left_ref[...], (((1,), (0,)), ((), ())), precision=lax.Precision.HIGHEST, preferred_element_type=F32
    )
    b_h, b_m, b_l = parts3(basis)
    f_h, f_m, f_l = parts3(factor_ref[...])
    basis6 = jnp.concatenate([b_h, b_m, b_l, b_h, b_m, b_h], 0)
    factor6 = jnp.concatenate([f_h, f_h, f_h, f_m, f_m, f_l], 0)
    total = mm(act_ref[...], cot_ref[...], 0, 0) + residual_ref[...].astype(F32)
    out_ref[...] = (total - mm(basis6, factor6, 0, 0)).astype(BF16)


def residual_call(act, cot, residual, left, inverse, factor, tile):
    k, d = act.shape
    cols, rank = cot.shape[1], left.shape[0]
    whole = lambda a: pl.BlockSpec(a.shape, lambda i: (0, 0))
    rows = pl.BlockSpec((tile, cols), lambda i: (i, 0))
    return pl.pallas_call(
        residual_kernel,
        out_shape=jax.ShapeDtypeStruct((d, cols), BF16),
        grid=(d // tile,),
        in_specs=[
            pl.BlockSpec((k, tile), lambda i: (0, i)),
            whole(cot),
            rows,
            pl.BlockSpec((rank, tile), lambda i: (0, i)),
            whole(inverse),
            whole(factor),
        ],
        out_specs=rows,
        compiler_params=pltpu.CompilerParams(vmem_limit_bytes=VMEM_LIMIT),
        cost_estimate=pl.CostEstimate(
            flops=2 * d * cols * (k + 6 * rank), bytes_accessed=2 * d * k + 4 * d * cols + 4 * d * rank, transcendentals=0
        ),
        name="new_residual",
    )(act, cot, residual, left, inverse, factor)


def input_kernel(n_cot, at_ref, *refs):
    cots, w_ref, outs = refs[:n_cot], refs[n_cot], refs[n_cot + 1 :]
    blocks, chips, cores = w_ref.shape[:3]
    tok, width = outs[0].shape
    total = jnp.zeros((tok * len(outs), width), F32)
    for s in range(chips):
        tokens = jnp.concatenate([jnp.concatenate([c[2 * s], c[2 * s + 1]], 1) for c in cots], 0)
        rows = [jnp.concatenate([w_ref[b, at_ref[s], at_ref[chips + c]] for c in range(cores)], 1) for b in range(blocks)]
        total = total + mm(tokens, jnp.concatenate(rows, 0), 1, 1)
    for i, out in enumerate(outs):
        out[...] = total[i * tok : (i + 1) * tok].astype(BF16)


def input_call(cots, weight, at, blocks):
    n, chips, cores, rows, cols = weight.shape
    _, tok, _ = cots[0].shape
    tokens = 4 * tok
    return pl.pallas_call(
        functools.partial(input_kernel, len(cots)),
        out_shape=[jax.ShapeDtypeStruct((tok, n * rows), BF16)] * 4,
        grid_spec=pltpu.PrefetchScalarGridSpec(
            num_scalar_prefetch=1,
            grid=(n // blocks,),
            in_specs=[pl.BlockSpec(c.shape, lambda i, q: (0, 0, 0)) for c in cots]
            + [pl.BlockSpec((blocks, chips, cores, rows, cols), lambda i, q: (i, 0, 0, 0, 0))],
            out_specs=[pl.BlockSpec((tok, blocks * rows), lambda i, q: (0, i))] * 4,
        ),
        compiler_params=pltpu.CompilerParams(vmem_limit_bytes=VMEM_LIMIT),
        cost_estimate=pl.CostEstimate(
            flops=2 * tokens * n * rows * cols * 8, bytes_accessed=16 * cols * (tokens + n * rows), transcendentals=0
        ),
        name="input_grads",
    )(jnp.stack(at).astype(jnp.int32), *cots, weight)


def copy_kernel(n_in, n_out, plan, at_ref, *refs):
    ins, outs, sems = refs[:n_in], refs[n_in : n_in + n_out], refs[n_in + n_out]
    copies = [pltpu.make_async_copy(*pair, sems.at[i]) for i, pair in enumerate(plan(at_ref, ins, outs))]
    for copy in copies:
        copy.start()
    for copy in copies:
        copy.wait()


def copy_call(plan, n_copies, ins, outs, at, name):
    any_spec = pl.BlockSpec(memory_space=pl.ANY)
    moved = sum(2 * math.prod(o.shape) * o.dtype.itemsize for o in outs)
    return pl.pallas_call(
        functools.partial(copy_kernel, len(ins), len(outs), plan),
        out_shape=outs,
        grid_spec=pltpu.PrefetchScalarGridSpec(
            num_scalar_prefetch=1,
            grid=(1,),
            in_specs=[any_spec] * len(ins),
            out_specs=[pl.BlockSpec(o.shape, lambda i, a, n=len(o.shape): (0,) * n) for o in outs],
            scratch_shapes=[pltpu.SemaphoreType.DMA((n_copies,))],
        ),
        compiler_params=pltpu.CompilerParams(vmem_limit_bytes=VMEM_LIMIT),
        cost_estimate=pl.CostEstimate(flops=0, bytes_accessed=moved, transcendentals=0),
        name=name,
    )(jnp.stack(at).astype(jnp.int32), *ins)


def part_of(ref, index, size):
    return ref.at[pl.ds(pl.multiple_of(index * size, size), size)]


def pack_plan(tok, at, ins, outs):
    return [
        (part_of(cot, at[s], tok), out.at[pl.ds(i * tok, tok)]) for s, out in zip((1, 2, 3), outs) for i, cot in enumerate(ins)
    ]


def unpack_plan(tok, at, ins, outs):
    cot, other, *got = ins
    pairs = [(part_of(cot, at[0], tok), outs[0].at[0]), (part_of(other, at[0], tok), outs[0].at[1])]
    return pairs + [(g.at[pl.ds(i * tok, tok)], outs[0].at[2 * s + 2 + i]) for s, g in enumerate(got) for i in (0, 1)]


def place_plan(width, at, ins, outs):
    return [(r, outs[0].at[:, pl.ds(pl.multiple_of(at[i] * width, width), width)]) for i, r in enumerate(ins)]


def per_device(activations, cotangent, weight, residual, warm_factor):
    iy, iz, ix, ic = (lax.axis_index(a) for a in ("y", "z", "x", "core"))
    tok, d = activations.shape
    tok_dev, cols = cotangent.shape
    rank = warm_factor.shape[1]
    residual = residual[0]
    scale = tok_dev ** (-0.5)
    quarter = d // 4
    sub = quarter // 4

    like = lambda *shape: jax.ShapeDtypeStruct(shape, BF16)
    w_send = lax.dynamic_slice_in_dim(weight, iz * quarter + iy * sub, sub, 0)
    w_all = lax.all_gather(w_send, ("y", "x", "core")).reshape(4, 4, 2, sub, cols)

    cot_other = shift(cotangent, "core", 1)
    at = [((ix + s) % 4) * 2 + ic for s in range(4)]
    packed = copy_call(functools.partial(pack_plan, tok), 6, [cotangent, cot_other], [like(2 * tok, cols)] * 3, at, "pack")
    got = [shift(p, "x", s) for s, p in zip((1, 2, 3), packed)]

    cot, w_send, *_ = lax.optimization_barrier((cotangent, w_send, *packed))
    warm3 = jnp.concatenate(split3(warm_factor.T), 0)
    cw = fold3(mm(warm3, cot, 1, 1)) * scale
    cw = reduce_scatter(cw.reshape(rank, 4, 2 * tok).transpose(1, 0, 2), "x")
    act, cw = lax.optimization_barrier((activations, cw))
    gathered = lax.all_gather(act, ("x", "core"), axis=0, tiled=True)
    cw = reduce_scatter(cw.reshape(rank, 2, tok).transpose(1, 0, 2), "core")

    cw3 = jnp.concatenate(split3(cw), 0)
    left = fold3(mm(cw3, activations, 1, 0)) + fold3(mm(warm3, residual, 1, 1))
    tiles = left.reshape(rank // 8, 8, d // 128, 128).transpose(0, 2, 1, 3).reshape(-1, 8, 128)
    n_tiles = tiles.shape[0]
    part = reduce_scatter(tiles.reshape(2, n_tiles // 2, 8, 128), "core")
    part = lax.all_to_all(part.reshape(16, n_tiles // 32, 8, 128), ("y", "z"), 0, 0).sum(0)
    part, *got = lax.optimization_barrier((part, *got))

    (cot_own,) = copy_call(
        functools.partial(unpack_plan, tok), 8, [cotangent, cot_other] + got, [like(8, tok, cols)], at, "unpack"
    )
    c_low, c_high = shift(cot_own, "z", 1), shift(cot_own, "z", -1)
    part = all_blocks(part, ("x",)).sum(0)
    part, cot_own = lax.optimization_barrier((part, cot_own))
    part = all_blocks(part, ("y", "z")).reshape(-1, 8, 128)
    part, c_low, c_high = lax.optimization_barrier((part, c_low, c_high))
    half = tok // 2
    c_far = [shift(c_low[:, :half], "z", 1), shift(c_high[:, half:], "z", -1)]
    part = both_cores(part)
    left = part.reshape(rank // 8, d // 128, 8, 128).transpose(0, 2, 1, 3).reshape(rank, d)

    left3 = jnp.concatenate(split3(left), 0)
    right = fold3(mm(left3, activations, 1, 1)) * scale
    right = all_blocks(both_cores(right), ("x",))

    right, *c_far = lax.optimization_barrier((right, *c_far))
    cots = [cot_own, c_low, c_high, *c_far]
    grads = input_call(cots, w_all, [(ix - s) % 4 for s in range(4)] + [ic, 1 - ic], 2)
    right, *grads = lax.optimization_barrier((right, *grads))
    back = [grads[0], shift(grads[1], "z", -1), shift(grads[2], "z", 1), shift(grads[3], "z", 2)]

    right = right.reshape(8, rank, tok).transpose(1, 0, 2).reshape(rank, 8 * tok)
    right3 = jnp.concatenate(split3(right), 0)
    sums = fold3(mm(right3, cotangent, 1, 0)) + fold3(mm(left3, residual, 1, 0))
    sums = all_sum(sums, "y")
    at = [(iz + s) % 4 for s in (0, 1, -1, 2)]
    (input_grads,) = copy_call(functools.partial(place_plan, quarter), 4, back, [like(tok, d)], at, "place")
    sums = all_sum(sums, "z")
    left3, right = lax.optimization_barrier((left3, right))
    inverse = inverse_of_factor(left3)
    factor = jnp.dot(inverse, sums, precision=lax.Precision.HIGHEST) * (1.0 / 16)
    cot_scaled = (cotangent.astype(F32) * scale).astype(BF16)
    new_residual = residual_call(gathered, cot_scaled, residual, left, inverse, factor, 1024)
    return factor.T, new_residual[None], input_grads


def solution(mesh):
    fine = Mesh(mesh.devices.reshape(4, 4, 4, 2), ("y", "z", "x", "core"))
    dp, tensor = ("y", "z"), ("x", "core")
    in_specs = (
        P(dp + tensor, None),
        P(dp, tensor),
        P(None, tensor),
        P(dp, None, tensor),
        P(tensor, None),
    )
    out_specs = (P(tensor, None), P(dp, None, tensor), P(dp + tensor, None))
    return jax.shard_map(per_device, mesh=fine, in_specs=in_specs, out_specs=out_specs, check_vma=False)
```

time: 493 us -> 183 us (0.37); the launches traced: 484 us -> 182 us
  waiting for transfers between devices: 184 us -> 34 us
  matrix products: 98.2 us -> 10.5 us
  other arithmetic: 65 us -> 6.49 us
  blocking collectives: 73.4 us -> 24.1 us
  starting transfers between devices: 0.33 us -> 43.8 us
  Pallas kernels: 0 us -> 39.1 us
  between operations: 37.3 us -> 14.6 us
  local copies, waits for them, and re-layouts: 26.1 us -> 9.35 us
    psum x1 -> x0, waiting for transfers between devices: 112 us -> none  [per_device(): left = lax.psum(partial_left, ('dp', 'tensor'))]
    dot_general x68 -> x7, matrix products: 98.2 us -> 10.5 us  [the longest x6 9.02 us: mm(): lax.dot_general(a, b, (((ca,), (cb,)), ((), ())), preferred_element_type=...]
    psum x1 -> x0, blocking collectives: 73.4 us -> none  [per_device(): new_factor = lax.psum(right_part, 'dp') / lax.axis_size('dp')]
    all_gather x1 -> x2, waiting for transfers between devices: 71.5 us -> 0.02 us  [the longest x1 0.02 us: per_device(): gathered = lax.all_gather(act, ('x', 'core'), axis=0, tiled=True)]
    another operation x62 -> x6, other arithmetic: 42.1 us -> 2.08 us  [the longest x2 1.21 us: copy_call(): jnp.stack(at).astype(jnp.int32)]
    pallas_call x0 -> x6, Pallas kernels: none -> 39.1 us  [the longest x1 14.4 us: residual_call(): pl.pallas_call(residual_kernel, out_shape=jax.ShapeDtypeStruct((d, cols),...]
    ppermute x0 -> x24, starting transfers between devices: none -> 32.1 us  [shift(): return lax.ppermute(value, axis, [(i, (i + step) % n) for i in range(n)])]
    ppermute x0 -> x24, waiting for transfers between devices: none -> 24.6 us  [shift(): return lax.ppermute(value, axis, [(i, (i + step) % n) for i in range(n)])]
  transfers between devices with their start and end apart: 3 -> 28, of which waited for: 2 -> 14; matrix products, arithmetic and copies ran while one was open for 33% -> 11% of each run, Pallas kernels for 0% -> 14%
where the time goes in v2:
time: 183 us; the launch traced here: 182 us
  starting transfers between devices  43.8 us (24%)
  Pallas kernels  39.1 us (21%)
  waiting for transfers between devices  34 us (19%)
  blocking collectives  24.1 us (13%)
  between operations  14.6 us (8%)
  matrix products  10.5 us (6%)
  local copies, waits for them, and re-layouts  9.35 us (5%)
  other arithmetic  6.49 us (4%)
    ppermute x24, starting transfers between devices, shift(): return lax.ppermute(value, axis, [(i, (i + step) % n) for i in range(n)])  32.1 us
    ppermute x24, waiting for transfers between devices, shift(): return lax.ppermute(value, axis, [(i, (i + step) % n) for i in range(n)])  24.6 us
    all_to_all x2, blocking collectives, all_blocks(): lax.all_to_all(jnp.broadcast_to(value[None], (n,) + value.shape), axis, 0...  24.1 us
    pallas_call x1, Pallas kernels, residual_call(): pl.pallas_call(residual_kernel, out_shape=jax.ShapeDtypeStruct((d, cols),...  14.4 us
    pallas_call x1, Pallas kernels, input_call(): pl.pallas_call(functools.partial(input_kernel, len(cots)), out_shape=[jax...  10.4 us
    dot_general x6, matrix products, mm(): lax.dot_general(a, b, (((ca,), (cb,)), ((), ())), preferred_element_type=...  9.02 us
    pallas_call x3, Pallas kernels, copy_call(): pl.pallas_call(functools.partial(copy_kernel, len(ins), len(outs), plan),...  8.71 us
    all_to_all x1, starting transfers between devices, per_device(): lax.all_to_all(part.reshape(16, n_tiles // 32, 8, 128), ('y', 'z'), 0, 0)  8.09 us
  transfers between devices with their start and end apart: 28, of which 14 were waited for; matrix products, arithmetic and copies ran while one was open for 11% of the time, Pallas kernels for 14%

profile of v2, /device:TPU:0, one launch (start us, length us, event | category | flops | bytes accessed | tf_op | source)
XLA Modules:
  0.0 181.9 jit_solution(5883252283676730917)
XLA Ops:
  7.2 1.8 constant_dynamic-slice_fusion.6
  9.2 0.6 pad_add_fusion.at_ref
  9.8 0.8 reduce-precision_convert_fusion.5
  10.6 1.0 collective-permute-done.refs_1_
  11.7 0.9 copy-done.4
  12.5 2.7 %pack.1 = (bf16[256,384]{1,0:T(8,128)(2,1)}, bf16[256,384]{1,0:T(8,128)(2,1)}, bf16[256,384]{1,0:T(8,128)(2,1)}) custom-call(s32[4]{0:T(128)} %pad_add_fusion.at_ref, bf16[1024,384]{1,0:T(8,128)(2,1)} %refs_0_.3, bf16[1024,384]{1,0:T(8,128)(2,1)} %copy-done.4), custom_call_target="tpu_custom_call" | custom-call | bytes 1179648 | tf_op jit(solution)/shard_map/pack/pallas_call | solution.py:189
  15.2 0.4 fusion.18
  15.8 1.6 collective-permute-start.1
  17.5 2.7 %collective-permute-start.2 = (f32[32,256]{1,0:T(8,128)S(1)}, f32[32,256]{1,0:T(8,128)S(1)}, u32[]{:S(2)}, u32[]{:S(2)}) collective-permute-start(f32[32,256]{1,0:T(8,128)S(1)} %bitcast.99), channel_id=1, source_target_pairs={{0,4},{2,6},{4,0},{6,2},{1,5},{3,7},{5,1},{7,3},{8,12},{10,14},{12... | collective-permute-start | bytes 98312 | tf_op jit(solution)/shard_map/ppermute | solution.py:18
  20.2 1.4 collective-permute-start.3
  21.6 1.2 collective-permute-done.2
  22.9 1.2 collective-permute-done.3
  24.4 4.0 %fusion.17 = f32[96,6144]{1,0:T(8,128)S(1)} fusion(bf16[32,384]{1,0:T(8,128)(2,1)S(1)} %get-tuple-element.72, bf16[32,384]{1,0:T(8,128)(2,1)S(1)} %get-tuple-element.73, bf16[32,384]{1,0:T(8,128)(2,1)S(1)} %get-tuple-element.71, bf16[1,6144,384]{2,1,0:T(8,128)(2,1)} %param.8), kind=kOutput, calls=%fused_computation.55 | convolution fusion | flops 453206016 | bytes 7151616 | tf_op jit(solution)/shard_map/dot_general | solution.py:34
  28.4 0.5 fusion.19
  28.9 0.4 fusion.1
  29.3 0.5 collective-permute-start.5
  29.8 1.3 collective-permute-done.5
  31.1 0.8 bitcast_add_fusion
  31.9 8.1 %all-to-all-start = ((f32[16,6,8,128]{3,2,1,0:T(8,128)}), f32[16,6,8,128]{3,2,1,0:T(8,128)S(1)}, u32[]{:S(2)}, u32[]{:S(2)}) async-start(f32[16,6,8,128]{3,2,1,0:T(8,128)} %bitcast.15), calls=%async_computation | async-start | bytes 786432 | tf_op jit(solution)/shard_map/all_to_all | solution.py:257
  40.0 0.3 collective-permute-start.6
  40.3 4.3 %collective-permute-start.7 = (bf16[256,384]{1,0:T(8,128)(2,1)S(1)}, bf16[256,384]{1,0:T(8,128)(2,1)S(1)}, u32[]{:S(2)}, u32[]{:S(2)}) collective-permute-start(bf16[256,384]{1,0:T(8,128)(2,1)S(1)} %copy-done.19), channel_id=1, source_target_pairs={{0,4},{2,6},{4,0},{6,2},{1,5},{3,7},{5,1},{7,3},{8,12},{10,14},{12... | collective-permute-start | bytes 589832 | tf_op jit(solution)/shard_map/ppermute | solution.py:18
  44.7 6.1 %all-to-all-done = f32[16,6,8,128]{3,2,1,0:T(8,128)S(1)} async-done(((f32[16,6,8,128]{3,2,1,0:T(8,128)}), f32[16,6,8,128]{3,2,1,0:T(8,128)S(1)}, u32[]{:S(2)}, u32[]{:S(2)}) %all-to-all-start) | async-done | bytes 393248 | tf_op jit(solution)/shard_map/all_to_all | solution.py:257
  50.9 10.0 %collective-permute-done.7.refs_3_ = bf16[256,384]{1,0:T(8,128)(2,1)S(1)} collective-permute-done((bf16[256,384]{1,0:T(8,128)(2,1)S(1)}, bf16[256,384]{1,0:T(8,128)(2,1)S(1)}, u32[]{:S(2)}, u32[]{:S(2)}) %collective-permute-start.7) | collective-permute-done | bytes 196640 | tf_op jit(solution)/shard_map/ppermute | solution.py:18
  60.9 0.6 collective-permute-done.8.refs_4_
  61.5 0.7 copy-done.10
  62.2 2.9 %unpack.1.refs_0_ = bf16[8,128,384]{2,1,0:T(8,128)(2,1)} custom-call(s32[4]{0:T(128)} %pad_add_fusion.at_ref, bf16[1024,384]{1,0:T(8,128)(2,1)} %refs_0_.3, bf16[1024,384]{1,0:T(8,128)(2,1)} %copy-done.4, bf16[256,384]{1,0:T(8,128)(2,1)} %copy-done.8, bf16[256,384]{1,0:T(8,128)(2,1)} %copy-done.9, bf16[256,384]{1,0:T(8,128)(2,1)} %copy-done.10), custom_call_target="tpu_custom_call" | custom-call | bytes 1572864 | tf_op jit(solution)/shard_map/unpack/pallas_call | solution.py:189
  65.1 3.3 %collective-permute-start.10 = (bf16[8,128,384]{2,1,0:T(8,128)(2,1)}, bf16[8,128,384]{2,1,0:T(8,128)(2,1)S(1)}, u32[]{:S(2)}, u32[]{:S(2)}) collective-permute-start(bf16[8,128,384]{2,1,0:T(8,128)(2,1)} %unpack.1.refs_0_), channel_id=1, source_target_pairs={{0,24},{8,0},{16,8},{24,16},{1,25},{9,1},{17,9},{25,17},{2,26},{10... | collective-permute-start | bytes 2359304 | tf_op jit(solution)/shard_map/ppermute | solution.py:18
  68.3 8.2 %all_to_all.20 = f32[4,6,8,128]{3,2,1,0:T(8,128)S(1)} all-to-all(f32[4,6,8,128]{3,2,1,0:T(8,128)S(1)} %broadcast_in_dim.8), channel_id=1, replica_groups=mesh['y'=4,'z'=4,'x'=4,'core'=2] {'x'}, dimensions={0} | all-to-all | bytes 196608 | tf_op jit(solution)/shard_map/all_to_all | solution.py:59
  76.6 15.9 %all_to_all.21 = f32[16,6,8,128]{3,2,1,0:T(8,128)S(1)} all-to-all(f32[16,6,8,128]{3,2,1,0:T(8,128)S(1)} %broadcast_in_dim.9), channel_id=1, replica_groups=mesh['y'=4,'z'=4,'x'=4,'core'=2] {'y','z'}, dimensions={0} | all-to-all | bytes 786432 | tf_op jit(solution)/shard_map/all_to_all | solution.py:59
  92.5 0.9 copy-done.11
  93.4 1.7 collective-permute-done.11
  95.4 0.6 fusion.34
  96.1 0.6 copy-done.13
  96.8 0.7 stack.91.at_ref
  97.5 1.0 slice.72
  98.6 0.4 collective-permute-start.13
  99.0 3.0 %collective-permute-start.14 = (bf16[8,64,384]{2,1,0:T(8,128)(2,1)S(1)}, bf16[8,64,384]{2,1,0:T(8,128)(2,1)S(1)}, u32[]{:S(2)}, u32[]{:S(2)}) collective-permute-start(bf16[8,64,384]{2,1,0:T(8,128)(2,1)S(1)} %slice.73), channel_id=1, source_target_pairs={{0,24},{8,0},{16,8},{24,16},{1,25},{9,1},{17,9},{25,17},{2,26},{10... | collective-permute-start | bytes 1179656 | tf_op jit(solution)/shard_map/ppermute | solution.py:18
  102.0 0.8 select_bitcast_fusion.3
  102.8 0.7 broadcast_in_dim.10
  103.5 3.5 %all-to-all-start.3 = ((f32[4,2,32,128]{3,1,2,0:T(2,128)}), f32[4,2,32,128]{3,1,2,0:T(2,128)S(1)}, u32[]{:S(2)}, u32[]{:S(2)}) async-start(f32[4,2,32,128]{3,1,2,0:T(2,128)} %broadcast_in_dim.10), calls=%async_computation.3 | async-start | bytes 262144 | tf_op jit(solution)/shard_map/all_to_all | solution.py:59
  107.0 3.2 %fusion.31 = f32[96,384]{1,0:T(8,128)S(1)} fusion(bf16[1,6144,384]{2,1,0:T(8,128)(2,1)} %param.8, bf16[32,6144]{1,0:T(8,128)(2,1)S(1)} %get-tuple-element.60, bf16[32,6144]{1,0:T(8,128)(2,1)S(1)} %get-tuple-element.61, bf16[32,6144]{1,0:T(8,128)(2,1)S(1)} %get-tuple-element.59), kind=kOutput, calls=%fused_computation.86 | convolution fusion | flops 456523776 | bytes 6045696 | tf_op jit(solution)/shard_map/dot_general | solution.py:34
  110.3 1.0 collective-permute-done.13.refs_3_
  111.2 3.2 %all-to-all-done.3 = f32[4,2,32,128]{3,1,2,0:T(2,128)S(1)} async-done(((f32[4,2,32,128]{3,1,2,0:T(2,128)}), f32[4,2,32,128]{3,1,2,0:T(2,128)S(1)}, u32[]{:S(2)}, u32[]{:S(2)}) %all-to-all-start.3) | async-done | bytes 131104 | tf_op jit(solution)/shard_map/all_to_all | solution.py:59
  114.5 10.4 %input_grads.1 = (bf16[128,1536]{1,0:T(8,128)(2,1)}, bf16[128,1536]{1,0:T(8,128)(2,1)}, bf16[128,1536]{1,0:T(8,128)(2,1)}, bf16[128,1536]{1,0:T(8,128)(2,1)}) custom-call(s32[6]{0:T(128)} %stack.91.at_ref, bf16[8,128,384]{2,1,0:T(8,128)(2,1)} %unpack.1.refs_0_, bf16[8,128,384]{2,1,0:T(8,128)(2,1)} %collective-permute-done.9.refs_1_, ...), custom_call_target="tpu_custom_call" | custom-call | flops 4831838208 | bytes 12582912 | tf_op jit(solution)/shard_map/input_grads/pallas_call | solution.py:159
  125.0 0.3 fusion.2
  125.5 2.7 %collective-permute-start.16 = (f32[32,384]{1,0:T(8,128)S(1)}, f32[32,384]{1,0:T(8,128)S(1)}, u32[]{:S(2)}, u32[]{:S(2)}) collective-permute-start(f32[32,384]{1,0:T(8,128)S(1)} %fusion.11), channel_id=1, source_target_pairs={{0,64},{32,96},{64,0},{96,32},{1,65},{33,97},{65,1},{97,33},{2,66}... | collective-permute-start | bytes 147464 | tf_op jit(solution)/shard_map/ppermute | solution.py:18
  128.2 1.2 collective-permute-start.17
  129.4 1.0 multiply_convert_fusion.cot_ref
  130.5 0.2 collective-permute-done.15
  130.7 0.5 collective-permute-done.16
  131.2 1.1 collective-permute-done.17
  132.4 0.6 pad_add_fusion.1.at_ref
  133.0 3.2 %collective-permute-start.21 = (bf16[128,1536]{1,0:T(8,128)(2,1)}, bf16[128,1536]{1,0:T(8,128)(2,1)S(1)}, u32[]{:S(2)}, u32[]{:S(2)}) collective-permute-start(bf16[128,1536]{1,0:T(8,128)(2,1)} %get-tuple-element.56), channel_id=1, source_target_pairs={{0,24},{8,0},{16,8},{24,16},{1,25},{9,1},{17,9},{25,17},{2,26},{10... | collective-permute-start | bytes 1179656 | tf_op jit(solution)/shard_map/ppermute | solution.py:18
  136.3 1.5 collective-permute-start.23
  137.7 2.1 %collective-permute-start.19 = (f32[32,384]{1,0:T(8,128)S(1)}, f32[32,384]{1,0:T(8,128)S(1)}, u32[]{:S(2)}, u32[]{:S(2)}) collective-permute-start(f32[32,384]{1,0:T(8,128)S(1)} %add_add_fusion), channel_id=1, source_target_pairs={{0,16},{8,24},{16,0},{24,8},{1,17},{9,25},{17,1},{25,9},{2,18},{10... | collective-permute-start | bytes 147464 | tf_op jit(solution)/shard_map/ppermute | solution.py:18
  139.9 3.2 %collective-permute-start.20 = (f32[32,384]{1,0:T(8,128)S(1)}, f32[32,384]{1,0:T(8,128)S(1)}, u32[]{:S(2)}, u32[]{:S(2)}) collective-permute-start(f32[32,384]{1,0:T(8,128)S(1)} %add_add_fusion), channel_id=1, source_target_pairs={{0,24},{8,0},{16,8},{24,16},{1,25},{9,1},{17,9},{25,17},{2,26},{10... | collective-permute-start | bytes 147464 | tf_op jit(solution)/shard_map/ppermute | solution.py:18
  143.0 1.1 pad_maximum_fusion.left_ref
  144.1 5.6 %inverse_of_factor.1.inverse_ref = f32[32,32]{1,0:T(8,128)} custom-call(bf16[96,6144]{1,0:T(8,128)(2,1)} %pad_maximum_fusion.left_ref), custom_call_target="tpu_custom_call" | custom-call | tf_op jit(solution)/shard_map/inverse_of_factor/pallas_call | solution.py:90
  149.7 4.6 %collective-permute-done.19 = f32[32,384]{1,0:T(8,128)S(1)} collective-permute-done((f32[32,384]{1,0:T(8,128)S(1)}, f32[32,384]{1,0:T(8,128)S(1)}, u32[]{:S(2)}, u32[]{:S(2)}) %collective-permute-start.19) | collective-permute-done | bytes 49184 | tf_op jit(solution)/shard_map/ppermute | solution.py:18
  154.3 1.5 convolution_multiply_fusion.factor_ref
  155.8 0.7 copy-done.5
  156.7 0.7 copy-done.7
  157.4 3.2 %place.1 = bf16[128,6144]{1,0:T(8,128)(2,1)} custom-call(s32[4]{0:T(128)} %pad_add_fusion.1.at_ref, bf16[128,1536]{1,0:T(8,128)(2,1)} %get-tuple-element.55.refs_0_, bf16[128,1536]{1,0:T(8,128)(2,1)} %copy-done.5, bf16[128,1536]{1,0:T(8,128)(2,1)} %copy-done.6, bf16[128,1536]{1,0:T(8,128)(2,1)} %copy-done.7), custom_call_target="tpu_custom_call" | custom-call | bytes 3145728 | tf_op jit(solution)/shard_map/place/pallas_call | solution.py:189
  160.7 14.4 %new_residual.1 = bf16[6144,384]{1,0:T(8,128)(2,1)} custom-call(bf16[1024,6144]{1,0:T(8,128)(2,1)} %all-gather.4.cloned.1.call-done.act_ref, bf16[1024,384]{1,0:T(8,128)(2,1)} %multiply_convert_fusion.cot_ref, bf16[6144,384]{1,0:T(8,128)(2,1)} %bitcast.87, f32[32,6144]{1,0:T(8,128)} %bitcast.89, f32[32,32]{1,0:T(8,128)} %inverse_of_factor.1.inverse_ref, ...), custom_call_target="tpu_custom_call" | custom-call | flops 5737807872 | bytes 22806528 | tf_op jit(solution)/shard_map/new_residual/pallas_call | solution.py:121
  (89 shorter events, 1.9 us)
Async XLA Ops:
  7.2 8.0 %copy-start = (bf16[1024,384]{1,0:T(8,128)(2,1)S(1)}, bf16[1024,384]{1,0:T(8,128)(2,1)}, u32[]{:S(2)}) copy-start(bf16[1024,384]{1,0:T(8,128)(2,1)} %refs_0_.3) | copy-start | bytes 2359300
  7.2 107.3 %all-gather.6.cloned.1.call-start = ((), (), s32[]{:S(2)}) async-start(), calls=%async_computation.5 | async-start | bytes 9732096 | tf_op jit(solution)/shard_map/all_gather | solution.py:237
  9.0 151.6 %all-gather.4.cloned.1.call-start = ((), (), s32[]{:S(2)}) async-start(), calls=%async_computation.4 | async-start | bytes 14155776 | tf_op jit(solution)/shard_map/all_gather | solution.py:249
  9.1 2.6 %collective-permute-start = (bf16[1024,384]{1,0:T(8,128)(2,1)}, bf16[1024,384]{1,0:T(8,128)(2,1)S(1)}, u32[]{:S(2)}, u32[]{:S(2)}) collective-permute-start(bf16[1024,384]{1,0:T(8,128)(2,1)} %refs_0_.3), channel_id=1, source_target_pairs={{0,1},{1,0},{2,3},{3,2},{4,5},{5,4},{6,7},{7,6},{8,9},{9,8},{10,11... | collective-permute-start | bytes 2359304 | tf_op jit(solution)/shard_map/ppermute | solution.py:18
  11.7 0.9 copy-start.4
  15.8 5.8 %collective-permute-start.1 = (f32[32,256]{1,0:T(8,128)S(1)}, f32[32,256]{1,0:T(8,128)S(1)}, u32[]{:S(2)}, u32[]{:S(2)}) collective-permute-start(f32[32,256]{1,0:T(8,128)S(1)} %bitcast.98), channel_id=1, source_target_pairs={{0,2},{2,4},{4,6},{6,0},{1,3},{3,5},{5,7},{7,1},{8,10},{10,12},{12... | collective-permute-start | bytes 98312 | tf_op jit(solution)/shard_map/ppermute | solution.py:18
  17.5 5.4 %collective-permute-start.2 = (f32[32,256]{1,0:T(8,128)S(1)}, f32[32,256]{1,0:T(8,128)S(1)}, u32[]{:S(2)}, u32[]{:S(2)}) collective-permute-start(f32[32,256]{1,0:T(8,128)S(1)} %bitcast.99), channel_id=1, source_target_pairs={{0,4},{2,6},{4,0},{6,2},{1,5},{3,7},{5,1},{7,3},{8,12},{10,14},{12... | collective-permute-start | bytes 98312 | tf_op jit(solution)/shard_map/ppermute | solution.py:18
  20.2 3.9 %collective-permute-start.3 = (f32[32,256]{1,0:T(8,128)S(1)}, f32[32,256]{1,0:T(8,128)S(1)}, u32[]{:S(2)}, u32[]{:S(2)}) collective-permute-start(f32[32,256]{1,0:T(8,128)S(1)} %bitcast.100), channel_id=1, source_target_pairs={{0,6},{2,0},{4,2},{6,4},{1,7},{3,1},{5,3},{7,5},{8,14},{10,8},{12,... | collective-permute-start | bytes 98312 | tf_op jit(solution)/shard_map/ppermute | solution.py:18
  24.2 4.1 %copy-start.3 = (bf16[128,6144]{1,0:T(8,128)(2,1)S(1)}, bf16[128,6144]{1,0:T(8,128)(2,1)}, u32[]{:S(2)}) copy-start(bf16[128,6144]{1,0:T(8,128)(2,1)} %param.5) | copy-start | bytes 4718596
  24.3 4.1 %collective-permute-start.4 = (f32[32,128]{1,0:T(8,128)S(1)}, f32[32,128]{1,0:T(8,128)S(1)}, u32[]{:S(2)}, u32[]{:S(2)}) collective-permute-start(f32[32,128]{1,0:T(8,128)S(1)} %bitcast.101), channel_id=1, source_target_pairs={{0,1},{1,0},{2,3},{3,2},{4,5},{5,4},{6,7},{7,6},{8,9},{9,8},{10,11... | collective-permute-start | bytes 49160 | tf_op jit(solution)/shard_map/ppermute | solution.py:18
  29.2 10.8 %copy-start.20 = (bf16[256,384]{1,0:T(8,128)(2,1)S(1)}, bf16[256,384]{1,0:T(8,128)(2,1)}, u32[]{:S(2)}) copy-start(bf16[256,384]{1,0:T(8,128)(2,1)} %get-tuple-element.31) | copy-start | bytes 589828
  29.2 11.1 %copy-start.19 = (bf16[256,384]{1,0:T(8,128)(2,1)S(1)}, bf16[256,384]{1,0:T(8,128)(2,1)}, u32[]{:S(2)}) copy-start(bf16[256,384]{1,0:T(8,128)(2,1)} %get-tuple-element.32) | copy-start | bytes 589828
  29.2 15.4 %copy-start.18 = (bf16[256,384]{1,0:T(8,128)(2,1)S(1)}, bf16[256,384]{1,0:T(8,128)(2,1)}, u32[]{:S(2)}) copy-start(bf16[256,384]{1,0:T(8,128)(2,1)} %get-tuple-element.33) | copy-start | bytes 589828
  29.3 1.8 %collective-permute-start.5 = (f32[96,8,128]{2,1,0:T(8,128)S(1)}, f32[96,8,128]{2,1,0:T(8,128)S(1)}, u32[]{:S(2)}, u32[]{:S(2)}) collective-permute-start(f32[96,8,128]{2,1,0:T(8,128)S(1)} %dynamic-slice_bitcast_fusion), channel_id=1, source_target_pairs={{0,1},{1,0},{2,3},{3,2},{4,5},{5,4},{6,7},{7,6},{8,9},{9,8},{10,11... | collective-permute-start | bytes 1179656 | tf_op jit(solution)/shard_map/ppermute | solution.py:18
  31.9 18.9 %all-to-all-start = ((f32[16,6,8,128]{3,2,1,0:T(8,128)}), f32[16,6,8,128]{3,2,1,0:T(8,128)S(1)}, u32[]{:S(2)}, u32[]{:S(2)}) async-start(f32[16,6,8,128]{3,2,1,0:T(8,128)} %bitcast.15), calls=%async_computation | async-start | bytes 786432 | tf_op jit(solution)/shard_map/all_to_all | solution.py:257
  40.0 10.8 %collective-permute-start.6 = (bf16[256,384]{1,0:T(8,128)(2,1)S(1)}, bf16[256,384]{1,0:T(8,128)(2,1)S(1)}, u32[]{:S(2)}, u32[]{:S(2)}) collective-permute-start(bf16[256,384]{1,0:T(8,128)(2,1)S(1)} %copy-done.20), channel_id=1, source_target_pairs={{0,2},{2,4},{4,6},{6,0},{1,3},{3,5},{5,7},{7,1},{8,10},{10,12},{12... | collective-permute-start | bytes 589832 | tf_op jit(solution)/shard_map/ppermute | solution.py:18
  40.3 20.5 %collective-permute-start.7 = (bf16[256,384]{1,0:T(8,128)(2,1)S(1)}, bf16[256,384]{1,0:T(8,128)(2,1)S(1)}, u32[]{:S(2)}, u32[]{:S(2)}) collective-permute-start(bf16[256,384]{1,0:T(8,128)(2,1)S(1)} %copy-done.19), channel_id=1, source_target_pairs={{0,4},{2,6},{4,0},{6,2},{1,5},{3,7},{5,1},{7,3},{8,12},{10,14},{12... | collective-permute-start | bytes 589832 | tf_op jit(solution)/shard_map/ppermute | solution.py:18
  44.7 16.8 %collective-permute-start.8 = (bf16[256,384]{1,0:T(8,128)(2,1)S(1)}, bf16[256,384]{1,0:T(8,128)(2,1)S(1)}, u32[]{:S(2)}, u32[]{:S(2)}) collective-permute-start(bf16[256,384]{1,0:T(8,128)(2,1)S(1)} %copy-done.18), channel_id=1, source_target_pairs={{0,6},{2,0},{4,2},{6,4},{1,7},{3,1},{5,3},{7,5},{8,14},{10,8},{12,... | collective-permute-start | bytes 589832 | tf_op jit(solution)/shard_map/ppermute | solution.py:18
  50.9 10.6 %copy-start.8 = (bf16[256,384]{1,0:T(8,128)(2,1)}, bf16[256,384]{1,0:T(8,128)(2,1)S(1)}, u32[]{:S(2)}) copy-start(bf16[256,384]{1,0:T(8,128)(2,1)S(1)} %collective-permute-done.6.refs_2_) | copy-start | bytes 589828
  60.9 0.7 copy-start.9
  61.5 0.7 copy-start.10
  65.1 27.4 %collective-permute-start.10 = (bf16[8,128,384]{2,1,0:T(8,128)(2,1)}, bf16[8,128,384]{2,1,0:T(8,128)(2,1)S(1)}, u32[]{:S(2)}, u32[]{:S(2)}) collective-permute-start(bf16[8,128,384]{2,1,0:T(8,128)(2,1)} %unpack.1.refs_0_), channel_id=1, source_target_pairs={{0,24},{8,0},{16,8},{24,16},{1,25},{9,1},{17,9},{25,17},{2,26},{10... | collective-permute-start | bytes 2359304 | tf_op jit(solution)/shard_map/ppermute | solution.py:18
  68.3 24.1 %collective-permute-start.9 = (bf16[8,128,384]{2,1,0:T(8,128)(2,1)}, bf16[8,128,384]{2,1,0:T(8,128)(2,1)}, u32[]{:S(2)}, u32[]{:S(2)}) collective-permute-start(bf16[8,128,384]{2,1,0:T(8,128)(2,1)} %unpack.1.refs_0_), channel_id=1, source_target_pairs={{0,8},{8,16},{16,24},{24,0},{1,9},{9,17},{17,25},{25,1},{2,10},{10... | collective-permute-start | bytes 2359304 | tf_op jit(solution)/shard_map/ppermute | solution.py:18
  92.5 0.9 copy-start.11
  93.3 1.7 collective-permute-start.11
  95.2 0.9 copy-start.2
  95.4 3.6 %copy-start.12 = (bf16[8,128,384]{2,1,0:T(8,128)(2,1)S(1)}, bf16[8,128,384]{2,1,0:T(8,128)(2,1)}, u32[]{:S(2)}) copy-start(bf16[8,128,384]{2,1,0:T(8,128)(2,1)} %copy-done.11) | copy-start | bytes 2359300
  96.1 0.6 copy-start.13
  96.7 5.3 %collective-permute-start.12 = (f32[32,128]{1,0:T(8,128)S(1)}, f32[32,128]{1,0:T(8,128)S(1)}, u32[]{:S(2)}, u32[]{:S(2)}) collective-permute-start(f32[32,128]{1,0:T(8,128)S(1)} %fusion.26), channel_id=1, source_target_pairs={{0,1},{1,0},{2,3},{3,2},{4,5},{5,4},{6,7},{7,6},{8,9},{9,8},{10,11... | collective-permute-start | bytes 49160 | tf_op jit(solution)/shard_map/ppermute | solution.py:18
  98.6 12.7 %collective-permute-start.13 = (bf16[8,64,384]{2,1,0:T(8,128)(2,1)S(1)}, bf16[8,64,384]{2,1,0:T(8,128)(2,1)S(1)}, u32[]{:S(2)}, u32[]{:S(2)}) collective-permute-start(bf16[8,64,384]{2,1,0:T(8,128)(2,1)S(1)} %slice.72), channel_id=1, source_target_pairs={{0,8},{8,16},{16,24},{24,0},{1,9},{9,17},{17,25},{25,1},{2,10},{10... | collective-permute-start | bytes 1179656 | tf_op jit(solution)/shard_map/ppermute | solution.py:18
  99.0 12.2 %collective-permute-start.14 = (bf16[8,64,384]{2,1,0:T(8,128)(2,1)S(1)}, bf16[8,64,384]{2,1,0:T(8,128)(2,1)S(1)}, u32[]{:S(2)}, u32[]{:S(2)}) collective-permute-start(bf16[8,64,384]{2,1,0:T(8,128)(2,1)S(1)} %slice.73), channel_id=1, source_target_pairs={{0,24},{8,0},{16,8},{24,16},{1,25},{9,1},{17,9},{25,17},{2,26},{10... | collective-permute-start | bytes 1179656 | tf_op jit(solution)/shard_map/ppermute | solution.py:18
  103.5 11.0 %all-to-all-start.3 = ((f32[4,2,32,128]{3,1,2,0:T(2,128)}), f32[4,2,32,128]{3,1,2,0:T(2,128)S(1)}, u32[]{:S(2)}, u32[]{:S(2)}) async-start(f32[4,2,32,128]{3,1,2,0:T(2,128)} %broadcast_in_dim.10), calls=%async_computation.3 | async-start | bytes 262144 | tf_op jit(solution)/shard_map/all_to_all | solution.py:59
  111.2 3.2 %copy-start.16 = (bf16[8,64,384]{2,1,0:T(8,128)(2,1)}, bf16[8,64,384]{2,1,0:T(8,128)(2,1)S(1)}, u32[]{:S(2)}) copy-start(bf16[8,64,384]{2,1,0:T(8,128)(2,1)S(1)} %collective-permute-done.13.refs_3_) | copy-start | bytes 1179652
  111.2 3.2 %copy-start.17 = (bf16[8,64,384]{2,1,0:T(8,128)(2,1)}, bf16[8,64,384]{2,1,0:T(8,128)(2,1)S(1)}, u32[]{:S(2)}) copy-start(bf16[8,64,384]{2,1,0:T(8,128)(2,1)S(1)} %collective-permute-done.14.refs_4_) | copy-start | bytes 1179652
  114.5 10.5 %copy-start.1 = (bf16[1024,384]{1,0:T(8,128)(2,1)S(1)}, bf16[1024,384]{1,0:T(8,128)(2,1)}, u32[]{:S(2)}) copy-start(bf16[1024,384]{1,0:T(8,128)(2,1)} %refs_0_.3) | copy-start | bytes 2359300
  124.9 11.4 %copy-start.15 = (bf16[128,1536]{1,0:T(8,128)(2,1)S(1)}, bf16[128,1536]{1,0:T(8,128)(2,1)}, u32[]{:S(2)}) copy-start(bf16[128,1536]{1,0:T(8,128)(2,1)} %get-tuple-element.57) | copy-start | bytes 1179652
  124.9 11.4 %copy-start.14 = (bf16[128,1536]{1,0:T(8,128)(2,1)S(1)}, bf16[128,1536]{1,0:T(8,128)(2,1)}, u32[]{:S(2)}) copy-start(bf16[128,1536]{1,0:T(8,128)(2,1)} %get-tuple-element.58) | copy-start | bytes 1179652
  125.3 5.4 %collective-permute-start.15 = (f32[32,384]{1,0:T(8,128)S(1)}, f32[32,384]{1,0:T(8,128)S(1)}, u32[]{:S(2)}, u32[]{:S(2)}) collective-permute-start(f32[32,384]{1,0:T(8,128)S(1)} %fusion.11), channel_id=1, source_target_pairs={{0,32},{32,64},{64,96},{96,0},{1,33},{33,65},{65,97},{97,1},{2,34}... | collective-permute-start | bytes 147464 | tf_op jit(solution)/shard_map/ppermute | solution.py:18
  125.5 5.7 %collective-permute-start.16 = (f32[32,384]{1,0:T(8,128)S(1)}, f32[32,384]{1,0:T(8,128)S(1)}, u32[]{:S(2)}, u32[]{:S(2)}) collective-permute-start(f32[32,384]{1,0:T(8,128)S(1)} %fusion.11), channel_id=1, source_target_pairs={{0,64},{32,96},{64,0},{96,32},{1,65},{33,97},{65,1},{97,33},{2,66}... | collective-permute-start | bytes 147464 | tf_op jit(solution)/shard_map/ppermute | solution.py:18
  128.2 4.1 %collective-permute-start.17 = (f32[32,384]{1,0:T(8,128)S(1)}, f32[32,384]{1,0:T(8,128)S(1)}, u32[]{:S(2)}, u32[]{:S(2)}) collective-permute-start(f32[32,384]{1,0:T(8,128)S(1)} %fusion.11), channel_id=1, source_target_pairs={{0,96},{32,0},{64,32},{96,64},{1,97},{33,1},{65,33},{97,65},{2,98}... | collective-permute-start | bytes 147464 | tf_op jit(solution)/shard_map/ppermute | solution.py:18
  132.3 7.5 %collective-permute-start.18 = (f32[32,384]{1,0:T(8,128)S(1)}, f32[32,384]{1,0:T(8,128)S(1)}, u32[]{:S(2)}, u32[]{:S(2)}) collective-permute-start(f32[32,384]{1,0:T(8,128)S(1)} %add_add_fusion), channel_id=1, source_target_pairs={{0,8},{8,16},{16,24},{24,0},{1,9},{9,17},{17,25},{25,1},{2,10},{10... | collective-permute-start | bytes 147464 | tf_op jit(solution)/shard_map/ppermute | solution.py:18
  133.0 22.8 %collective-permute-start.21 = (bf16[128,1536]{1,0:T(8,128)(2,1)}, bf16[128,1536]{1,0:T(8,128)(2,1)S(1)}, u32[]{:S(2)}, u32[]{:S(2)}) collective-permute-start(bf16[128,1536]{1,0:T(8,128)(2,1)} %get-tuple-element.56), channel_id=1, source_target_pairs={{0,24},{8,0},{16,8},{24,16},{1,25},{9,1},{17,9},{25,17},{2,26},{10... | collective-permute-start | bytes 1179656 | tf_op jit(solution)/shard_map/ppermute | solution.py:18
  136.2 19.6 %collective-permute-start.22 = (bf16[128,1536]{1,0:T(8,128)(2,1)S(1)}, bf16[128,1536]{1,0:T(8,128)(2,1)S(1)}, u32[]{:S(2)}, u32[]{:S(2)}) collective-permute-start(bf16[128,1536]{1,0:T(8,128)(2,1)S(1)} %copy-done.15), channel_id=1, source_target_pairs={{0,8},{8,16},{16,24},{24,0},{1,9},{9,17},{17,25},{25,1},{2,10},{10... | collective-permute-start | bytes 1179656 | tf_op jit(solution)/shard_map/ppermute | solution.py:18
  136.3 19.6 %collective-permute-start.23 = (bf16[128,1536]{1,0:T(8,128)(2,1)S(1)}, bf16[128,1536]{1,0:T(8,128)(2,1)S(1)}, u32[]{:S(2)}, u32[]{:S(2)}) collective-permute-start(bf16[128,1536]{1,0:T(8,128)(2,1)S(1)} %copy-done.14), channel_id=1, source_target_pairs={{0,16},{8,24},{16,0},{24,8},{1,17},{9,25},{17,1},{25,9},{2,18},{10... | collective-permute-start | bytes 1179656 | tf_op jit(solution)/shard_map/ppermute | solution.py:18
  137.7 16.6 %collective-permute-start.19 = (f32[32,384]{1,0:T(8,128)S(1)}, f32[32,384]{1,0:T(8,128)S(1)}, u32[]{:S(2)}, u32[]{:S(2)}) collective-permute-start(f32[32,384]{1,0:T(8,128)S(1)} %add_add_fusion), channel_id=1, source_target_pairs={{0,16},{8,24},{16,0},{24,8},{1,17},{9,25},{17,1},{25,9},{2,18},{10... | collective-permute-start | bytes 147464 | tf_op jit(solution)/shard_map/ppermute | solution.py:18
  139.9 14.4 %collective-permute-start.20 = (f32[32,384]{1,0:T(8,128)S(1)}, f32[32,384]{1,0:T(8,128)S(1)}, u32[]{:S(2)}, u32[]{:S(2)}) collective-permute-start(f32[32,384]{1,0:T(8,128)S(1)} %add_add_fusion), channel_id=1, source_target_pairs={{0,24},{8,0},{16,8},{24,16},{1,25},{9,1},{17,9},{25,17},{2,26},{10... | collective-permute-start | bytes 147464 | tf_op jit(solution)/shard_map/ppermute | solution.py:18
  155.8 0.7 copy-start.5
  155.8 0.9 copy-start.6
  156.7 0.7 copy-start.7
Sparse Core Ops, SparseCore 0:
  10.3 64.0 all-gather.5
  76.1 72.9 all-gather.3

commit v3 on v2

--- a/solution.py
+++ b/solution.py
@@ -23,6 +23,13 @@
     rest = value - high
     mid = lax.reduce_precision(rest, 8, 7)
     return high.astype(BF16), mid.astype(BF16), (rest - mid).astype(BF16)
+
+
+def parts3(value):
+    high = value.astype(BF16)
+    rest = value - high.astype(F32)
+    mid = rest.astype(BF16)
+    return high, mid, (rest - mid.astype(F32)).astype(BF16)
 
 
 def fold3(value):
@@ -67,41 +74,34 @@
 
 def inverse_kernel(left_ref, out_ref):
     n = out_ref.shape[0]
-    grams = mm(left_ref[...], left_ref[...], 1, 1)
+    left3 = jnp.concatenate(parts3(left_ref[...]), 0)
+    grams = mm(left3, left3, 1, 1)
     gram = fold3(grams[:, :n] + grams[:, n : 2 * n] + grams[:, 2 * n :])
     row = lax.broadcasted_iota(jnp.int32, (n, 2 * n), 0)
     col = lax.broadcasted_iota(jnp.int32, (n, 2 * n), 1)
     eye = jnp.where(row + n == col, 1.0, 0.0).astype(F32)
     work = jnp.concatenate([gram, jnp.zeros((n, n), F32)], axis=1) + eye
-    for k in range(n):
+    for k in range(n - 1):
         pivot_row = work[k : k + 1, :]
         pivot = jnp.sum(jnp.where(col[:1] == k, pivot_row, 0.0), axis=1, keepdims=True)
         column = jnp.sum(jnp.where(col == k, work, 0.0), axis=1, keepdims=True)
-        factor = jnp.where(row[:, :1] > k, column / pivot, 0.0)
-        root = lax.rsqrt(pivot)
-        root = root * (1.5 - 0.5 * pivot * root * root)
-        scale = jnp.where(row[:, :1] == k, root, 1.0)
-        work = (work - factor * pivot_row) * scale
-    out_ref[...] = work[:, n:]
-
-
-def inverse_of_factor(left3):
-    rank = left3.shape[0] // 3
+        work = work - jnp.where(row[:, :1] > k, column / pivot, 0.0) * pivot_row
+    pivots = jnp.sum(jnp.where(row == col, work, 0.0), axis=1, keepdims=True)
+    root = lax.rsqrt(pivots)
+    root = root * (1.5 - 0.5 * pivots * root * root)
+    out_ref[...] = work[:, n:] * root
+
+
+def inverse_of_factor(left):
+    rank = left.shape[0]
     return pl.pallas_call(
         inverse_kernel,
         out_shape=jax.ShapeDtypeStruct((rank, rank), F32),
         name="inverse_of_factor",
-    )(left3)
-
-
-def parts3(value):
-    high = value.astype(BF16)
-    rest = value - high.astype(F32)
-    mid = rest.astype(BF16)
-    return high, mid, (rest - mid.astype(F32)).astype(BF16)
-
-
-def residual_kernel(act_ref, cot_ref, residual_ref, left_ref, inverse_ref, factor_ref, out_ref):
+    )(left)
+
+
+def residual_kernel(scale, act_ref, cot_ref, residual_ref, left_ref, inverse_ref, factor_ref, out_ref):
     basis = lax.dot_general(
         inverse_ref[...], left_ref[...], (((1,), (0,)), ((), ())), precision=lax.Precision.HIGHEST, preferred_element_type=F32
     )
@@ -109,17 +109,17 @@
     f_h, f_m, f_l = parts3(factor_ref[...])
     basis6 = jnp.concatenate([b_h, b_m, b_l, b_h, b_m, b_h], 0)
     factor6 = jnp.concatenate([f_h, f_h, f_h, f_m, f_m, f_l], 0)
-    total = mm(act_ref[...], cot_ref[...], 0, 0) + residual_ref[...].astype(F32)
+    total = mm(act_ref[...], cot_ref[...], 0, 0) * scale + residual_ref[...].astype(F32)
     out_ref[...] = (total - mm(basis6, factor6, 0, 0)).astype(BF16)
 
 
-def residual_call(act, cot, residual, left, inverse, factor, tile):
+def residual_call(scale, act, cot, residual, left, inverse, factor, tile):
     k, d = act.shape
     cols, rank = cot.shape[1], left.shape[0]
     whole = lambda a: pl.BlockSpec(a.shape, lambda i: (0, 0))
     rows = pl.BlockSpec((tile, cols), lambda i: (i, 0))
     return pl.pallas_call(
-        residual_kernel,
+        functools.partial(residual_kernel, scale),
         out_shape=jax.ShapeDtypeStruct((d, cols), BF16),
         grid=(d // tile,),
         in_specs=[
@@ -131,7 +131,7 @@
             whole(factor),
         ],
         out_specs=rows,
-        compiler_params=pltpu.CompilerParams(vmem_limit_bytes=VMEM_LIMIT),
+        compiler_params=pltpu.CompilerParams(vmem_limit_bytes=52 * 1024 * 1024),
         cost_estimate=pl.CostEstimate(
             flops=2 * d * cols * (k + 6 * rank), bytes_accessed=2 * d * k + 4 * d * cols + 4 * d * rank, transcendentals=0
         ),
@@ -140,20 +140,20 @@
 
 
 def input_kernel(n_cot, at_ref, *refs):
-    cots, w_ref, outs = refs[:n_cot], refs[n_cot], refs[n_cot + 1 :]
-    blocks, chips, cores = w_ref.shape[:3]
+    cots, weights, outs = refs[:n_cot], refs[n_cot : n_cot + 2], refs[n_cot + 2 :]
+    blocks, chips = weights[0].shape[:2]
     tok, width = outs[0].shape
     total = jnp.zeros((tok * len(outs), width), F32)
     for s in range(chips):
         tokens = jnp.concatenate([jnp.concatenate([c[2 * s], c[2 * s + 1]], 1) for c in cots], 0)
-        rows = [jnp.concatenate([w_ref[b, at_ref[s], at_ref[chips + c]] for c in range(cores)], 1) for b in range(blocks)]
+        rows = [jnp.concatenate([w[b, at_ref[4 + s]] for w in weights], 1) for b in range(blocks)]
         total = total + mm(tokens, jnp.concatenate(rows, 0), 1, 1)
     for i, out in enumerate(outs):
         out[...] = total[i * tok : (i + 1) * tok].astype(BF16)
 
 
-def input_call(cots, weight, at, blocks):
-    n, chips, cores, rows, cols = weight.shape
+def input_call(cots, weight, other, at, blocks):
+    n, chips, rows, cols = weight.shape
     _, tok, _ = cots[0].shape
     tokens = 4 * tok
     return pl.pallas_call(
@@ -163,7 +163,7 @@
             num_scalar_prefetch=1,
             grid=(n // blocks,),
             in_specs=[pl.BlockSpec(c.shape, lambda i, q: (0, 0, 0)) for c in cots]
-            + [pl.BlockSpec((blocks, chips, cores, rows, cols), lambda i, q: (i, 0, 0, 0, 0))],
+            + [pl.BlockSpec((blocks, chips, rows, cols), lambda i, q: (i, 0, 0, 0))] * 2,
             out_specs=[pl.BlockSpec((tok, blocks * rows), lambda i, q: (0, i))] * 4,
         ),
         compiler_params=pltpu.CompilerParams(vmem_limit_bytes=VMEM_LIMIT),
@@ -171,7 +171,7 @@
             flops=2 * tokens * n * rows * cols * 8, bytes_accessed=16 * cols * (tokens + n * rows), transcendentals=0
         ),
         name="input_grads",
-    )(jnp.stack(at).astype(jnp.int32), *cots, weight)
+    )(at, *cots, weight, other)
 
 
 def copy_kernel(n_in, n_out, plan, at_ref, *refs):
@@ -199,7 +199,7 @@
         compiler_params=pltpu.CompilerParams(vmem_limit_bytes=VMEM_LIMIT),
         cost_estimate=pl.CostEstimate(flops=0, bytes_accessed=moved, transcendentals=0),
         name=name,
-    )(jnp.stack(at).astype(jnp.int32), *ins)
+    )(at, *ins)
 
 
 def part_of(ref, index, size):
@@ -219,7 +219,7 @@
 
 
 def place_plan(width, at, ins, outs):
-    return [(r, outs[0].at[:, pl.ds(pl.multiple_of(at[i] * width, width), width)]) for i, r in enumerate(ins)]
+    return [(r, outs[0].at[:, pl.ds(pl.multiple_of(at[8 + i] * width, width), width)]) for i, r in enumerate(ins)]
 
 
 def per_device(activations, cotangent, weight, residual, warm_factor):
@@ -234,18 +234,18 @@
 
     like = lambda *shape: jax.ShapeDtypeStruct(shape, BF16)
     w_send = lax.dynamic_slice_in_dim(weight, iz * quarter + iy * sub, sub, 0)
-    w_all = lax.all_gather(w_send, ("y", "x", "core")).reshape(4, 4, 2, sub, cols)
+    w_all = lax.all_gather(w_send, ("y", "x")).reshape(4, 4, sub, cols)
 
     cot_other = shift(cotangent, "core", 1)
-    at = [((ix + s) % 4) * 2 + ic for s in range(4)]
+    at = [((ix + s) % 4) * 2 + ic for s in range(4)] + [(ix - s) % 4 for s in range(4)]
+    at = jnp.stack(at + [(iz + s) % 4 for s in (0, 1, -1, 2)]).astype(jnp.int32)
     packed = copy_call(functools.partial(pack_plan, tok), 6, [cotangent, cot_other], [like(2 * tok, cols)] * 3, at, "pack")
+
+    warm3 = jnp.concatenate(split3(warm_factor.T), 0)
+    cw = fold3(mm(warm3, cotangent, 1, 1)) * scale
+    cw = reduce_scatter(cw.reshape(rank, 4, 2 * tok).transpose(1, 0, 2), "x")
+    act, cw, *packed = lax.optimization_barrier((activations, cw, *packed))
     got = [shift(p, "x", s) for s, p in zip((1, 2, 3), packed)]
-
-    cot, w_send, *_ = lax.optimization_barrier((cotangent, w_send, *packed))
-    warm3 = jnp.concatenate(split3(warm_factor.T), 0)
-    cw = fold3(mm(warm3, cot, 1, 1)) * scale
-    cw = reduce_scatter(cw.reshape(rank, 4, 2 * tok).transpose(1, 0, 2), "x")
-    act, cw = lax.optimization_barrier((activations, cw))
     gathered = lax.all_gather(act, ("x", "core"), axis=0, tiled=True)
     cw = reduce_scatter(cw.reshape(rank, 2, tok).transpose(1, 0, 2), "core")
 
@@ -254,44 +254,39 @@
     tiles = left.reshape(rank // 8, 8, d // 128, 128).transpose(0, 2, 1, 3).reshape(-1, 8, 128)
     n_tiles = tiles.shape[0]
     part = reduce_scatter(tiles.reshape(2, n_tiles // 2, 8, 128), "core")
-    part = lax.all_to_all(part.reshape(16, n_tiles // 32, 8, 128), ("y", "z"), 0, 0).sum(0)
     part, *got = lax.optimization_barrier((part, *got))
 
     (cot_own,) = copy_call(
         functools.partial(unpack_plan, tok), 8, [cotangent, cot_other] + got, [like(8, tok, cols)], at, "unpack"
     )
     c_low, c_high = shift(cot_own, "z", 1), shift(cot_own, "z", -1)
-    part = all_blocks(part, ("x",)).sum(0)
-    part, cot_own = lax.optimization_barrier((part, cot_own))
-    part = all_blocks(part, ("y", "z")).reshape(-1, 8, 128)
-    part, c_low, c_high = lax.optimization_barrier((part, c_low, c_high))
+    part = lax.all_to_all(part.reshape(16, n_tiles // 32, 8, 128), ("y", "z"), 0, 0).sum(0)
+    part, c_low, c_high, w_all = lax.optimization_barrier((part, c_low, c_high, w_all))
+    w_other = shift(w_all, "core", 1)
     half = tok // 2
     c_far = [shift(c_low[:, :half], "z", 1), shift(c_high[:, half:], "z", -1)]
+    part = all_blocks(part, ("x",)).sum(0)
+    part = all_blocks(part, ("y", "z")).reshape(-1, 8, 128)
+    grads = input_call([cot_own, c_low, c_high, *c_far], w_all, w_other, at, 2)
+    part, *grads = lax.optimization_barrier((part, *grads))
+    back = [grads[0], shift(grads[1], "z", -1), shift(grads[2], "z", 1), shift(grads[3], "z", 2)]
     part = both_cores(part)
     left = part.reshape(rank // 8, d // 128, 8, 128).transpose(0, 2, 1, 3).reshape(rank, d)
 
     left3 = jnp.concatenate(split3(left), 0)
     right = fold3(mm(left3, activations, 1, 1)) * scale
     right = all_blocks(both_cores(right), ("x",))
-
-    right, *c_far = lax.optimization_barrier((right, *c_far))
-    cots = [cot_own, c_low, c_high, *c_far]
-    grads = input_call(cots, w_all, [(ix - s) % 4 for s in range(4)] + [ic, 1 - ic], 2)
-    right, *grads = lax.optimization_barrier((right, *grads))
-    back = [grads[0], shift(grads[1], "z", -1), shift(grads[2], "z", 1), shift(grads[3], "z", 2)]
-
     right = right.reshape(8, rank, tok).transpose(1, 0, 2).reshape(rank, 8 * tok)
     right3 = jnp.concatenate(split3(right), 0)
     sums = fold3(mm(right3, cotangent, 1, 0)) + fold3(mm(left3, residual, 1, 0))
+    left, right = lax.optimization_barrier((left, right))
+    inverse = inverse_of_factor(left)
     sums = all_sum(sums, "y")
-    at = [(iz + s) % 4 for s in (0, 1, -1, 2)]
+    sums, inverse, *back = lax.optimization_barrier((sums, inverse, *back))
     (input_grads,) = copy_call(functools.partial(place_plan, quarter), 4, back, [like(tok, d)], at, "place")
     sums = all_sum(sums, "z")
-    left3, right = lax.optimization_barrier((left3, right))
-    inverse = inverse_of_factor(left3)
     factor = jnp.dot(inverse, sums, precision=lax.Precision.HIGHEST) * (1.0 / 16)
-    cot_scaled = (cotangent.astype(F32) * scale).astype(BF16)
-    new_residual = residual_call(gathered, cot_scaled, residual, left, inverse, factor, 1024)
+    new_residual = residual_call(scale, gathered, cotangent, residual, left, inverse, factor, 1536 if d % 1536 == 0 else 1024)
     return factor.T, new_residual[None], input_grads
 
 

time: 183 us -> 170 us (0.929)
  waiting for transfers between devices: 34 us -> 18.1 us
  blocking collectives: 24.1 us -> 34 us
  other arithmetic: 6.49 us -> 3.19 us
  starting transfers between devices: 43.8 us -> 41.9 us
    all_to_all x0 -> x1, blocking collectives: none -> 24.5 us  [per_device(): lax.all_to_all(part.reshape(16, n_tiles // 32, 8, 128), ('y', 'z'), 0, 0)]
    all_to_all x2 -> x1, blocking collectives: 24.1 us -> 9.5 us  [all_blocks(): lax.all_to_all(jnp.broadcast_to(value[None], (n,) + value.shape), axis, 0...]
    ppermute x24 -> x25, waiting for transfers between devices: 24.6 us -> 14.8 us  [shift(): return lax.ppermute(value, axis, [(i, (i + step) % n) for i in range(n)])]
    all_to_all x1 -> x0, starting transfers between devices: 8.09 us -> none  [per_device(): lax.all_to_all(part.reshape(16, n_tiles // 32, 8, 128), ('y', 'z'), 0, 0)]
    all_to_all x1 -> x0, waiting for transfers between devices: 6.13 us -> none  [per_device(): lax.all_to_all(part.reshape(16, n_tiles // 32, 8, 128), ('y', 'z'), 0, 0)]
    all_to_all x1 -> x2, starting transfers between devices: 3.51 us -> 7.59 us  [all_blocks(): lax.all_to_all(jnp.broadcast_to(value[None], (n,) + value.shape), axis, 0...]
    unnamed x45 -> x37, local copies, waits for them, and re-layouts: 4.79 us -> 2.37 us
    ppermute x24 -> x25, starting transfers between devices: 32.1 us -> 34.2 us  [shift(): return lax.ppermute(value, axis, [(i, (i + step) % n) for i in range(n)])]
  transfers between devices with their start and end apart: 28 -> 29, of which waited for: 14 -> 7; matrix products, arithmetic and copies ran while one was open for 11% -> 11% of each run, Pallas kernels for 14% -> 14%
where the time goes in v3:
time: 170 us; the launch traced here: 169 us
  starting transfers between devices  41.9 us (25%)
  Pallas kernels  37.4 us (22%)
  blocking collectives  34 us (20%)
  waiting for transfers between devices  18.1 us (11%)
  between operations  14.6 us (9%)
  matrix products  11.3 us (7%)
  local copies, waits for them, and re-layouts  8.58 us (5%)
  other arithmetic  3.19 us (2%)
    ppermute x25, starting transfers between devices, shift(): return lax.ppermute(value, axis, [(i, (i + step) % n) for i in range(n)])  34.2 us
    all_to_all x1, blocking collectives, per_device(): lax.all_to_all(part.reshape(16, n_tiles // 32, 8, 128), ('y', 'z'), 0, 0)  24.5 us
    ppermute x25, waiting for transfers between devices, shift(): return lax.ppermute(value, axis, [(i, (i + step) % n) for i in range(n)])  14.8 us
    pallas_call x1, Pallas kernels, residual_call(): pl.pallas_call(functools.partial(residual_kernel, scale), out_shape=jax.S...  13.3 us
    dot_general x6, matrix products, mm(): lax.dot_general(a, b, (((ca,), (cb,)), ((), ())), preferred_element_type=...  11.1 us
    pallas_call x1, Pallas kernels, input_call(): pl.pallas_call(functools.partial(input_kernel, len(cots)), out_shape=[jax...  10.2 us
    all_to_all x1, blocking collectives, all_blocks(): lax.all_to_all(jnp.broadcast_to(value[None], (n,) + value.shape), axis, 0...  9.5 us
    pallas_call x3, Pallas kernels, copy_call(): pl.pallas_call(functools.partial(copy_kernel, len(ins), len(outs), plan),...  8.71 us
  transfers between devices with their start and end apart: 29, of which 7 were waited for; matrix products, arithmetic and copies ran while one was open for 11% of the time, Pallas kernels for 14%

profile of v3, /device:TPU:0, one launch (start us, length us, event | category | flops | bytes accessed | tf_op | source)
XLA Modules:
  0.0 169.1 jit_solution(12309094894374670799)
XLA Ops:
  7.2 1.7 %constant_dynamic-slice_fusion = bf16[384,384]{1,0:T(8,128)(2,1)} fusion(bf16[6144,384]{1,0:T(8,128)(2,1)} %param.7, s32[]{:T(128)S(6)} %select_n.131), kind=kLoop, calls=%fused_computation.74 | loop fusion | bytes 589828 | tf_op jit(solution)/shard_map/dynamic_slice | solution.py:236
  9.0 0.1 collective-permute-start.3
  9.2 0.8 reduce-precision_convert_fusion.5
  10.0 1.5 fusion.20
  11.5 0.1 reshape.51
  11.6 0.1 constant_dynamic-slice_fusion.6
  11.7 1.6 collective-permute-start
  13.4 2.7 %collective-permute-start.1 = (f32[32,256]{1,0:T(8,128)S(1)}, f32[32,256]{1,0:T(8,128)S(1)}, u32[]{:S(2)}, u32[]{:S(2)}) collective-permute-start(f32[32,256]{1,0:T(8,128)S(1)} %bitcast.99), channel_id=1, source_target_pairs={{0,4},{2,6},{4,0},{6,2},{1,5},{3,7},{5,1},{7,3},{8,12},{10,14},{12... | collective-permute-start | bytes 98312 | tf_op jit(solution)/shard_map/ppermute | solution.py:18
  16.1 1.4 collective-permute-start.2
  17.6 0.7 stack.69.at_ref
  18.2 0.6 collective-permute-done.1
  18.8 1.2 collective-permute-done.2
  20.1 0.9 copy-done.6
  20.9 2.7 %pack.1 = (bf16[256,384]{1,0:T(8,128)(2,1)}, bf16[256,384]{1,0:T(8,128)(2,1)}, bf16[256,384]{1,0:T(8,128)(2,1)}) custom-call(s32[12]{0:T(128)} %stack.69.at_ref, bf16[1024,384]{1,0:T(8,128)(2,1)} %cot_ref.1, bf16[1024,384]{1,0:T(8,128)(2,1)} %copy-done.6), custom_call_target="tpu_custom_call" | custom-call | bytes 1179648 | tf_op jit(solution)/shard_map/pack/pallas_call | solution.py:189
  23.8 0.1 collective-permute-start.4
  23.8 4.0 %fusion.19 = f32[96,6144]{1,0:T(8,128)S(1)} fusion(bf16[32,384]{1,0:T(8,128)(2,1)S(1)} %get-tuple-element.80, bf16[32,384]{1,0:T(8,128)(2,1)S(1)} %get-tuple-element.81, bf16[32,384]{1,0:T(8,128)(2,1)S(1)} %get-tuple-element.79, bf16[1,6144,384]{2,1,0:T(8,128)(2,1)} %param.8), kind=kOutput, calls=%fused_computation.56 | convolution fusion | flops 453206016 | bytes 7151616 | tf_op jit(solution)/shard_map/dot_general | solution.py:41
  27.9 0.5 fusion.21
  28.4 0.4 fusion.1
  28.8 0.5 collective-permute-start.5
  29.3 0.4 collective-permute-start.6
  29.6 3.8 %collective-permute-start.7 = (bf16[256,384]{1,0:T(8,128)(2,1)S(1)}, bf16[256,384]{1,0:T(8,128)(2,1)S(1)}, u32[]{:S(2)}, u32[]{:S(2)}) collective-permute-start(bf16[256,384]{1,0:T(8,128)(2,1)S(1)} %copy-done.15), channel_id=1, source_target_pairs={{0,4},{2,6},{4,0},{6,2},{1,5},{3,7},{5,1},{7,3},{8,12},{10,14},{12... | collective-permute-start | bytes 589832 | tf_op jit(solution)/shard_map/ppermute | solution.py:18
  33.4 0.1 collective-permute-start.8
  33.6 5.1 %collective-permute-done.6.refs_2_ = bf16[256,384]{1,0:T(8,128)(2,1)S(1)} collective-permute-done((bf16[256,384]{1,0:T(8,128)(2,1)S(1)}, bf16[256,384]{1,0:T(8,128)(2,1)S(1)}, u32[]{:S(2)}, u32[]{:S(2)}) %collective-permute-start.6) | collective-permute-done | bytes 196640 | tf_op jit(solution)/shard_map/ppermute | solution.py:18
  38.7 4.9 %collective-permute-done.7.refs_3_ = bf16[256,384]{1,0:T(8,128)(2,1)S(1)} collective-permute-done((bf16[256,384]{1,0:T(8,128)(2,1)S(1)}, bf16[256,384]{1,0:T(8,128)(2,1)S(1)}, u32[]{:S(2)}, u32[]{:S(2)}) %collective-permute-start.7) | collective-permute-done | bytes 196640 | tf_op jit(solution)/shard_map/ppermute | solution.py:18
  43.6 0.7 copy-done.11
  44.3 0.7 copy-done.12
  45.0 2.8 %unpack.1.refs_0_ = bf16[8,128,384]{2,1,0:T(8,128)(2,1)} custom-call(s32[12]{0:T(128)} %stack.69.at_ref, bf16[1024,384]{1,0:T(8,128)(2,1)} %cot_ref.1, bf16[1024,384]{1,0:T(8,128)(2,1)} %copy-done.6, bf16[256,384]{1,0:T(8,128)(2,1)} %copy-done.10, bf16[256,384]{1,0:T(8,128)(2,1)} %copy-done.11, bf16[256,384]{1,0:T(8,128)(2,1)} %copy-done.12), custom_call_target="tpu_custom_call" | custom-call | bytes 1572864 | tf_op jit(solution)/shard_map/unpack/pallas_call | solution.py:189
  47.8 4.0 %collective-permute-start.10 = (bf16[8,128,384]{2,1,0:T(8,128)(2,1)}, bf16[8,128,384]{2,1,0:T(8,128)(2,1)S(1)}, u32[]{:S(2)}, u32[]{:S(2)}) collective-permute-start(bf16[8,128,384]{2,1,0:T(8,128)(2,1)} %unpack.1.refs_0_), channel_id=1, source_target_pairs={{0,24},{8,0},{16,8},{24,16},{1,25},{9,1},{17,9},{25,17},{2,26},{10... | collective-permute-start | bytes 2359304 | tf_op jit(solution)/shard_map/ppermute | solution.py:18
  51.8 24.5 %all_to_all.20 = f32[16,6,8,128]{3,2,1,0:T(8,128)S(1)} all-to-all(f32[16,6,8,128]{3,2,1,0:T(8,128)S(1)} %bitcast.95), channel_id=1, replica_groups=mesh['y'=4,'z'=4,'x'=4,'core'=2] {'y','z'}, dimensions={0} | all-to-all | bytes 786432 | tf_op jit(solution)/shard_map/all_to_all | solution.py:263
  76.3 0.6 reduce_sum.18
  77.0 0.1 collective-permute-start.13
  77.1 1.2 slice.69
  78.3 0.1 collective-permute-start.11
  78.4 3.3 %collective-permute-start.12 = (bf16[8,64,384]{2,1,0:T(8,128)(2,1)S(1)}, bf16[8,64,384]{2,1,0:T(8,128)(2,1)}, u32[]{:S(2)}, u32[]{:S(2)}) collective-permute-start(bf16[8,64,384]{2,1,0:T(8,128)(2,1)S(1)} %slice.70), channel_id=1, source_target_pairs={{0,24},{8,0},{16,8},{24,16},{1,25},{9,1},{17,9},{25,17},{2,26},{10... | collective-permute-start | bytes 1179656 | tf_op jit(solution)/shard_map/ppermute | solution.py:18
  81.7 0.7 broadcast_in_dim.8
  82.5 9.5 %all_to_all.21 = f32[4,6,8,128]{3,2,1,0:T(8,128)S(1)} all-to-all(f32[4,6,8,128]{3,2,1,0:T(8,128)S(1)} %broadcast_in_dim.8), channel_id=1, replica_groups=mesh['y'=4,'z'=4,'x'=4,'core'=2] {'x'}, dimensions={0} | all-to-all | bytes 196608 | tf_op jit(solution)/shard_map/all_to_all | solution.py:66
  92.0 0.8 broadcast_in_dim.9
  92.8 4.3 %all-to-all-start.2 = ((f32[16,6,8,128]{3,2,1,0:T(8,128)}), f32[16,6,8,128]{3,2,1,0:T(8,128)S(1)}, u32[]{:S(2)}, u32[]{:S(2)}) async-start(f32[16,6,8,128]{3,2,1,0:T(8,128)} %broadcast_in_dim.9), calls=%async_computation.2 | async-start | bytes 786432 | tf_op jit(solution)/shard_map/all_to_all | solution.py:66
  97.1 10.2 %input_grads.1 = (bf16[128,1536]{1,0:T(8,128)(2,1)}, bf16[128,1536]{1,0:T(8,128)(2,1)}, bf16[128,1536]{1,0:T(8,128)(2,1)}, bf16[128,1536]{1,0:T(8,128)(2,1)}) custom-call(s32[12]{0:T(128)} %stack.69.at_ref, bf16[8,128,384]{2,1,0:T(8,128)(2,1)} %unpack.1.refs_0_, bf16[8,128,384]{2,1,0:T(8,128)(2,1)} %collective-permute-done.9.refs_1_, ...), custom_call_target="tpu_custom_call" | custom-call | flops 4831838208 | bytes 12582912 | tf_op jit(solution)/shard_map/input_grads/pallas_call | solution.py:159
  107.3 0.1 collective-permute-start.14
  107.4 1.9 %collective-permute-done.14 = f32[96,8,128]{2,1,0:T(8,128)S(1)} collective-permute-done((f32[96,8,128]{2,1,0:T(8,128)S(1)}, f32[96,8,128]{2,1,0:T(8,128)S(1)}, u32[]{:S(2)}, u32[]{:S(2)}) %collective-permute-start.14) | collective-permute-done | bytes 393248 | tf_op jit(solution)/shard_map/ppermute | solution.py:18
  109.3 0.1 select_bitcast_fusion.1
  109.4 0.2 reduce-precision_convert_fusion.1
  109.6 0.6 fusion.3
  110.3 0.2 collective-permute-start.15
  110.5 3.4 %collective-permute-start.19 = (bf16[128,1536]{1,0:T(8,128)(2,1)}, bf16[128,1536]{1,0:T(8,128)(2,1)S(1)}, u32[]{:S(2)}, u32[]{:S(2)}) collective-permute-start(bf16[128,1536]{1,0:T(8,128)(2,1)} %get-tuple-element.57), channel_id=1, source_target_pairs={{0,24},{8,0},{16,8},{24,16},{1,25},{9,1},{17,9},{25,17},{2,26},{10... | collective-permute-start | bytes 1179656 | tf_op jit(solution)/shard_map/ppermute | solution.py:18
  113.9 2.2 %collective-permute-start.21 = (bf16[128,1536]{1,0:T(8,128)(2,1)}, bf16[128,1536]{1,0:T(8,128)(2,1)S(1)}, u32[]{:S(2)}, u32[]{:S(2)}) collective-permute-start(bf16[128,1536]{1,0:T(8,128)(2,1)} %get-tuple-element.59), channel_id=1, source_target_pairs={{0,16},{8,24},{16,0},{24,8},{1,17},{9,25},{17,1},{25,9},{2,18},{10... | collective-permute-start | bytes 1179656 | tf_op jit(solution)/shard_map/ppermute | solution.py:18
  116.2 0.7 broadcast_in_dim.10
  116.9 3.3 %all-to-all-start.3 = ((f32[4,2,32,128]{3,1,2,0:T(2,128)}), f32[4,2,32,128]{3,1,2,0:T(2,128)S(1)}, u32[]{:S(2)}, u32[]{:S(2)}) async-start(f32[4,2,32,128]{3,1,2,0:T(2,128)} %broadcast_in_dim.10), calls=%async_computation.3 | async-start | bytes 262144 | tf_op jit(solution)/shard_map/all_to_all | solution.py:66
  120.2 4.2 %fusion.2 = f32[96,384]{1,0:T(8,128)} fusion(bf16[32,6144]{1,0:T(8,128)(2,1)S(1)} %get-tuple-element.68, bf16[32,6144]{1,0:T(8,128)(2,1)S(1)} %get-tuple-element.69, bf16[32,6144]{1,0:T(8,128)(2,1)S(1)} %get-tuple-element.67, bf16[1,6144,384]{2,1,0:T(8,128)(2,1)} %param.8), kind=kOutput, calls=%fused_computation.13 | convolution fusion | flops 456523776 | bytes 6045696 | tf_op jit(solution)/shard_map/dot_general | solution.py:41
  124.4 3.3 %all-to-all-done.3 = f32[4,2,32,128]{3,1,2,0:T(2,128)S(1)} async-done(((f32[4,2,32,128]{3,1,2,0:T(2,128)}), f32[4,2,32,128]{3,1,2,0:T(2,128)S(1)}, u32[]{:S(2)}, u32[]{:S(2)}) %all-to-all-start.3) | async-done | bytes 131104 | tf_op jit(solution)/shard_map/all_to_all | solution.py:66
  127.7 0.3 fusion.4
  128.0 0.9 fusion.13
  129.0 1.6 collective-permute-start.16
  130.5 2.7 %collective-permute-start.17 = (f32[32,384]{1,0:T(8,128)S(1)}, f32[32,384]{1,0:T(8,128)S(1)}, u32[]{:S(2)}, u32[]{:S(2)}) collective-permute-start(f32[32,384]{1,0:T(8,128)S(1)} %fusion.13), channel_id=1, source_target_pairs={{0,64},{32,96},{64,0},{96,32},{1,65},{33,97},{65,1},{97,33},{2,66}... | collective-permute-start | bytes 147464 | tf_op jit(solution)/shard_map/ppermute | solution.py:18
  133.3 1.1 collective-permute-done.16
  134.4 1.5 collective-permute-start.18
  135.9 5.2 %inverse_of_factor.1.inverse_ref = f32[32,32]{1,0:T(8,128)} custom-call(f32[32,6144]{1,0:T(8,128)} %bitcast.86), custom_call_target="tpu_custom_call" | custom-call | tf_op jit(solution)/shard_map/inverse_of_factor/pallas_call | solution.py:97
  141.2 1.5 collective-permute-start.22
  142.7 1.1 collective-permute-start.23
  143.8 1.7 %collective-permute-start.24 = (f32[32,384]{1,0:T(8,128)S(1)}, f32[32,384]{1,0:T(8,128)S(1)}, u32[]{:S(2)}, u32[]{:S(2)}) collective-permute-start(f32[32,384]{1,0:T(8,128)S(1)} %add_add_fusion), channel_id=1, source_target_pairs={{0,24},{8,0},{16,8},{24,16},{1,25},{9,1},{17,9},{25,17},{2,26},{10... | collective-permute-start | bytes 147464 | tf_op jit(solution)/shard_map/ppermute | solution.py:18
  145.5 3.2 %place.1 = bf16[128,6144]{1,0:T(8,128)(2,1)} custom-call(s32[12]{0:T(128)} %stack.69.at_ref, bf16[128,1536]{1,0:T(8,128)(2,1)} %get-tuple-element.63.refs_0_, bf16[128,1536]{1,0:T(8,128)(2,1)} %copy-done.7, bf16[128,1536]{1,0:T(8,128)(2,1)} %copy-done.8, bf16[128,1536]{1,0:T(8,128)(2,1)} %copy-done.9), custom_call_target="tpu_custom_call" | custom-call | bytes 3145728 | tf_op jit(solution)/shard_map/place/pallas_call | solution.py:189
  148.8 0.2 convolution_multiply_fusion.factor_ref
  149.0 13.3 %new_residual.1 = bf16[6144,384]{1,0:T(8,128)(2,1)} custom-call(bf16[1024,6144]{1,0:T(8,128)(2,1)} %all-gather.4.cloned.1.call-done.act_ref, bf16[1024,384]{1,0:T(8,128)(2,1)S(1)} %copy-done, bf16[6144,384]{1,0:T(8,128)(2,1)} %bitcast.89, f32[32,6144]{1,0:T(8,128)S(1)} %bitcast.87, f32[32,32]{1,0:T(8,128)S(1)} %copy-done.4, ...), custom_call_target="tpu_custom_call" | custom-call | flops 5737807872 | bytes 22806528 | tf_op jit(solution)/shard_map/new_residual/pallas_call | solution.py:121
  (79 shorter events, 0.8 us)
Async XLA Ops:
  7.2 69.8 %all-gather.6.cloned.1.call-start = ((), (), s32[]{:S(2)}) async-start(), calls=%async_computation.5 | async-start | bytes 5013504 | tf_op jit(solution)/shard_map/all_gather | solution.py:237
  9.0 140.0 %all-gather.4.cloned.1.call-start = ((), (), s32[]{:S(2)}) async-start(), calls=%async_computation.4 | async-start | bytes 14155776 | tf_op jit(solution)/shard_map/all_gather | solution.py:249
  9.0 11.0 %collective-permute-start.3 = (bf16[1024,384]{1,0:T(8,128)(2,1)}, bf16[1024,384]{1,0:T(8,128)(2,1)S(1)}, u32[]{:S(2)}, u32[]{:S(2)}) collective-permute-start(bf16[1024,384]{1,0:T(8,128)(2,1)} %cot_ref.1), channel_id=1, source_target_pairs={{0,1},{1,0},{2,3},{3,2},{4,5},{5,4},{6,7},{7,6},{8,9},{9,8},{10,11... | collective-permute-start | bytes 2359304 | tf_op jit(solution)/shard_map/ppermute | solution.py:18
  11.7 6.5 %collective-permute-start = (f32[32,256]{1,0:T(8,128)S(1)}, f32[32,256]{1,0:T(8,128)S(1)}, u32[]{:S(2)}, u32[]{:S(2)}) collective-permute-start(f32[32,256]{1,0:T(8,128)S(1)} %bitcast.98), channel_id=1, source_target_pairs={{0,2},{2,4},{4,6},{6,0},{1,3},{3,5},{5,7},{7,1},{8,10},{10,12},{12... | collective-permute-start | bytes 98312 | tf_op jit(solution)/shard_map/ppermute | solution.py:18
  13.4 5.4 %collective-permute-start.1 = (f32[32,256]{1,0:T(8,128)S(1)}, f32[32,256]{1,0:T(8,128)S(1)}, u32[]{:S(2)}, u32[]{:S(2)}) collective-permute-start(f32[32,256]{1,0:T(8,128)S(1)} %bitcast.99), channel_id=1, source_target_pairs={{0,4},{2,6},{4,0},{6,2},{1,5},{3,7},{5,1},{7,3},{8,12},{10,14},{12... | collective-permute-start | bytes 98312 | tf_op jit(solution)/shard_map/ppermute | solution.py:18
  16.1 3.9 %collective-permute-start.2 = (f32[32,256]{1,0:T(8,128)S(1)}, f32[32,256]{1,0:T(8,128)S(1)}, u32[]{:S(2)}, u32[]{:S(2)}) collective-permute-start(f32[32,256]{1,0:T(8,128)S(1)} %bitcast.100), channel_id=1, source_target_pairs={{0,6},{2,0},{4,2},{6,4},{1,7},{3,1},{5,3},{7,5},{8,14},{10,8},{12,... | collective-permute-start | bytes 98312 | tf_op jit(solution)/shard_map/ppermute | solution.py:18
  20.1 0.9 copy-start.6
  23.7 4.1 %copy-start.5 = (bf16[128,6144]{1,0:T(8,128)(2,1)S(1)}, bf16[128,6144]{1,0:T(8,128)(2,1)}, u32[]{:S(2)}) copy-start(bf16[128,6144]{1,0:T(8,128)(2,1)} %param.5) | copy-start | bytes 4718596
  23.8 4.1 %collective-permute-start.4 = (f32[32,128]{1,0:T(8,128)S(1)}, f32[32,128]{1,0:T(8,128)S(1)}, u32[]{:S(2)}, u32[]{:S(2)}) collective-permute-start(f32[32,128]{1,0:T(8,128)S(1)} %bitcast.101), channel_id=1, source_target_pairs={{0,1},{1,0},{2,3},{3,2},{4,5},{5,4},{6,7},{7,6},{8,9},{9,8},{10,11... | collective-permute-start | bytes 49160 | tf_op jit(solution)/shard_map/ppermute | solution.py:18
  28.4 0.9 copy-start.16
  28.4 1.3 copy-start.15
  28.4 5.0 %copy-start.14 = (bf16[256,384]{1,0:T(8,128)(2,1)S(1)}, bf16[256,384]{1,0:T(8,128)(2,1)}, u32[]{:S(2)}) copy-start(bf16[256,384]{1,0:T(8,128)(2,1)} %get-tuple-element.41) | copy-start | bytes 589828
  28.8 4.8 %collective-permute-start.5 = (f32[96,8,128]{2,1,0:T(8,128)S(1)}, f32[96,8,128]{2,1,0:T(8,128)S(1)}, u32[]{:S(2)}, u32[]{:S(2)}) collective-permute-start(f32[96,8,128]{2,1,0:T(8,128)S(1)} %dynamic-slice_bitcast_fusion), channel_id=1, source_target_pairs={{0,1},{1,0},{2,3},{3,2},{4,5},{5,4},{6,7},{7,6},{8,9},{9,8},{10,11... | collective-permute-start | bytes 1179656 | tf_op jit(solution)/shard_map/ppermute | solution.py:18
  29.3 9.4 %collective-permute-start.6 = (bf16[256,384]{1,0:T(8,128)(2,1)S(1)}, bf16[256,384]{1,0:T(8,128)(2,1)S(1)}, u32[]{:S(2)}, u32[]{:S(2)}) collective-permute-start(bf16[256,384]{1,0:T(8,128)(2,1)S(1)} %copy-done.16), channel_id=1, source_target_pairs={{0,2},{2,4},{4,6},{6,0},{1,3},{3,5},{5,7},{7,1},{8,10},{10,12},{12... | collective-permute-start | bytes 589832 | tf_op jit(solution)/shard_map/ppermute | solution.py:18
  29.6 14.0 %collective-permute-start.7 = (bf16[256,384]{1,0:T(8,128)(2,1)S(1)}, bf16[256,384]{1,0:T(8,128)(2,1)S(1)}, u32[]{:S(2)}, u32[]{:S(2)}) collective-permute-start(bf16[256,384]{1,0:T(8,128)(2,1)S(1)} %copy-done.15), channel_id=1, source_target_pairs={{0,4},{2,6},{4,0},{6,2},{1,5},{3,7},{5,1},{7,3},{8,12},{10,14},{12... | collective-permute-start | bytes 589832 | tf_op jit(solution)/shard_map/ppermute | solution.py:18
  33.4 10.2 %collective-permute-start.8 = (bf16[256,384]{1,0:T(8,128)(2,1)S(1)}, bf16[256,384]{1,0:T(8,128)(2,1)S(1)}, u32[]{:S(2)}, u32[]{:S(2)}) collective-permute-start(bf16[256,384]{1,0:T(8,128)(2,1)S(1)} %copy-done.14), channel_id=1, source_target_pairs={{0,6},{2,0},{4,2},{6,4},{1,7},{3,1},{5,3},{7,5},{8,14},{10,8},{12,... | collective-permute-start | bytes 589832 | tf_op jit(solution)/shard_map/ppermute | solution.py:18
  38.7 4.9 %copy-start.10 = (bf16[256,384]{1,0:T(8,128)(2,1)}, bf16[256,384]{1,0:T(8,128)(2,1)S(1)}, u32[]{:S(2)}) copy-start(bf16[256,384]{1,0:T(8,128)(2,1)S(1)} %collective-permute-done.6.refs_2_) | copy-start | bytes 589828
  43.6 0.7 copy-start.11
  44.3 0.7 copy-start.12
  47.8 29.1 %collective-permute-start.10 = (bf16[8,128,384]{2,1,0:T(8,128)(2,1)}, bf16[8,128,384]{2,1,0:T(8,128)(2,1)S(1)}, u32[]{:S(2)}, u32[]{:S(2)}) collective-permute-start(bf16[8,128,384]{2,1,0:T(8,128)(2,1)} %unpack.1.refs_0_), channel_id=1, source_target_pairs={{0,24},{8,0},{16,8},{24,16},{1,25},{9,1},{17,9},{25,17},{2,26},{10... | collective-permute-start | bytes 2359304 | tf_op jit(solution)/shard_map/ppermute | solution.py:18
  51.8 25.1 %collective-permute-start.9 = (bf16[8,128,384]{2,1,0:T(8,128)(2,1)}, bf16[8,128,384]{2,1,0:T(8,128)(2,1)}, u32[]{:S(2)}, u32[]{:S(2)}) collective-permute-start(bf16[8,128,384]{2,1,0:T(8,128)(2,1)} %unpack.1.refs_0_), channel_id=1, source_target_pairs={{0,8},{8,16},{16,24},{24,0},{1,9},{9,17},{17,25},{25,1},{2,10},{10... | collective-permute-start | bytes 2359304 | tf_op jit(solution)/shard_map/ppermute | solution.py:18
  76.9 20.1 %copy-start.13 = (bf16[8,128,384]{2,1,0:T(8,128)(2,1)}, bf16[8,128,384]{2,1,0:T(8,128)(2,1)S(1)}, u32[]{:S(2)}) copy-start(bf16[8,128,384]{2,1,0:T(8,128)(2,1)S(1)} %collective-permute-done.10.refs_2_) | copy-start | bytes 2359300
  77.0 20.1 %collective-permute-start.13 = (bf16[4,4,384,384]{3,2,1,0:T(8,128)(2,1)}, bf16[4,4,384,384]{3,2,1,0:T(8,128)(2,1)}, u32[]{:S(2)}, u32[]{:S(2)}) collective-permute-start(bf16[4,4,384,384]{3,2,1,0:T(8,128)(2,1)} %bitcast.102), channel_id=1, source_target_pairs={{0,1},{1,0},{2,3},{3,2},{4,5},{5,4},{6,7},{7,6},{8,9},{9,8},{10,11... | collective-permute-start | bytes 14155784 | tf_op jit(solution)/shard_map/ppermute | solution.py:18
  78.3 18.8 %collective-permute-start.11 = (bf16[8,64,384]{2,1,0:T(8,128)(2,1)S(1)}, bf16[8,64,384]{2,1,0:T(8,128)(2,1)}, u32[]{:S(2)}, u32[]{:S(2)}) collective-permute-start(bf16[8,64,384]{2,1,0:T(8,128)(2,1)S(1)} %slice.69), channel_id=1, source_target_pairs={{0,8},{8,16},{16,24},{24,0},{1,9},{9,17},{17,25},{25,1},{2,10},{10... | collective-permute-start | bytes 1179656 | tf_op jit(solution)/shard_map/ppermute | solution.py:18
  78.4 18.6 %collective-permute-start.12 = (bf16[8,64,384]{2,1,0:T(8,128)(2,1)S(1)}, bf16[8,64,384]{2,1,0:T(8,128)(2,1)}, u32[]{:S(2)}, u32[]{:S(2)}) collective-permute-start(bf16[8,64,384]{2,1,0:T(8,128)(2,1)S(1)} %slice.70), channel_id=1, source_target_pairs={{0,24},{8,0},{16,8},{24,16},{1,25},{9,1},{17,9},{25,17},{2,26},{10... | collective-permute-start | bytes 1179656 | tf_op jit(solution)/shard_map/ppermute | solution.py:18
  92.8 14.5 %all-to-all-start.2 = ((f32[16,6,8,128]{3,2,1,0:T(8,128)}), f32[16,6,8,128]{3,2,1,0:T(8,128)S(1)}, u32[]{:S(2)}, u32[]{:S(2)}) async-start(f32[16,6,8,128]{3,2,1,0:T(8,128)} %broadcast_in_dim.9), calls=%async_computation.2 | async-start | bytes 786432 | tf_op jit(solution)/shard_map/all_to_all | solution.py:66
  107.3 2.0 %collective-permute-start.14 = (f32[96,8,128]{2,1,0:T(8,128)S(1)}, f32[96,8,128]{2,1,0:T(8,128)S(1)}, u32[]{:S(2)}, u32[]{:S(2)}) collective-permute-start(f32[96,8,128]{2,1,0:T(8,128)S(1)} %bitcast.93), channel_id=1, source_target_pairs={{0,1},{1,0},{2,3},{3,2},{4,5},{5,4},{6,7},{7,6},{8,9},{9,8},{10,11... | collective-permute-start | bytes 1179656 | tf_op jit(solution)/shard_map/ppermute | solution.py:18
  109.4 0.9 copy-start.1
  110.3 5.9 %collective-permute-start.15 = (f32[32,128]{1,0:T(8,128)S(1)}, f32[32,128]{1,0:T(8,128)S(1)}, u32[]{:S(2)}, u32[]{:S(2)}) collective-permute-start(f32[32,128]{1,0:T(8,128)S(1)} %fusion.28), channel_id=1, source_target_pairs={{0,1},{1,0},{2,3},{3,2},{4,5},{5,4},{6,7},{7,6},{8,9},{9,8},{10,11... | collective-permute-start | bytes 49160 | tf_op jit(solution)/shard_map/ppermute | solution.py:18
  110.5 30.7 %collective-permute-start.19 = (bf16[128,1536]{1,0:T(8,128)(2,1)}, bf16[128,1536]{1,0:T(8,128)(2,1)S(1)}, u32[]{:S(2)}, u32[]{:S(2)}) collective-permute-start(bf16[128,1536]{1,0:T(8,128)(2,1)} %get-tuple-element.57), channel_id=1, source_target_pairs={{0,24},{8,0},{16,8},{24,16},{1,25},{9,1},{17,9},{25,17},{2,26},{10... | collective-permute-start | bytes 1179656 | tf_op jit(solution)/shard_map/ppermute | solution.py:18
  113.9 27.3 %collective-permute-start.20 = (bf16[128,1536]{1,0:T(8,128)(2,1)}, bf16[128,1536]{1,0:T(8,128)(2,1)S(1)}, u32[]{:S(2)}, u32[]{:S(2)}) collective-permute-start(bf16[128,1536]{1,0:T(8,128)(2,1)} %get-tuple-element.58), channel_id=1, source_target_pairs={{0,8},{8,16},{16,24},{24,0},{1,9},{9,17},{17,25},{25,1},{2,10},{10... | collective-permute-start | bytes 1179656 | tf_op jit(solution)/shard_map/ppermute | solution.py:18
  113.9 27.3 %collective-permute-start.21 = (bf16[128,1536]{1,0:T(8,128)(2,1)}, bf16[128,1536]{1,0:T(8,128)(2,1)S(1)}, u32[]{:S(2)}, u32[]{:S(2)}) collective-permute-start(bf16[128,1536]{1,0:T(8,128)(2,1)} %get-tuple-element.59), channel_id=1, source_target_pairs={{0,16},{8,24},{16,0},{24,8},{1,17},{9,25},{17,1},{25,9},{2,18},{10... | collective-permute-start | bytes 1179656 | tf_op jit(solution)/shard_map/ppermute | solution.py:18
  116.9 10.8 %all-to-all-start.3 = ((f32[4,2,32,128]{3,1,2,0:T(2,128)}), f32[4,2,32,128]{3,1,2,0:T(2,128)S(1)}, u32[]{:S(2)}, u32[]{:S(2)}) async-start(f32[4,2,32,128]{3,1,2,0:T(2,128)} %broadcast_in_dim.10), calls=%async_computation.3 | async-start | bytes 262144 | tf_op jit(solution)/shard_map/all_to_all | solution.py:66
  120.2 7.5 %copy-start = (bf16[1024,384]{1,0:T(8,128)(2,1)S(1)}, bf16[1024,384]{1,0:T(8,128)(2,1)}, u32[]{:S(2)}) copy-start(bf16[1024,384]{1,0:T(8,128)(2,1)} %cot_ref.1) | copy-start | bytes 2359300
  128.0 21.0 %copy-start.2 = (f32[2,96,8,128]{3,2,1,0:T(8,128)S(1)}, f32[2,96,8,128]{3,2,1,0:T(8,128)}, u32[]{:S(2)}) copy-start(f32[2,96,8,128]{3,2,1,0:T(8,128)} %copy-done.1) | copy-start | bytes 2359300
  129.0 5.4 %collective-permute-start.16 = (f32[32,384]{1,0:T(8,128)S(1)}, f32[32,384]{1,0:T(8,128)S(1)}, u32[]{:S(2)}, u32[]{:S(2)}) collective-permute-start(f32[32,384]{1,0:T(8,128)S(1)} %fusion.13), channel_id=1, source_target_pairs={{0,32},{32,64},{64,96},{96,0},{1,33},{33,65},{65,97},{97,1},{2,34}... | collective-permute-start | bytes 147464 | tf_op jit(solution)/shard_map/ppermute | solution.py:18
  130.5 10.6 %collective-permute-start.17 = (f32[32,384]{1,0:T(8,128)S(1)}, f32[32,384]{1,0:T(8,128)S(1)}, u32[]{:S(2)}, u32[]{:S(2)}) collective-permute-start(f32[32,384]{1,0:T(8,128)S(1)} %fusion.13), channel_id=1, source_target_pairs={{0,64},{32,96},{64,0},{96,32},{1,65},{33,97},{65,1},{97,33},{2,66}... | collective-permute-start | bytes 147464 | tf_op jit(solution)/shard_map/ppermute | solution.py:18
  134.4 6.7 %collective-permute-start.18 = (f32[32,384]{1,0:T(8,128)S(1)}, f32[32,384]{1,0:T(8,128)S(1)}, u32[]{:S(2)}, u32[]{:S(2)}) collective-permute-start(f32[32,384]{1,0:T(8,128)S(1)} %fusion.13), channel_id=1, source_target_pairs={{0,96},{32,0},{64,32},{96,64},{1,97},{33,1},{65,33},{97,65},{2,98}... | collective-permute-start | bytes 147464 | tf_op jit(solution)/shard_map/ppermute | solution.py:18
  141.1 7.6 %copy-start.4 = (f32[32,32]{1,0:T(8,128)S(1)}, f32[32,32]{1,0:T(8,128)}, u32[]{:S(2)}) copy-start(f32[32,32]{1,0:T(8,128)} %inverse_of_factor.1.inverse_ref) | copy-start | bytes 12292
  141.1 4.4 %copy-start.7 = (bf16[128,1536]{1,0:T(8,128)(2,1)}, bf16[128,1536]{1,0:T(8,128)(2,1)S(1)}, u32[]{:S(2)}) copy-start(bf16[128,1536]{1,0:T(8,128)(2,1)S(1)} %collective-permute-done.19.refs_1_) | copy-start | bytes 1179652
  141.2 4.3 %copy-start.8 = (bf16[128,1536]{1,0:T(8,128)(2,1)}, bf16[128,1536]{1,0:T(8,128)(2,1)S(1)}, u32[]{:S(2)}) copy-start(bf16[128,1536]{1,0:T(8,128)(2,1)S(1)} %collective-permute-done.20.refs_2_) | copy-start | bytes 1179652
  141.2 4.3 %copy-start.9 = (bf16[128,1536]{1,0:T(8,128)(2,1)}, bf16[128,1536]{1,0:T(8,128)(2,1)S(1)}, u32[]{:S(2)}) copy-start(bf16[128,1536]{1,0:T(8,128)(2,1)S(1)} %collective-permute-done.21.refs_3_) | copy-start | bytes 1179652
  141.2 7.5 %collective-permute-start.22 = (f32[32,384]{1,0:T(8,128)S(1)}, f32[32,384]{1,0:T(8,128)S(1)}, u32[]{:S(2)}, u32[]{:S(2)}) collective-permute-start(f32[32,384]{1,0:T(8,128)S(1)} %add_add_fusion), channel_id=1, source_target_pairs={{0,8},{8,16},{16,24},{24,0},{1,9},{9,17},{17,25},{25,1},{2,10},{10... | collective-permute-start | bytes 147464 | tf_op jit(solution)/shard_map/ppermute | solution.py:18
  142.7 6.0 %collective-permute-start.23 = (f32[32,384]{1,0:T(8,128)S(1)}, f32[32,384]{1,0:T(8,128)S(1)}, u32[]{:S(2)}, u32[]{:S(2)}) collective-permute-start(f32[32,384]{1,0:T(8,128)S(1)} %add_add_fusion), channel_id=1, source_target_pairs={{0,16},{8,24},{16,0},{24,8},{1,17},{9,25},{17,1},{25,9},{2,18},{10... | collective-permute-start | bytes 147464 | tf_op jit(solution)/shard_map/ppermute | solution.py:18
  143.8 4.9 %collective-permute-start.24 = (f32[32,384]{1,0:T(8,128)S(1)}, f32[32,384]{1,0:T(8,128)S(1)}, u32[]{:S(2)}, u32[]{:S(2)}) collective-permute-start(f32[32,384]{1,0:T(8,128)S(1)} %add_add_fusion), channel_id=1, source_target_pairs={{0,24},{8,0},{16,8},{24,16},{1,25},{9,1},{17,9},{25,17},{2,26},{10... | collective-permute-start | bytes 147464 | tf_op jit(solution)/shard_map/ppermute | solution.py:18
  148.9 13.4 %copy-start.3 = (f32[32,384]{1,0:T(8,128)}, f32[32,384]{1,0:T(8,128)S(1)}, u32[]{:S(2)}) copy-start(f32[32,384]{1,0:T(8,128)S(1)} %convolution_multiply_fusion.factor_ref) | copy-start | bytes 147460
Sparse Core Ops, SparseCore 0:
  10.1 63.7 all-gather.5
  75.6 68.9 all-gather.3

commit v4 on v3

--- a/solution.py
+++ b/solution.py
@@ -184,7 +184,7 @@
 
 
 def copy_call(plan, n_copies, ins, outs, at, name):
-    any_spec = pl.BlockSpec(memory_space=pl.ANY)
+    any_spec = pl.BlockSpec(memory_space=pltpu.HBM)
     moved = sum(2 * math.prod(o.shape) * o.dtype.itemsize for o in outs)
     return pl.pallas_call(
         functools.partial(copy_kernel, len(ins), len(outs), plan),
@@ -244,29 +244,33 @@
     warm3 = jnp.concatenate(split3(warm_factor.T), 0)
     cw = fold3(mm(warm3, cotangent, 1, 1)) * scale
     cw = reduce_scatter(cw.reshape(rank, 4, 2 * tok).transpose(1, 0, 2), "x")
-    act, cw, *packed = lax.optimization_barrier((activations, cw, *packed))
+    left = fold3(mm(warm3, residual, 1, 1))
+    act, cw, left, *packed = lax.optimization_barrier((activations, cw, left, *packed))
     got = [shift(p, "x", s) for s, p in zip((1, 2, 3), packed)]
     gathered = lax.all_gather(act, ("x", "core"), axis=0, tiled=True)
     cw = reduce_scatter(cw.reshape(rank, 2, tok).transpose(1, 0, 2), "core")
 
     cw3 = jnp.concatenate(split3(cw), 0)
-    left = fold3(mm(cw3, activations, 1, 0)) + fold3(mm(warm3, residual, 1, 1))
+    left = left + fold3(mm(cw3, activations, 1, 0))
     tiles = left.reshape(rank // 8, 8, d // 128, 128).transpose(0, 2, 1, 3).reshape(-1, 8, 128)
     n_tiles = tiles.shape[0]
     part = reduce_scatter(tiles.reshape(2, n_tiles // 2, 8, 128), "core")
+
+    part = reduce_scatter(part.reshape(4, n_tiles // 8, 8, 128), "z")
     part, *got = lax.optimization_barrier((part, *got))
 
     (cot_own,) = copy_call(
         functools.partial(unpack_plan, tok), 8, [cotangent, cot_other] + got, [like(8, tok, cols)], at, "unpack"
     )
+    part, cot_own = lax.optimization_barrier((part, cot_own))
     c_low, c_high = shift(cot_own, "z", 1), shift(cot_own, "z", -1)
-    part = lax.all_to_all(part.reshape(16, n_tiles // 32, 8, 128), ("y", "z"), 0, 0).sum(0)
+    part = reduce_scatter(part.reshape(4, n_tiles // 32, 8, 128), "y")
+    part = all_sum(part, "x")
     part, c_low, c_high, w_all = lax.optimization_barrier((part, c_low, c_high, w_all))
     w_other = shift(w_all, "core", 1)
     half = tok // 2
     c_far = [shift(c_low[:, :half], "z", 1), shift(c_high[:, half:], "z", -1)]
-    part = all_blocks(part, ("x",)).sum(0)
-    part = all_blocks(part, ("y", "z")).reshape(-1, 8, 128)
+    part = all_blocks(part, ("z", "y")).reshape(-1, 8, 128)
     grads = input_call([cot_own, c_low, c_high, *c_far], w_all, w_other, at, 2)
     part, *grads = lax.optimization_barrier((part, *grads))
     back = [grads[0], shift(grads[1], "z", -1), shift(grads[2], "z", 1), shift(grads[3], "z", 2)]
@@ -275,8 +279,10 @@
 
     left3 = jnp.concatenate(split3(left), 0)
     right = fold3(mm(left3, activations, 1, 1)) * scale
-    right = all_blocks(both_cores(right), ("x",))
-    right = right.reshape(8, rank, tok).transpose(1, 0, 2).reshape(rank, 8 * tok)
+    right = both_cores(right)
+    pieces = [right] + [shift(right, "x", s) for s in (1, 2, 3)]
+    right = [sum(jnp.where((ix - s) % 4 == k, p, 0.0) for s, p in enumerate(pieces)) for k in range(4)]
+    right = jnp.concatenate([r[c] for r in right for c in (0, 1)], 1)
     right3 = jnp.concatenate(split3(right), 0)
     sums = fold3(mm(right3, cotangent, 1, 0)) + fold3(mm(left3, residual, 1, 0))
     left, right = lax.optimization_barrier((left, right))

time: 170 us -> 161 us (0.947)
  blocking collectives: 34 us -> 0 us
  starting transfers between devices: 41.9 us -> 63.8 us
  waiting for transfers between devices: 18.1 us -> 24.4 us
    all_to_all x2 -> x0, blocking collectives: 34 us -> none  [the longest x1 24.5 us: per_device(): lax.all_to_all(part.reshape(16, n_tiles // 32, 8, 128), ('y', 'z'), 0, 0)]
    ppermute x25 -> x37, starting transfers between devices: 34.2 us -> 58 us  [shift(): return lax.ppermute(value, axis, [(i, (i + step) % n) for i in range(n)])]
    ppermute x25 -> x37, waiting for transfers between devices: 14.8 us -> 23.3 us  [shift(): return lax.ppermute(value, axis, [(i, (i + step) % n) for i in range(n)])]
    all_to_all x2 -> x1, waiting for transfers between devices: 3.28 us -> 0.01 us  [all_blocks(): lax.all_to_all(jnp.broadcast_to(value[None], (n,) + value.shape), axis, 0...]
    all_to_all x2 -> x1, starting transfers between devices: 7.59 us -> 5.73 us  [all_blocks(): lax.all_to_all(jnp.broadcast_to(value[None], (n,) + value.shape), axis, 0...]
  transfers between devices with their start and end apart: 29 -> 40, of which waited for: 7 -> 17; matrix products, arithmetic and copies ran while one was open for 11% -> 9% of each run, Pallas kernels for 14% -> 15%
where the time goes in v4:
time: 161 us; the launch traced here: 160 us
  starting transfers between devices  63.8 us (40%)
  Pallas kernels  37.2 us (23%)
  waiting for transfers between devices  24.4 us (15%)
  between operations  14.8 us (9%)
  matrix products  10.3 us (6%)
  local copies, waits for them, and re-layouts  7.24 us (4%)
  other arithmetic  1.66 us (1%)
    ppermute x37, starting transfers between devices, shift(): return lax.ppermute(value, axis, [(i, (i + step) % n) for i in range(n)])  58 us
    ppermute x37, waiting for transfers between devices, shift(): return lax.ppermute(value, axis, [(i, (i + step) % n) for i in range(n)])  23.3 us
    pallas_call x1, Pallas kernels, residual_call(): pl.pallas_call(functools.partial(residual_kernel, scale), out_shape=jax.S...  13.3 us
    dot_general x6, matrix products, mm(): lax.dot_general(a, b, (((ca,), (cb,)), ((), ())), preferred_element_type=...  10.1 us
    pallas_call x1, Pallas kernels, input_call(): pl.pallas_call(functools.partial(input_kernel, len(cots)), out_shape=[jax...  10.1 us
    pallas_call x3, Pallas kernels, copy_call(): pl.pallas_call(functools.partial(copy_kernel, len(ins), len(outs), plan),...  8.66 us
    all_to_all x1, starting transfers between devices, all_blocks(): lax.all_to_all(jnp.broadcast_to(value[None], (n,) + value.shape), axis, 0...  5.73 us
    pallas_call x1, Pallas kernels, inverse_of_factor(): pl.pallas_call(inverse_kernel, out_shape=jax.ShapeDtypeStruct((rank, rank...  5.21 us
  transfers between devices with their start and end apart: 40, of which 17 were waited for; matrix products, arithmetic and copies ran while one was open for 9% of the time, Pallas kernels for 15%

profile of v4, /device:TPU:0, one launch (start us, length us, event | category | flops | bytes accessed | tf_op | source)
XLA Modules:
  0.0 159.5 jit_solution(74446442234377849)
XLA Ops:
  7.2 1.7 %constant_dynamic-slice_fusion = bf16[384,384]{1,0:T(8,128)(2,1)} fusion(bf16[6144,384]{1,0:T(8,128)(2,1)} %param.7, s32[]{:T(128)S(6)} %select_n.320), kind=kLoop, calls=%fused_computation.106 | loop fusion | bytes 589828 | tf_op jit(solution)/shard_map/dynamic_slice | solution.py:236
  9.2 0.8 reduce-precision_convert_fusion.5
  10.0 1.5 fusion.22
  11.7 1.6 %collective-permute-start = (f32[32,256]{1,0:T(8,128)S(1)}, f32[32,256]{1,0:T(8,128)S(1)}, u32[]{:S(2)}, u32[]{:S(2)}) collective-permute-start(f32[32,256]{1,0:T(8,128)S(1)} %bitcast.145), channel_id=1, source_target_pairs={{0,2},{2,4},{4,6},{6,0},{1,3},{3,5},{5,7},{7,1},{8,10},{10,12},{12... | collective-permute-start | bytes 98312 | tf_op jit(solution)/shard_map/ppermute | solution.py:18
  13.4 2.7 %collective-permute-start.1 = (f32[32,256]{1,0:T(8,128)S(1)}, f32[32,256]{1,0:T(8,128)S(1)}, u32[]{:S(2)}, u32[]{:S(2)}) collective-permute-start(f32[32,256]{1,0:T(8,128)S(1)} %bitcast.146), channel_id=1, source_target_pairs={{0,4},{2,6},{4,0},{6,2},{1,5},{3,7},{5,1},{7,3},{8,12},{10,14},{12... | collective-permute-start | bytes 98312 | tf_op jit(solution)/shard_map/ppermute | solution.py:18
  16.1 1.4 collective-permute-start.2
  17.6 3.9 %fusion.21 = f32[96,6144]{1,0:T(8,128)S(1)} fusion(bf16[32,384]{1,0:T(8,128)(2,1)S(1)} %get-tuple-element.96, bf16[32,384]{1,0:T(8,128)(2,1)S(1)} %get-tuple-element.97, bf16[32,384]{1,0:T(8,128)(2,1)S(1)} %get-tuple-element.95, bf16[1,6144,384]{2,1,0:T(8,128)(2,1)} %param.8), kind=kOutput, calls=%fused_computation.65 | convolution fusion | flops 453206016 | bytes 7151616 | tf_op jit(solution)/shard_map/dot_general | solution.py:41
  21.7 0.6 stack.69.at_ref
  22.4 0.9 copy-done.6
  23.3 2.6 %pack.1 = (bf16[256,384]{1,0:T(8,128)(2,1)}, bf16[256,384]{1,0:T(8,128)(2,1)}, bf16[256,384]{1,0:T(8,128)(2,1)}) custom-call(s32[12]{0:T(128)} %stack.69.at_ref, bf16[1024,384]{1,0:T(8,128)(2,1)} %cot_ref.1, bf16[1024,384]{1,0:T(8,128)(2,1)} %copy-done.6), custom_call_target="tpu_custom_call" | custom-call | bytes 1179648 | tf_op jit(solution)/shard_map/pack/pallas_call | solution.py:189
  26.1 1.2 collective-permute-done.4
  27.3 0.5 fusion.23
  28.3 1.6 collective-permute-done.5
  29.9 2.0 %collective-permute-start.6 = (f32[24,8,128]{2,1,0:T(8,128)S(1)}, f32[24,8,128]{2,1,0:T(8,128)S(1)}, u32[]{:S(2)}, u32[]{:S(2)}) collective-permute-start(f32[24,8,128]{2,1,0:T(8,128)S(1)} %get-tuple-element.78), channel_id=1, source_target_pairs={{0,8},{8,16},{16,24},{24,0},{1,9},{9,17},{17,25},{25,1},{2,10},{10... | collective-permute-start | bytes 294920 | tf_op jit(solution)/shard_map/ppermute | solution.py:18
  31.9 3.6 %collective-permute-start.7 = (f32[24,8,128]{2,1,0:T(8,128)S(1)}, f32[24,8,128]{2,1,0:T(8,128)S(1)}, u32[]{:S(2)}, u32[]{:S(2)}) collective-permute-start(f32[24,8,128]{2,1,0:T(8,128)S(1)} %get-tuple-element.80), channel_id=1, source_target_pairs={{0,16},{8,24},{16,0},{24,8},{1,17},{9,25},{17,1},{25,9},{2,18},{10... | collective-permute-start | bytes 294920 | tf_op jit(solution)/shard_map/ppermute | solution.py:18
  35.5 1.0 collective-permute-start.8
  36.5 0.6 collective-permute-start.10
  37.1 2.7 %collective-permute-start.11 = (bf16[256,384]{1,0:T(8,128)(2,1)S(1)}, bf16[256,384]{1,0:T(8,128)(2,1)S(1)}, u32[]{:S(2)}, u32[]{:S(2)}) collective-permute-start(bf16[256,384]{1,0:T(8,128)(2,1)S(1)} %copy-done.17), channel_id=1, source_target_pairs={{0,6},{2,0},{4,2},{6,4},{1,7},{3,1},{5,3},{7,5},{8,14},{10,8},{12,... | collective-permute-start | bytes 589832 | tf_op jit(solution)/shard_map/ppermute | solution.py:18
  39.8 0.7 collective-permute-done.7
  40.5 5.6 %collective-permute-done.10.refs_3_ = bf16[256,384]{1,0:T(8,128)(2,1)S(1)} collective-permute-done((bf16[256,384]{1,0:T(8,128)(2,1)}, bf16[256,384]{1,0:T(8,128)(2,1)S(1)}, u32[]{:S(2)}, u32[]{:S(2)}) %collective-permute-start.10) | collective-permute-done | bytes 196640 | tf_op jit(solution)/shard_map/ppermute | solution.py:18
  46.3 2.3 %collective-permute-done.9.refs_2_ = bf16[256,384]{1,0:T(8,128)(2,1)S(1)} collective-permute-done((bf16[256,384]{1,0:T(8,128)(2,1)S(1)}, bf16[256,384]{1,0:T(8,128)(2,1)S(1)}, u32[]{:S(2)}, u32[]{:S(2)}) %collective-permute-start.9) | collective-permute-done | bytes 196640 | tf_op jit(solution)/shard_map/ppermute | solution.py:18
  48.6 0.7 copy-done.12
  49.3 2.8 %unpack.1.refs_0_ = bf16[8,128,384]{2,1,0:T(8,128)(2,1)} custom-call(s32[12]{0:T(128)} %stack.69.at_ref, bf16[1024,384]{1,0:T(8,128)(2,1)} %cot_ref.1, bf16[1024,384]{1,0:T(8,128)(2,1)} %copy-done.6, bf16[256,384]{1,0:T(8,128)(2,1)} %copy-done.12, bf16[256,384]{1,0:T(8,128)(2,1)} %copy-done.10, bf16[256,384]{1,0:T(8,128)(2,1)} %copy-done.11), custom_call_target="tpu_custom_call" | custom-call | bytes 1572864 | tf_op jit(solution)/shard_map/unpack/pallas_call | solution.py:189
  52.1 1.1 collective-permute-start.18
  53.2 2.2 %collective-permute-start.19 = (bf16[8,128,384]{2,1,0:T(8,128)(2,1)}, bf16[8,128,384]{2,1,0:T(8,128)(2,1)S(1)}, u32[]{:S(2)}, u32[]{:S(2)}) collective-permute-start(bf16[8,128,384]{2,1,0:T(8,128)(2,1)} %unpack.1.refs_0_), channel_id=1, source_target_pairs={{0,24},{8,0},{16,8},{24,16},{1,25},{9,1},{17,9},{25,17},{2,26},{10... | collective-permute-start | bytes 2359304 | tf_op jit(solution)/shard_map/ppermute | solution.py:18
  55.4 1.6 collective-permute-start.12
  57.0 3.0 %collective-permute-start.13 = (f32[6,8,128]{2,1,0:T(8,128)S(1)}, f32[6,8,128]{2,1,0:T(8,128)S(1)}, u32[]{:S(2)}, u32[]{:S(2)}) collective-permute-start(f32[6,8,128]{2,1,0:T(8,128)S(1)} %get-tuple-element.94), channel_id=1, source_target_pairs={{0,64},{32,96},{64,0},{96,32},{1,65},{33,97},{65,1},{97,33},{2,66}... | collective-permute-start | bytes 73736 | tf_op jit(solution)/shard_map/ppermute | solution.py:18
  60.0 1.3 collective-permute-start.14
  61.3 1.8 %collective-permute-done.13 = f32[6,8,128]{2,1,0:T(8,128)S(1)} collective-permute-done((f32[6,8,128]{2,1,0:T(8,128)S(1)}, f32[6,8,128]{2,1,0:T(8,128)S(1)}, u32[]{:S(2)}, u32[]{:S(2)}) %collective-permute-start.13) | collective-permute-done | bytes 24608 | tf_op jit(solution)/shard_map/ppermute | solution.py:18
  63.1 1.2 collective-permute-done.14
  64.3 0.4 collective-permute-start.15
  64.8 2.0 %collective-permute-start.16 = (f32[6,8,128]{2,1,0:T(8,128)S(1)}, f32[6,8,128]{2,1,0:T(8,128)S(1)}, u32[]{:S(2)}, u32[]{:S(2)}) collective-permute-start(f32[6,8,128]{2,1,0:T(8,128)S(1)} %fusion.30), channel_id=1, source_target_pairs={{0,4},{2,6},{4,0},{6,2},{1,5},{3,7},{5,1},{7,3},{8,12},{10,14},{12... | collective-permute-start | bytes 73736 | tf_op jit(solution)/shard_map/ppermute | solution.py:18
  66.8 2.1 %collective-permute-start.17 = (f32[6,8,128]{2,1,0:T(8,128)S(1)}, f32[6,8,128]{2,1,0:T(8,128)S(1)}, u32[]{:S(2)}, u32[]{:S(2)}) collective-permute-start(f32[6,8,128]{2,1,0:T(8,128)S(1)} %fusion.30), channel_id=1, source_target_pairs={{0,6},{2,0},{4,2},{6,4},{1,7},{3,1},{5,3},{7,5},{8,14},{10,8},{12,... | collective-permute-start | bytes 73736 | tf_op jit(solution)/shard_map/ppermute | solution.py:18
  68.9 0.6 collective-permute-done.15
  69.4 0.6 collective-permute-done.16
  70.1 0.5 collective-permute-done.17
  70.6 1.5 collective-permute-done.18.refs_1_
  72.2 0.9 copy-done.14
  73.2 1.0 slice.94
  74.3 3.3 %collective-permute-start.21 = (bf16[8,64,384]{2,1,0:T(8,128)(2,1)S(1)}, bf16[8,64,384]{2,1,0:T(8,128)(2,1)}, u32[]{:S(2)}, u32[]{:S(2)}) collective-permute-start(bf16[8,64,384]{2,1,0:T(8,128)(2,1)S(1)} %slice.94), channel_id=1, source_target_pairs={{0,24},{8,0},{16,8},{24,16},{1,25},{9,1},{17,9},{25,17},{2,26},{10... | collective-permute-start | bytes 1179656 | tf_op jit(solution)/shard_map/ppermute | solution.py:18
  77.5 0.8 broadcast_in_dim.28
  78.4 5.7 %all-to-all-start = ((f32[16,6,8,128]{3,2,1,0:T(8,128)}), f32[16,6,8,128]{3,2,1,0:T(8,128)S(1)}, u32[]{:S(2)}, u32[]{:S(2)}) async-start(f32[16,6,8,128]{3,2,1,0:T(8,128)} %broadcast_in_dim.28), calls=%async_computation | async-start | bytes 786432 | tf_op jit(solution)/shard_map/all_to_all | solution.py:66
  84.1 1.9 %collective-permute-done.20.refs_3_ = bf16[8,64,384]{2,1,0:T(8,128)(2,1)} collective-permute-done((bf16[8,64,384]{2,1,0:T(8,128)(2,1)S(1)}, bf16[8,64,384]{2,1,0:T(8,128)(2,1)}, u32[]{:S(2)}, u32[]{:S(2)}) %collective-permute-start.20) | collective-permute-done | bytes 393248 | tf_op jit(solution)/shard_map/ppermute | solution.py:18
  86.0 0.8 collective-permute-done.21.refs_4_
  86.9 10.1 %input_grads.1 = (bf16[128,1536]{1,0:T(8,128)(2,1)}, bf16[128,1536]{1,0:T(8,128)(2,1)}, bf16[128,1536]{1,0:T(8,128)(2,1)}, bf16[128,1536]{1,0:T(8,128)(2,1)}) custom-call(s32[12]{0:T(128)} %stack.69.at_ref, bf16[8,128,384]{2,1,0:T(8,128)(2,1)} %unpack.1.refs_0_, bf16[8,128,384]{2,1,0:T(8,128)(2,1)} %copy-done.13, bf16[8,128,384]{2,1,0:T(8,128)(2,1)} %copy-done.14, ...), custom_call_target="tpu_custom_call" | custom-call | flops 4831838208 | bytes 12582912 | tf_op jit(solution)/shard_map/input_grads/pallas_call | solution.py:159
  97.0 1.7 %collective-permute-done.23 = f32[96,8,128]{2,1,0:T(8,128)S(1)} collective-permute-done((f32[96,8,128]{2,1,0:T(8,128)S(1)}, f32[96,8,128]{2,1,0:T(8,128)S(1)}, u32[]{:S(2)}, u32[]{:S(2)}) %collective-permute-start.23) | collective-permute-done | bytes 393248 | tf_op jit(solution)/shard_map/ppermute | solution.py:18
  99.1 0.6 fusion.3
  100.0 5.2 %collective-permute-start.31 = (bf16[128,1536]{1,0:T(8,128)(2,1)}, bf16[128,1536]{1,0:T(8,128)(2,1)S(1)}, u32[]{:S(2)}, u32[]{:S(2)}) collective-permute-start(bf16[128,1536]{1,0:T(8,128)(2,1)} %get-tuple-element.63), channel_id=1, source_target_pairs={{0,24},{8,0},{16,8},{24,16},{1,25},{9,1},{17,9},{25,17},{2,26},{10... | collective-permute-start | bytes 1179656 | tf_op jit(solution)/shard_map/ppermute | solution.py:18
  105.2 0.5 collective-permute-start.25
  105.6 5.0 %collective-permute-start.26 = (f32[2,32,128]{2,1,0:T(8,128)S(1)}, f32[2,32,128]{2,1,0:T(8,128)S(1)}, u32[]{:S(2)}, u32[]{:S(2)}) collective-permute-start(f32[2,32,128]{2,1,0:T(8,128)S(1)} %pad_maximum_fusion.5), channel_id=1, source_target_pairs={{0,4},{2,6},{4,0},{6,2},{1,5},{3,7},{5,1},{7,3},{8,12},{10,14},{12... | collective-permute-start | bytes 98312 | tf_op jit(solution)/shard_map/ppermute | solution.py:18
  110.6 3.3 %fusion.2 = f32[96,384]{1,0:T(8,128)S(1)} fusion(bf16[32,6144]{1,0:T(8,128)(2,1)S(1)} %get-tuple-element.74, bf16[32,6144]{1,0:T(8,128)(2,1)S(1)} %get-tuple-element.75, bf16[32,6144]{1,0:T(8,128)(2,1)S(1)} %get-tuple-element.73, bf16[1,6144,384]{2,1,0:T(8,128)(2,1)} %param.8), kind=kOutput, calls=%fused_computation.13 | convolution fusion | flops 456523776 | bytes 6045696 | tf_op jit(solution)/shard_map/dot_general | solution.py:41
  114.0 1.5 collective-permute-start.33
  115.7 0.3 fusion.4
  116.0 2.7 %collective-permute-start.28 = (f32[32,384]{1,0:T(8,128)S(1)}, f32[32,384]{1,0:T(8,128)S(1)}, u32[]{:S(2)}, u32[]{:S(2)}) collective-permute-start(f32[32,384]{1,0:T(8,128)S(1)} %fusion.15), channel_id=1, source_target_pairs={{0,32},{32,64},{64,96},{96,0},{1,33},{33,65},{65,97},{97,1},{2,34}... | collective-permute-start | bytes 147464 | tf_op jit(solution)/shard_map/ppermute | solution.py:18
  118.7 2.8 %collective-permute-start.29 = (f32[32,384]{1,0:T(8,128)S(1)}, f32[32,384]{1,0:T(8,128)S(1)}, u32[]{:S(2)}, u32[]{:S(2)}) collective-permute-start(f32[32,384]{1,0:T(8,128)S(1)} %fusion.15), channel_id=1, source_target_pairs={{0,64},{32,96},{64,0},{96,32},{1,65},{33,97},{65,1},{97,33},{2,66}... | collective-permute-start | bytes 147464 | tf_op jit(solution)/shard_map/ppermute | solution.py:18
  121.4 1.0 collective-permute-done.28
  122.5 1.6 collective-permute-start.30
  124.1 5.2 %inverse_of_factor.1.inverse_ref = f32[32,32]{1,0:T(8,128)} custom-call(f32[32,6144]{1,0:T(8,128)} %bitcast.131), custom_call_target="tpu_custom_call" | custom-call | tf_op jit(solution)/shard_map/inverse_of_factor/pallas_call | solution.py:97
  129.4 2.8 %collective-permute-start.34 = (f32[32,384]{1,0:T(8,128)S(1)}, f32[32,384]{1,0:T(8,128)S(1)}, u32[]{:S(2)}, u32[]{:S(2)}) collective-permute-start(f32[32,384]{1,0:T(8,128)S(1)} %add_add_fusion), channel_id=1, source_target_pairs={{0,8},{8,16},{16,24},{24,0},{1,9},{9,17},{17,25},{25,1},{2,10},{10... | collective-permute-start | bytes 147464 | tf_op jit(solution)/shard_map/ppermute | solution.py:18
  132.1 1.0 collective-permute-start.35
  133.1 1.8 %collective-permute-start.36 = (f32[32,384]{1,0:T(8,128)S(1)}, f32[32,384]{1,0:T(8,128)S(1)}, u32[]{:S(2)}, u32[]{:S(2)}) collective-permute-start(f32[32,384]{1,0:T(8,128)S(1)} %add_add_fusion), channel_id=1, source_target_pairs={{0,24},{8,0},{16,8},{24,16},{1,25},{9,1},{17,9},{25,17},{2,26},{10... | collective-permute-start | bytes 147464 | tf_op jit(solution)/shard_map/ppermute | solution.py:18
  134.9 3.2 %place.1 = bf16[128,6144]{1,0:T(8,128)(2,1)} custom-call(s32[12]{0:T(128)} %stack.69.at_ref, bf16[128,1536]{1,0:T(8,128)(2,1)} %get-tuple-element.69.refs_0_, bf16[128,1536]{1,0:T(8,128)(2,1)} %copy-done.7, bf16[128,1536]{1,0:T(8,128)(2,1)} %copy-done.8, bf16[128,1536]{1,0:T(8,128)(2,1)} %copy-done.9), custom_call_target="tpu_custom_call" | custom-call | bytes 3145728 | tf_op jit(solution)/shard_map/place/pallas_call | solution.py:189
  138.3 1.1 all-gather.4.cloned.1.call-done.act_ref
  139.4 13.3 %new_residual.1 = bf16[6144,384]{1,0:T(8,128)(2,1)} custom-call(bf16[1024,6144]{1,0:T(8,128)(2,1)} %all-gather.4.cloned.1.call-done.act_ref, bf16[1024,384]{1,0:T(8,128)(2,1)S(1)} %copy-done, bf16[6144,384]{1,0:T(8,128)(2,1)} %bitcast.134, f32[32,6144]{1,0:T(8,128)S(1)} %bitcast.132, f32[32,32]{1,0:T(8,128)S(1)} %copy-done.4, ...), custom_call_target="tpu_custom_call" | custom-call | flops 5737807872 | bytes 22806528 | tf_op jit(solution)/shard_map/new_residual/pallas_call | solution.py:121
  (111 shorter events, 2.7 us)
Async XLA Ops:
  7.2 65.0 %all-gather.6.cloned.1.call-start = ((), (), s32[]{:S(2)}) async-start(), calls=%async_computation.2 | async-start | bytes 5013504 | tf_op jit(solution)/shard_map/all_gather | solution.py:237
  9.0 130.4 %all-gather.4.cloned.1.call-start = ((), (), s32[]{:S(2)}) async-start(), calls=%async_computation.1 | async-start | bytes 14155776 | tf_op jit(solution)/shard_map/all_gather | solution.py:250
  9.0 13.4 %collective-permute-start.3 = (bf16[1024,384]{1,0:T(8,128)(2,1)}, bf16[1024,384]{1,0:T(8,128)(2,1)S(1)}, u32[]{:S(2)}, u32[]{:S(2)}) collective-permute-start(bf16[1024,384]{1,0:T(8,128)(2,1)} %cot_ref.1), channel_id=1, source_target_pairs={{0,1},{1,0},{2,3},{3,2},{4,5},{5,4},{6,7},{7,6},{8,9},{9,8},{10,11... | collective-permute-start | bytes 2359304 | tf_op jit(solution)/shard_map/ppermute | solution.py:18
  11.7 10.6 %collective-permute-start = (f32[32,256]{1,0:T(8,128)S(1)}, f32[32,256]{1,0:T(8,128)S(1)}, u32[]{:S(2)}, u32[]{:S(2)}) collective-permute-start(f32[32,256]{1,0:T(8,128)S(1)} %bitcast.145), channel_id=1, source_target_pairs={{0,2},{2,4},{4,6},{6,0},{1,3},{3,5},{5,7},{7,1},{8,10},{10,12},{12... | collective-permute-start | bytes 98312 | tf_op jit(solution)/shard_map/ppermute | solution.py:18
  13.4 9.0 %collective-permute-start.1 = (f32[32,256]{1,0:T(8,128)S(1)}, f32[32,256]{1,0:T(8,128)S(1)}, u32[]{:S(2)}, u32[]{:S(2)}) collective-permute-start(f32[32,256]{1,0:T(8,128)S(1)} %bitcast.146), channel_id=1, source_target_pairs={{0,4},{2,6},{4,0},{6,2},{1,5},{3,7},{5,1},{7,3},{8,12},{10,14},{12... | collective-permute-start | bytes 98312 | tf_op jit(solution)/shard_map/ppermute | solution.py:18
  16.1 6.2 %collective-permute-start.2 = (f32[32,256]{1,0:T(8,128)S(1)}, f32[32,256]{1,0:T(8,128)S(1)}, u32[]{:S(2)}, u32[]{:S(2)}) collective-permute-start(f32[32,256]{1,0:T(8,128)S(1)} %bitcast.147), channel_id=1, source_target_pairs={{0,6},{2,0},{4,2},{6,4},{1,7},{3,1},{5,3},{7,5},{8,14},{10,8},{12,... | collective-permute-start | bytes 98312 | tf_op jit(solution)/shard_map/ppermute | solution.py:18
  21.6 5.7 %copy-start.5 = (bf16[128,6144]{1,0:T(8,128)(2,1)S(1)}, bf16[128,6144]{1,0:T(8,128)(2,1)}, u32[]{:S(2)}) copy-start(bf16[128,6144]{1,0:T(8,128)(2,1)} %param.5) | copy-start | bytes 4718596
  22.4 0.9 copy-start.6
  26.0 1.3 collective-permute-start.4
  27.8 9.3 %copy-start.17 = (bf16[256,384]{1,0:T(8,128)(2,1)S(1)}, bf16[256,384]{1,0:T(8,128)(2,1)}, u32[]{:S(2)}) copy-start(bf16[256,384]{1,0:T(8,128)(2,1)} %get-tuple-element.45) | copy-start | bytes 589828
  27.8 12.0 %copy-start.16 = (bf16[256,384]{1,0:T(8,128)(2,1)S(1)}, bf16[256,384]{1,0:T(8,128)(2,1)}, u32[]{:S(2)}) copy-start(bf16[256,384]{1,0:T(8,128)(2,1)} %get-tuple-element.43) | copy-start | bytes 589828
  28.1 1.8 %collective-permute-start.5 = (f32[96,8,128]{2,1,0:T(8,128)S(1)}, f32[96,8,128]{2,1,0:T(8,128)S(1)}, u32[]{:S(2)}, u32[]{:S(2)}) collective-permute-start(f32[96,8,128]{2,1,0:T(8,128)S(1)} %dynamic-slice_bitcast_fusion), channel_id=1, source_target_pairs={{0,1},{1,0},{2,3},{3,2},{4,5},{5,4},{6,7},{7,6},{8,9},{9,8},{10,11... | collective-permute-start | bytes 1179656 | tf_op jit(solution)/shard_map/ppermute | solution.py:18
  29.9 9.9 %collective-permute-start.6 = (f32[24,8,128]{2,1,0:T(8,128)S(1)}, f32[24,8,128]{2,1,0:T(8,128)S(1)}, u32[]{:S(2)}, u32[]{:S(2)}) collective-permute-start(f32[24,8,128]{2,1,0:T(8,128)S(1)} %get-tuple-element.78), channel_id=1, source_target_pairs={{0,8},{8,16},{16,24},{24,0},{1,9},{9,17},{17,25},{25,1},{2,10},{10... | collective-permute-start | bytes 294920 | tf_op jit(solution)/shard_map/ppermute | solution.py:18
  31.9 8.5 %collective-permute-start.7 = (f32[24,8,128]{2,1,0:T(8,128)S(1)}, f32[24,8,128]{2,1,0:T(8,128)S(1)}, u32[]{:S(2)}, u32[]{:S(2)}) collective-permute-start(f32[24,8,128]{2,1,0:T(8,128)S(1)} %get-tuple-element.80), channel_id=1, source_target_pairs={{0,16},{8,24},{16,0},{24,8},{1,17},{9,25},{17,1},{25,9},{2,18},{10... | collective-permute-start | bytes 294920 | tf_op jit(solution)/shard_map/ppermute | solution.py:18
  35.5 4.9 %collective-permute-start.8 = (f32[24,8,128]{2,1,0:T(8,128)S(1)}, f32[24,8,128]{2,1,0:T(8,128)S(1)}, u32[]{:S(2)}, u32[]{:S(2)}) collective-permute-start(f32[24,8,128]{2,1,0:T(8,128)S(1)} %get-tuple-element.79), channel_id=1, source_target_pairs={{0,24},{8,0},{16,8},{24,16},{1,25},{9,1},{17,9},{25,17},{2,26},{10... | collective-permute-start | bytes 294920 | tf_op jit(solution)/shard_map/ppermute | solution.py:18
  36.5 9.6 %collective-permute-start.10 = (bf16[256,384]{1,0:T(8,128)(2,1)}, bf16[256,384]{1,0:T(8,128)(2,1)S(1)}, u32[]{:S(2)}, u32[]{:S(2)}) collective-permute-start(bf16[256,384]{1,0:T(8,128)(2,1)} %get-tuple-element.44), channel_id=1, source_target_pairs={{0,4},{2,6},{4,0},{6,2},{1,5},{3,7},{5,1},{7,3},{8,12},{10,14},{12... | collective-permute-start | bytes 589832 | tf_op jit(solution)/shard_map/ppermute | solution.py:18
  37.1 9.2 %collective-permute-start.11 = (bf16[256,384]{1,0:T(8,128)(2,1)S(1)}, bf16[256,384]{1,0:T(8,128)(2,1)S(1)}, u32[]{:S(2)}, u32[]{:S(2)}) collective-permute-start(bf16[256,384]{1,0:T(8,128)(2,1)S(1)} %copy-done.17), channel_id=1, source_target_pairs={{0,6},{2,0},{4,2},{6,4},{1,7},{3,1},{5,3},{7,5},{8,14},{10,8},{12,... | collective-permute-start | bytes 589832 | tf_op jit(solution)/shard_map/ppermute | solution.py:18
  39.8 8.8 %collective-permute-start.9 = (bf16[256,384]{1,0:T(8,128)(2,1)S(1)}, bf16[256,384]{1,0:T(8,128)(2,1)S(1)}, u32[]{:S(2)}, u32[]{:S(2)}) collective-permute-start(bf16[256,384]{1,0:T(8,128)(2,1)S(1)} %copy-done.16), channel_id=1, source_target_pairs={{0,2},{2,4},{4,6},{6,0},{1,3},{3,5},{5,7},{7,1},{8,10},{10,12},{12... | collective-permute-start | bytes 589832 | tf_op jit(solution)/shard_map/ppermute | solution.py:18
  46.1 2.5 %copy-start.10 = (bf16[256,384]{1,0:T(8,128)(2,1)}, bf16[256,384]{1,0:T(8,128)(2,1)S(1)}, u32[]{:S(2)}) copy-start(bf16[256,384]{1,0:T(8,128)(2,1)S(1)} %collective-permute-done.10.refs_3_) | copy-start | bytes 589828
  46.3 2.3 %copy-start.11 = (bf16[256,384]{1,0:T(8,128)(2,1)}, bf16[256,384]{1,0:T(8,128)(2,1)S(1)}, u32[]{:S(2)}) copy-start(bf16[256,384]{1,0:T(8,128)(2,1)S(1)} %collective-permute-done.11.refs_4_) | copy-start | bytes 589828
  48.6 0.7 copy-start.12
  52.1 20.0 %collective-permute-start.18 = (bf16[8,128,384]{2,1,0:T(8,128)(2,1)}, bf16[8,128,384]{2,1,0:T(8,128)(2,1)S(1)}, u32[]{:S(2)}, u32[]{:S(2)}) collective-permute-start(bf16[8,128,384]{2,1,0:T(8,128)(2,1)} %unpack.1.refs_0_), channel_id=1, source_target_pairs={{0,8},{8,16},{16,24},{24,0},{1,9},{9,17},{17,25},{25,1},{2,10},{10... | collective-permute-start | bytes 2359304 | tf_op jit(solution)/shard_map/ppermute | solution.py:18
  53.2 18.9 %collective-permute-start.19 = (bf16[8,128,384]{2,1,0:T(8,128)(2,1)}, bf16[8,128,384]{2,1,0:T(8,128)(2,1)S(1)}, u32[]{:S(2)}, u32[]{:S(2)}) collective-permute-start(bf16[8,128,384]{2,1,0:T(8,128)(2,1)} %unpack.1.refs_0_), channel_id=1, source_target_pairs={{0,24},{8,0},{16,8},{24,16},{1,25},{9,1},{17,9},{25,17},{2,26},{10... | collective-permute-start | bytes 2359304 | tf_op jit(solution)/shard_map/ppermute | solution.py:18
  55.4 5.8 %collective-permute-start.12 = (f32[6,8,128]{2,1,0:T(8,128)S(1)}, f32[6,8,128]{2,1,0:T(8,128)S(1)}, u32[]{:S(2)}, u32[]{:S(2)}) collective-permute-start(f32[6,8,128]{2,1,0:T(8,128)S(1)} %get-tuple-element.92), channel_id=1, source_target_pairs={{0,32},{32,64},{64,96},{96,0},{1,33},{33,65},{65,97},{97,1},{2,34}... | collective-permute-start | bytes 73736 | tf_op jit(solution)/shard_map/ppermute | solution.py:18
  57.0 6.1 %collective-permute-start.13 = (f32[6,8,128]{2,1,0:T(8,128)S(1)}, f32[6,8,128]{2,1,0:T(8,128)S(1)}, u32[]{:S(2)}, u32[]{:S(2)}) collective-permute-start(f32[6,8,128]{2,1,0:T(8,128)S(1)} %get-tuple-element.94), channel_id=1, source_target_pairs={{0,64},{32,96},{64,0},{96,32},{1,65},{33,97},{65,1},{97,33},{2,66}... | collective-permute-start | bytes 73736 | tf_op jit(solution)/shard_map/ppermute | solution.py:18
  60.0 4.3 %collective-permute-start.14 = (f32[6,8,128]{2,1,0:T(8,128)S(1)}, f32[6,8,128]{2,1,0:T(8,128)S(1)}, u32[]{:S(2)}, u32[]{:S(2)}) collective-permute-start(f32[6,8,128]{2,1,0:T(8,128)S(1)} %get-tuple-element.93), channel_id=1, source_target_pairs={{0,96},{32,0},{64,32},{96,64},{1,97},{33,1},{65,33},{97,65},{2,98}... | collective-permute-start | bytes 73736 | tf_op jit(solution)/shard_map/ppermute | solution.py:18
  64.3 5.1 %collective-permute-start.15 = (f32[6,8,128]{2,1,0:T(8,128)S(1)}, f32[6,8,128]{2,1,0:T(8,128)S(1)}, u32[]{:S(2)}, u32[]{:S(2)}) collective-permute-start(f32[6,8,128]{2,1,0:T(8,128)S(1)} %fusion.30), channel_id=1, source_target_pairs={{0,2},{2,4},{4,6},{6,0},{1,3},{3,5},{5,7},{7,1},{8,10},{10,12},{12... | collective-permute-start | bytes 73736 | tf_op jit(solution)/shard_map/ppermute | solution.py:18
  64.8 5.3 %collective-permute-start.16 = (f32[6,8,128]{2,1,0:T(8,128)S(1)}, f32[6,8,128]{2,1,0:T(8,128)S(1)}, u32[]{:S(2)}, u32[]{:S(2)}) collective-permute-start(f32[6,8,128]{2,1,0:T(8,128)S(1)} %fusion.30), channel_id=1, source_target_pairs={{0,4},{2,6},{4,0},{6,2},{1,5},{3,7},{5,1},{7,3},{8,12},{10,14},{12... | collective-permute-start | bytes 73736 | tf_op jit(solution)/shard_map/ppermute | solution.py:18
  66.8 3.8 %collective-permute-start.17 = (f32[6,8,128]{2,1,0:T(8,128)S(1)}, f32[6,8,128]{2,1,0:T(8,128)S(1)}, u32[]{:S(2)}, u32[]{:S(2)}) collective-permute-start(f32[6,8,128]{2,1,0:T(8,128)S(1)} %fusion.30), channel_id=1, source_target_pairs={{0,6},{2,0},{4,2},{6,4},{1,7},{3,1},{5,3},{7,5},{8,14},{10,8},{12,... | collective-permute-start | bytes 73736 | tf_op jit(solution)/shard_map/ppermute | solution.py:18
  72.1 14.7 %copy-start.13 = (bf16[8,128,384]{2,1,0:T(8,128)(2,1)}, bf16[8,128,384]{2,1,0:T(8,128)(2,1)S(1)}, u32[]{:S(2)}) copy-start(bf16[8,128,384]{2,1,0:T(8,128)(2,1)S(1)} %collective-permute-done.18.refs_1_) | copy-start | bytes 2359300
  72.1 0.9 copy-start.14
  73.1 13.8 %collective-permute-start.22 = (bf16[4,4,384,384]{3,2,1,0:T(8,128)(2,1)}, bf16[4,4,384,384]{3,2,1,0:T(8,128)(2,1)}, u32[]{:S(2)}, u32[]{:S(2)}) collective-permute-start(bf16[4,4,384,384]{3,2,1,0:T(8,128)(2,1)} %bitcast.149), channel_id=1, source_target_pairs={{0,1},{1,0},{2,3},{3,2},{4,5},{5,4},{6,7},{7,6},{8,9},{9,8},{10,11... | collective-permute-start | bytes 14155784 | tf_op jit(solution)/shard_map/ppermute | solution.py:18
  73.1 12.9 %collective-permute-start.20 = (bf16[8,64,384]{2,1,0:T(8,128)(2,1)S(1)}, bf16[8,64,384]{2,1,0:T(8,128)(2,1)}, u32[]{:S(2)}, u32[]{:S(2)}) collective-permute-start(bf16[8,64,384]{2,1,0:T(8,128)(2,1)S(1)} %slice.93), channel_id=1, source_target_pairs={{0,8},{8,16},{16,24},{24,0},{1,9},{9,17},{17,25},{25,1},{2,10},{10... | collective-permute-start | bytes 1179656 | tf_op jit(solution)/shard_map/ppermute | solution.py:18
  74.3 12.6 %collective-permute-start.21 = (bf16[8,64,384]{2,1,0:T(8,128)(2,1)S(1)}, bf16[8,64,384]{2,1,0:T(8,128)(2,1)}, u32[]{:S(2)}, u32[]{:S(2)}) collective-permute-start(bf16[8,64,384]{2,1,0:T(8,128)(2,1)S(1)} %slice.94), channel_id=1, source_target_pairs={{0,24},{8,0},{16,8},{24,16},{1,25},{9,1},{17,9},{25,17},{2,26},{10... | collective-permute-start | bytes 1179656 | tf_op jit(solution)/shard_map/ppermute | solution.py:18
  78.4 18.6 %all-to-all-start = ((f32[16,6,8,128]{3,2,1,0:T(8,128)}), f32[16,6,8,128]{3,2,1,0:T(8,128)S(1)}, u32[]{:S(2)}, u32[]{:S(2)}) async-start(f32[16,6,8,128]{3,2,1,0:T(8,128)} %broadcast_in_dim.28), calls=%async_computation | async-start | bytes 786432 | tf_op jit(solution)/shard_map/all_to_all | solution.py:66
  97.0 1.8 %collective-permute-start.23 = (f32[96,8,128]{2,1,0:T(8,128)S(1)}, f32[96,8,128]{2,1,0:T(8,128)S(1)}, u32[]{:S(2)}, u32[]{:S(2)}) collective-permute-start(f32[96,8,128]{2,1,0:T(8,128)S(1)} %bitcast.138), channel_id=1, source_target_pairs={{0,1},{1,0},{2,3},{3,2},{4,5},{5,4},{6,7},{7,6},{8,9},{9,8},{10,11... | collective-permute-start | bytes 1179656 | tf_op jit(solution)/shard_map/ppermute | solution.py:18
  98.9 0.9 copy-start.1
  99.8 5.4 %collective-permute-start.24 = (f32[32,128]{1,0:T(8,128)S(1)}, f32[32,128]{1,0:T(8,128)S(1)}, u32[]{:S(2)}, u32[]{:S(2)}) collective-permute-start(f32[32,128]{1,0:T(8,128)S(1)} %fusion.32), channel_id=1, source_target_pairs={{0,1},{1,0},{2,3},{3,2},{4,5},{5,4},{6,7},{7,6},{8,9},{9,8},{10,11... | collective-permute-start | bytes 49160 | tf_op jit(solution)/shard_map/ppermute | solution.py:18
  100.0 29.3 %collective-permute-start.31 = (bf16[128,1536]{1,0:T(8,128)(2,1)}, bf16[128,1536]{1,0:T(8,128)(2,1)S(1)}, u32[]{:S(2)}, u32[]{:S(2)}) collective-permute-start(bf16[128,1536]{1,0:T(8,128)(2,1)} %get-tuple-element.63), channel_id=1, source_target_pairs={{0,24},{8,0},{16,8},{24,16},{1,25},{9,1},{17,9},{25,17},{2,26},{10... | collective-permute-start | bytes 1179656 | tf_op jit(solution)/shard_map/ppermute | solution.py:18
  105.1 24.2 %collective-permute-start.32 = (bf16[128,1536]{1,0:T(8,128)(2,1)}, bf16[128,1536]{1,0:T(8,128)(2,1)S(1)}, u32[]{:S(2)}, u32[]{:S(2)}) collective-permute-start(bf16[128,1536]{1,0:T(8,128)(2,1)} %get-tuple-element.64), channel_id=1, source_target_pairs={{0,8},{8,16},{16,24},{24,0},{1,9},{9,17},{17,25},{25,1},{2,10},{10... | collective-permute-start | bytes 1179656 | tf_op jit(solution)/shard_map/ppermute | solution.py:18
  105.2 8.8 %copy-start.15 = (bf16[128,1536]{1,0:T(8,128)(2,1)S(1)}, bf16[128,1536]{1,0:T(8,128)(2,1)}, u32[]{:S(2)}) copy-start(bf16[128,1536]{1,0:T(8,128)(2,1)} %get-tuple-element.65) | copy-start | bytes 1179652
  105.2 10.5 %copy-start = (bf16[1024,384]{1,0:T(8,128)(2,1)S(1)}, bf16[1024,384]{1,0:T(8,128)(2,1)}, u32[]{:S(2)}) copy-start(bf16[1024,384]{1,0:T(8,128)(2,1)} %cot_ref.1) | copy-start | bytes 2359300
  105.2 8.8 %collective-permute-start.25 = (f32[2,32,128]{2,1,0:T(8,128)S(1)}, f32[2,32,128]{2,1,0:T(8,128)S(1)}, u32[]{:S(2)}, u32[]{:S(2)}) collective-permute-start(f32[2,32,128]{2,1,0:T(8,128)S(1)} %pad_maximum_fusion.5), channel_id=1, source_target_pairs={{0,2},{2,4},{4,6},{6,0},{1,3},{3,5},{5,7},{7,1},{8,10},{10,12},{12... | collective-permute-start | bytes 98312 | tf_op jit(solution)/shard_map/ppermute | solution.py:18
  105.6 9.8 %collective-permute-start.26 = (f32[2,32,128]{2,1,0:T(8,128)S(1)}, f32[2,32,128]{2,1,0:T(8,128)S(1)}, u32[]{:S(2)}, u32[]{:S(2)}) collective-permute-start(f32[2,32,128]{2,1,0:T(8,128)S(1)} %pad_maximum_fusion.5), channel_id=1, source_target_pairs={{0,4},{2,6},{4,0},{6,2},{1,5},{3,7},{5,1},{7,3},{8,12},{10,14},{12... | collective-permute-start | bytes 98312 | tf_op jit(solution)/shard_map/ppermute | solution.py:18
  110.6 4.9 %collective-permute-start.27 = (f32[2,32,128]{2,1,0:T(8,128)S(1)}, f32[2,32,128]{2,1,0:T(8,128)S(1)}, u32[]{:S(2)}, u32[]{:S(2)}) collective-permute-start(f32[2,32,128]{2,1,0:T(8,128)S(1)} %pad_maximum_fusion.5), channel_id=1, source_target_pairs={{0,6},{2,0},{4,2},{6,4},{1,7},{3,1},{5,3},{7,5},{8,14},{10,8},{12,... | collective-permute-start | bytes 98312 | tf_op jit(solution)/shard_map/ppermute | solution.py:18
  114.0 15.4 %collective-permute-start.33 = (bf16[128,1536]{1,0:T(8,128)(2,1)S(1)}, bf16[128,1536]{1,0:T(8,128)(2,1)S(1)}, u32[]{:S(2)}, u32[]{:S(2)}) collective-permute-start(bf16[128,1536]{1,0:T(8,128)(2,1)S(1)} %copy-done.15), channel_id=1, source_target_pairs={{0,16},{8,24},{16,0},{24,8},{1,17},{9,25},{17,1},{25,9},{2,18},{10... | collective-permute-start | bytes 1179656 | tf_op jit(solution)/shard_map/ppermute | solution.py:18
  116.0 23.4 %copy-start.2 = (f32[2,96,8,128]{3,2,1,0:T(8,128)S(1)}, f32[2,96,8,128]{3,2,1,0:T(8,128)}, u32[]{:S(2)}) copy-start(f32[2,96,8,128]{3,2,1,0:T(8,128)} %copy-done.1) | copy-start | bytes 2359300
  116.0 6.5 %collective-permute-start.28 = (f32[32,384]{1,0:T(8,128)S(1)}, f32[32,384]{1,0:T(8,128)S(1)}, u32[]{:S(2)}, u32[]{:S(2)}) collective-permute-start(f32[32,384]{1,0:T(8,128)S(1)} %fusion.15), channel_id=1, source_target_pairs={{0,32},{32,64},{64,96},{96,0},{1,33},{33,65},{65,97},{97,1},{2,34}... | collective-permute-start | bytes 147464 | tf_op jit(solution)/shard_map/ppermute | solution.py:18
  118.7 10.6 %collective-permute-start.29 = (f32[32,384]{1,0:T(8,128)S(1)}, f32[32,384]{1,0:T(8,128)S(1)}, u32[]{:S(2)}, u32[]{:S(2)}) collective-permute-start(f32[32,384]{1,0:T(8,128)S(1)} %fusion.15), channel_id=1, source_target_pairs={{0,64},{32,96},{64,0},{96,32},{1,65},{33,97},{65,1},{97,33},{2,66}... | collective-permute-start | bytes 147464 | tf_op jit(solution)/shard_map/ppermute | solution.py:18
  122.5 6.8 %collective-permute-start.30 = (f32[32,384]{1,0:T(8,128)S(1)}, f32[32,384]{1,0:T(8,128)S(1)}, u32[]{:S(2)}, u32[]{:S(2)}) collective-permute-start(f32[32,384]{1,0:T(8,128)S(1)} %fusion.15), channel_id=1, source_target_pairs={{0,96},{32,0},{64,32},{96,64},{1,97},{33,1},{65,33},{97,65},{2,98}... | collective-permute-start | bytes 147464 | tf_op jit(solution)/shard_map/ppermute | solution.py:18
  129.3 8.9 %copy-start.4 = (f32[32,32]{1,0:T(8,128)S(1)}, f32[32,32]{1,0:T(8,128)}, u32[]{:S(2)}) copy-start(f32[32,32]{1,0:T(8,128)} %inverse_of_factor.1.inverse_ref) | copy-start | bytes 12292
  129.3 5.6 %copy-start.7 = (bf16[128,1536]{1,0:T(8,128)(2,1)}, bf16[128,1536]{1,0:T(8,128)(2,1)S(1)}, u32[]{:S(2)}) copy-start(bf16[128,1536]{1,0:T(8,128)(2,1)S(1)} %collective-permute-done.31.refs_1_) | copy-start | bytes 1179652
  129.3 5.6 %copy-start.8 = (bf16[128,1536]{1,0:T(8,128)(2,1)}, bf16[128,1536]{1,0:T(8,128)(2,1)S(1)}, u32[]{:S(2)}) copy-start(bf16[128,1536]{1,0:T(8,128)(2,1)S(1)} %collective-permute-done.32.refs_2_) | copy-start | bytes 1179652
  129.3 5.5 %copy-start.9 = (bf16[128,1536]{1,0:T(8,128)(2,1)}, bf16[128,1536]{1,0:T(8,128)(2,1)S(1)}, u32[]{:S(2)}) copy-start(bf16[128,1536]{1,0:T(8,128)(2,1)S(1)} %collective-permute-done.33.refs_3_) | copy-start | bytes 1179652
  129.4 8.7 %collective-permute-start.34 = (f32[32,384]{1,0:T(8,128)S(1)}, f32[32,384]{1,0:T(8,128)S(1)}, u32[]{:S(2)}, u32[]{:S(2)}) collective-permute-start(f32[32,384]{1,0:T(8,128)S(1)} %add_add_fusion), channel_id=1, source_target_pairs={{0,8},{8,16},{16,24},{24,0},{1,9},{9,17},{17,25},{25,1},{2,10},{10... | collective-permute-start | bytes 147464 | tf_op jit(solution)/shard_map/ppermute | solution.py:18
  132.1 6.0 %collective-permute-start.35 = (f32[32,384]{1,0:T(8,128)S(1)}, f32[32,384]{1,0:T(8,128)S(1)}, u32[]{:S(2)}, u32[]{:S(2)}) collective-permute-start(f32[32,384]{1,0:T(8,128)S(1)} %add_add_fusion), channel_id=1, source_target_pairs={{0,16},{8,24},{16,0},{24,8},{1,17},{9,25},{17,1},{25,9},{2,18},{10... | collective-permute-start | bytes 147464 | tf_op jit(solution)/shard_map/ppermute | solution.py:18
  133.1 5.0 %collective-permute-start.36 = (f32[32,384]{1,0:T(8,128)S(1)}, f32[32,384]{1,0:T(8,128)S(1)}, u32[]{:S(2)}, u32[]{:S(2)}) collective-permute-start(f32[32,384]{1,0:T(8,128)S(1)} %add_add_fusion), channel_id=1, source_target_pairs={{0,24},{8,0},{16,8},{24,16},{1,25},{9,1},{17,9},{25,17},{2,26},{10... | collective-permute-start | bytes 147464 | tf_op jit(solution)/shard_map/ppermute | solution.py:18
  138.3 14.4 %copy-start.3 = (f32[32,384]{1,0:T(8,128)}, f32[32,384]{1,0:T(8,128)S(1)}, u32[]{:S(2)}) copy-start(f32[32,384]{1,0:T(8,128)S(1)} %convolution_multiply_fusion.factor_ref) | copy-start | bytes 147460
Sparse Core Ops, SparseCore 0:
  10.1 59.0 all-gather.5
  70.9 68.4 all-gather.3

commit v5 on v4

--- a/solution.py
+++ b/solution.py
@@ -101,36 +101,66 @@
     )(left)
 
 
-def residual_kernel(scale, act_ref, cot_ref, residual_ref, left_ref, inverse_ref, factor_ref, out_ref):
-    basis = lax.dot_general(
-        inverse_ref[...], left_ref[...], (((1,), (0,)), ((), ())), precision=lax.Precision.HIGHEST, preferred_element_type=F32
-    )
-    b_h, b_m, b_l = parts3(basis)
+def residual_kernel(scale, sizes, act_ref, cot_ref, residual_ref, left_ref, inverse_ref, factor_ref, out_ref, acts, olds, news, sems):
     f_h, f_m, f_l = parts3(factor_ref[...])
-    basis6 = jnp.concatenate([b_h, b_m, b_l, b_h, b_m, b_h], 0)
     factor6 = jnp.concatenate([f_h, f_h, f_h, f_m, f_m, f_l], 0)
-    total = mm(act_ref[...], cot_ref[...], 0, 0) * scale + residual_ref[...].astype(F32)
-    out_ref[...] = (total - mm(basis6, factor6, 0, 0)).astype(BF16)
-
-
-def residual_call(scale, act, cot, residual, left, inverse, factor, tile):
+    starts = [sum(sizes[:i]) for i in range(len(sizes))]
+
+    def loads(i):
+        slot, span = i % 2, pl.ds(starts[i], sizes[i])
+        return (
+            pltpu.make_async_copy(act_ref.at[:, span], acts.at[slot, :, pl.ds(0, sizes[i])], sems.at[0, slot]),
+            pltpu.make_async_copy(residual_ref.at[span], olds.at[slot, pl.ds(0, sizes[i])], sems.at[1, slot]),
+        )
+
+    def store(i):
+        slot = i % 2
+        return pltpu.make_async_copy(news.at[slot, pl.ds(0, sizes[i])], out_ref.at[pl.ds(starts[i], sizes[i])], sems.at[2, slot])
+
+    for i in (0, 1):
+        for copy in loads(i):
+            copy.start()
+    for i, size in enumerate(sizes):
+        slot = i % 2
+        basis = lax.dot_general(
+            inverse_ref[...],
+            left_ref[:, starts[i] : starts[i] + size],
+            (((1,), (0,)), ((), ())),
+            precision=lax.Precision.HIGHEST,
+            preferred_element_type=F32,
+        )
+        b_h, b_m, b_l = parts3(basis)
+        basis6 = jnp.concatenate([b_h, b_m, b_l, b_h, b_m, b_h], 0)
+        for copy in loads(i):
+            copy.wait()
+        if i >= 2:
+            store(i - 2).wait()
+        total = mm(acts[slot, :, :size], cot_ref[...], 0, 0) * scale + olds[slot, :size].astype(F32)
+        news[slot, :size] = (total - mm(basis6, factor6, 0, 0)).astype(BF16)
+        store(i).start()
+        if i + 2 < len(sizes):
+            for copy in loads(i + 2):
+                copy.start()
+    for i in range(len(sizes))[-2:]:
+        store(i).wait()
+
+
+def residual_call(scale, act, cot, residual, left, inverse, factor, sizes):
     k, d = act.shape
     cols, rank = cot.shape[1], left.shape[0]
-    whole = lambda a: pl.BlockSpec(a.shape, lambda i: (0, 0))
-    rows = pl.BlockSpec((tile, cols), lambda i: (i, 0))
+    held, most = pl.BlockSpec(memory_space=pl.ANY), max(sizes)
+    whole = pl.BlockSpec(memory_space=pltpu.VMEM)
     return pl.pallas_call(
-        functools.partial(residual_kernel, scale),
+        functools.partial(residual_kernel, scale, tuple(sizes)),
         out_shape=jax.ShapeDtypeStruct((d, cols), BF16),
-        grid=(d // tile,),
-        in_specs=[
-            pl.BlockSpec((k, tile), lambda i: (0, i)),
-            whole(cot),
-            rows,
-            pl.BlockSpec((rank, tile), lambda i: (0, i)),
-            whole(inverse),
-            whole(factor),
+        in_specs=[held, whole, held, whole, whole, whole],
+        out_specs=held,
+        scratch_shapes=[
+            pltpu.VMEM((2, k, most), BF16),
+            pltpu.VMEM((2, most, cols), BF16),
+            pltpu.VMEM((2, most, cols), BF16),
+            pltpu.SemaphoreType.DMA((3, 2)),
         ],
-        out_specs=rows,
         compiler_params=pltpu.CompilerParams(vmem_limit_bytes=52 * 1024 * 1024),
         cost_estimate=pl.CostEstimate(
             flops=2 * d * cols * (k + 6 * rank), bytes_accessed=2 * d * k + 4 * d * cols + 4 * d * rank, transcendentals=0
@@ -183,7 +213,7 @@
         copy.wait()
 
 
-def copy_call(plan, n_copies, ins, outs, at, name):
+def copy_call(plan, n_copies, ins, outs, at, name, vmem=16 * 1024 * 1024):
     any_spec = pl.BlockSpec(memory_space=pltpu.HBM)
     moved = sum(2 * math.prod(o.shape) * o.dtype.itemsize for o in outs)
     return pl.pallas_call(
@@ -196,7 +226,7 @@
             out_specs=[pl.BlockSpec(o.shape, lambda i, a, n=len(o.shape): (0,) * n) for o in outs],
             scratch_shapes=[pltpu.SemaphoreType.DMA((n_copies,))],
         ),
-        compiler_params=pltpu.CompilerParams(vmem_limit_bytes=VMEM_LIMIT),
+        compiler_params=pltpu.CompilerParams(vmem_limit_bytes=vmem),
         cost_estimate=pl.CostEstimate(flops=0, bytes_accessed=moved, transcendentals=0),
         name=name,
     )(at, *ins)
@@ -239,7 +269,7 @@
     cot_other = shift(cotangent, "core", 1)
     at = [((ix + s) % 4) * 2 + ic for s in range(4)] + [(ix - s) % 4 for s in range(4)]
     at = jnp.stack(at + [(iz + s) % 4 for s in (0, 1, -1, 2)]).astype(jnp.int32)
-    packed = copy_call(functools.partial(pack_plan, tok), 6, [cotangent, cot_other], [like(2 * tok, cols)] * 3, at, "pack")
+    packed = copy_call(functools.partial(pack_plan, tok), 6, [cotangent, cot_other], [like(2 * tok, cols)] * 3, at, "pack", VMEM_LIMIT)
 
     warm3 = jnp.concatenate(split3(warm_factor.T), 0)
     cw = fold3(mm(warm3, cotangent, 1, 1)) * scale
@@ -292,7 +322,8 @@
     (input_grads,) = copy_call(functools.partial(place_plan, quarter), 4, back, [like(tok, d)], at, "place")
     sums = all_sum(sums, "z")
     factor = jnp.dot(inverse, sums, precision=lax.Precision.HIGHEST) * (1.0 / 16)
-    new_residual = residual_call(scale, gathered, cotangent, residual, left, inverse, factor, 1536 if d % 1536 == 0 else 1024)
+    sizes = [d // 12 * w for w in (1, 2, 3, 3, 2, 1)] if d % 1536 == 0 else [d // 2] * 2
+    new_residual = residual_call(scale, gathered, cotangent, residual, left, inverse, factor, sizes)
     return factor.T, new_residual[None], input_grads
 
 

time: 161 us -> 161 us (level)
  waiting for transfers between devices: 24.4 us -> 28.3 us
  Pallas kernels: 37.2 us -> 34.2 us
    pallas_call x3, Pallas kernels: 8.66 us -> 6.15 us  [copy_call(): pl.pallas_call(functools.partial(copy_kernel, len(ins), len(outs), plan),...]
    all_gather x1, waiting for transfers between devices: 1.05 us -> 3.53 us  [per_device(): gathered = lax.all_gather(act, ('x', 'core'), axis=0, tiled=True)]
  transfers between devices with their start and end apart: 40 -> 40, of which waited for: 17 -> 18; matrix products, arithmetic and copies ran while one was open for 9% -> 9% of each run, Pallas kernels for 15% -> 14%
where the time goes in v5:
time: 161 us; the launch traced here: 159 us
  starting transfers between devices  63.1 us (39%)
  Pallas kernels  34.2 us (21%)
  waiting for transfers between devices  28.3 us (18%)
  between operations  14.8 us (9%)
  matrix products  10.2 us (6%)
  local copies, waits for them, and re-layouts  6.53 us (4%)
  other arithmetic  1.66 us (1%)
    ppermute x37, starting transfers between devices, shift(): return lax.ppermute(value, axis, [(i, (i + step) % n) for i in range(n)])  57.3 us
    ppermute x37, waiting for transfers between devices, shift(): return lax.ppermute(value, axis, [(i, (i + step) % n) for i in range(n)])  24.7 us
    pallas_call x1, Pallas kernels, residual_call(): pl.pallas_call(functools.partial(residual_kernel, scale, tuple(sizes)), o...  12.7 us
    pallas_call x1, Pallas kernels, input_call(): pl.pallas_call(functools.partial(input_kernel, len(cots)), out_shape=[jax...  10.1 us
    dot_general x6, matrix products, mm(): lax.dot_general(a, b, (((ca,), (cb,)), ((), ())), preferred_element_type=...  10 us
    pallas_call x3, Pallas kernels, copy_call(): pl.pallas_call(functools.partial(copy_kernel, len(ins), len(outs), plan),...  6.15 us
    all_to_all x1, starting transfers between devices, all_blocks(): lax.all_to_all(jnp.broadcast_to(value[None], (n,) + value.shape), axis, 0...  5.71 us
    pallas_call x1, Pallas kernels, inverse_of_factor(): pl.pallas_call(inverse_kernel, out_shape=jax.ShapeDtypeStruct((rank, rank...  5.22 us
  transfers between devices with their start and end apart: 40, of which 18 were waited for; matrix products, arithmetic and copies ran while one was open for 9% of the time, Pallas kernels for 14%

profile of v5, /device:TPU:0, one launch (start us, length us, event | category | flops | bytes accessed | tf_op | source)
XLA Modules:
  0.0 158.9 jit_solution(10886873234213090750)
XLA Ops:
  7.2 1.7 %constant_dynamic-slice_fusion = bf16[384,384]{1,0:T(8,128)(2,1)} fusion(bf16[6144,384]{1,0:T(8,128)(2,1)} %param.7, s32[]{:T(128)S(6)} %select_n.320), kind=kLoop, calls=%fused_computation.106 | loop fusion | bytes 589828 | tf_op jit(solution)/shard_map/dynamic_slice | solution.py:266
  9.2 0.8 reduce-precision_convert_fusion.5
  10.0 1.5 fusion.22
  11.7 1.6 %collective-permute-start = (f32[32,256]{1,0:T(8,128)S(1)}, f32[32,256]{1,0:T(8,128)S(1)}, u32[]{:S(2)}, u32[]{:S(2)}) collective-permute-start(f32[32,256]{1,0:T(8,128)S(1)} %bitcast.145), channel_id=1, source_target_pairs={{0,2},{2,4},{4,6},{6,0},{1,3},{3,5},{5,7},{7,1},{8,10},{10,12},{12... | collective-permute-start | bytes 98312 | tf_op jit(solution)/shard_map/ppermute | solution.py:18
  13.4 2.7 %collective-permute-start.1 = (f32[32,256]{1,0:T(8,128)S(1)}, f32[32,256]{1,0:T(8,128)S(1)}, u32[]{:S(2)}, u32[]{:S(2)}) collective-permute-start(f32[32,256]{1,0:T(8,128)S(1)} %bitcast.146), channel_id=1, source_target_pairs={{0,4},{2,6},{4,0},{6,2},{1,5},{3,7},{5,1},{7,3},{8,12},{10,14},{12... | collective-permute-start | bytes 98312 | tf_op jit(solution)/shard_map/ppermute | solution.py:18
  16.1 1.4 collective-permute-start.2
  17.6 3.9 %fusion.21 = f32[96,6144]{1,0:T(8,128)S(1)} fusion(bf16[32,384]{1,0:T(8,128)(2,1)S(1)} %get-tuple-element.96, bf16[32,384]{1,0:T(8,128)(2,1)S(1)} %get-tuple-element.97, bf16[32,384]{1,0:T(8,128)(2,1)S(1)} %get-tuple-element.95, bf16[1,6144,384]{2,1,0:T(8,128)(2,1)} %param.8), kind=kOutput, calls=%fused_computation.65 | convolution fusion | flops 453206016 | bytes 7151616 | tf_op jit(solution)/shard_map/dot_general | solution.py:41
  21.7 0.7 stack.69.at_ref
  22.4 0.9 copy-done.3
  23.3 2.6 %pack.1 = (bf16[256,384]{1,0:T(8,128)(2,1)}, bf16[256,384]{1,0:T(8,128)(2,1)}, bf16[256,384]{1,0:T(8,128)(2,1)}) custom-call(s32[12]{0:T(128)} %stack.69.at_ref, bf16[1024,384]{1,0:T(8,128)(2,1)} %cot_ref.1, bf16[1024,384]{1,0:T(8,128)(2,1)} %copy-done.3), custom_call_target="tpu_custom_call" | custom-call | bytes 1179648 | tf_op jit(solution)/shard_map/pack/pallas_call | solution.py:219
  26.2 1.2 collective-permute-done.4
  27.4 0.5 fusion.23
  28.4 1.6 collective-permute-done.5
  30.0 2.0 %collective-permute-start.6 = (f32[24,8,128]{2,1,0:T(8,128)S(1)}, f32[24,8,128]{2,1,0:T(8,128)S(1)}, u32[]{:S(2)}, u32[]{:S(2)}) collective-permute-start(f32[24,8,128]{2,1,0:T(8,128)S(1)} %get-tuple-element.78), channel_id=1, source_target_pairs={{0,8},{8,16},{16,24},{24,0},{1,9},{9,17},{17,25},{25,1},{2,10},{10... | collective-permute-start | bytes 294920 | tf_op jit(solution)/shard_map/ppermute | solution.py:18
  32.0 3.6 %collective-permute-start.7 = (f32[24,8,128]{2,1,0:T(8,128)S(1)}, f32[24,8,128]{2,1,0:T(8,128)S(1)}, u32[]{:S(2)}, u32[]{:S(2)}) collective-permute-start(f32[24,8,128]{2,1,0:T(8,128)S(1)} %get-tuple-element.80), channel_id=1, source_target_pairs={{0,16},{8,24},{16,0},{24,8},{1,17},{9,25},{17,1},{25,9},{2,18},{10... | collective-permute-start | bytes 294920 | tf_op jit(solution)/shard_map/ppermute | solution.py:18
  35.6 1.0 collective-permute-start.8
  36.6 0.5 collective-permute-start.10
  37.1 2.7 %collective-permute-start.11 = (bf16[256,384]{1,0:T(8,128)(2,1)}, bf16[256,384]{1,0:T(8,128)(2,1)S(1)}, u32[]{:S(2)}, u32[]{:S(2)}) collective-permute-start(bf16[256,384]{1,0:T(8,128)(2,1)} %get-tuple-element.45), channel_id=1, source_target_pairs={{0,6},{2,0},{4,2},{6,4},{1,7},{3,1},{5,3},{7,5},{8,14},{10,8},{12,... | collective-permute-start | bytes 589832 | tf_op jit(solution)/shard_map/ppermute | solution.py:18
  39.9 0.7 collective-permute-done.7
  40.5 5.6 %collective-permute-done.10.refs_3_ = bf16[256,384]{1,0:T(8,128)(2,1)S(1)} collective-permute-done((bf16[256,384]{1,0:T(8,128)(2,1)}, bf16[256,384]{1,0:T(8,128)(2,1)S(1)}, u32[]{:S(2)}, u32[]{:S(2)}) %collective-permute-start.10) | collective-permute-done | bytes 196640 | tf_op jit(solution)/shard_map/ppermute | solution.py:18
  46.3 2.4 %collective-permute-done.9.refs_2_ = bf16[256,384]{1,0:T(8,128)(2,1)S(1)} collective-permute-done((bf16[256,384]{1,0:T(8,128)(2,1)S(1)}, bf16[256,384]{1,0:T(8,128)(2,1)S(1)}, u32[]{:S(2)}, u32[]{:S(2)}) %collective-permute-start.9) | collective-permute-done | bytes 196640 | tf_op jit(solution)/shard_map/ppermute | solution.py:18
  48.7 1.6 %unpack.1.refs_0_ = bf16[8,128,384]{2,1,0:T(8,128)(2,1)S(1)} custom-call(s32[12]{0:T(128)S(1)} %copy-done.9, bf16[1024,384]{1,0:T(8,128)(2,1)S(1)} %copy-done, bf16[1024,384]{1,0:T(8,128)(2,1)S(1)} %copy-done.4, bf16[256,384]{1,0:T(8,128)(2,1)S(1)} %collective-permute-done.9.refs_2_, bf16[256,384]{1,0:T(8,128)(2,1)S(1)} %collective-permute-done.10.refs_3_, ...), custom_call_target="tpu_custom_call" | custom-call | bytes 1572864 | tf_op jit(solution)/shard_map/unpack/pallas_call | solution.py:219
  50.3 1.1 collective-permute-start.18
  51.4 2.2 %collective-permute-start.19 = (bf16[8,128,384]{2,1,0:T(8,128)(2,1)S(1)}, bf16[8,128,384]{2,1,0:T(8,128)(2,1)S(1)}, u32[]{:S(2)}, u32[]{:S(2)}) collective-permute-start(bf16[8,128,384]{2,1,0:T(8,128)(2,1)S(1)} %unpack.1.refs_0_), channel_id=1, source_target_pairs={{0,24},{8,0},{16,8},{24,16},{1,25},{9,1},{17,9},{25,17},{2,26},{10... | collective-permute-start | bytes 2359304 | tf_op jit(solution)/shard_map/ppermute | solution.py:18
  53.6 1.7 %collective-permute-start.12 = (f32[6,8,128]{2,1,0:T(8,128)S(1)}, f32[6,8,128]{2,1,0:T(8,128)S(1)}, u32[]{:S(2)}, u32[]{:S(2)}) collective-permute-start(f32[6,8,128]{2,1,0:T(8,128)S(1)} %get-tuple-element.92), channel_id=1, source_target_pairs={{0,32},{32,64},{64,96},{96,0},{1,33},{33,65},{65,97},{97,1},{2,34}... | collective-permute-start | bytes 73736 | tf_op jit(solution)/shard_map/ppermute | solution.py:18
  55.3 3.4 %collective-permute-start.13 = (f32[6,8,128]{2,1,0:T(8,128)S(1)}, f32[6,8,128]{2,1,0:T(8,128)S(1)}, u32[]{:S(2)}, u32[]{:S(2)}) collective-permute-start(f32[6,8,128]{2,1,0:T(8,128)S(1)} %get-tuple-element.94), channel_id=1, source_target_pairs={{0,64},{32,96},{64,0},{96,32},{1,65},{33,97},{65,1},{97,33},{2,66}... | collective-permute-start | bytes 73736 | tf_op jit(solution)/shard_map/ppermute | solution.py:18
  58.7 1.2 collective-permute-start.14
  59.8 1.9 %collective-permute-done.13 = f32[6,8,128]{2,1,0:T(8,128)S(1)} collective-permute-done((f32[6,8,128]{2,1,0:T(8,128)S(1)}, f32[6,8,128]{2,1,0:T(8,128)S(1)}, u32[]{:S(2)}, u32[]{:S(2)}) %collective-permute-start.13) | collective-permute-done | bytes 24608 | tf_op jit(solution)/shard_map/ppermute | solution.py:18
  61.8 1.2 collective-permute-done.14
  63.1 1.4 collective-permute-start.16
  64.5 1.9 %collective-permute-start.17 = (f32[6,8,128]{2,1,0:T(8,128)S(1)}, f32[6,8,128]{2,1,0:T(8,128)S(1)}, u32[]{:S(2)}, u32[]{:S(2)}) collective-permute-start(f32[6,8,128]{2,1,0:T(8,128)S(1)} %fusion.30), channel_id=1, source_target_pairs={{0,6},{2,0},{4,2},{6,4},{1,7},{3,1},{5,3},{7,5},{8,14},{10,8},{12,... | collective-permute-start | bytes 73736 | tf_op jit(solution)/shard_map/ppermute | solution.py:18
  66.5 1.8 %collective-permute-done.15 = f32[6,8,128]{2,1,0:T(8,128)S(1)} collective-permute-done((f32[6,8,128]{2,1,0:T(8,128)S(1)}, f32[6,8,128]{2,1,0:T(8,128)S(1)}, u32[]{:S(2)}, u32[]{:S(2)}) %collective-permute-start.15) | collective-permute-done | bytes 24608 | tf_op jit(solution)/shard_map/ppermute | solution.py:18
  68.3 0.5 collective-permute-done.16
  68.8 0.5 collective-permute-done.17
  69.3 0.9 collective-permute-done.18.refs_1_
  70.2 0.9 copy-done.14
  71.2 1.0 slice.94
  72.3 3.3 %collective-permute-start.21 = (bf16[8,64,384]{2,1,0:T(8,128)(2,1)S(1)}, bf16[8,64,384]{2,1,0:T(8,128)(2,1)}, u32[]{:S(2)}, u32[]{:S(2)}) collective-permute-start(bf16[8,64,384]{2,1,0:T(8,128)(2,1)S(1)} %slice.94), channel_id=1, source_target_pairs={{0,24},{8,0},{16,8},{24,16},{1,25},{9,1},{17,9},{25,17},{2,26},{10... | collective-permute-start | bytes 1179656 | tf_op jit(solution)/shard_map/ppermute | solution.py:18
  75.6 0.8 broadcast_in_dim.28
  76.4 5.7 %all-to-all-start = ((f32[16,6,8,128]{3,2,1,0:T(8,128)}), f32[16,6,8,128]{3,2,1,0:T(8,128)S(1)}, u32[]{:S(2)}, u32[]{:S(2)}) async-start(f32[16,6,8,128]{3,2,1,0:T(8,128)} %broadcast_in_dim.28), calls=%async_computation | async-start | bytes 786432 | tf_op jit(solution)/shard_map/all_to_all | solution.py:66
  82.1 2.0 %collective-permute-done.20.refs_3_ = bf16[8,64,384]{2,1,0:T(8,128)(2,1)} collective-permute-done((bf16[8,64,384]{2,1,0:T(8,128)(2,1)S(1)}, bf16[8,64,384]{2,1,0:T(8,128)(2,1)}, u32[]{:S(2)}, u32[]{:S(2)}) %collective-permute-start.20) | collective-permute-done | bytes 393248 | tf_op jit(solution)/shard_map/ppermute | solution.py:18
  84.1 0.8 collective-permute-done.21.refs_4_
  84.9 10.1 %input_grads.1 = (bf16[128,1536]{1,0:T(8,128)(2,1)}, bf16[128,1536]{1,0:T(8,128)(2,1)}, bf16[128,1536]{1,0:T(8,128)(2,1)}, bf16[128,1536]{1,0:T(8,128)(2,1)}) custom-call(s32[12]{0:T(128)} %stack.69.at_ref, bf16[8,128,384]{2,1,0:T(8,128)(2,1)} %copy-done.5, bf16[8,128,384]{2,1,0:T(8,128)(2,1)} %copy-done.13, bf16[8,128,384]{2,1,0:T(8,128)(2,1)} %copy-done.14, ...), custom_call_target="tpu_custom_call" | custom-call | flops 4831838208 | bytes 12582912 | tf_op jit(solution)/shard_map/input_grads/pallas_call | solution.py:189
  95.1 1.7 %collective-permute-done.23 = f32[96,8,128]{2,1,0:T(8,128)S(1)} collective-permute-done((f32[96,8,128]{2,1,0:T(8,128)S(1)}, f32[96,8,128]{2,1,0:T(8,128)S(1)}, u32[]{:S(2)}, u32[]{:S(2)}) %collective-permute-start.23) | collective-permute-done | bytes 393248 | tf_op jit(solution)/shard_map/ppermute | solution.py:18
  97.1 0.7 fusion.3
  98.1 6.1 %collective-permute-start.31 = (bf16[128,1536]{1,0:T(8,128)(2,1)}, bf16[128,1536]{1,0:T(8,128)(2,1)S(1)}, u32[]{:S(2)}, u32[]{:S(2)}) collective-permute-start(bf16[128,1536]{1,0:T(8,128)(2,1)} %get-tuple-element.63), channel_id=1, source_target_pairs={{0,24},{8,0},{16,8},{24,16},{1,25},{9,1},{17,9},{25,17},{2,26},{10... | collective-permute-start | bytes 1179656 | tf_op jit(solution)/shard_map/ppermute | solution.py:18
  104.2 2.3 %collective-permute-start.25 = (f32[2,32,128]{2,1,0:T(8,128)S(1)}, f32[2,32,128]{2,1,0:T(8,128)S(1)}, u32[]{:S(2)}, u32[]{:S(2)}) collective-permute-start(f32[2,32,128]{2,1,0:T(8,128)S(1)} %pad_maximum_fusion.5), channel_id=1, source_target_pairs={{0,2},{2,4},{4,6},{6,0},{1,3},{3,5},{5,7},{7,1},{8,10},{10,12},{12... | collective-permute-start | bytes 98312 | tf_op jit(solution)/shard_map/ppermute | solution.py:18
  106.4 2.3 %collective-permute-start.26 = (f32[2,32,128]{2,1,0:T(8,128)S(1)}, f32[2,32,128]{2,1,0:T(8,128)S(1)}, u32[]{:S(2)}, u32[]{:S(2)}) collective-permute-start(f32[2,32,128]{2,1,0:T(8,128)S(1)} %pad_maximum_fusion.5), channel_id=1, source_target_pairs={{0,4},{2,6},{4,0},{6,2},{1,5},{3,7},{5,1},{7,3},{8,12},{10,14},{12... | collective-permute-start | bytes 98312 | tf_op jit(solution)/shard_map/ppermute | solution.py:18
  108.7 0.5 collective-permute-start.27
  109.2 3.2 %fusion.2 = f32[96,384]{1,0:T(8,128)S(1)} fusion(bf16[32,6144]{1,0:T(8,128)(2,1)S(1)} %get-tuple-element.74, bf16[32,6144]{1,0:T(8,128)(2,1)S(1)} %get-tuple-element.75, bf16[32,6144]{1,0:T(8,128)(2,1)S(1)} %get-tuple-element.73, bf16[1,6144,384]{2,1,0:T(8,128)(2,1)} %param.8), kind=kOutput, calls=%fused_computation.13 | convolution fusion | flops 456523776 | bytes 6045696 | tf_op jit(solution)/shard_map/dot_general | solution.py:41
  112.5 1.7 %collective-permute-start.33 = (bf16[128,1536]{1,0:T(8,128)(2,1)}, bf16[128,1536]{1,0:T(8,128)(2,1)S(1)}, u32[]{:S(2)}, u32[]{:S(2)}) collective-permute-start(bf16[128,1536]{1,0:T(8,128)(2,1)} %get-tuple-element.65), channel_id=1, source_target_pairs={{0,16},{8,24},{16,0},{24,8},{1,17},{9,25},{17,1},{25,9},{2,18},{10... | collective-permute-start | bytes 1179656 | tf_op jit(solution)/shard_map/ppermute | solution.py:18
  114.4 0.3 fusion.4
  114.7 2.1 %collective-permute-start.28 = (f32[32,384]{1,0:T(8,128)S(1)}, f32[32,384]{1,0:T(8,128)S(1)}, u32[]{:S(2)}, u32[]{:S(2)}) collective-permute-start(f32[32,384]{1,0:T(8,128)S(1)} %fusion.15), channel_id=1, source_target_pairs={{0,32},{32,64},{64,96},{96,0},{1,33},{33,65},{65,97},{97,1},{2,34}... | collective-permute-start | bytes 147464 | tf_op jit(solution)/shard_map/ppermute | solution.py:18
  116.8 2.9 %collective-permute-start.29 = (f32[32,384]{1,0:T(8,128)S(1)}, f32[32,384]{1,0:T(8,128)S(1)}, u32[]{:S(2)}, u32[]{:S(2)}) collective-permute-start(f32[32,384]{1,0:T(8,128)S(1)} %fusion.15), channel_id=1, source_target_pairs={{0,64},{32,96},{64,0},{96,32},{1,65},{33,97},{65,1},{97,33},{2,66}... | collective-permute-start | bytes 147464 | tf_op jit(solution)/shard_map/ppermute | solution.py:18
  119.7 0.9 collective-permute-done.28
  120.5 1.8 %collective-permute-start.30 = (f32[32,384]{1,0:T(8,128)S(1)}, f32[32,384]{1,0:T(8,128)S(1)}, u32[]{:S(2)}, u32[]{:S(2)}) collective-permute-start(f32[32,384]{1,0:T(8,128)S(1)} %fusion.15), channel_id=1, source_target_pairs={{0,96},{32,0},{64,32},{96,64},{1,97},{33,1},{65,33},{97,65},{2,98}... | collective-permute-start | bytes 147464 | tf_op jit(solution)/shard_map/ppermute | solution.py:18
  122.3 5.2 %inverse_of_factor.1.inverse_ref = f32[32,32]{1,0:T(8,128)} custom-call(f32[32,6144]{1,0:T(8,128)} %bitcast.131), custom_call_target="tpu_custom_call" | custom-call | tf_op jit(solution)/shard_map/inverse_of_factor/pallas_call | solution.py:97
  127.6 2.4 %collective-permute-start.34 = (f32[32,384]{1,0:T(8,128)S(1)}, f32[32,384]{1,0:T(8,128)S(1)}, u32[]{:S(2)}, u32[]{:S(2)}) collective-permute-start(f32[32,384]{1,0:T(8,128)S(1)} %add_add_fusion), channel_id=1, source_target_pairs={{0,8},{8,16},{16,24},{24,0},{1,9},{9,17},{17,25},{25,1},{2,10},{10... | collective-permute-start | bytes 147464 | tf_op jit(solution)/shard_map/ppermute | solution.py:18
  129.9 1.4 collective-permute-start.35
  131.4 1.4 collective-permute-start.36
  132.7 1.9 %place.1 = bf16[128,6144]{1,0:T(8,128)(2,1)} custom-call(s32[12]{0:T(128)S(1)} %copy-done.10, bf16[128,1536]{1,0:T(8,128)(2,1)S(1)} %copy-done.6, bf16[128,1536]{1,0:T(8,128)(2,1)S(1)} %collective-permute-done.31.refs_1_, bf16[128,1536]{1,0:T(8,128)(2,1)S(1)} %collective-permute-done.32.refs_2_, bf16[128,1536]{1,0:T(8,128)(2,1)S(1)} %collective-permute-done.33.refs_3_), custom_call_target="tpu_custom_call" | custom-call | bytes 3145728 | tf_op jit(solution)/shard_map/place/pallas_call | solution.py:219
  134.6 0.9 collective-permute-done.35
  135.7 3.5 %all-gather.4.cloned.1.call-done.act_ref = bf16[1024,6144]{1,0:T(8,128)(2,1)} async-done(((bf16[128,6144]{1,0:T(8,128)(2,1)}), bf16[1024,6144]{1,0:T(8,128)(2,1)}) %all-gather.4.cloned.1.call-update) | async-done | bytes 12582928 | tf_op jit(solution)/shard_map/all_gather | solution.py:280
  139.3 12.7 %new_residual.1 = bf16[6144,384]{1,0:T(8,128)(2,1)} custom-call(bf16[1024,6144]{1,0:T(8,128)(2,1)} %all-gather.4.cloned.1.call-done.act_ref, bf16[1024,384]{1,0:T(8,128)(2,1)S(1)} %copy-done, bf16[6144,384]{1,0:T(8,128)(2,1)} %bitcast.134, f32[32,6144]{1,0:T(8,128)S(1)} %bitcast.132, f32[32,32]{1,0:T(8,128)S(1)} %copy-done.8, ...), custom_call_target="tpu_custom_call" | custom-call | flops 5737807872 | bytes 22806528 | tf_op jit(solution)/shard_map/new_residual/pallas_call | solution.py:153
  (107 shorter events, 2.7 us)
Async XLA Ops:
  7.2 63.0 %all-gather.6.cloned.1.call-start = ((), (), s32[]{:S(2)}) async-start(), calls=%async_computation.2 | async-start | bytes 5013504 | tf_op jit(solution)/shard_map/all_gather | solution.py:267
  9.0 130.3 %all-gather.4.cloned.1.call-start = ((), (), s32[]{:S(2)}) async-start(), calls=%async_computation.1 | async-start | bytes 14155776 | tf_op jit(solution)/shard_map/all_gather | solution.py:280
  9.0 13.4 %collective-permute-start.3 = (bf16[1024,384]{1,0:T(8,128)(2,1)}, bf16[1024,384]{1,0:T(8,128)(2,1)S(1)}, u32[]{:S(2)}, u32[]{:S(2)}) collective-permute-start(bf16[1024,384]{1,0:T(8,128)(2,1)} %cot_ref.1), channel_id=1, source_target_pairs={{0,1},{1,0},{2,3},{3,2},{4,5},{5,4},{6,7},{7,6},{8,9},{9,8},{10,11... | collective-permute-start | bytes 2359304 | tf_op jit(solution)/shard_map/ppermute | solution.py:18
  11.7 10.7 %collective-permute-start = (f32[32,256]{1,0:T(8,128)S(1)}, f32[32,256]{1,0:T(8,128)S(1)}, u32[]{:S(2)}, u32[]{:S(2)}) collective-permute-start(f32[32,256]{1,0:T(8,128)S(1)} %bitcast.145), channel_id=1, source_target_pairs={{0,2},{2,4},{4,6},{6,0},{1,3},{3,5},{5,7},{7,1},{8,10},{10,12},{12... | collective-permute-start | bytes 98312 | tf_op jit(solution)/shard_map/ppermute | solution.py:18
  13.4 9.0 %collective-permute-start.1 = (f32[32,256]{1,0:T(8,128)S(1)}, f32[32,256]{1,0:T(8,128)S(1)}, u32[]{:S(2)}, u32[]{:S(2)}) collective-permute-start(f32[32,256]{1,0:T(8,128)S(1)} %bitcast.146), channel_id=1, source_target_pairs={{0,4},{2,6},{4,0},{6,2},{1,5},{3,7},{5,1},{7,3},{8,12},{10,14},{12... | collective-permute-start | bytes 98312 | tf_op jit(solution)/shard_map/ppermute | solution.py:18
  16.1 6.3 %collective-permute-start.2 = (f32[32,256]{1,0:T(8,128)S(1)}, f32[32,256]{1,0:T(8,128)S(1)}, u32[]{:S(2)}, u32[]{:S(2)}) collective-permute-start(f32[32,256]{1,0:T(8,128)S(1)} %bitcast.147), channel_id=1, source_target_pairs={{0,6},{2,0},{4,2},{6,4},{1,7},{3,1},{5,3},{7,5},{8,14},{10,8},{12,... | collective-permute-start | bytes 98312 | tf_op jit(solution)/shard_map/ppermute | solution.py:18
  21.6 5.8 %copy-start.11 = (bf16[128,6144]{1,0:T(8,128)(2,1)S(1)}, bf16[128,6144]{1,0:T(8,128)(2,1)}, u32[]{:S(2)}) copy-start(bf16[128,6144]{1,0:T(8,128)(2,1)} %param.5) | copy-start | bytes 4718596
  22.4 0.9 copy-start.3
  26.1 1.3 collective-permute-start.4
  27.8 12.0 %copy-start.15 = (bf16[256,384]{1,0:T(8,128)(2,1)S(1)}, bf16[256,384]{1,0:T(8,128)(2,1)}, u32[]{:S(2)}) copy-start(bf16[256,384]{1,0:T(8,128)(2,1)} %get-tuple-element.43) | copy-start | bytes 589828
  28.0 20.6 %copy-start = (bf16[1024,384]{1,0:T(8,128)(2,1)S(1)}, bf16[1024,384]{1,0:T(8,128)(2,1)}, u32[]{:S(2)}) copy-start(bf16[1024,384]{1,0:T(8,128)(2,1)} %cot_ref.1) | copy-start | bytes 2359300
  28.0 20.6 %copy-start.4 = (bf16[1024,384]{1,0:T(8,128)(2,1)S(1)}, bf16[1024,384]{1,0:T(8,128)(2,1)}, u32[]{:S(2)}) copy-start(bf16[1024,384]{1,0:T(8,128)(2,1)} %copy-done.3) | copy-start | bytes 2359300
  28.1 20.6 %copy-start.9 = (s32[12]{0:T(128)S(1)}, s32[12]{0:T(128)}, u32[]{:S(2)}) copy-start(s32[12]{0:T(128)} %stack.69.at_ref) | copy-start | bytes 148
  28.1 1.8 %collective-permute-start.5 = (f32[96,8,128]{2,1,0:T(8,128)S(1)}, f32[96,8,128]{2,1,0:T(8,128)S(1)}, u32[]{:S(2)}, u32[]{:S(2)}) collective-permute-start(f32[96,8,128]{2,1,0:T(8,128)S(1)} %dynamic-slice_bitcast_fusion), channel_id=1, source_target_pairs={{0,1},{1,0},{2,3},{3,2},{4,5},{5,4},{6,7},{7,6},{8,9},{9,8},{10,11... | collective-permute-start | bytes 1179656 | tf_op jit(solution)/shard_map/ppermute | solution.py:18
  30.0 9.9 %collective-permute-start.6 = (f32[24,8,128]{2,1,0:T(8,128)S(1)}, f32[24,8,128]{2,1,0:T(8,128)S(1)}, u32[]{:S(2)}, u32[]{:S(2)}) collective-permute-start(f32[24,8,128]{2,1,0:T(8,128)S(1)} %get-tuple-element.78), channel_id=1, source_target_pairs={{0,8},{8,16},{16,24},{24,0},{1,9},{9,17},{17,25},{25,1},{2,10},{10... | collective-permute-start | bytes 294920 | tf_op jit(solution)/shard_map/ppermute | solution.py:18
  32.0 8.5 %collective-permute-start.7 = (f32[24,8,128]{2,1,0:T(8,128)S(1)}, f32[24,8,128]{2,1,0:T(8,128)S(1)}, u32[]{:S(2)}, u32[]{:S(2)}) collective-permute-start(f32[24,8,128]{2,1,0:T(8,128)S(1)} %get-tuple-element.80), channel_id=1, source_target_pairs={{0,16},{8,24},{16,0},{24,8},{1,17},{9,25},{17,1},{25,9},{2,18},{10... | collective-permute-start | bytes 294920 | tf_op jit(solution)/shard_map/ppermute | solution.py:18
  35.6 4.9 %collective-permute-start.8 = (f32[24,8,128]{2,1,0:T(8,128)S(1)}, f32[24,8,128]{2,1,0:T(8,128)S(1)}, u32[]{:S(2)}, u32[]{:S(2)}) collective-permute-start(f32[24,8,128]{2,1,0:T(8,128)S(1)} %get-tuple-element.79), channel_id=1, source_target_pairs={{0,24},{8,0},{16,8},{24,16},{1,25},{9,1},{17,9},{25,17},{2,26},{10... | collective-permute-start | bytes 294920 | tf_op jit(solution)/shard_map/ppermute | solution.py:18
  36.6 9.6 %collective-permute-start.10 = (bf16[256,384]{1,0:T(8,128)(2,1)}, bf16[256,384]{1,0:T(8,128)(2,1)S(1)}, u32[]{:S(2)}, u32[]{:S(2)}) collective-permute-start(bf16[256,384]{1,0:T(8,128)(2,1)} %get-tuple-element.44), channel_id=1, source_target_pairs={{0,4},{2,6},{4,0},{6,2},{1,5},{3,7},{5,1},{7,3},{8,12},{10,14},{12... | collective-permute-start | bytes 589832 | tf_op jit(solution)/shard_map/ppermute | solution.py:18
  37.1 9.1 %collective-permute-start.11 = (bf16[256,384]{1,0:T(8,128)(2,1)}, bf16[256,384]{1,0:T(8,128)(2,1)S(1)}, u32[]{:S(2)}, u32[]{:S(2)}) collective-permute-start(bf16[256,384]{1,0:T(8,128)(2,1)} %get-tuple-element.45), channel_id=1, source_target_pairs={{0,6},{2,0},{4,2},{6,4},{1,7},{3,1},{5,3},{7,5},{8,14},{10,8},{12,... | collective-permute-start | bytes 589832 | tf_op jit(solution)/shard_map/ppermute | solution.py:18
  39.9 8.8 %collective-permute-start.9 = (bf16[256,384]{1,0:T(8,128)(2,1)S(1)}, bf16[256,384]{1,0:T(8,128)(2,1)S(1)}, u32[]{:S(2)}, u32[]{:S(2)}) collective-permute-start(bf16[256,384]{1,0:T(8,128)(2,1)S(1)} %copy-done.15), channel_id=1, source_target_pairs={{0,2},{2,4},{4,6},{6,0},{1,3},{3,5},{5,7},{7,1},{8,10},{10,12},{12... | collective-permute-start | bytes 589832 | tf_op jit(solution)/shard_map/ppermute | solution.py:18
  50.3 34.6 %copy-start.5 = (bf16[8,128,384]{2,1,0:T(8,128)(2,1)}, bf16[8,128,384]{2,1,0:T(8,128)(2,1)S(1)}, u32[]{:S(2)}) copy-start(bf16[8,128,384]{2,1,0:T(8,128)(2,1)S(1)} %unpack.1.refs_0_) | copy-start | bytes 2359300
  50.3 19.8 %collective-permute-start.18 = (bf16[8,128,384]{2,1,0:T(8,128)(2,1)S(1)}, bf16[8,128,384]{2,1,0:T(8,128)(2,1)S(1)}, u32[]{:S(2)}, u32[]{:S(2)}) collective-permute-start(bf16[8,128,384]{2,1,0:T(8,128)(2,1)S(1)} %unpack.1.refs_0_), channel_id=1, source_target_pairs={{0,8},{8,16},{16,24},{24,0},{1,9},{9,17},{17,25},{25,1},{2,10},{10... | collective-permute-start | bytes 2359304 | tf_op jit(solution)/shard_map/ppermute | solution.py:18
  51.4 18.7 %collective-permute-start.19 = (bf16[8,128,384]{2,1,0:T(8,128)(2,1)S(1)}, bf16[8,128,384]{2,1,0:T(8,128)(2,1)S(1)}, u32[]{:S(2)}, u32[]{:S(2)}) collective-permute-start(bf16[8,128,384]{2,1,0:T(8,128)(2,1)S(1)} %unpack.1.refs_0_), channel_id=1, source_target_pairs={{0,24},{8,0},{16,8},{24,16},{1,25},{9,1},{17,9},{25,17},{2,26},{10... | collective-permute-start | bytes 2359304 | tf_op jit(solution)/shard_map/ppermute | solution.py:18
  53.6 6.2 %collective-permute-start.12 = (f32[6,8,128]{2,1,0:T(8,128)S(1)}, f32[6,8,128]{2,1,0:T(8,128)S(1)}, u32[]{:S(2)}, u32[]{:S(2)}) collective-permute-start(f32[6,8,128]{2,1,0:T(8,128)S(1)} %get-tuple-element.92), channel_id=1, source_target_pairs={{0,32},{32,64},{64,96},{96,0},{1,33},{33,65},{65,97},{97,1},{2,34}... | collective-permute-start | bytes 73736 | tf_op jit(solution)/shard_map/ppermute | solution.py:18
  55.3 6.5 %collective-permute-start.13 = (f32[6,8,128]{2,1,0:T(8,128)S(1)}, f32[6,8,128]{2,1,0:T(8,128)S(1)}, u32[]{:S(2)}, u32[]{:S(2)}) collective-permute-start(f32[6,8,128]{2,1,0:T(8,128)S(1)} %get-tuple-element.94), channel_id=1, source_target_pairs={{0,64},{32,96},{64,0},{96,32},{1,65},{33,97},{65,1},{97,33},{2,66}... | collective-permute-start | bytes 73736 | tf_op jit(solution)/shard_map/ppermute | solution.py:18
  58.7 4.3 %collective-permute-start.14 = (f32[6,8,128]{2,1,0:T(8,128)S(1)}, f32[6,8,128]{2,1,0:T(8,128)S(1)}, u32[]{:S(2)}, u32[]{:S(2)}) collective-permute-start(f32[6,8,128]{2,1,0:T(8,128)S(1)} %get-tuple-element.93), channel_id=1, source_target_pairs={{0,96},{32,0},{64,32},{96,64},{1,97},{33,1},{65,33},{97,65},{2,98}... | collective-permute-start | bytes 73736 | tf_op jit(solution)/shard_map/ppermute | solution.py:18
  63.0 5.2 %collective-permute-start.15 = (f32[6,8,128]{2,1,0:T(8,128)S(1)}, f32[6,8,128]{2,1,0:T(8,128)S(1)}, u32[]{:S(2)}, u32[]{:S(2)}) collective-permute-start(f32[6,8,128]{2,1,0:T(8,128)S(1)} %fusion.30), channel_id=1, source_target_pairs={{0,2},{2,4},{4,6},{6,0},{1,3},{3,5},{5,7},{7,1},{8,10},{10,12},{12... | collective-permute-start | bytes 73736 | tf_op jit(solution)/shard_map/ppermute | solution.py:18
  63.1 5.7 %collective-permute-start.16 = (f32[6,8,128]{2,1,0:T(8,128)S(1)}, f32[6,8,128]{2,1,0:T(8,128)S(1)}, u32[]{:S(2)}, u32[]{:S(2)}) collective-permute-start(f32[6,8,128]{2,1,0:T(8,128)S(1)} %fusion.30), channel_id=1, source_target_pairs={{0,4},{2,6},{4,0},{6,2},{1,5},{3,7},{5,1},{7,3},{8,12},{10,14},{12... | collective-permute-start | bytes 73736 | tf_op jit(solution)/shard_map/ppermute | solution.py:18
  64.5 4.7 %collective-permute-start.17 = (f32[6,8,128]{2,1,0:T(8,128)S(1)}, f32[6,8,128]{2,1,0:T(8,128)S(1)}, u32[]{:S(2)}, u32[]{:S(2)}) collective-permute-start(f32[6,8,128]{2,1,0:T(8,128)S(1)} %fusion.30), channel_id=1, source_target_pairs={{0,6},{2,0},{4,2},{6,4},{1,7},{3,1},{5,3},{7,5},{8,14},{10,8},{12,... | collective-permute-start | bytes 73736 | tf_op jit(solution)/shard_map/ppermute | solution.py:18
  70.1 14.8 %copy-start.13 = (bf16[8,128,384]{2,1,0:T(8,128)(2,1)}, bf16[8,128,384]{2,1,0:T(8,128)(2,1)S(1)}, u32[]{:S(2)}) copy-start(bf16[8,128,384]{2,1,0:T(8,128)(2,1)S(1)} %collective-permute-done.18.refs_1_) | copy-start | bytes 2359300
  70.1 1.0 copy-start.14
  71.1 13.8 %collective-permute-start.22 = (bf16[4,4,384,384]{3,2,1,0:T(8,128)(2,1)}, bf16[4,4,384,384]{3,2,1,0:T(8,128)(2,1)}, u32[]{:S(2)}, u32[]{:S(2)}) collective-permute-start(bf16[4,4,384,384]{3,2,1,0:T(8,128)(2,1)} %bitcast.149), channel_id=1, source_target_pairs={{0,1},{1,0},{2,3},{3,2},{4,5},{5,4},{6,7},{7,6},{8,9},{9,8},{10,11... | collective-permute-start | bytes 14155784 | tf_op jit(solution)/shard_map/ppermute | solution.py:18
  71.2 12.9 %collective-permute-start.20 = (bf16[8,64,384]{2,1,0:T(8,128)(2,1)S(1)}, bf16[8,64,384]{2,1,0:T(8,128)(2,1)}, u32[]{:S(2)}, u32[]{:S(2)}) collective-permute-start(bf16[8,64,384]{2,1,0:T(8,128)(2,1)S(1)} %slice.93), channel_id=1, source_target_pairs={{0,8},{8,16},{16,24},{24,0},{1,9},{9,17},{17,25},{25,1},{2,10},{10... | collective-permute-start | bytes 1179656 | tf_op jit(solution)/shard_map/ppermute | solution.py:18
  72.3 12.6 %collective-permute-start.21 = (bf16[8,64,384]{2,1,0:T(8,128)(2,1)S(1)}, bf16[8,64,384]{2,1,0:T(8,128)(2,1)}, u32[]{:S(2)}, u32[]{:S(2)}) collective-permute-start(bf16[8,64,384]{2,1,0:T(8,128)(2,1)S(1)} %slice.94), channel_id=1, source_target_pairs={{0,24},{8,0},{16,8},{24,16},{1,25},{9,1},{17,9},{25,17},{2,26},{10... | collective-permute-start | bytes 1179656 | tf_op jit(solution)/shard_map/ppermute | solution.py:18
  76.4 18.6 %all-to-all-start = ((f32[16,6,8,128]{3,2,1,0:T(8,128)}), f32[16,6,8,128]{3,2,1,0:T(8,128)S(1)}, u32[]{:S(2)}, u32[]{:S(2)}) async-start(f32[16,6,8,128]{3,2,1,0:T(8,128)} %broadcast_in_dim.28), calls=%async_computation | async-start | bytes 786432 | tf_op jit(solution)/shard_map/all_to_all | solution.py:66
  95.0 1.8 %collective-permute-start.23 = (f32[96,8,128]{2,1,0:T(8,128)S(1)}, f32[96,8,128]{2,1,0:T(8,128)S(1)}, u32[]{:S(2)}, u32[]{:S(2)}) collective-permute-start(f32[96,8,128]{2,1,0:T(8,128)S(1)} %bitcast.138), channel_id=1, source_target_pairs={{0,1},{1,0},{2,3},{3,2},{4,5},{5,4},{6,7},{7,6},{8,9},{9,8},{10,11... | collective-permute-start | bytes 1179656 | tf_op jit(solution)/shard_map/ppermute | solution.py:18
  95.1 2.0 %copy-start.12 = (bf16[128,6144]{1,0:T(8,128)(2,1)S(1)}, bf16[128,6144]{1,0:T(8,128)(2,1)}, u32[]{:S(2)}) copy-start(bf16[128,6144]{1,0:T(8,128)(2,1)} %param.5) | copy-start | bytes 4718596
  96.9 0.9 copy-start.1
  97.8 6.3 %collective-permute-start.24 = (f32[32,128]{1,0:T(8,128)S(1)}, f32[32,128]{1,0:T(8,128)S(1)}, u32[]{:S(2)}, u32[]{:S(2)}) collective-permute-start(f32[32,128]{1,0:T(8,128)S(1)} %fusion.32), channel_id=1, source_target_pairs={{0,1},{1,0},{2,3},{3,2},{4,5},{5,4},{6,7},{7,6},{8,9},{9,8},{10,11... | collective-permute-start | bytes 49160 | tf_op jit(solution)/shard_map/ppermute | solution.py:18
  98.1 29.5 %collective-permute-start.31 = (bf16[128,1536]{1,0:T(8,128)(2,1)}, bf16[128,1536]{1,0:T(8,128)(2,1)S(1)}, u32[]{:S(2)}, u32[]{:S(2)}) collective-permute-start(bf16[128,1536]{1,0:T(8,128)(2,1)} %get-tuple-element.63), channel_id=1, source_target_pairs={{0,24},{8,0},{16,8},{24,16},{1,25},{9,1},{17,9},{25,17},{2,26},{10... | collective-permute-start | bytes 1179656 | tf_op jit(solution)/shard_map/ppermute | solution.py:18
  104.2 23.4 %collective-permute-start.32 = (bf16[128,1536]{1,0:T(8,128)(2,1)}, bf16[128,1536]{1,0:T(8,128)(2,1)S(1)}, u32[]{:S(2)}, u32[]{:S(2)}) collective-permute-start(bf16[128,1536]{1,0:T(8,128)(2,1)} %get-tuple-element.64), channel_id=1, source_target_pairs={{0,8},{8,16},{16,24},{24,0},{1,9},{9,17},{17,25},{25,1},{2,10},{10... | collective-permute-start | bytes 1179656 | tf_op jit(solution)/shard_map/ppermute | solution.py:18
  104.2 8.3 %collective-permute-start.25 = (f32[2,32,128]{2,1,0:T(8,128)S(1)}, f32[2,32,128]{2,1,0:T(8,128)S(1)}, u32[]{:S(2)}, u32[]{:S(2)}) collective-permute-start(f32[2,32,128]{2,1,0:T(8,128)S(1)} %pad_maximum_fusion.5), channel_id=1, source_target_pairs={{0,2},{2,4},{4,6},{6,0},{1,3},{3,5},{5,7},{7,1},{8,10},{10,12},{12... | collective-permute-start | bytes 98312 | tf_op jit(solution)/shard_map/ppermute | solution.py:18
  106.4 7.7 %collective-permute-start.26 = (f32[2,32,128]{2,1,0:T(8,128)S(1)}, f32[2,32,128]{2,1,0:T(8,128)S(1)}, u32[]{:S(2)}, u32[]{:S(2)}) collective-permute-start(f32[2,32,128]{2,1,0:T(8,128)S(1)} %pad_maximum_fusion.5), channel_id=1, source_target_pairs={{0,4},{2,6},{4,0},{6,2},{1,5},{3,7},{5,1},{7,3},{8,12},{10,14},{12... | collective-permute-start | bytes 98312 | tf_op jit(solution)/shard_map/ppermute | solution.py:18
  108.7 5.5 %collective-permute-start.27 = (f32[2,32,128]{2,1,0:T(8,128)S(1)}, f32[2,32,128]{2,1,0:T(8,128)S(1)}, u32[]{:S(2)}, u32[]{:S(2)}) collective-permute-start(f32[2,32,128]{2,1,0:T(8,128)S(1)} %pad_maximum_fusion.5), channel_id=1, source_target_pairs={{0,6},{2,0},{4,2},{6,4},{1,7},{3,1},{5,3},{7,5},{8,14},{10,8},{12,... | collective-permute-start | bytes 98312 | tf_op jit(solution)/shard_map/ppermute | solution.py:18
  112.4 20.3 %copy-start.6 = (bf16[128,1536]{1,0:T(8,128)(2,1)S(1)}, bf16[128,1536]{1,0:T(8,128)(2,1)}, u32[]{:S(2)}) copy-start(bf16[128,1536]{1,0:T(8,128)(2,1)} %get-tuple-element.69.refs_0_) | copy-start | bytes 1179652
  112.4 20.3 %copy-start.10 = (s32[12]{0:T(128)S(1)}, s32[12]{0:T(128)}, u32[]{:S(2)}) copy-start(s32[12]{0:T(128)} %stack.69.at_ref) | copy-start | bytes 148
  112.5 15.1 %collective-permute-start.33 = (bf16[128,1536]{1,0:T(8,128)(2,1)}, bf16[128,1536]{1,0:T(8,128)(2,1)S(1)}, u32[]{:S(2)}, u32[]{:S(2)}) collective-permute-start(bf16[128,1536]{1,0:T(8,128)(2,1)} %get-tuple-element.65), channel_id=1, source_target_pairs={{0,16},{8,24},{16,0},{24,8},{1,17},{9,25},{17,1},{25,9},{2,18},{10... | collective-permute-start | bytes 1179656 | tf_op jit(solution)/shard_map/ppermute | solution.py:18
  114.7 24.6 %copy-start.2 = (f32[2,96,8,128]{3,2,1,0:T(8,128)S(1)}, f32[2,96,8,128]{3,2,1,0:T(8,128)}, u32[]{:S(2)}) copy-start(f32[2,96,8,128]{3,2,1,0:T(8,128)} %copy-done.1) | copy-start | bytes 2359300
  114.7 5.8 %collective-permute-start.28 = (f32[32,384]{1,0:T(8,128)S(1)}, f32[32,384]{1,0:T(8,128)S(1)}, u32[]{:S(2)}, u32[]{:S(2)}) collective-permute-start(f32[32,384]{1,0:T(8,128)S(1)} %fusion.15), channel_id=1, source_target_pairs={{0,32},{32,64},{64,96},{96,0},{1,33},{33,65},{65,97},{97,1},{2,34}... | collective-permute-start | bytes 147464 | tf_op jit(solution)/shard_map/ppermute | solution.py:18
  116.8 10.7 %collective-permute-start.29 = (f32[32,384]{1,0:T(8,128)S(1)}, f32[32,384]{1,0:T(8,128)S(1)}, u32[]{:S(2)}, u32[]{:S(2)}) collective-permute-start(f32[32,384]{1,0:T(8,128)S(1)} %fusion.15), channel_id=1, source_target_pairs={{0,64},{32,96},{64,0},{96,32},{1,65},{33,97},{65,1},{97,33},{2,66}... | collective-permute-start | bytes 147464 | tf_op jit(solution)/shard_map/ppermute | solution.py:18
  120.5 7.0 %collective-permute-start.30 = (f32[32,384]{1,0:T(8,128)S(1)}, f32[32,384]{1,0:T(8,128)S(1)}, u32[]{:S(2)}, u32[]{:S(2)}) collective-permute-start(f32[32,384]{1,0:T(8,128)S(1)} %fusion.15), channel_id=1, source_target_pairs={{0,96},{32,0},{64,32},{96,64},{1,97},{33,1},{65,33},{97,65},{2,98}... | collective-permute-start | bytes 147464 | tf_op jit(solution)/shard_map/ppermute | solution.py:18
  127.5 8.0 %copy-start.8 = (f32[32,32]{1,0:T(8,128)S(1)}, f32[32,32]{1,0:T(8,128)}, u32[]{:S(2)}) copy-start(f32[32,32]{1,0:T(8,128)} %inverse_of_factor.1.inverse_ref) | copy-start | bytes 12292
  127.6 7.0 %collective-permute-start.34 = (f32[32,384]{1,0:T(8,128)S(1)}, f32[32,384]{1,0:T(8,128)S(1)}, u32[]{:S(2)}, u32[]{:S(2)}) collective-permute-start(f32[32,384]{1,0:T(8,128)S(1)} %add_add_fusion), channel_id=1, source_target_pairs={{0,8},{8,16},{16,24},{24,0},{1,9},{9,17},{17,25},{25,1},{2,10},{10... | collective-permute-start | bytes 147464 | tf_op jit(solution)/shard_map/ppermute | solution.py:18
  129.9 5.6 %collective-permute-start.35 = (f32[32,384]{1,0:T(8,128)S(1)}, f32[32,384]{1,0:T(8,128)S(1)}, u32[]{:S(2)}, u32[]{:S(2)}) collective-permute-start(f32[32,384]{1,0:T(8,128)S(1)} %add_add_fusion), channel_id=1, source_target_pairs={{0,16},{8,24},{16,0},{24,8},{1,17},{9,25},{17,1},{25,9},{2,18},{10... | collective-permute-start | bytes 147464 | tf_op jit(solution)/shard_map/ppermute | solution.py:18
  131.4 4.2 %collective-permute-start.36 = (f32[32,384]{1,0:T(8,128)S(1)}, f32[32,384]{1,0:T(8,128)S(1)}, u32[]{:S(2)}, u32[]{:S(2)}) collective-permute-start(f32[32,384]{1,0:T(8,128)S(1)} %add_add_fusion), channel_id=1, source_target_pairs={{0,24},{8,0},{16,8},{24,16},{1,25},{9,1},{17,9},{25,17},{2,26},{10... | collective-permute-start | bytes 147464 | tf_op jit(solution)/shard_map/ppermute | solution.py:18
  135.7 16.3 %copy-start.7 = (f32[32,384]{1,0:T(8,128)}, f32[32,384]{1,0:T(8,128)S(1)}, u32[]{:S(2)}) copy-start(f32[32,384]{1,0:T(8,128)S(1)} %convolution_multiply_fusion.factor_ref) | copy-start | bytes 147460
Sparse Core Ops, SparseCore 0:
  10.1 58.9 all-gather.5
  70.8 68.4 all-gather.3

commit v6 on v5

--- a/solution.py
+++ b/solution.py
@@ -120,6 +120,7 @@
     for i in (0, 1):
         for copy in loads(i):
             copy.start()
+    cot = cot_ref[...].T
     for i, size in enumerate(sizes):
         slot = i % 2
         basis = lax.dot_general(
@@ -135,8 +136,8 @@
             copy.wait()
         if i >= 2:
             store(i - 2).wait()
-        total = mm(acts[slot, :, :size], cot_ref[...], 0, 0) * scale + olds[slot, :size].astype(F32)
-        news[slot, :size] = (total - mm(basis6, factor6, 0, 0)).astype(BF16)
+        total = mm(cot, acts[slot, :, :size], 1, 0) * scale - mm(factor6, basis6, 0, 0)
+        news[slot, :size] = (total.T + olds[slot, :size].astype(F32)).astype(BF16)
         store(i).start()
         if i + 2 < len(sizes):
             for copy in loads(i + 2):

time: 161 us -> 160 us (level)
  no operation moved by 1% of the time
where the time goes in v6:
time: 160 us; the launch traced here: 158 us
  starting transfers between devices  63.1 us (39%)
  Pallas kernels  33.7 us (21%)
  waiting for transfers between devices  28.3 us (18%)
  between operations  14.8 us (9%)
  matrix products  10.2 us (6%)
  local copies, waits for them, and re-layouts  6.53 us (4%)
  other arithmetic  1.66 us (1%)
    ppermute x37, starting transfers between devices, shift(): return lax.ppermute(value, axis, [(i, (i + step) % n) for i in range(n)])  57.3 us
    ppermute x37, waiting for transfers between devices, shift(): return lax.ppermute(value, axis, [(i, (i + step) % n) for i in range(n)])  24.7 us
    pallas_call x1, Pallas kernels, residual_call(): pl.pallas_call(functools.partial(residual_kernel, scale, tuple(sizes)), o...  12.2 us
    pallas_call x1, Pallas kernels, input_call(): pl.pallas_call(functools.partial(input_kernel, len(cots)), out_shape=[jax...  10.1 us
    dot_general x6, matrix products, mm(): lax.dot_general(a, b, (((ca,), (cb,)), ((), ())), preferred_element_type=...  10 us
    pallas_call x3, Pallas kernels, copy_call(): pl.pallas_call(functools.partial(copy_kernel, len(ins), len(outs), plan),...  6.15 us
    all_to_all x1, starting transfers between devices, all_blocks(): lax.all_to_all(jnp.broadcast_to(value[None], (n,) + value.shape), axis, 0...  5.71 us
    pallas_call x1, Pallas kernels, inverse_of_factor(): pl.pallas_call(inverse_kernel, out_shape=jax.ShapeDtypeStruct((rank, rank...  5.22 us
  transfers between devices with their start and end apart: 40, of which 18 were waited for; matrix products, arithmetic and copies ran while one was open for 9% of the time, Pallas kernels for 14%

profile of v6, /device:TPU:0, one launch (start us, length us, event | category | flops | bytes accessed | tf_op | source)
XLA Modules:
  0.0 158.3 jit_solution(1336987935093818048)
XLA Ops:
  7.2 1.7 %constant_dynamic-slice_fusion = bf16[384,384]{1,0:T(8,128)(2,1)} fusion(bf16[6144,384]{1,0:T(8,128)(2,1)} %param.7, s32[]{:T(128)S(6)} %select_n.320), kind=kLoop, calls=%fused_computation.106 | loop fusion | bytes 589828 | tf_op jit(solution)/shard_map/dynamic_slice | solution.py:267
  9.2 0.8 reduce-precision_convert_fusion.5
  10.0 1.5 fusion.22
  11.7 1.6 %collective-permute-start = (f32[32,256]{1,0:T(8,128)S(1)}, f32[32,256]{1,0:T(8,128)S(1)}, u32[]{:S(2)}, u32[]{:S(2)}) collective-permute-start(f32[32,256]{1,0:T(8,128)S(1)} %bitcast.145), channel_id=1, source_target_pairs={{0,2},{2,4},{4,6},{6,0},{1,3},{3,5},{5,7},{7,1},{8,10},{10,12},{12... | collective-permute-start | bytes 98312 | tf_op jit(solution)/shard_map/ppermute | solution.py:18
  13.4 2.7 %collective-permute-start.1 = (f32[32,256]{1,0:T(8,128)S(1)}, f32[32,256]{1,0:T(8,128)S(1)}, u32[]{:S(2)}, u32[]{:S(2)}) collective-permute-start(f32[32,256]{1,0:T(8,128)S(1)} %bitcast.146), channel_id=1, source_target_pairs={{0,4},{2,6},{4,0},{6,2},{1,5},{3,7},{5,1},{7,3},{8,12},{10,14},{12... | collective-permute-start | bytes 98312 | tf_op jit(solution)/shard_map/ppermute | solution.py:18
  16.1 1.4 collective-permute-start.2
  17.6 3.9 %fusion.21 = f32[96,6144]{1,0:T(8,128)S(1)} fusion(bf16[32,384]{1,0:T(8,128)(2,1)S(1)} %get-tuple-element.96, bf16[32,384]{1,0:T(8,128)(2,1)S(1)} %get-tuple-element.97, bf16[32,384]{1,0:T(8,128)(2,1)S(1)} %get-tuple-element.95, bf16[1,6144,384]{2,1,0:T(8,128)(2,1)} %param.8), kind=kOutput, calls=%fused_computation.65 | convolution fusion | flops 453206016 | bytes 7151616 | tf_op jit(solution)/shard_map/dot_general | solution.py:41
  21.7 0.7 stack.69.at_ref
  22.4 0.9 copy-done.3
  23.3 2.6 %pack.1 = (bf16[256,384]{1,0:T(8,128)(2,1)}, bf16[256,384]{1,0:T(8,128)(2,1)}, bf16[256,384]{1,0:T(8,128)(2,1)}) custom-call(s32[12]{0:T(128)} %stack.69.at_ref, bf16[1024,384]{1,0:T(8,128)(2,1)} %cot_ref.1, bf16[1024,384]{1,0:T(8,128)(2,1)} %copy-done.3), custom_call_target="tpu_custom_call" | custom-call | bytes 1179648 | tf_op jit(solution)/shard_map/pack/pallas_call | solution.py:220
  26.2 1.2 collective-permute-done.4
  27.4 0.5 fusion.23
  28.4 1.6 collective-permute-done.5
  30.0 2.0 %collective-permute-start.6 = (f32[24,8,128]{2,1,0:T(8,128)S(1)}, f32[24,8,128]{2,1,0:T(8,128)S(1)}, u32[]{:S(2)}, u32[]{:S(2)}) collective-permute-start(f32[24,8,128]{2,1,0:T(8,128)S(1)} %get-tuple-element.78), channel_id=1, source_target_pairs={{0,8},{8,16},{16,24},{24,0},{1,9},{9,17},{17,25},{25,1},{2,10},{10... | collective-permute-start | bytes 294920 | tf_op jit(solution)/shard_map/ppermute | solution.py:18
  32.0 3.6 %collective-permute-start.7 = (f32[24,8,128]{2,1,0:T(8,128)S(1)}, f32[24,8,128]{2,1,0:T(8,128)S(1)}, u32[]{:S(2)}, u32[]{:S(2)}) collective-permute-start(f32[24,8,128]{2,1,0:T(8,128)S(1)} %get-tuple-element.80), channel_id=1, source_target_pairs={{0,16},{8,24},{16,0},{24,8},{1,17},{9,25},{17,1},{25,9},{2,18},{10... | collective-permute-start | bytes 294920 | tf_op jit(solution)/shard_map/ppermute | solution.py:18
  35.6 1.0 collective-permute-start.8
  36.6 0.5 collective-permute-start.10
  37.1 2.7 %collective-permute-start.11 = (bf16[256,384]{1,0:T(8,128)(2,1)}, bf16[256,384]{1,0:T(8,128)(2,1)S(1)}, u32[]{:S(2)}, u32[]{:S(2)}) collective-permute-start(bf16[256,384]{1,0:T(8,128)(2,1)} %get-tuple-element.45), channel_id=1, source_target_pairs={{0,6},{2,0},{4,2},{6,4},{1,7},{3,1},{5,3},{7,5},{8,14},{10,8},{12,... | collective-permute-start | bytes 589832 | tf_op jit(solution)/shard_map/ppermute | solution.py:18
  39.9 0.7 collective-permute-done.7
  40.5 5.6 %collective-permute-done.10.refs_3_ = bf16[256,384]{1,0:T(8,128)(2,1)S(1)} collective-permute-done((bf16[256,384]{1,0:T(8,128)(2,1)}, bf16[256,384]{1,0:T(8,128)(2,1)S(1)}, u32[]{:S(2)}, u32[]{:S(2)}) %collective-permute-start.10) | collective-permute-done | bytes 196640 | tf_op jit(solution)/shard_map/ppermute | solution.py:18
  46.3 2.4 %collective-permute-done.9.refs_2_ = bf16[256,384]{1,0:T(8,128)(2,1)S(1)} collective-permute-done((bf16[256,384]{1,0:T(8,128)(2,1)S(1)}, bf16[256,384]{1,0:T(8,128)(2,1)S(1)}, u32[]{:S(2)}, u32[]{:S(2)}) %collective-permute-start.9) | collective-permute-done | bytes 196640 | tf_op jit(solution)/shard_map/ppermute | solution.py:18
  48.7 1.6 %unpack.1.refs_0_ = bf16[8,128,384]{2,1,0:T(8,128)(2,1)S(1)} custom-call(s32[12]{0:T(128)S(1)} %copy-done.9, bf16[1024,384]{1,0:T(8,128)(2,1)S(1)} %copy-done, bf16[1024,384]{1,0:T(8,128)(2,1)S(1)} %copy-done.4, bf16[256,384]{1,0:T(8,128)(2,1)S(1)} %collective-permute-done.9.refs_2_, bf16[256,384]{1,0:T(8,128)(2,1)S(1)} %collective-permute-done.10.refs_3_, ...), custom_call_target="tpu_custom_call" | custom-call | bytes 1572864 | tf_op jit(solution)/shard_map/unpack/pallas_call | solution.py:220
  50.3 1.1 collective-permute-start.18
  51.4 2.2 %collective-permute-start.19 = (bf16[8,128,384]{2,1,0:T(8,128)(2,1)S(1)}, bf16[8,128,384]{2,1,0:T(8,128)(2,1)S(1)}, u32[]{:S(2)}, u32[]{:S(2)}) collective-permute-start(bf16[8,128,384]{2,1,0:T(8,128)(2,1)S(1)} %unpack.1.refs_0_), channel_id=1, source_target_pairs={{0,24},{8,0},{16,8},{24,16},{1,25},{9,1},{17,9},{25,17},{2,26},{10... | collective-permute-start | bytes 2359304 | tf_op jit(solution)/shard_map/ppermute | solution.py:18
  53.6 1.7 %collective-permute-start.12 = (f32[6,8,128]{2,1,0:T(8,128)S(1)}, f32[6,8,128]{2,1,0:T(8,128)S(1)}, u32[]{:S(2)}, u32[]{:S(2)}) collective-permute-start(f32[6,8,128]{2,1,0:T(8,128)S(1)} %get-tuple-element.92), channel_id=1, source_target_pairs={{0,32},{32,64},{64,96},{96,0},{1,33},{33,65},{65,97},{97,1},{2,34}... | collective-permute-start | bytes 73736 | tf_op jit(solution)/shard_map/ppermute | solution.py:18
  55.3 3.4 %collective-permute-start.13 = (f32[6,8,128]{2,1,0:T(8,128)S(1)}, f32[6,8,128]{2,1,0:T(8,128)S(1)}, u32[]{:S(2)}, u32[]{:S(2)}) collective-permute-start(f32[6,8,128]{2,1,0:T(8,128)S(1)} %get-tuple-element.94), channel_id=1, source_target_pairs={{0,64},{32,96},{64,0},{96,32},{1,65},{33,97},{65,1},{97,33},{2,66}... | collective-permute-start | bytes 73736 | tf_op jit(solution)/shard_map/ppermute | solution.py:18
  58.7 1.2 collective-permute-start.14
  59.8 1.9 %collective-permute-done.13 = f32[6,8,128]{2,1,0:T(8,128)S(1)} collective-permute-done((f32[6,8,128]{2,1,0:T(8,128)S(1)}, f32[6,8,128]{2,1,0:T(8,128)S(1)}, u32[]{:S(2)}, u32[]{:S(2)}) %collective-permute-start.13) | collective-permute-done | bytes 24608 | tf_op jit(solution)/shard_map/ppermute | solution.py:18
  61.8 1.2 collective-permute-done.14
  63.1 1.4 collective-permute-start.16
  64.5 1.9 %collective-permute-start.17 = (f32[6,8,128]{2,1,0:T(8,128)S(1)}, f32[6,8,128]{2,1,0:T(8,128)S(1)}, u32[]{:S(2)}, u32[]{:S(2)}) collective-permute-start(f32[6,8,128]{2,1,0:T(8,128)S(1)} %fusion.30), channel_id=1, source_target_pairs={{0,6},{2,0},{4,2},{6,4},{1,7},{3,1},{5,3},{7,5},{8,14},{10,8},{12,... | collective-permute-start | bytes 73736 | tf_op jit(solution)/shard_map/ppermute | solution.py:18
  66.5 1.8 %collective-permute-done.15 = f32[6,8,128]{2,1,0:T(8,128)S(1)} collective-permute-done((f32[6,8,128]{2,1,0:T(8,128)S(1)}, f32[6,8,128]{2,1,0:T(8,128)S(1)}, u32[]{:S(2)}, u32[]{:S(2)}) %collective-permute-start.15) | collective-permute-done | bytes 24608 | tf_op jit(solution)/shard_map/ppermute | solution.py:18
  68.3 0.5 collective-permute-done.16
  68.8 0.5 collective-permute-done.17
  69.3 0.9 collective-permute-done.18.refs_1_
  70.2 0.9 copy-done.14
  71.2 1.0 slice.94
  72.3 3.3 %collective-permute-start.21 = (bf16[8,64,384]{2,1,0:T(8,128)(2,1)S(1)}, bf16[8,64,384]{2,1,0:T(8,128)(2,1)}, u32[]{:S(2)}, u32[]{:S(2)}) collective-permute-start(bf16[8,64,384]{2,1,0:T(8,128)(2,1)S(1)} %slice.94), channel_id=1, source_target_pairs={{0,24},{8,0},{16,8},{24,16},{1,25},{9,1},{17,9},{25,17},{2,26},{10... | collective-permute-start | bytes 1179656 | tf_op jit(solution)/shard_map/ppermute | solution.py:18
  75.6 0.8 broadcast_in_dim.28
  76.4 5.7 %all-to-all-start = ((f32[16,6,8,128]{3,2,1,0:T(8,128)}), f32[16,6,8,128]{3,2,1,0:T(8,128)S(1)}, u32[]{:S(2)}, u32[]{:S(2)}) async-start(f32[16,6,8,128]{3,2,1,0:T(8,128)} %broadcast_in_dim.28), calls=%async_computation | async-start | bytes 786432 | tf_op jit(solution)/shard_map/all_to_all | solution.py:66
  82.1 2.0 %collective-permute-done.20.refs_3_ = bf16[8,64,384]{2,1,0:T(8,128)(2,1)} collective-permute-done((bf16[8,64,384]{2,1,0:T(8,128)(2,1)S(1)}, bf16[8,64,384]{2,1,0:T(8,128)(2,1)}, u32[]{:S(2)}, u32[]{:S(2)}) %collective-permute-start.20) | collective-permute-done | bytes 393248 | tf_op jit(solution)/shard_map/ppermute | solution.py:18
  84.1 0.8 collective-permute-done.21.refs_4_
  84.9 10.1 %input_grads.1 = (bf16[128,1536]{1,0:T(8,128)(2,1)}, bf16[128,1536]{1,0:T(8,128)(2,1)}, bf16[128,1536]{1,0:T(8,128)(2,1)}, bf16[128,1536]{1,0:T(8,128)(2,1)}) custom-call(s32[12]{0:T(128)} %stack.69.at_ref, bf16[8,128,384]{2,1,0:T(8,128)(2,1)} %copy-done.5, bf16[8,128,384]{2,1,0:T(8,128)(2,1)} %copy-done.13, bf16[8,128,384]{2,1,0:T(8,128)(2,1)} %copy-done.14, ...), custom_call_target="tpu_custom_call" | custom-call | flops 4831838208 | bytes 12582912 | tf_op jit(solution)/shard_map/input_grads/pallas_call | solution.py:190
  95.1 1.7 %collective-permute-done.23 = f32[96,8,128]{2,1,0:T(8,128)S(1)} collective-permute-done((f32[96,8,128]{2,1,0:T(8,128)S(1)}, f32[96,8,128]{2,1,0:T(8,128)S(1)}, u32[]{:S(2)}, u32[]{:S(2)}) %collective-permute-start.23) | collective-permute-done | bytes 393248 | tf_op jit(solution)/shard_map/ppermute | solution.py:18
  97.1 0.7 fusion.3
  98.1 6.1 %collective-permute-start.31 = (bf16[128,1536]{1,0:T(8,128)(2,1)}, bf16[128,1536]{1,0:T(8,128)(2,1)S(1)}, u32[]{:S(2)}, u32[]{:S(2)}) collective-permute-start(bf16[128,1536]{1,0:T(8,128)(2,1)} %get-tuple-element.63), channel_id=1, source_target_pairs={{0,24},{8,0},{16,8},{24,16},{1,25},{9,1},{17,9},{25,17},{2,26},{10... | collective-permute-start | bytes 1179656 | tf_op jit(solution)/shard_map/ppermute | solution.py:18
  104.2 2.3 %collective-permute-start.25 = (f32[2,32,128]{2,1,0:T(8,128)S(1)}, f32[2,32,128]{2,1,0:T(8,128)S(1)}, u32[]{:S(2)}, u32[]{:S(2)}) collective-permute-start(f32[2,32,128]{2,1,0:T(8,128)S(1)} %pad_maximum_fusion.5), channel_id=1, source_target_pairs={{0,2},{2,4},{4,6},{6,0},{1,3},{3,5},{5,7},{7,1},{8,10},{10,12},{12... | collective-permute-start | bytes 98312 | tf_op jit(solution)/shard_map/ppermute | solution.py:18
  106.4 2.3 %collective-permute-start.26 = (f32[2,32,128]{2,1,0:T(8,128)S(1)}, f32[2,32,128]{2,1,0:T(8,128)S(1)}, u32[]{:S(2)}, u32[]{:S(2)}) collective-permute-start(f32[2,32,128]{2,1,0:T(8,128)S(1)} %pad_maximum_fusion.5), channel_id=1, source_target_pairs={{0,4},{2,6},{4,0},{6,2},{1,5},{3,7},{5,1},{7,3},{8,12},{10,14},{12... | collective-permute-start | bytes 98312 | tf_op jit(solution)/shard_map/ppermute | solution.py:18
  108.7 0.5 collective-permute-start.27
  109.2 3.2 %fusion.2 = f32[96,384]{1,0:T(8,128)S(1)} fusion(bf16[32,6144]{1,0:T(8,128)(2,1)S(1)} %get-tuple-element.74, bf16[32,6144]{1,0:T(8,128)(2,1)S(1)} %get-tuple-element.75, bf16[32,6144]{1,0:T(8,128)(2,1)S(1)} %get-tuple-element.73, bf16[1,6144,384]{2,1,0:T(8,128)(2,1)} %param.8), kind=kOutput, calls=%fused_computation.13 | convolution fusion | flops 456523776 | bytes 6045696 | tf_op jit(solution)/shard_map/dot_general | solution.py:41
  112.5 1.7 %collective-permute-start.33 = (bf16[128,1536]{1,0:T(8,128)(2,1)}, bf16[128,1536]{1,0:T(8,128)(2,1)S(1)}, u32[]{:S(2)}, u32[]{:S(2)}) collective-permute-start(bf16[128,1536]{1,0:T(8,128)(2,1)} %get-tuple-element.65), channel_id=1, source_target_pairs={{0,16},{8,24},{16,0},{24,8},{1,17},{9,25},{17,1},{25,9},{2,18},{10... | collective-permute-start | bytes 1179656 | tf_op jit(solution)/shard_map/ppermute | solution.py:18
  114.4 0.3 fusion.4
  114.7 2.1 %collective-permute-start.28 = (f32[32,384]{1,0:T(8,128)S(1)}, f32[32,384]{1,0:T(8,128)S(1)}, u32[]{:S(2)}, u32[]{:S(2)}) collective-permute-start(f32[32,384]{1,0:T(8,128)S(1)} %fusion.15), channel_id=1, source_target_pairs={{0,32},{32,64},{64,96},{96,0},{1,33},{33,65},{65,97},{97,1},{2,34}... | collective-permute-start | bytes 147464 | tf_op jit(solution)/shard_map/ppermute | solution.py:18
  116.8 2.9 %collective-permute-start.29 = (f32[32,384]{1,0:T(8,128)S(1)}, f32[32,384]{1,0:T(8,128)S(1)}, u32[]{:S(2)}, u32[]{:S(2)}) collective-permute-start(f32[32,384]{1,0:T(8,128)S(1)} %fusion.15), channel_id=1, source_target_pairs={{0,64},{32,96},{64,0},{96,32},{1,65},{33,97},{65,1},{97,33},{2,66}... | collective-permute-start | bytes 147464 | tf_op jit(solution)/shard_map/ppermute | solution.py:18
  119.7 0.9 collective-permute-done.28
  120.5 1.8 %collective-permute-start.30 = (f32[32,384]{1,0:T(8,128)S(1)}, f32[32,384]{1,0:T(8,128)S(1)}, u32[]{:S(2)}, u32[]{:S(2)}) collective-permute-start(f32[32,384]{1,0:T(8,128)S(1)} %fusion.15), channel_id=1, source_target_pairs={{0,96},{32,0},{64,32},{96,64},{1,97},{33,1},{65,33},{97,65},{2,98}... | collective-permute-start | bytes 147464 | tf_op jit(solution)/shard_map/ppermute | solution.py:18
  122.3 5.2 %inverse_of_factor.1.inverse_ref = f32[32,32]{1,0:T(8,128)} custom-call(f32[32,6144]{1,0:T(8,128)} %bitcast.131), custom_call_target="tpu_custom_call" | custom-call | tf_op jit(solution)/shard_map/inverse_of_factor/pallas_call | solution.py:97
  127.6 2.4 %collective-permute-start.34 = (f32[32,384]{1,0:T(8,128)S(1)}, f32[32,384]{1,0:T(8,128)S(1)}, u32[]{:S(2)}, u32[]{:S(2)}) collective-permute-start(f32[32,384]{1,0:T(8,128)S(1)} %add_add_fusion), channel_id=1, source_target_pairs={{0,8},{8,16},{16,24},{24,0},{1,9},{9,17},{17,25},{25,1},{2,10},{10... | collective-permute-start | bytes 147464 | tf_op jit(solution)/shard_map/ppermute | solution.py:18
  129.9 1.4 collective-permute-start.35
  131.4 1.4 collective-permute-start.36
  132.7 1.9 %place.1 = bf16[128,6144]{1,0:T(8,128)(2,1)} custom-call(s32[12]{0:T(128)S(1)} %copy-done.10, bf16[128,1536]{1,0:T(8,128)(2,1)S(1)} %copy-done.6, bf16[128,1536]{1,0:T(8,128)(2,1)S(1)} %collective-permute-done.31.refs_1_, bf16[128,1536]{1,0:T(8,128)(2,1)S(1)} %collective-permute-done.32.refs_2_, bf16[128,1536]{1,0:T(8,128)(2,1)S(1)} %collective-permute-done.33.refs_3_), custom_call_target="tpu_custom_call" | custom-call | bytes 3145728 | tf_op jit(solution)/shard_map/place/pallas_call | solution.py:220
  134.6 0.9 collective-permute-done.35
  135.7 3.5 %all-gather.4.cloned.1.call-done.act_ref = bf16[1024,6144]{1,0:T(8,128)(2,1)} async-done(((bf16[128,6144]{1,0:T(8,128)(2,1)}), bf16[1024,6144]{1,0:T(8,128)(2,1)}) %all-gather.4.cloned.1.call-update) | async-done | bytes 12582928 | tf_op jit(solution)/shard_map/all_gather | solution.py:281
  139.3 12.2 %new_residual.1 = bf16[6144,384]{1,0:T(8,128)(2,1)} custom-call(bf16[1024,6144]{1,0:T(8,128)(2,1)} %all-gather.4.cloned.1.call-done.act_ref, bf16[1024,384]{1,0:T(8,128)(2,1)S(1)} %copy-done, bf16[6144,384]{1,0:T(8,128)(2,1)} %bitcast.134, f32[32,6144]{1,0:T(8,128)S(1)} %bitcast.132, f32[32,32]{1,0:T(8,128)S(1)} %copy-done.8, ...), custom_call_target="tpu_custom_call" | custom-call | flops 5737807872 | bytes 22806528 | tf_op jit(solution)/shard_map/new_residual/pallas_call | solution.py:154
  (107 shorter events, 2.7 us)
Async XLA Ops:
  7.2 63.0 %all-gather.6.cloned.1.call-start = ((), (), s32[]{:S(2)}) async-start(), calls=%async_computation.2 | async-start | bytes 5013504 | tf_op jit(solution)/shard_map/all_gather | solution.py:268
  9.0 130.3 %all-gather.4.cloned.1.call-start = ((), (), s32[]{:S(2)}) async-start(), calls=%async_computation.1 | async-start | bytes 14155776 | tf_op jit(solution)/shard_map/all_gather | solution.py:281
  9.0 13.4 %collective-permute-start.3 = (bf16[1024,384]{1,0:T(8,128)(2,1)}, bf16[1024,384]{1,0:T(8,128)(2,1)S(1)}, u32[]{:S(2)}, u32[]{:S(2)}) collective-permute-start(bf16[1024,384]{1,0:T(8,128)(2,1)} %cot_ref.1), channel_id=1, source_target_pairs={{0,1},{1,0},{2,3},{3,2},{4,5},{5,4},{6,7},{7,6},{8,9},{9,8},{10,11... | collective-permute-start | bytes 2359304 | tf_op jit(solution)/shard_map/ppermute | solution.py:18
  11.7 10.7 %collective-permute-start = (f32[32,256]{1,0:T(8,128)S(1)}, f32[32,256]{1,0:T(8,128)S(1)}, u32[]{:S(2)}, u32[]{:S(2)}) collective-permute-start(f32[32,256]{1,0:T(8,128)S(1)} %bitcast.145), channel_id=1, source_target_pairs={{0,2},{2,4},{4,6},{6,0},{1,3},{3,5},{5,7},{7,1},{8,10},{10,12},{12... | collective-permute-start | bytes 98312 | tf_op jit(solution)/shard_map/ppermute | solution.py:18
  13.4 9.0 %collective-permute-start.1 = (f32[32,256]{1,0:T(8,128)S(1)}, f32[32,256]{1,0:T(8,128)S(1)}, u32[]{:S(2)}, u32[]{:S(2)}) collective-permute-start(f32[32,256]{1,0:T(8,128)S(1)} %bitcast.146), channel_id=1, source_target_pairs={{0,4},{2,6},{4,0},{6,2},{1,5},{3,7},{5,1},{7,3},{8,12},{10,14},{12... | collective-permute-start | bytes 98312 | tf_op jit(solution)/shard_map/ppermute | solution.py:18
  16.1 6.3 %collective-permute-start.2 = (f32[32,256]{1,0:T(8,128)S(1)}, f32[32,256]{1,0:T(8,128)S(1)}, u32[]{:S(2)}, u32[]{:S(2)}) collective-permute-start(f32[32,256]{1,0:T(8,128)S(1)} %bitcast.147), channel_id=1, source_target_pairs={{0,6},{2,0},{4,2},{6,4},{1,7},{3,1},{5,3},{7,5},{8,14},{10,8},{12,... | collective-permute-start | bytes 98312 | tf_op jit(solution)/shard_map/ppermute | solution.py:18
  21.6 5.8 %copy-start.11 = (bf16[128,6144]{1,0:T(8,128)(2,1)S(1)}, bf16[128,6144]{1,0:T(8,128)(2,1)}, u32[]{:S(2)}) copy-start(bf16[128,6144]{1,0:T(8,128)(2,1)} %param.5) | copy-start | bytes 4718596
  22.4 0.9 copy-start.3
  26.1 1.3 collective-permute-start.4
  27.8 12.0 %copy-start.15 = (bf16[256,384]{1,0:T(8,128)(2,1)S(1)}, bf16[256,384]{1,0:T(8,128)(2,1)}, u32[]{:S(2)}) copy-start(bf16[256,384]{1,0:T(8,128)(2,1)} %get-tuple-element.43) | copy-start | bytes 589828
  28.0 20.6 %copy-start = (bf16[1024,384]{1,0:T(8,128)(2,1)S(1)}, bf16[1024,384]{1,0:T(8,128)(2,1)}, u32[]{:S(2)}) copy-start(bf16[1024,384]{1,0:T(8,128)(2,1)} %cot_ref.1) | copy-start | bytes 2359300
  28.0 20.6 %copy-start.4 = (bf16[1024,384]{1,0:T(8,128)(2,1)S(1)}, bf16[1024,384]{1,0:T(8,128)(2,1)}, u32[]{:S(2)}) copy-start(bf16[1024,384]{1,0:T(8,128)(2,1)} %copy-done.3) | copy-start | bytes 2359300
  28.1 20.6 %copy-start.9 = (s32[12]{0:T(128)S(1)}, s32[12]{0:T(128)}, u32[]{:S(2)}) copy-start(s32[12]{0:T(128)} %stack.69.at_ref) | copy-start | bytes 148
  28.1 1.8 %collective-permute-start.5 = (f32[96,8,128]{2,1,0:T(8,128)S(1)}, f32[96,8,128]{2,1,0:T(8,128)S(1)}, u32[]{:S(2)}, u32[]{:S(2)}) collective-permute-start(f32[96,8,128]{2,1,0:T(8,128)S(1)} %dynamic-slice_bitcast_fusion), channel_id=1, source_target_pairs={{0,1},{1,0},{2,3},{3,2},{4,5},{5,4},{6,7},{7,6},{8,9},{9,8},{10,11... | collective-permute-start | bytes 1179656 | tf_op jit(solution)/shard_map/ppermute | solution.py:18
  30.0 9.9 %collective-permute-start.6 = (f32[24,8,128]{2,1,0:T(8,128)S(1)}, f32[24,8,128]{2,1,0:T(8,128)S(1)}, u32[]{:S(2)}, u32[]{:S(2)}) collective-permute-start(f32[24,8,128]{2,1,0:T(8,128)S(1)} %get-tuple-element.78), channel_id=1, source_target_pairs={{0,8},{8,16},{16,24},{24,0},{1,9},{9,17},{17,25},{25,1},{2,10},{10... | collective-permute-start | bytes 294920 | tf_op jit(solution)/shard_map/ppermute | solution.py:18
  32.0 8.5 %collective-permute-start.7 = (f32[24,8,128]{2,1,0:T(8,128)S(1)}, f32[24,8,128]{2,1,0:T(8,128)S(1)}, u32[]{:S(2)}, u32[]{:S(2)}) collective-permute-start(f32[24,8,128]{2,1,0:T(8,128)S(1)} %get-tuple-element.80), channel_id=1, source_target_pairs={{0,16},{8,24},{16,0},{24,8},{1,17},{9,25},{17,1},{25,9},{2,18},{10... | collective-permute-start | bytes 294920 | tf_op jit(solution)/shard_map/ppermute | solution.py:18
  35.6 4.9 %collective-permute-start.8 = (f32[24,8,128]{2,1,0:T(8,128)S(1)}, f32[24,8,128]{2,1,0:T(8,128)S(1)}, u32[]{:S(2)}, u32[]{:S(2)}) collective-permute-start(f32[24,8,128]{2,1,0:T(8,128)S(1)} %get-tuple-element.79), channel_id=1, source_target_pairs={{0,24},{8,0},{16,8},{24,16},{1,25},{9,1},{17,9},{25,17},{2,26},{10... | collective-permute-start | bytes 294920 | tf_op jit(solution)/shard_map/ppermute | solution.py:18
  36.6 9.6 %collective-permute-start.10 = (bf16[256,384]{1,0:T(8,128)(2,1)}, bf16[256,384]{1,0:T(8,128)(2,1)S(1)}, u32[]{:S(2)}, u32[]{:S(2)}) collective-permute-start(bf16[256,384]{1,0:T(8,128)(2,1)} %get-tuple-element.44), channel_id=1, source_target_pairs={{0,4},{2,6},{4,0},{6,2},{1,5},{3,7},{5,1},{7,3},{8,12},{10,14},{12... | collective-permute-start | bytes 589832 | tf_op jit(solution)/shard_map/ppermute | solution.py:18
  37.1 9.1 %collective-permute-start.11 = (bf16[256,384]{1,0:T(8,128)(2,1)}, bf16[256,384]{1,0:T(8,128)(2,1)S(1)}, u32[]{:S(2)}, u32[]{:S(2)}) collective-permute-start(bf16[256,384]{1,0:T(8,128)(2,1)} %get-tuple-element.45), channel_id=1, source_target_pairs={{0,6},{2,0},{4,2},{6,4},{1,7},{3,1},{5,3},{7,5},{8,14},{10,8},{12,... | collective-permute-start | bytes 589832 | tf_op jit(solution)/shard_map/ppermute | solution.py:18
  39.9 8.8 %collective-permute-start.9 = (bf16[256,384]{1,0:T(8,128)(2,1)S(1)}, bf16[256,384]{1,0:T(8,128)(2,1)S(1)}, u32[]{:S(2)}, u32[]{:S(2)}) collective-permute-start(bf16[256,384]{1,0:T(8,128)(2,1)S(1)} %copy-done.15), channel_id=1, source_target_pairs={{0,2},{2,4},{4,6},{6,0},{1,3},{3,5},{5,7},{7,1},{8,10},{10,12},{12... | collective-permute-start | bytes 589832 | tf_op jit(solution)/shard_map/ppermute | solution.py:18
  50.3 34.6 %copy-start.5 = (bf16[8,128,384]{2,1,0:T(8,128)(2,1)}, bf16[8,128,384]{2,1,0:T(8,128)(2,1)S(1)}, u32[]{:S(2)}) copy-start(bf16[8,128,384]{2,1,0:T(8,128)(2,1)S(1)} %unpack.1.refs_0_) | copy-start | bytes 2359300
  50.3 19.8 %collective-permute-start.18 = (bf16[8,128,384]{2,1,0:T(8,128)(2,1)S(1)}, bf16[8,128,384]{2,1,0:T(8,128)(2,1)S(1)}, u32[]{:S(2)}, u32[]{:S(2)}) collective-permute-start(bf16[8,128,384]{2,1,0:T(8,128)(2,1)S(1)} %unpack.1.refs_0_), channel_id=1, source_target_pairs={{0,8},{8,16},{16,24},{24,0},{1,9},{9,17},{17,25},{25,1},{2,10},{10... | collective-permute-start | bytes 2359304 | tf_op jit(solution)/shard_map/ppermute | solution.py:18
  51.4 18.7 %collective-permute-start.19 = (bf16[8,128,384]{2,1,0:T(8,128)(2,1)S(1)}, bf16[8,128,384]{2,1,0:T(8,128)(2,1)S(1)}, u32[]{:S(2)}, u32[]{:S(2)}) collective-permute-start(bf16[8,128,384]{2,1,0:T(8,128)(2,1)S(1)} %unpack.1.refs_0_), channel_id=1, source_target_pairs={{0,24},{8,0},{16,8},{24,16},{1,25},{9,1},{17,9},{25,17},{2,26},{10... | collective-permute-start | bytes 2359304 | tf_op jit(solution)/shard_map/ppermute | solution.py:18
  53.6 6.2 %collective-permute-start.12 = (f32[6,8,128]{2,1,0:T(8,128)S(1)}, f32[6,8,128]{2,1,0:T(8,128)S(1)}, u32[]{:S(2)}, u32[]{:S(2)}) collective-permute-start(f32[6,8,128]{2,1,0:T(8,128)S(1)} %get-tuple-element.92), channel_id=1, source_target_pairs={{0,32},{32,64},{64,96},{96,0},{1,33},{33,65},{65,97},{97,1},{2,34}... | collective-permute-start | bytes 73736 | tf_op jit(solution)/shard_map/ppermute | solution.py:18
  55.3 6.5 %collective-permute-start.13 = (f32[6,8,128]{2,1,0:T(8,128)S(1)}, f32[6,8,128]{2,1,0:T(8,128)S(1)}, u32[]{:S(2)}, u32[]{:S(2)}) collective-permute-start(f32[6,8,128]{2,1,0:T(8,128)S(1)} %get-tuple-element.94), channel_id=1, source_target_pairs={{0,64},{32,96},{64,0},{96,32},{1,65},{33,97},{65,1},{97,33},{2,66}... | collective-permute-start | bytes 73736 | tf_op jit(solution)/shard_map/ppermute | solution.py:18
  58.7 4.3 %collective-permute-start.14 = (f32[6,8,128]{2,1,0:T(8,128)S(1)}, f32[6,8,128]{2,1,0:T(8,128)S(1)}, u32[]{:S(2)}, u32[]{:S(2)}) collective-permute-start(f32[6,8,128]{2,1,0:T(8,128)S(1)} %get-tuple-element.93), channel_id=1, source_target_pairs={{0,96},{32,0},{64,32},{96,64},{1,97},{33,1},{65,33},{97,65},{2,98}... | collective-permute-start | bytes 73736 | tf_op jit(solution)/shard_map/ppermute | solution.py:18
  63.0 5.2 %collective-permute-start.15 = (f32[6,8,128]{2,1,0:T(8,128)S(1)}, f32[6,8,128]{2,1,0:T(8,128)S(1)}, u32[]{:S(2)}, u32[]{:S(2)}) collective-permute-start(f32[6,8,128]{2,1,0:T(8,128)S(1)} %fusion.30), channel_id=1, source_target_pairs={{0,2},{2,4},{4,6},{6,0},{1,3},{3,5},{5,7},{7,1},{8,10},{10,12},{12... | collective-permute-start | bytes 73736 | tf_op jit(solution)/shard_map/ppermute | solution.py:18
  63.1 5.7 %collective-permute-start.16 = (f32[6,8,128]{2,1,0:T(8,128)S(1)}, f32[6,8,128]{2,1,0:T(8,128)S(1)}, u32[]{:S(2)}, u32[]{:S(2)}) collective-permute-start(f32[6,8,128]{2,1,0:T(8,128)S(1)} %fusion.30), channel_id=1, source_target_pairs={{0,4},{2,6},{4,0},{6,2},{1,5},{3,7},{5,1},{7,3},{8,12},{10,14},{12... | collective-permute-start | bytes 73736 | tf_op jit(solution)/shard_map/ppermute | solution.py:18
  64.5 4.7 %collective-permute-start.17 = (f32[6,8,128]{2,1,0:T(8,128)S(1)}, f32[6,8,128]{2,1,0:T(8,128)S(1)}, u32[]{:S(2)}, u32[]{:S(2)}) collective-permute-start(f32[6,8,128]{2,1,0:T(8,128)S(1)} %fusion.30), channel_id=1, source_target_pairs={{0,6},{2,0},{4,2},{6,4},{1,7},{3,1},{5,3},{7,5},{8,14},{10,8},{12,... | collective-permute-start | bytes 73736 | tf_op jit(solution)/shard_map/ppermute | solution.py:18
  70.1 14.8 %copy-start.13 = (bf16[8,128,384]{2,1,0:T(8,128)(2,1)}, bf16[8,128,384]{2,1,0:T(8,128)(2,1)S(1)}, u32[]{:S(2)}) copy-start(bf16[8,128,384]{2,1,0:T(8,128)(2,1)S(1)} %collective-permute-done.18.refs_1_) | copy-start | bytes 2359300
  70.1 1.0 copy-start.14
  71.1 13.8 %collective-permute-start.22 = (bf16[4,4,384,384]{3,2,1,0:T(8,128)(2,1)}, bf16[4,4,384,384]{3,2,1,0:T(8,128)(2,1)}, u32[]{:S(2)}, u32[]{:S(2)}) collective-permute-start(bf16[4,4,384,384]{3,2,1,0:T(8,128)(2,1)} %bitcast.149), channel_id=1, source_target_pairs={{0,1},{1,0},{2,3},{3,2},{4,5},{5,4},{6,7},{7,6},{8,9},{9,8},{10,11... | collective-permute-start | bytes 14155784 | tf_op jit(solution)/shard_map/ppermute | solution.py:18
  71.2 12.9 %collective-permute-start.20 = (bf16[8,64,384]{2,1,0:T(8,128)(2,1)S(1)}, bf16[8,64,384]{2,1,0:T(8,128)(2,1)}, u32[]{:S(2)}, u32[]{:S(2)}) collective-permute-start(bf16[8,64,384]{2,1,0:T(8,128)(2,1)S(1)} %slice.93), channel_id=1, source_target_pairs={{0,8},{8,16},{16,24},{24,0},{1,9},{9,17},{17,25},{25,1},{2,10},{10... | collective-permute-start | bytes 1179656 | tf_op jit(solution)/shard_map/ppermute | solution.py:18
  72.3 12.6 %collective-permute-start.21 = (bf16[8,64,384]{2,1,0:T(8,128)(2,1)S(1)}, bf16[8,64,384]{2,1,0:T(8,128)(2,1)}, u32[]{:S(2)}, u32[]{:S(2)}) collective-permute-start(bf16[8,64,384]{2,1,0:T(8,128)(2,1)S(1)} %slice.94), channel_id=1, source_target_pairs={{0,24},{8,0},{16,8},{24,16},{1,25},{9,1},{17,9},{25,17},{2,26},{10... | collective-permute-start | bytes 1179656 | tf_op jit(solution)/shard_map/ppermute | solution.py:18
  76.4 18.6 %all-to-all-start = ((f32[16,6,8,128]{3,2,1,0:T(8,128)}), f32[16,6,8,128]{3,2,1,0:T(8,128)S(1)}, u32[]{:S(2)}, u32[]{:S(2)}) async-start(f32[16,6,8,128]{3,2,1,0:T(8,128)} %broadcast_in_dim.28), calls=%async_computation | async-start | bytes 786432 | tf_op jit(solution)/shard_map/all_to_all | solution.py:66
  95.0 1.8 %collective-permute-start.23 = (f32[96,8,128]{2,1,0:T(8,128)S(1)}, f32[96,8,128]{2,1,0:T(8,128)S(1)}, u32[]{:S(2)}, u32[]{:S(2)}) collective-permute-start(f32[96,8,128]{2,1,0:T(8,128)S(1)} %bitcast.138), channel_id=1, source_target_pairs={{0,1},{1,0},{2,3},{3,2},{4,5},{5,4},{6,7},{7,6},{8,9},{9,8},{10,11... | collective-permute-start | bytes 1179656 | tf_op jit(solution)/shard_map/ppermute | solution.py:18
  95.1 2.0 %copy-start.12 = (bf16[128,6144]{1,0:T(8,128)(2,1)S(1)}, bf16[128,6144]{1,0:T(8,128)(2,1)}, u32[]{:S(2)}) copy-start(bf16[128,6144]{1,0:T(8,128)(2,1)} %param.5) | copy-start | bytes 4718596
  96.9 0.9 copy-start.1
  97.8 6.3 %collective-permute-start.24 = (f32[32,128]{1,0:T(8,128)S(1)}, f32[32,128]{1,0:T(8,128)S(1)}, u32[]{:S(2)}, u32[]{:S(2)}) collective-permute-start(f32[32,128]{1,0:T(8,128)S(1)} %fusion.32), channel_id=1, source_target_pairs={{0,1},{1,0},{2,3},{3,2},{4,5},{5,4},{6,7},{7,6},{8,9},{9,8},{10,11... | collective-permute-start | bytes 49160 | tf_op jit(solution)/shard_map/ppermute | solution.py:18
  98.1 29.5 %collective-permute-start.31 = (bf16[128,1536]{1,0:T(8,128)(2,1)}, bf16[128,1536]{1,0:T(8,128)(2,1)S(1)}, u32[]{:S(2)}, u32[]{:S(2)}) collective-permute-start(bf16[128,1536]{1,0:T(8,128)(2,1)} %get-tuple-element.63), channel_id=1, source_target_pairs={{0,24},{8,0},{16,8},{24,16},{1,25},{9,1},{17,9},{25,17},{2,26},{10... | collective-permute-start | bytes 1179656 | tf_op jit(solution)/shard_map/ppermute | solution.py:18
  104.2 23.4 %collective-permute-start.32 = (bf16[128,1536]{1,0:T(8,128)(2,1)}, bf16[128,1536]{1,0:T(8,128)(2,1)S(1)}, u32[]{:S(2)}, u32[]{:S(2)}) collective-permute-start(bf16[128,1536]{1,0:T(8,128)(2,1)} %get-tuple-element.64), channel_id=1, source_target_pairs={{0,8},{8,16},{16,24},{24,0},{1,9},{9,17},{17,25},{25,1},{2,10},{10... | collective-permute-start | bytes 1179656 | tf_op jit(solution)/shard_map/ppermute | solution.py:18
  104.2 8.3 %collective-permute-start.25 = (f32[2,32,128]{2,1,0:T(8,128)S(1)}, f32[2,32,128]{2,1,0:T(8,128)S(1)}, u32[]{:S(2)}, u32[]{:S(2)}) collective-permute-start(f32[2,32,128]{2,1,0:T(8,128)S(1)} %pad_maximum_fusion.5), channel_id=1, source_target_pairs={{0,2},{2,4},{4,6},{6,0},{1,3},{3,5},{5,7},{7,1},{8,10},{10,12},{12... | collective-permute-start | bytes 98312 | tf_op jit(solution)/shard_map/ppermute | solution.py:18
  106.4 7.7 %collective-permute-start.26 = (f32[2,32,128]{2,1,0:T(8,128)S(1)}, f32[2,32,128]{2,1,0:T(8,128)S(1)}, u32[]{:S(2)}, u32[]{:S(2)}) collective-permute-start(f32[2,32,128]{2,1,0:T(8,128)S(1)} %pad_maximum_fusion.5), channel_id=1, source_target_pairs={{0,4},{2,6},{4,0},{6,2},{1,5},{3,7},{5,1},{7,3},{8,12},{10,14},{12... | collective-permute-start | bytes 98312 | tf_op jit(solution)/shard_map/ppermute | solution.py:18
  108.7 5.5 %collective-permute-start.27 = (f32[2,32,128]{2,1,0:T(8,128)S(1)}, f32[2,32,128]{2,1,0:T(8,128)S(1)}, u32[]{:S(2)}, u32[]{:S(2)}) collective-permute-start(f32[2,32,128]{2,1,0:T(8,128)S(1)} %pad_maximum_fusion.5), channel_id=1, source_target_pairs={{0,6},{2,0},{4,2},{6,4},{1,7},{3,1},{5,3},{7,5},{8,14},{10,8},{12,... | collective-permute-start | bytes 98312 | tf_op jit(solution)/shard_map/ppermute | solution.py:18
  112.4 20.3 %copy-start.6 = (bf16[128,1536]{1,0:T(8,128)(2,1)S(1)}, bf16[128,1536]{1,0:T(8,128)(2,1)}, u32[]{:S(2)}) copy-start(bf16[128,1536]{1,0:T(8,128)(2,1)} %get-tuple-element.69.refs_0_) | copy-start | bytes 1179652
  112.4 20.3 %copy-start.10 = (s32[12]{0:T(128)S(1)}, s32[12]{0:T(128)}, u32[]{:S(2)}) copy-start(s32[12]{0:T(128)} %stack.69.at_ref) | copy-start | bytes 148
  112.5 15.1 %collective-permute-start.33 = (bf16[128,1536]{1,0:T(8,128)(2,1)}, bf16[128,1536]{1,0:T(8,128)(2,1)S(1)}, u32[]{:S(2)}, u32[]{:S(2)}) collective-permute-start(bf16[128,1536]{1,0:T(8,128)(2,1)} %get-tuple-element.65), channel_id=1, source_target_pairs={{0,16},{8,24},{16,0},{24,8},{1,17},{9,25},{17,1},{25,9},{2,18},{10... | collective-permute-start | bytes 1179656 | tf_op jit(solution)/shard_map/ppermute | solution.py:18
  114.7 24.6 %copy-start.2 = (f32[2,96,8,128]{3,2,1,0:T(8,128)S(1)}, f32[2,96,8,128]{3,2,1,0:T(8,128)}, u32[]{:S(2)}) copy-start(f32[2,96,8,128]{3,2,1,0:T(8,128)} %copy-done.1) | copy-start | bytes 2359300
  114.7 5.8 %collective-permute-start.28 = (f32[32,384]{1,0:T(8,128)S(1)}, f32[32,384]{1,0:T(8,128)S(1)}, u32[]{:S(2)}, u32[]{:S(2)}) collective-permute-start(f32[32,384]{1,0:T(8,128)S(1)} %fusion.15), channel_id=1, source_target_pairs={{0,32},{32,64},{64,96},{96,0},{1,33},{33,65},{65,97},{97,1},{2,34}... | collective-permute-start | bytes 147464 | tf_op jit(solution)/shard_map/ppermute | solution.py:18
  116.8 10.7 %collective-permute-start.29 = (f32[32,384]{1,0:T(8,128)S(1)}, f32[32,384]{1,0:T(8,128)S(1)}, u32[]{:S(2)}, u32[]{:S(2)}) collective-permute-start(f32[32,384]{1,0:T(8,128)S(1)} %fusion.15), channel_id=1, source_target_pairs={{0,64},{32,96},{64,0},{96,32},{1,65},{33,97},{65,1},{97,33},{2,66}... | collective-permute-start | bytes 147464 | tf_op jit(solution)/shard_map/ppermute | solution.py:18
  120.5 7.0 %collective-permute-start.30 = (f32[32,384]{1,0:T(8,128)S(1)}, f32[32,384]{1,0:T(8,128)S(1)}, u32[]{:S(2)}, u32[]{:S(2)}) collective-permute-start(f32[32,384]{1,0:T(8,128)S(1)} %fusion.15), channel_id=1, source_target_pairs={{0,96},{32,0},{64,32},{96,64},{1,97},{33,1},{65,33},{97,65},{2,98}... | collective-permute-start | bytes 147464 | tf_op jit(solution)/shard_map/ppermute | solution.py:18
  127.5 8.0 %copy-start.8 = (f32[32,32]{1,0:T(8,128)S(1)}, f32[32,32]{1,0:T(8,128)}, u32[]{:S(2)}) copy-start(f32[32,32]{1,0:T(8,128)} %inverse_of_factor.1.inverse_ref) | copy-start | bytes 12292
  127.6 7.0 %collective-permute-start.34 = (f32[32,384]{1,0:T(8,128)S(1)}, f32[32,384]{1,0:T(8,128)S(1)}, u32[]{:S(2)}, u32[]{:S(2)}) collective-permute-start(f32[32,384]{1,0:T(8,128)S(1)} %add_add_fusion), channel_id=1, source_target_pairs={{0,8},{8,16},{16,24},{24,0},{1,9},{9,17},{17,25},{25,1},{2,10},{10... | collective-permute-start | bytes 147464 | tf_op jit(solution)/shard_map/ppermute | solution.py:18
  129.9 5.6 %collective-permute-start.35 = (f32[32,384]{1,0:T(8,128)S(1)}, f32[32,384]{1,0:T(8,128)S(1)}, u32[]{:S(2)}, u32[]{:S(2)}) collective-permute-start(f32[32,384]{1,0:T(8,128)S(1)} %add_add_fusion), channel_id=1, source_target_pairs={{0,16},{8,24},{16,0},{24,8},{1,17},{9,25},{17,1},{25,9},{2,18},{10... | collective-permute-start | bytes 147464 | tf_op jit(solution)/shard_map/ppermute | solution.py:18
  131.4 4.2 %collective-permute-start.36 = (f32[32,384]{1,0:T(8,128)S(1)}, f32[32,384]{1,0:T(8,128)S(1)}, u32[]{:S(2)}, u32[]{:S(2)}) collective-permute-start(f32[32,384]{1,0:T(8,128)S(1)} %add_add_fusion), channel_id=1, source_target_pairs={{0,24},{8,0},{16,8},{24,16},{1,25},{9,1},{17,9},{25,17},{2,26},{10... | collective-permute-start | bytes 147464 | tf_op jit(solution)/shard_map/ppermute | solution.py:18
  135.7 15.7 %copy-start.7 = (f32[32,384]{1,0:T(8,128)}, f32[32,384]{1,0:T(8,128)S(1)}, u32[]{:S(2)}) copy-start(f32[32,384]{1,0:T(8,128)S(1)} %convolution_multiply_fusion.factor_ref) | copy-start | bytes 147460
Sparse Core Ops, SparseCore 0:
  10.1 58.9 all-gather.5
  70.8 68.4 all-gather.3

commit v7 on v6

--- a/solution.py
+++ b/solution.py
@@ -323,7 +323,7 @@
     (input_grads,) = copy_call(functools.partial(place_plan, quarter), 4, back, [like(tok, d)], at, "place")
     sums = all_sum(sums, "z")
     factor = jnp.dot(inverse, sums, precision=lax.Precision.HIGHEST) * (1.0 / 16)
-    sizes = [d // 12 * w for w in (1, 2, 3, 3, 2, 1)] if d % 1536 == 0 else [d // 2] * 2
+    sizes = [d // 12 * w for w in (1, 2, 2, 2, 2, 2, 1)] if d % 1536 == 0 else [d // 2] * 2
     new_residual = residual_call(scale, gathered, cotangent, residual, left, inverse, factor, sizes)
     return factor.T, new_residual[None], input_grads
 

time: 160 us -> 161 us (level)
  no operation moved by 1% of the time
where the time goes in v7:
time: 161 us; the launch traced here: 159 us
  starting transfers between devices  63.1 us (39%)
  Pallas kernels  34.3 us (21%)
  waiting for transfers between devices  28.3 us (18%)
  between operations  14.8 us (9%)
  matrix products  10.2 us (6%)
  local copies, waits for them, and re-layouts  6.53 us (4%)
  other arithmetic  1.66 us (1%)
    ppermute x37, starting transfers between devices, shift(): return lax.ppermute(value, axis, [(i, (i + step) % n) for i in range(n)])  57.3 us
    ppermute x37, waiting for transfers between devices, shift(): return lax.ppermute(value, axis, [(i, (i + step) % n) for i in range(n)])  24.7 us
    pallas_call x1, Pallas kernels, residual_call(): pl.pallas_call(functools.partial(residual_kernel, scale, tuple(sizes)), o...  12.8 us
    pallas_call x1, Pallas kernels, input_call(): pl.pallas_call(functools.partial(input_kernel, len(cots)), out_shape=[jax...  10.1 us
    dot_general x6, matrix products, mm(): lax.dot_general(a, b, (((ca,), (cb,)), ((), ())), preferred_element_type=...  10 us
    pallas_call x3, Pallas kernels, copy_call(): pl.pallas_call(functools.partial(copy_kernel, len(ins), len(outs), plan),...  6.15 us
    all_to_all x1, starting transfers between devices, all_blocks(): lax.all_to_all(jnp.broadcast_to(value[None], (n,) + value.shape), axis, 0...  5.71 us
    pallas_call x1, Pallas kernels, inverse_of_factor(): pl.pallas_call(inverse_kernel, out_shape=jax.ShapeDtypeStruct((rank, rank...  5.22 us
  transfers between devices with their start and end apart: 40, of which 18 were waited for; matrix products, arithmetic and copies ran while one was open for 9% of the time, Pallas kernels for 14%

profile of v7, /device:TPU:0, one launch (start us, length us, event | category | flops | bytes accessed | tf_op | source)
XLA Modules:
  0.0 158.9 jit_solution(8183396531714942225)
XLA Ops:
  7.2 1.7 %constant_dynamic-slice_fusion = bf16[384,384]{1,0:T(8,128)(2,1)} fusion(bf16[6144,384]{1,0:T(8,128)(2,1)} %param.7, s32[]{:T(128)S(6)} %select_n.320), kind=kLoop, calls=%fused_computation.106 | loop fusion | bytes 589828 | tf_op jit(solution)/shard_map/dynamic_slice | solution.py:267
  9.2 0.8 reduce-precision_convert_fusion.5
  10.0 1.5 fusion.22
  11.7 1.6 %collective-permute-start = (f32[32,256]{1,0:T(8,128)S(1)}, f32[32,256]{1,0:T(8,128)S(1)}, u32[]{:S(2)}, u32[]{:S(2)}) collective-permute-start(f32[32,256]{1,0:T(8,128)S(1)} %bitcast.145), channel_id=1, source_target_pairs={{0,2},{2,4},{4,6},{6,0},{1,3},{3,5},{5,7},{7,1},{8,10},{10,12},{12... | collective-permute-start | bytes 98312 | tf_op jit(solution)/shard_map/ppermute | solution.py:18
  13.4 2.7 %collective-permute-start.1 = (f32[32,256]{1,0:T(8,128)S(1)}, f32[32,256]{1,0:T(8,128)S(1)}, u32[]{:S(2)}, u32[]{:S(2)}) collective-permute-start(f32[32,256]{1,0:T(8,128)S(1)} %bitcast.146), channel_id=1, source_target_pairs={{0,4},{2,6},{4,0},{6,2},{1,5},{3,7},{5,1},{7,3},{8,12},{10,14},{12... | collective-permute-start | bytes 98312 | tf_op jit(solution)/shard_map/ppermute | solution.py:18
  16.1 1.4 collective-permute-start.2
  17.6 3.9 %fusion.21 = f32[96,6144]{1,0:T(8,128)S(1)} fusion(bf16[32,384]{1,0:T(8,128)(2,1)S(1)} %get-tuple-element.96, bf16[32,384]{1,0:T(8,128)(2,1)S(1)} %get-tuple-element.97, bf16[32,384]{1,0:T(8,128)(2,1)S(1)} %get-tuple-element.95, bf16[1,6144,384]{2,1,0:T(8,128)(2,1)} %param.8), kind=kOutput, calls=%fused_computation.65 | convolution fusion | flops 453206016 | bytes 7151616 | tf_op jit(solution)/shard_map/dot_general | solution.py:41
  21.7 0.7 stack.69.at_ref
  22.4 0.9 copy-done.3
  23.3 2.6 %pack.1 = (bf16[256,384]{1,0:T(8,128)(2,1)}, bf16[256,384]{1,0:T(8,128)(2,1)}, bf16[256,384]{1,0:T(8,128)(2,1)}) custom-call(s32[12]{0:T(128)} %stack.69.at_ref, bf16[1024,384]{1,0:T(8,128)(2,1)} %cot_ref.1, bf16[1024,384]{1,0:T(8,128)(2,1)} %copy-done.3), custom_call_target="tpu_custom_call" | custom-call | bytes 1179648 | tf_op jit(solution)/shard_map/pack/pallas_call | solution.py:220
  26.2 1.2 collective-permute-done.4
  27.4 0.5 fusion.23
  28.4 1.6 collective-permute-done.5
  30.0 2.0 %collective-permute-start.6 = (f32[24,8,128]{2,1,0:T(8,128)S(1)}, f32[24,8,128]{2,1,0:T(8,128)S(1)}, u32[]{:S(2)}, u32[]{:S(2)}) collective-permute-start(f32[24,8,128]{2,1,0:T(8,128)S(1)} %get-tuple-element.78), channel_id=1, source_target_pairs={{0,8},{8,16},{16,24},{24,0},{1,9},{9,17},{17,25},{25,1},{2,10},{10... | collective-permute-start | bytes 294920 | tf_op jit(solution)/shard_map/ppermute | solution.py:18
  32.0 3.6 %collective-permute-start.7 = (f32[24,8,128]{2,1,0:T(8,128)S(1)}, f32[24,8,128]{2,1,0:T(8,128)S(1)}, u32[]{:S(2)}, u32[]{:S(2)}) collective-permute-start(f32[24,8,128]{2,1,0:T(8,128)S(1)} %get-tuple-element.80), channel_id=1, source_target_pairs={{0,16},{8,24},{16,0},{24,8},{1,17},{9,25},{17,1},{25,9},{2,18},{10... | collective-permute-start | bytes 294920 | tf_op jit(solution)/shard_map/ppermute | solution.py:18
  35.6 1.0 collective-permute-start.8
  36.6 0.5 collective-permute-start.10
  37.1 2.7 %collective-permute-start.11 = (bf16[256,384]{1,0:T(8,128)(2,1)}, bf16[256,384]{1,0:T(8,128)(2,1)S(1)}, u32[]{:S(2)}, u32[]{:S(2)}) collective-permute-start(bf16[256,384]{1,0:T(8,128)(2,1)} %get-tuple-element.45), channel_id=1, source_target_pairs={{0,6},{2,0},{4,2},{6,4},{1,7},{3,1},{5,3},{7,5},{8,14},{10,8},{12,... | collective-permute-start | bytes 589832 | tf_op jit(solution)/shard_map/ppermute | solution.py:18
  39.9 0.7 collective-permute-done.7
  40.5 5.6 %collective-permute-done.10.refs_3_ = bf16[256,384]{1,0:T(8,128)(2,1)S(1)} collective-permute-done((bf16[256,384]{1,0:T(8,128)(2,1)}, bf16[256,384]{1,0:T(8,128)(2,1)S(1)}, u32[]{:S(2)}, u32[]{:S(2)}) %collective-permute-start.10) | collective-permute-done | bytes 196640 | tf_op jit(solution)/shard_map/ppermute | solution.py:18
  46.3 2.4 %collective-permute-done.9.refs_2_ = bf16[256,384]{1,0:T(8,128)(2,1)S(1)} collective-permute-done((bf16[256,384]{1,0:T(8,128)(2,1)S(1)}, bf16[256,384]{1,0:T(8,128)(2,1)S(1)}, u32[]{:S(2)}, u32[]{:S(2)}) %collective-permute-start.9) | collective-permute-done | bytes 196640 | tf_op jit(solution)/shard_map/ppermute | solution.py:18
  48.7 1.6 %unpack.1.refs_0_ = bf16[8,128,384]{2,1,0:T(8,128)(2,1)S(1)} custom-call(s32[12]{0:T(128)S(1)} %copy-done.9, bf16[1024,384]{1,0:T(8,128)(2,1)S(1)} %copy-done, bf16[1024,384]{1,0:T(8,128)(2,1)S(1)} %copy-done.4, bf16[256,384]{1,0:T(8,128)(2,1)S(1)} %collective-permute-done.9.refs_2_, bf16[256,384]{1,0:T(8,128)(2,1)S(1)} %collective-permute-done.10.refs_3_, ...), custom_call_target="tpu_custom_call" | custom-call | bytes 1572864 | tf_op jit(solution)/shard_map/unpack/pallas_call | solution.py:220
  50.3 1.1 collective-permute-start.18
  51.4 2.2 %collective-permute-start.19 = (bf16[8,128,384]{2,1,0:T(8,128)(2,1)S(1)}, bf16[8,128,384]{2,1,0:T(8,128)(2,1)S(1)}, u32[]{:S(2)}, u32[]{:S(2)}) collective-permute-start(bf16[8,128,384]{2,1,0:T(8,128)(2,1)S(1)} %unpack.1.refs_0_), channel_id=1, source_target_pairs={{0,24},{8,0},{16,8},{24,16},{1,25},{9,1},{17,9},{25,17},{2,26},{10... | collective-permute-start | bytes 2359304 | tf_op jit(solution)/shard_map/ppermute | solution.py:18
  53.6 1.7 %collective-permute-start.12 = (f32[6,8,128]{2,1,0:T(8,128)S(1)}, f32[6,8,128]{2,1,0:T(8,128)S(1)}, u32[]{:S(2)}, u32[]{:S(2)}) collective-permute-start(f32[6,8,128]{2,1,0:T(8,128)S(1)} %get-tuple-element.92), channel_id=1, source_target_pairs={{0,32},{32,64},{64,96},{96,0},{1,33},{33,65},{65,97},{97,1},{2,34}... | collective-permute-start | bytes 73736 | tf_op jit(solution)/shard_map/ppermute | solution.py:18
  55.3 3.4 %collective-permute-start.13 = (f32[6,8,128]{2,1,0:T(8,128)S(1)}, f32[6,8,128]{2,1,0:T(8,128)S(1)}, u32[]{:S(2)}, u32[]{:S(2)}) collective-permute-start(f32[6,8,128]{2,1,0:T(8,128)S(1)} %get-tuple-element.94), channel_id=1, source_target_pairs={{0,64},{32,96},{64,0},{96,32},{1,65},{33,97},{65,1},{97,33},{2,66}... | collective-permute-start | bytes 73736 | tf_op jit(solution)/shard_map/ppermute | solution.py:18
  58.7 1.2 collective-permute-start.14
  59.8 1.9 %collective-permute-done.13 = f32[6,8,128]{2,1,0:T(8,128)S(1)} collective-permute-done((f32[6,8,128]{2,1,0:T(8,128)S(1)}, f32[6,8,128]{2,1,0:T(8,128)S(1)}, u32[]{:S(2)}, u32[]{:S(2)}) %collective-permute-start.13) | collective-permute-done | bytes 24608 | tf_op jit(solution)/shard_map/ppermute | solution.py:18
  61.8 1.2 collective-permute-done.14
  63.1 1.4 collective-permute-start.16
  64.5 1.9 %collective-permute-start.17 = (f32[6,8,128]{2,1,0:T(8,128)S(1)}, f32[6,8,128]{2,1,0:T(8,128)S(1)}, u32[]{:S(2)}, u32[]{:S(2)}) collective-permute-start(f32[6,8,128]{2,1,0:T(8,128)S(1)} %fusion.30), channel_id=1, source_target_pairs={{0,6},{2,0},{4,2},{6,4},{1,7},{3,1},{5,3},{7,5},{8,14},{10,8},{12,... | collective-permute-start | bytes 73736 | tf_op jit(solution)/shard_map/ppermute | solution.py:18
  66.5 1.8 %collective-permute-done.15 = f32[6,8,128]{2,1,0:T(8,128)S(1)} collective-permute-done((f32[6,8,128]{2,1,0:T(8,128)S(1)}, f32[6,8,128]{2,1,0:T(8,128)S(1)}, u32[]{:S(2)}, u32[]{:S(2)}) %collective-permute-start.15) | collective-permute-done | bytes 24608 | tf_op jit(solution)/shard_map/ppermute | solution.py:18
  68.3 0.5 collective-permute-done.16
  68.8 0.5 collective-permute-done.17
  69.3 0.9 collective-permute-done.18.refs_1_
  70.2 0.9 copy-done.14
  71.2 1.0 slice.94
  72.3 3.3 %collective-permute-start.21 = (bf16[8,64,384]{2,1,0:T(8,128)(2,1)S(1)}, bf16[8,64,384]{2,1,0:T(8,128)(2,1)}, u32[]{:S(2)}, u32[]{:S(2)}) collective-permute-start(bf16[8,64,384]{2,1,0:T(8,128)(2,1)S(1)} %slice.94), channel_id=1, source_target_pairs={{0,24},{8,0},{16,8},{24,16},{1,25},{9,1},{17,9},{25,17},{2,26},{10... | collective-permute-start | bytes 1179656 | tf_op jit(solution)/shard_map/ppermute | solution.py:18
  75.6 0.8 broadcast_in_dim.28
  76.4 5.7 %all-to-all-start = ((f32[16,6,8,128]{3,2,1,0:T(8,128)}), f32[16,6,8,128]{3,2,1,0:T(8,128)S(1)}, u32[]{:S(2)}, u32[]{:S(2)}) async-start(f32[16,6,8,128]{3,2,1,0:T(8,128)} %broadcast_in_dim.28), calls=%async_computation | async-start | bytes 786432 | tf_op jit(solution)/shard_map/all_to_all | solution.py:66
  82.1 2.0 %collective-permute-done.20.refs_3_ = bf16[8,64,384]{2,1,0:T(8,128)(2,1)} collective-permute-done((bf16[8,64,384]{2,1,0:T(8,128)(2,1)S(1)}, bf16[8,64,384]{2,1,0:T(8,128)(2,1)}, u32[]{:S(2)}, u32[]{:S(2)}) %collective-permute-start.20) | collective-permute-done | bytes 393248 | tf_op jit(solution)/shard_map/ppermute | solution.py:18
  84.1 0.8 collective-permute-done.21.refs_4_
  84.9 10.1 %input_grads.1 = (bf16[128,1536]{1,0:T(8,128)(2,1)}, bf16[128,1536]{1,0:T(8,128)(2,1)}, bf16[128,1536]{1,0:T(8,128)(2,1)}, bf16[128,1536]{1,0:T(8,128)(2,1)}) custom-call(s32[12]{0:T(128)} %stack.69.at_ref, bf16[8,128,384]{2,1,0:T(8,128)(2,1)} %copy-done.5, bf16[8,128,384]{2,1,0:T(8,128)(2,1)} %copy-done.13, bf16[8,128,384]{2,1,0:T(8,128)(2,1)} %copy-done.14, ...), custom_call_target="tpu_custom_call" | custom-call | flops 4831838208 | bytes 12582912 | tf_op jit(solution)/shard_map/input_grads/pallas_call | solution.py:190
  95.1 1.7 %collective-permute-done.23 = f32[96,8,128]{2,1,0:T(8,128)S(1)} collective-permute-done((f32[96,8,128]{2,1,0:T(8,128)S(1)}, f32[96,8,128]{2,1,0:T(8,128)S(1)}, u32[]{:S(2)}, u32[]{:S(2)}) %collective-permute-start.23) | collective-permute-done | bytes 393248 | tf_op jit(solution)/shard_map/ppermute | solution.py:18
  97.1 0.7 fusion.3
  98.1 6.1 %collective-permute-start.31 = (bf16[128,1536]{1,0:T(8,128)(2,1)}, bf16[128,1536]{1,0:T(8,128)(2,1)S(1)}, u32[]{:S(2)}, u32[]{:S(2)}) collective-permute-start(bf16[128,1536]{1,0:T(8,128)(2,1)} %get-tuple-element.63), channel_id=1, source_target_pairs={{0,24},{8,0},{16,8},{24,16},{1,25},{9,1},{17,9},{25,17},{2,26},{10... | collective-permute-start | bytes 1179656 | tf_op jit(solution)/shard_map/ppermute | solution.py:18
  104.2 2.3 %collective-permute-start.25 = (f32[2,32,128]{2,1,0:T(8,128)S(1)}, f32[2,32,128]{2,1,0:T(8,128)S(1)}, u32[]{:S(2)}, u32[]{:S(2)}) collective-permute-start(f32[2,32,128]{2,1,0:T(8,128)S(1)} %pad_maximum_fusion.5), channel_id=1, source_target_pairs={{0,2},{2,4},{4,6},{6,0},{1,3},{3,5},{5,7},{7,1},{8,10},{10,12},{12... | collective-permute-start | bytes 98312 | tf_op jit(solution)/shard_map/ppermute | solution.py:18
  106.4 2.3 %collective-permute-start.26 = (f32[2,32,128]{2,1,0:T(8,128)S(1)}, f32[2,32,128]{2,1,0:T(8,128)S(1)}, u32[]{:S(2)}, u32[]{:S(2)}) collective-permute-start(f32[2,32,128]{2,1,0:T(8,128)S(1)} %pad_maximum_fusion.5), channel_id=1, source_target_pairs={{0,4},{2,6},{4,0},{6,2},{1,5},{3,7},{5,1},{7,3},{8,12},{10,14},{12... | collective-permute-start | bytes 98312 | tf_op jit(solution)/shard_map/ppermute | solution.py:18
  108.7 0.5 collective-permute-start.27
  109.2 3.2 %fusion.2 = f32[96,384]{1,0:T(8,128)S(1)} fusion(bf16[32,6144]{1,0:T(8,128)(2,1)S(1)} %get-tuple-element.74, bf16[32,6144]{1,0:T(8,128)(2,1)S(1)} %get-tuple-element.75, bf16[32,6144]{1,0:T(8,128)(2,1)S(1)} %get-tuple-element.73, bf16[1,6144,384]{2,1,0:T(8,128)(2,1)} %param.8), kind=kOutput, calls=%fused_computation.13 | convolution fusion | flops 456523776 | bytes 6045696 | tf_op jit(solution)/shard_map/dot_general | solution.py:41
  112.5 1.7 %collective-permute-start.33 = (bf16[128,1536]{1,0:T(8,128)(2,1)}, bf16[128,1536]{1,0:T(8,128)(2,1)S(1)}, u32[]{:S(2)}, u32[]{:S(2)}) collective-permute-start(bf16[128,1536]{1,0:T(8,128)(2,1)} %get-tuple-element.65), channel_id=1, source_target_pairs={{0,16},{8,24},{16,0},{24,8},{1,17},{9,25},{17,1},{25,9},{2,18},{10... | collective-permute-start | bytes 1179656 | tf_op jit(solution)/shard_map/ppermute | solution.py:18
  114.4 0.3 fusion.4
  114.7 2.1 %collective-permute-start.28 = (f32[32,384]{1,0:T(8,128)S(1)}, f32[32,384]{1,0:T(8,128)S(1)}, u32[]{:S(2)}, u32[]{:S(2)}) collective-permute-start(f32[32,384]{1,0:T(8,128)S(1)} %fusion.15), channel_id=1, source_target_pairs={{0,32},{32,64},{64,96},{96,0},{1,33},{33,65},{65,97},{97,1},{2,34}... | collective-permute-start | bytes 147464 | tf_op jit(solution)/shard_map/ppermute | solution.py:18
  116.8 2.9 %collective-permute-start.29 = (f32[32,384]{1,0:T(8,128)S(1)}, f32[32,384]{1,0:T(8,128)S(1)}, u32[]{:S(2)}, u32[]{:S(2)}) collective-permute-start(f32[32,384]{1,0:T(8,128)S(1)} %fusion.15), channel_id=1, source_target_pairs={{0,64},{32,96},{64,0},{96,32},{1,65},{33,97},{65,1},{97,33},{2,66}... | collective-permute-start | bytes 147464 | tf_op jit(solution)/shard_map/ppermute | solution.py:18
  119.7 0.9 collective-permute-done.28
  120.5 1.8 %collective-permute-start.30 = (f32[32,384]{1,0:T(8,128)S(1)}, f32[32,384]{1,0:T(8,128)S(1)}, u32[]{:S(2)}, u32[]{:S(2)}) collective-permute-start(f32[32,384]{1,0:T(8,128)S(1)} %fusion.15), channel_id=1, source_target_pairs={{0,96},{32,0},{64,32},{96,64},{1,97},{33,1},{65,33},{97,65},{2,98}... | collective-permute-start | bytes 147464 | tf_op jit(solution)/shard_map/ppermute | solution.py:18
  122.3 5.2 %inverse_of_factor.1.inverse_ref = f32[32,32]{1,0:T(8,128)} custom-call(f32[32,6144]{1,0:T(8,128)} %bitcast.131), custom_call_target="tpu_custom_call" | custom-call | tf_op jit(solution)/shard_map/inverse_of_factor/pallas_call | solution.py:97
  127.6 2.4 %collective-permute-start.34 = (f32[32,384]{1,0:T(8,128)S(1)}, f32[32,384]{1,0:T(8,128)S(1)}, u32[]{:S(2)}, u32[]{:S(2)}) collective-permute-start(f32[32,384]{1,0:T(8,128)S(1)} %add_add_fusion), channel_id=1, source_target_pairs={{0,8},{8,16},{16,24},{24,0},{1,9},{9,17},{17,25},{25,1},{2,10},{10... | collective-permute-start | bytes 147464 | tf_op jit(solution)/shard_map/ppermute | solution.py:18
  129.9 1.4 collective-permute-start.35
  131.4 1.4 collective-permute-start.36
  132.7 1.9 %place.1 = bf16[128,6144]{1,0:T(8,128)(2,1)} custom-call(s32[12]{0:T(128)S(1)} %copy-done.10, bf16[128,1536]{1,0:T(8,128)(2,1)S(1)} %copy-done.6, bf16[128,1536]{1,0:T(8,128)(2,1)S(1)} %collective-permute-done.31.refs_1_, bf16[128,1536]{1,0:T(8,128)(2,1)S(1)} %collective-permute-done.32.refs_2_, bf16[128,1536]{1,0:T(8,128)(2,1)S(1)} %collective-permute-done.33.refs_3_), custom_call_target="tpu_custom_call" | custom-call | bytes 3145728 | tf_op jit(solution)/shard_map/place/pallas_call | solution.py:220
  134.6 0.9 collective-permute-done.35
  135.7 3.5 %all-gather.4.cloned.1.call-done.act_ref = bf16[1024,6144]{1,0:T(8,128)(2,1)} async-done(((bf16[128,6144]{1,0:T(8,128)(2,1)}), bf16[1024,6144]{1,0:T(8,128)(2,1)}) %all-gather.4.cloned.1.call-update) | async-done | bytes 12582928 | tf_op jit(solution)/shard_map/all_gather | solution.py:281
  139.3 12.8 %new_residual.1 = bf16[6144,384]{1,0:T(8,128)(2,1)} custom-call(bf16[1024,6144]{1,0:T(8,128)(2,1)} %all-gather.4.cloned.1.call-done.act_ref, bf16[1024,384]{1,0:T(8,128)(2,1)S(1)} %copy-done, bf16[6144,384]{1,0:T(8,128)(2,1)} %bitcast.134, f32[32,6144]{1,0:T(8,128)S(1)} %bitcast.132, f32[32,32]{1,0:T(8,128)S(1)} %copy-done.8, ...), custom_call_target="tpu_custom_call" | custom-call | flops 5737807872 | bytes 22806528 | tf_op jit(solution)/shard_map/new_residual/pallas_call | solution.py:154
  (107 shorter events, 2.7 us)
Async XLA Ops:
  7.2 63.0 %all-gather.6.cloned.1.call-start = ((), (), s32[]{:S(2)}) async-start(), calls=%async_computation.2 | async-start | bytes 5013504 | tf_op jit(solution)/shard_map/all_gather | solution.py:268
  9.0 130.3 %all-gather.4.cloned.1.call-start = ((), (), s32[]{:S(2)}) async-start(), calls=%async_computation.1 | async-start | bytes 14155776 | tf_op jit(solution)/shard_map/all_gather | solution.py:281
  9.0 13.4 %collective-permute-start.3 = (bf16[1024,384]{1,0:T(8,128)(2,1)}, bf16[1024,384]{1,0:T(8,128)(2,1)S(1)}, u32[]{:S(2)}, u32[]{:S(2)}) collective-permute-start(bf16[1024,384]{1,0:T(8,128)(2,1)} %cot_ref.1), channel_id=1, source_target_pairs={{0,1},{1,0},{2,3},{3,2},{4,5},{5,4},{6,7},{7,6},{8,9},{9,8},{10,11... | collective-permute-start | bytes 2359304 | tf_op jit(solution)/shard_map/ppermute | solution.py:18
  11.7 10.7 %collective-permute-start = (f32[32,256]{1,0:T(8,128)S(1)}, f32[32,256]{1,0:T(8,128)S(1)}, u32[]{:S(2)}, u32[]{:S(2)}) collective-permute-start(f32[32,256]{1,0:T(8,128)S(1)} %bitcast.145), channel_id=1, source_target_pairs={{0,2},{2,4},{4,6},{6,0},{1,3},{3,5},{5,7},{7,1},{8,10},{10,12},{12... | collective-permute-start | bytes 98312 | tf_op jit(solution)/shard_map/ppermute | solution.py:18
  13.4 9.0 %collective-permute-start.1 = (f32[32,256]{1,0:T(8,128)S(1)}, f32[32,256]{1,0:T(8,128)S(1)}, u32[]{:S(2)}, u32[]{:S(2)}) collective-permute-start(f32[32,256]{1,0:T(8,128)S(1)} %bitcast.146), channel_id=1, source_target_pairs={{0,4},{2,6},{4,0},{6,2},{1,5},{3,7},{5,1},{7,3},{8,12},{10,14},{12... | collective-permute-start | bytes 98312 | tf_op jit(solution)/shard_map/ppermute | solution.py:18
  16.1 6.3 %collective-permute-start.2 = (f32[32,256]{1,0:T(8,128)S(1)}, f32[32,256]{1,0:T(8,128)S(1)}, u32[]{:S(2)}, u32[]{:S(2)}) collective-permute-start(f32[32,256]{1,0:T(8,128)S(1)} %bitcast.147), channel_id=1, source_target_pairs={{0,6},{2,0},{4,2},{6,4},{1,7},{3,1},{5,3},{7,5},{8,14},{10,8},{12,... | collective-permute-start | bytes 98312 | tf_op jit(solution)/shard_map/ppermute | solution.py:18
  21.6 5.8 %copy-start.11 = (bf16[128,6144]{1,0:T(8,128)(2,1)S(1)}, bf16[128,6144]{1,0:T(8,128)(2,1)}, u32[]{:S(2)}) copy-start(bf16[128,6144]{1,0:T(8,128)(2,1)} %param.5) | copy-start | bytes 4718596
  22.4 0.9 copy-start.3
  26.1 1.3 collective-permute-start.4
  27.8 12.0 %copy-start.15 = (bf16[256,384]{1,0:T(8,128)(2,1)S(1)}, bf16[256,384]{1,0:T(8,128)(2,1)}, u32[]{:S(2)}) copy-start(bf16[256,384]{1,0:T(8,128)(2,1)} %get-tuple-element.43) | copy-start | bytes 589828
  28.0 20.6 %copy-start = (bf16[1024,384]{1,0:T(8,128)(2,1)S(1)}, bf16[1024,384]{1,0:T(8,128)(2,1)}, u32[]{:S(2)}) copy-start(bf16[1024,384]{1,0:T(8,128)(2,1)} %cot_ref.1) | copy-start | bytes 2359300
  28.0 20.6 %copy-start.4 = (bf16[1024,384]{1,0:T(8,128)(2,1)S(1)}, bf16[1024,384]{1,0:T(8,128)(2,1)}, u32[]{:S(2)}) copy-start(bf16[1024,384]{1,0:T(8,128)(2,1)} %copy-done.3) | copy-start | bytes 2359300
  28.1 20.6 %copy-start.9 = (s32[12]{0:T(128)S(1)}, s32[12]{0:T(128)}, u32[]{:S(2)}) copy-start(s32[12]{0:T(128)} %stack.69.at_ref) | copy-start | bytes 148
  28.1 1.8 %collective-permute-start.5 = (f32[96,8,128]{2,1,0:T(8,128)S(1)}, f32[96,8,128]{2,1,0:T(8,128)S(1)}, u32[]{:S(2)}, u32[]{:S(2)}) collective-permute-start(f32[96,8,128]{2,1,0:T(8,128)S(1)} %dynamic-slice_bitcast_fusion), channel_id=1, source_target_pairs={{0,1},{1,0},{2,3},{3,2},{4,5},{5,4},{6,7},{7,6},{8,9},{9,8},{10,11... | collective-permute-start | bytes 1179656 | tf_op jit(solution)/shard_map/ppermute | solution.py:18
  30.0 9.9 %collective-permute-start.6 = (f32[24,8,128]{2,1,0:T(8,128)S(1)}, f32[24,8,128]{2,1,0:T(8,128)S(1)}, u32[]{:S(2)}, u32[]{:S(2)}) collective-permute-start(f32[24,8,128]{2,1,0:T(8,128)S(1)} %get-tuple-element.78), channel_id=1, source_target_pairs={{0,8},{8,16},{16,24},{24,0},{1,9},{9,17},{17,25},{25,1},{2,10},{10... | collective-permute-start | bytes 294920 | tf_op jit(solution)/shard_map/ppermute | solution.py:18
  32.0 8.5 %collective-permute-start.7 = (f32[24,8,128]{2,1,0:T(8,128)S(1)}, f32[24,8,128]{2,1,0:T(8,128)S(1)}, u32[]{:S(2)}, u32[]{:S(2)}) collective-permute-start(f32[24,8,128]{2,1,0:T(8,128)S(1)} %get-tuple-element.80), channel_id=1, source_target_pairs={{0,16},{8,24},{16,0},{24,8},{1,17},{9,25},{17,1},{25,9},{2,18},{10... | collective-permute-start | bytes 294920 | tf_op jit(solution)/shard_map/ppermute | solution.py:18
  35.6 4.9 %collective-permute-start.8 = (f32[24,8,128]{2,1,0:T(8,128)S(1)}, f32[24,8,128]{2,1,0:T(8,128)S(1)}, u32[]{:S(2)}, u32[]{:S(2)}) collective-permute-start(f32[24,8,128]{2,1,0:T(8,128)S(1)} %get-tuple-element.79), channel_id=1, source_target_pairs={{0,24},{8,0},{16,8},{24,16},{1,25},{9,1},{17,9},{25,17},{2,26},{10... | collective-permute-start | bytes 294920 | tf_op jit(solution)/shard_map/ppermute | solution.py:18
  36.6 9.6 %collective-permute-start.10 = (bf16[256,384]{1,0:T(8,128)(2,1)}, bf16[256,384]{1,0:T(8,128)(2,1)S(1)}, u32[]{:S(2)}, u32[]{:S(2)}) collective-permute-start(bf16[256,384]{1,0:T(8,128)(2,1)} %get-tuple-element.44), channel_id=1, source_target_pairs={{0,4},{2,6},{4,0},{6,2},{1,5},{3,7},{5,1},{7,3},{8,12},{10,14},{12... | collective-permute-start | bytes 589832 | tf_op jit(solution)/shard_map/ppermute | solution.py:18
  37.1 9.1 %collective-permute-start.11 = (bf16[256,384]{1,0:T(8,128)(2,1)}, bf16[256,384]{1,0:T(8,128)(2,1)S(1)}, u32[]{:S(2)}, u32[]{:S(2)}) collective-permute-start(bf16[256,384]{1,0:T(8,128)(2,1)} %get-tuple-element.45), channel_id=1, source_target_pairs={{0,6},{2,0},{4,2},{6,4},{1,7},{3,1},{5,3},{7,5},{8,14},{10,8},{12,... | collective-permute-start | bytes 589832 | tf_op jit(solution)/shard_map/ppermute | solution.py:18
  39.9 8.8 %collective-permute-start.9 = (bf16[256,384]{1,0:T(8,128)(2,1)S(1)}, bf16[256,384]{1,0:T(8,128)(2,1)S(1)}, u32[]{:S(2)}, u32[]{:S(2)}) collective-permute-start(bf16[256,384]{1,0:T(8,128)(2,1)S(1)} %copy-done.15), channel_id=1, source_target_pairs={{0,2},{2,4},{4,6},{6,0},{1,3},{3,5},{5,7},{7,1},{8,10},{10,12},{12... | collective-permute-start | bytes 589832 | tf_op jit(solution)/shard_map/ppermute | solution.py:18
  50.3 34.6 %copy-start.5 = (bf16[8,128,384]{2,1,0:T(8,128)(2,1)}, bf16[8,128,384]{2,1,0:T(8,128)(2,1)S(1)}, u32[]{:S(2)}) copy-start(bf16[8,128,384]{2,1,0:T(8,128)(2,1)S(1)} %unpack.1.refs_0_) | copy-start | bytes 2359300
  50.3 19.8 %collective-permute-start.18 = (bf16[8,128,384]{2,1,0:T(8,128)(2,1)S(1)}, bf16[8,128,384]{2,1,0:T(8,128)(2,1)S(1)}, u32[]{:S(2)}, u32[]{:S(2)}) collective-permute-start(bf16[8,128,384]{2,1,0:T(8,128)(2,1)S(1)} %unpack.1.refs_0_), channel_id=1, source_target_pairs={{0,8},{8,16},{16,24},{24,0},{1,9},{9,17},{17,25},{25,1},{2,10},{10... | collective-permute-start | bytes 2359304 | tf_op jit(solution)/shard_map/ppermute | solution.py:18
  51.4 18.7 %collective-permute-start.19 = (bf16[8,128,384]{2,1,0:T(8,128)(2,1)S(1)}, bf16[8,128,384]{2,1,0:T(8,128)(2,1)S(1)}, u32[]{:S(2)}, u32[]{:S(2)}) collective-permute-start(bf16[8,128,384]{2,1,0:T(8,128)(2,1)S(1)} %unpack.1.refs_0_), channel_id=1, source_target_pairs={{0,24},{8,0},{16,8},{24,16},{1,25},{9,1},{17,9},{25,17},{2,26},{10... | collective-permute-start | bytes 2359304 | tf_op jit(solution)/shard_map/ppermute | solution.py:18
  53.6 6.2 %collective-permute-start.12 = (f32[6,8,128]{2,1,0:T(8,128)S(1)}, f32[6,8,128]{2,1,0:T(8,128)S(1)}, u32[]{:S(2)}, u32[]{:S(2)}) collective-permute-start(f32[6,8,128]{2,1,0:T(8,128)S(1)} %get-tuple-element.92), channel_id=1, source_target_pairs={{0,32},{32,64},{64,96},{96,0},{1,33},{33,65},{65,97},{97,1},{2,34}... | collective-permute-start | bytes 73736 | tf_op jit(solution)/shard_map/ppermute | solution.py:18
  55.3 6.5 %collective-permute-start.13 = (f32[6,8,128]{2,1,0:T(8,128)S(1)}, f32[6,8,128]{2,1,0:T(8,128)S(1)}, u32[]{:S(2)}, u32[]{:S(2)}) collective-permute-start(f32[6,8,128]{2,1,0:T(8,128)S(1)} %get-tuple-element.94), channel_id=1, source_target_pairs={{0,64},{32,96},{64,0},{96,32},{1,65},{33,97},{65,1},{97,33},{2,66}... | collective-permute-start | bytes 73736 | tf_op jit(solution)/shard_map/ppermute | solution.py:18
  58.7 4.3 %collective-permute-start.14 = (f32[6,8,128]{2,1,0:T(8,128)S(1)}, f32[6,8,128]{2,1,0:T(8,128)S(1)}, u32[]{:S(2)}, u32[]{:S(2)}) collective-permute-start(f32[6,8,128]{2,1,0:T(8,128)S(1)} %get-tuple-element.93), channel_id=1, source_target_pairs={{0,96},{32,0},{64,32},{96,64},{1,97},{33,1},{65,33},{97,65},{2,98}... | collective-permute-start | bytes 73736 | tf_op jit(solution)/shard_map/ppermute | solution.py:18
  63.0 5.2 %collective-permute-start.15 = (f32[6,8,128]{2,1,0:T(8,128)S(1)}, f32[6,8,128]{2,1,0:T(8,128)S(1)}, u32[]{:S(2)}, u32[]{:S(2)}) collective-permute-start(f32[6,8,128]{2,1,0:T(8,128)S(1)} %fusion.30), channel_id=1, source_target_pairs={{0,2},{2,4},{4,6},{6,0},{1,3},{3,5},{5,7},{7,1},{8,10},{10,12},{12... | collective-permute-start | bytes 73736 | tf_op jit(solution)/shard_map/ppermute | solution.py:18
  63.1 5.7 %collective-permute-start.16 = (f32[6,8,128]{2,1,0:T(8,128)S(1)}, f32[6,8,128]{2,1,0:T(8,128)S(1)}, u32[]{:S(2)}, u32[]{:S(2)}) collective-permute-start(f32[6,8,128]{2,1,0:T(8,128)S(1)} %fusion.30), channel_id=1, source_target_pairs={{0,4},{2,6},{4,0},{6,2},{1,5},{3,7},{5,1},{7,3},{8,12},{10,14},{12... | collective-permute-start | bytes 73736 | tf_op jit(solution)/shard_map/ppermute | solution.py:18
  64.5 4.7 %collective-permute-start.17 = (f32[6,8,128]{2,1,0:T(8,128)S(1)}, f32[6,8,128]{2,1,0:T(8,128)S(1)}, u32[]{:S(2)}, u32[]{:S(2)}) collective-permute-start(f32[6,8,128]{2,1,0:T(8,128)S(1)} %fusion.30), channel_id=1, source_target_pairs={{0,6},{2,0},{4,2},{6,4},{1,7},{3,1},{5,3},{7,5},{8,14},{10,8},{12,... | collective-permute-start | bytes 73736 | tf_op jit(solution)/shard_map/ppermute | solution.py:18
  70.1 14.8 %copy-start.13 = (bf16[8,128,384]{2,1,0:T(8,128)(2,1)}, bf16[8,128,384]{2,1,0:T(8,128)(2,1)S(1)}, u32[]{:S(2)}) copy-start(bf16[8,128,384]{2,1,0:T(8,128)(2,1)S(1)} %collective-permute-done.18.refs_1_) | copy-start | bytes 2359300
  70.1 1.0 copy-start.14
  71.1 13.8 %collective-permute-start.22 = (bf16[4,4,384,384]{3,2,1,0:T(8,128)(2,1)}, bf16[4,4,384,384]{3,2,1,0:T(8,128)(2,1)}, u32[]{:S(2)}, u32[]{:S(2)}) collective-permute-start(bf16[4,4,384,384]{3,2,1,0:T(8,128)(2,1)} %bitcast.149), channel_id=1, source_target_pairs={{0,1},{1,0},{2,3},{3,2},{4,5},{5,4},{6,7},{7,6},{8,9},{9,8},{10,11... | collective-permute-start | bytes 14155784 | tf_op jit(solution)/shard_map/ppermute | solution.py:18
  71.2 12.9 %collective-permute-start.20 = (bf16[8,64,384]{2,1,0:T(8,128)(2,1)S(1)}, bf16[8,64,384]{2,1,0:T(8,128)(2,1)}, u32[]{:S(2)}, u32[]{:S(2)}) collective-permute-start(bf16[8,64,384]{2,1,0:T(8,128)(2,1)S(1)} %slice.93), channel_id=1, source_target_pairs={{0,8},{8,16},{16,24},{24,0},{1,9},{9,17},{17,25},{25,1},{2,10},{10... | collective-permute-start | bytes 1179656 | tf_op jit(solution)/shard_map/ppermute | solution.py:18
  72.3 12.6 %collective-permute-start.21 = (bf16[8,64,384]{2,1,0:T(8,128)(2,1)S(1)}, bf16[8,64,384]{2,1,0:T(8,128)(2,1)}, u32[]{:S(2)}, u32[]{:S(2)}) collective-permute-start(bf16[8,64,384]{2,1,0:T(8,128)(2,1)S(1)} %slice.94), channel_id=1, source_target_pairs={{0,24},{8,0},{16,8},{24,16},{1,25},{9,1},{17,9},{25,17},{2,26},{10... | collective-permute-start | bytes 1179656 | tf_op jit(solution)/shard_map/ppermute | solution.py:18
  76.4 18.6 %all-to-all-start = ((f32[16,6,8,128]{3,2,1,0:T(8,128)}), f32[16,6,8,128]{3,2,1,0:T(8,128)S(1)}, u32[]{:S(2)}, u32[]{:S(2)}) async-start(f32[16,6,8,128]{3,2,1,0:T(8,128)} %broadcast_in_dim.28), calls=%async_computation | async-start | bytes 786432 | tf_op jit(solution)/shard_map/all_to_all | solution.py:66
  95.0 1.8 %collective-permute-start.23 = (f32[96,8,128]{2,1,0:T(8,128)S(1)}, f32[96,8,128]{2,1,0:T(8,128)S(1)}, u32[]{:S(2)}, u32[]{:S(2)}) collective-permute-start(f32[96,8,128]{2,1,0:T(8,128)S(1)} %bitcast.138), channel_id=1, source_target_pairs={{0,1},{1,0},{2,3},{3,2},{4,5},{5,4},{6,7},{7,6},{8,9},{9,8},{10,11... | collective-permute-start | bytes 1179656 | tf_op jit(solution)/shard_map/ppermute | solution.py:18
  95.1 2.0 %copy-start.12 = (bf16[128,6144]{1,0:T(8,128)(2,1)S(1)}, bf16[128,6144]{1,0:T(8,128)(2,1)}, u32[]{:S(2)}) copy-start(bf16[128,6144]{1,0:T(8,128)(2,1)} %param.5) | copy-start | bytes 4718596
  96.9 0.9 copy-start.1
  97.8 6.3 %collective-permute-start.24 = (f32[32,128]{1,0:T(8,128)S(1)}, f32[32,128]{1,0:T(8,128)S(1)}, u32[]{:S(2)}, u32[]{:S(2)}) collective-permute-start(f32[32,128]{1,0:T(8,128)S(1)} %fusion.32), channel_id=1, source_target_pairs={{0,1},{1,0},{2,3},{3,2},{4,5},{5,4},{6,7},{7,6},{8,9},{9,8},{10,11... | collective-permute-start | bytes 49160 | tf_op jit(solution)/shard_map/ppermute | solution.py:18
  98.1 29.5 %collective-permute-start.31 = (bf16[128,1536]{1,0:T(8,128)(2,1)}, bf16[128,1536]{1,0:T(8,128)(2,1)S(1)}, u32[]{:S(2)}, u32[]{:S(2)}) collective-permute-start(bf16[128,1536]{1,0:T(8,128)(2,1)} %get-tuple-element.63), channel_id=1, source_target_pairs={{0,24},{8,0},{16,8},{24,16},{1,25},{9,1},{17,9},{25,17},{2,26},{10... | collective-permute-start | bytes 1179656 | tf_op jit(solution)/shard_map/ppermute | solution.py:18
  104.2 23.4 %collective-permute-start.32 = (bf16[128,1536]{1,0:T(8,128)(2,1)}, bf16[128,1536]{1,0:T(8,128)(2,1)S(1)}, u32[]{:S(2)}, u32[]{:S(2)}) collective-permute-start(bf16[128,1536]{1,0:T(8,128)(2,1)} %get-tuple-element.64), channel_id=1, source_target_pairs={{0,8},{8,16},{16,24},{24,0},{1,9},{9,17},{17,25},{25,1},{2,10},{10... | collective-permute-start | bytes 1179656 | tf_op jit(solution)/shard_map/ppermute | solution.py:18
  104.2 8.3 %collective-permute-start.25 = (f32[2,32,128]{2,1,0:T(8,128)S(1)}, f32[2,32,128]{2,1,0:T(8,128)S(1)}, u32[]{:S(2)}, u32[]{:S(2)}) collective-permute-start(f32[2,32,128]{2,1,0:T(8,128)S(1)} %pad_maximum_fusion.5), channel_id=1, source_target_pairs={{0,2},{2,4},{4,6},{6,0},{1,3},{3,5},{5,7},{7,1},{8,10},{10,12},{12... | collective-permute-start | bytes 98312 | tf_op jit(solution)/shard_map/ppermute | solution.py:18
  106.4 7.7 %collective-permute-start.26 = (f32[2,32,128]{2,1,0:T(8,128)S(1)}, f32[2,32,128]{2,1,0:T(8,128)S(1)}, u32[]{:S(2)}, u32[]{:S(2)}) collective-permute-start(f32[2,32,128]{2,1,0:T(8,128)S(1)} %pad_maximum_fusion.5), channel_id=1, source_target_pairs={{0,4},{2,6},{4,0},{6,2},{1,5},{3,7},{5,1},{7,3},{8,12},{10,14},{12... | collective-permute-start | bytes 98312 | tf_op jit(solution)/shard_map/ppermute | solution.py:18
  108.7 5.5 %collective-permute-start.27 = (f32[2,32,128]{2,1,0:T(8,128)S(1)}, f32[2,32,128]{2,1,0:T(8,128)S(1)}, u32[]{:S(2)}, u32[]{:S(2)}) collective-permute-start(f32[2,32,128]{2,1,0:T(8,128)S(1)} %pad_maximum_fusion.5), channel_id=1, source_target_pairs={{0,6},{2,0},{4,2},{6,4},{1,7},{3,1},{5,3},{7,5},{8,14},{10,8},{12,... | collective-permute-start | bytes 98312 | tf_op jit(solution)/shard_map/ppermute | solution.py:18
  112.4 20.3 %copy-start.6 = (bf16[128,1536]{1,0:T(8,128)(2,1)S(1)}, bf16[128,1536]{1,0:T(8,128)(2,1)}, u32[]{:S(2)}) copy-start(bf16[128,1536]{1,0:T(8,128)(2,1)} %get-tuple-element.69.refs_0_) | copy-start | bytes 1179652
  112.4 20.3 %copy-start.10 = (s32[12]{0:T(128)S(1)}, s32[12]{0:T(128)}, u32[]{:S(2)}) copy-start(s32[12]{0:T(128)} %stack.69.at_ref) | copy-start | bytes 148
  112.5 15.1 %collective-permute-start.33 = (bf16[128,1536]{1,0:T(8,128)(2,1)}, bf16[128,1536]{1,0:T(8,128)(2,1)S(1)}, u32[]{:S(2)}, u32[]{:S(2)}) collective-permute-start(bf16[128,1536]{1,0:T(8,128)(2,1)} %get-tuple-element.65), channel_id=1, source_target_pairs={{0,16},{8,24},{16,0},{24,8},{1,17},{9,25},{17,1},{25,9},{2,18},{10... | collective-permute-start | bytes 1179656 | tf_op jit(solution)/shard_map/ppermute | solution.py:18
  114.7 24.6 %copy-start.2 = (f32[2,96,8,128]{3,2,1,0:T(8,128)S(1)}, f32[2,96,8,128]{3,2,1,0:T(8,128)}, u32[]{:S(2)}) copy-start(f32[2,96,8,128]{3,2,1,0:T(8,128)} %copy-done.1) | copy-start | bytes 2359300
  114.7 5.8 %collective-permute-start.28 = (f32[32,384]{1,0:T(8,128)S(1)}, f32[32,384]{1,0:T(8,128)S(1)}, u32[]{:S(2)}, u32[]{:S(2)}) collective-permute-start(f32[32,384]{1,0:T(8,128)S(1)} %fusion.15), channel_id=1, source_target_pairs={{0,32},{32,64},{64,96},{96,0},{1,33},{33,65},{65,97},{97,1},{2,34}... | collective-permute-start | bytes 147464 | tf_op jit(solution)/shard_map/ppermute | solution.py:18
  116.8 10.7 %collective-permute-start.29 = (f32[32,384]{1,0:T(8,128)S(1)}, f32[32,384]{1,0:T(8,128)S(1)}, u32[]{:S(2)}, u32[]{:S(2)}) collective-permute-start(f32[32,384]{1,0:T(8,128)S(1)} %fusion.15), channel_id=1, source_target_pairs={{0,64},{32,96},{64,0},{96,32},{1,65},{33,97},{65,1},{97,33},{2,66}... | collective-permute-start | bytes 147464 | tf_op jit(solution)/shard_map/ppermute | solution.py:18
  120.5 7.0 %collective-permute-start.30 = (f32[32,384]{1,0:T(8,128)S(1)}, f32[32,384]{1,0:T(8,128)S(1)}, u32[]{:S(2)}, u32[]{:S(2)}) collective-permute-start(f32[32,384]{1,0:T(8,128)S(1)} %fusion.15), channel_id=1, source_target_pairs={{0,96},{32,0},{64,32},{96,64},{1,97},{33,1},{65,33},{97,65},{2,98}... | collective-permute-start | bytes 147464 | tf_op jit(solution)/shard_map/ppermute | solution.py:18
  127.5 8.0 %copy-start.8 = (f32[32,32]{1,0:T(8,128)S(1)}, f32[32,32]{1,0:T(8,128)}, u32[]{:S(2)}) copy-start(f32[32,32]{1,0:T(8,128)} %inverse_of_factor.1.inverse_ref) | copy-start | bytes 12292
  127.6 7.0 %collective-permute-start.34 = (f32[32,384]{1,0:T(8,128)S(1)}, f32[32,384]{1,0:T(8,128)S(1)}, u32[]{:S(2)}, u32[]{:S(2)}) collective-permute-start(f32[32,384]{1,0:T(8,128)S(1)} %add_add_fusion), channel_id=1, source_target_pairs={{0,8},{8,16},{16,24},{24,0},{1,9},{9,17},{17,25},{25,1},{2,10},{10... | collective-permute-start | bytes 147464 | tf_op jit(solution)/shard_map/ppermute | solution.py:18
  129.9 5.6 %collective-permute-start.35 = (f32[32,384]{1,0:T(8,128)S(1)}, f32[32,384]{1,0:T(8,128)S(1)}, u32[]{:S(2)}, u32[]{:S(2)}) collective-permute-start(f32[32,384]{1,0:T(8,128)S(1)} %add_add_fusion), channel_id=1, source_target_pairs={{0,16},{8,24},{16,0},{24,8},{1,17},{9,25},{17,1},{25,9},{2,18},{10... | collective-permute-start | bytes 147464 | tf_op jit(solution)/shard_map/ppermute | solution.py:18
  131.4 4.2 %collective-permute-start.36 = (f32[32,384]{1,0:T(8,128)S(1)}, f32[32,384]{1,0:T(8,128)S(1)}, u32[]{:S(2)}, u32[]{:S(2)}) collective-permute-start(f32[32,384]{1,0:T(8,128)S(1)} %add_add_fusion), channel_id=1, source_target_pairs={{0,24},{8,0},{16,8},{24,16},{1,25},{9,1},{17,9},{25,17},{2,26},{10... | collective-permute-start | bytes 147464 | tf_op jit(solution)/shard_map/ppermute | solution.py:18
  135.7 16.3 %copy-start.7 = (f32[32,384]{1,0:T(8,128)}, f32[32,384]{1,0:T(8,128)S(1)}, u32[]{:S(2)}) copy-start(f32[32,384]{1,0:T(8,128)S(1)} %convolution_multiply_fusion.factor_ref) | copy-start | bytes 147460
Sparse Core Ops, SparseCore 0:
  10.1 58.9 all-gather.5
  70.8 68.4 all-gather.3
